TPU v7x, 32 devices: a whole 2x2x4 slice. The times are simulated.
32 devices in a mesh: group: 2 (over y), tile: 4 (over x, core), seq: 4 (over z).
Axes of the slice: x: 2, y: 2, z: 4, core: 2. Of those that a mesh axis runs over, the one named last changes fastest.
Arguments:
- hidden: bfloat16 [8, 1024, 3072], P(('group', 'tile'), 'seq'), parts along dimension 0
- modulation: float32 [10, 3072], P('group'), parts along dimension 0, may hold values from -3 to 3
- w_qkv: bfloat16 [3072, 9216], P('tile', 'seq')
- w_out: bfloat16 [3072, 3072], P('seq', 'tile'), may hold values from -0.109375 to 0.109375
- w_head: bfloat16 [3072, 64], replicated, may hold values from -0.109375 to 0.109375
- latent: float32 [8, 1024, 64], P(('group', 'tile'), 'seq'), parts along dimension 0, may hold values from -6 to 6
- weights_int: int32 [8, 1024], P(('group', 'tile'), 'seq'), parts along dimension 0, may hold values from 1 to 8
- step_index: int32 [2], P('group'), parts along dimension 0, may hold values from 0 to 13
Outputs:
- stepped: float32 [8, 1024, 64], P(('group', 'tile'), 'seq'), parts along dimension 0
- clean: float32 [8, 1024, 64], P(('group', 'tile'), 'seq'), parts along dimension 0
There are 2 independent parts, one for each index of `group`. A program takes and returns all parts, laid end to end along the dimension named above; an argument that names none is the same for every part. Nothing has to cross between parts.
All inputs are finite; a program needn't handle non-finite values.
Results may differ from a plain program's by a relative error of at most 0.0055.
Values may be sent and summed in bfloat16 or wider, within the bound.
No kernel may reach another device: no remote copies, remote signals or barrier semaphores. Data moves between devices by JAX's collectives and lax.ppermute only.
A program may use at most 64 MiB of HBM per device.

v0:
```python
import math

import jax
import jax.numpy as jnp
from jax import lax
from jax.sharding import PartitionSpec as P

HD = 128
NSTEPS = 28


def shifted(value, axis, steps):
    count = lax.axis_size(axis)
    leading, last = (max(0, -steps), min(count, count - steps))
    return lax.ppermute(value, axis, [(source, source + steps) for source in range(leading, last)])


def layer_norm(values):
    mean = jnp.mean(values, axis=-1, keepdims=True)
    centred = values - mean
    spread = jnp.mean(centred * centred, axis=-1, keepdims=True)
    return centred * lax.rsqrt(spread + 1e-06)


def root_norm(values):
    return values * lax.rsqrt(jnp.mean(values * values, axis=-1, keepdims=True) + 1e-06)


def noise_level(index, steps):
    level = 1.0 - index / steps
    return 3.0 * level / (1.0 + 2.0 * level)


def shards(hidden, modulation, w_qkv, w_out, w_head, latent, weights_int, step_index):
    local = hidden[0].astype(jnp.float32)
    norm_in = (layer_norm(local) * (1.0 + modulation[1]) + modulation[0]).astype(jnp.bfloat16)
    gathered = lax.all_gather(norm_in, "seq", axis=0, tiled=True)
    length = gathered.shape[0]
    heads_here = w_qkv.shape[1] // (3 * HD)
    projected = jnp.dot(
        gathered,
        lax.all_gather(w_qkv, "tile", axis=0, tiled=True),
        preferred_element_type=jnp.float32,
    )
    full_out = lax.all_gather(w_out, "tile", axis=1, tiled=True)
    projected = projected.reshape(length, heads_here, 3, HD)
    queries = root_norm(projected[:, :, 0]).astype(jnp.bfloat16)
    keys = root_norm(projected[:, :, 1]).astype(jnp.bfloat16)
    values = projected[:, :, 2].astype(jnp.bfloat16)
    block = min(512, length)
    scale = 1.0 / math.sqrt(HD)
    pieces = []
    for first in range(0, length, block):
        scores = (
            jnp.einsum(
                "qhe,khe->hqk",
                queries[first : first + block],
                keys,
                preferred_element_type=jnp.float32,
            )
            * scale
        )
        expo = jnp.exp(scores)
        probs = (expo / jnp.sum(expo, axis=-1, keepdims=True)).astype(jnp.bfloat16)
        pieces.append(
            jnp.einsum("hqk,khe->qhe", probs, values, preferred_element_type=jnp.float32).astype(
                jnp.bfloat16
            )
        )
    attended = jnp.concatenate(pieces, axis=0).reshape(length, heads_here * HD)
    summed = lax.psum_scatter(
        jnp.dot(attended, full_out, preferred_element_type=jnp.float32).astype(jnp.bfloat16),
        "seq",
        scatter_dimension=0,
        tiled=True,
    ).astype(jnp.float32)
    mixed = local + modulation[2] * summed
    norm_out = (layer_norm(mixed) * (1.0 + modulation[4]) + modulation[3]).astype(jnp.bfloat16)
    velocity = jnp.dot(norm_out, w_head, preferred_element_type=jnp.float32)
    index = step_index[0].astype(jnp.float32)
    now = noise_level(index, NSTEPS)
    after = noise_level(index + 1.0, NSTEPS)
    base = latent[0]
    weight = weights_int[0].astype(jnp.float32)
    moved = base + (after - now) * velocity
    guess = base - now * velocity
    weighted = jnp.concatenate([moved, guess], axis=1) * weight[:, None]
    seq_count = lax.axis_size("seq")
    place = lax.axis_index("seq")
    prev_tile = (
        shifted(weighted.astype(jnp.bfloat16), "tile", 1).astype(weighted.dtype),
        shifted(weight.astype(jnp.bfloat16), "tile", 1).astype(weight.dtype),
    )
    prev_sums, prev_weight = (
        shifted(prev_tile[0].astype(jnp.bfloat16), "seq", -(seq_count - 2)).astype(jnp.float32),
        shifted(prev_tile[1].astype(jnp.bfloat16), "seq", -(seq_count - 2)).astype(jnp.float32),
    )
    next_tile = (
        shifted(weighted.astype(jnp.bfloat16), "tile", -1).astype(weighted.dtype),
        shifted(weight.astype(jnp.bfloat16), "tile", -1).astype(weight.dtype),
    )
    next_sums, next_weight = (
        shifted(next_tile[0].astype(jnp.bfloat16), "seq", seq_count - 2).astype(jnp.float32),
        shifted(next_tile[1].astype(jnp.bfloat16), "seq", seq_count - 2).astype(jnp.float32),
    )
    take_prev = place < 2
    take_next = place >= seq_count - 2
    totals = weighted + jnp.where(take_prev, prev_sums, 0.0) + jnp.where(take_next, next_sums, 0.0)
    norms = weight + jnp.where(take_prev, prev_weight, 0.0) + jnp.where(take_next, next_weight, 0.0)
    joined = totals / norms[:, None]
    channels = velocity.shape[1]
    return (joined[None, :, :channels], joined[None, :, channels:])


def solution(mesh):
    in_specs = (
        P(("group", "tile"), "seq", None),
        P("group", None),
        P("tile", "seq"),
        P("seq", "tile"),
        P(),
        P(("group", "tile"), "seq", None),
        P(("group", "tile"), "seq"),
        P("group"),
    )
    out_specs = (P(("group", "tile"), "seq", None), P(("group", "tile"), "seq", None))
    return jax.shard_map(shards, mesh=mesh, in_specs=in_specs, out_specs=out_specs, check_vma=False)
```

profile of v0, /device:TPU:1, one launch (start us, length us, event | category | flops | bytes accessed | tf_op | source)
XLA Modules:
  0.0 436.5 jit_solution(16859526870282650366)
XLA Ops:
  7.2 1.9 fusion.30
  9.1 1.7 convert_reduce_fusion
  10.8 2.0 fusion.8
  12.8 1.9 fusion.11
  16.3 116.3 %all-gather.4.cloned.1.call-done = bf16[1024,3072]{1,0:T(8,128)(2,1)} async-done(((bf16[256,3072]{1,0:T(8,128)(2,1)}), bf16[1024,3072]{1,0:T(8,128)(2,1)}) %all-gather.4.cloned.1.call-update) | async-done | bytes 6291472 | tf_op jit(solution)/shard_map/all_gather | solution.py:37
  132.6 91.1 %all-gather.6.cloned.1.call-done = bf16[3072,2304]{1,0:T(8,128)(2,1)} async-done(((bf16[768,2304]{1,0:T(8,128)(2,1)}), bf16[3072,2304]{1,0:T(8,128)(2,1)}) %all-gather.6.cloned.1.call-update) | async-done | bytes 14155792 | tf_op jit(solution)/shard_map/all_gather | solution.py:42
  223.6 19.6 %fusion.31 = f32[1024,2304]{0,1:T(8,128)S(1)} fusion(bf16[1024,3072]{1,0:T(8,128)(2,1)} %all-gather.4.cloned.1.call-done, bf16[3072,2304]{1,0:T(8,128)(2,1)} %all-gather.6.cloned.1.call-done), kind=kOutput, calls=%fused_computation.60 | convolution fusion | flops 14495514624 | bytes 29884416 | tf_op jit(solution)/shard_map/dot_general | solution.py:40
  243.2 3.5 copy-done.3
  246.8 2.0 slice.50
  248.8 3.6 copy.21
  252.4 2.9 fusion.12
  255.3 2.3 multiply_reduce_fusion.1
  257.7 1.0 fusion.13
  258.7 8.2 %fusion = (f32[6,512]{1,0:T(8,128)S(1)}, f32[6,512,1024]{2,1,0:T(8,128)}) fusion(f32[1024,6,3,128]{0,3,2,1:T(8,128)} %bitcast.78, f32[1024,6]{0,1:T(8,128)S(1)} %add_rsqrt_fusion, bf16[1024,6,128]{2,0,1:T(8,128)(2,1)S(1)} %fusion.13), kind=kOutput, calls=%fused_computation.4 | convolution fusion | flops 813167616 | bytes 16560128 | tf_op jit(solution)/shard_map/qhe,khe->hqk/dot_general | solution.py:55
  266.9 2.7 fusion.1
  269.6 6.0 %fusion.19 = bf16[512,6,128]{0,2,1:T(8,128)(2,1)S(1)} fusion(f32[6,512,1024]{2,1,0:T(8,128)} %get-tuple-element.14, f32[6,512]{1,0:T(8,128)S(1)} %get-tuple-element.13, f32[1024,6,3,128]{0,3,2,1:T(8,128)S(1)} %bitcast.82), kind=kOutput, calls=%fused_computation.35 | convolution fusion | flops 815136768 | bytes 14958592 | tf_op jit(solution)/shard_map/hqk,khe->qhe/dot_general | solution.py:66
  275.6 2.9 fusion.20
  278.8 9.5 %convolution_convert_fusion = bf16[1024,3072]{1,0:T(8,128)(2,1)} fusion(bf16[1024,768]{0,1:T(8,128)(2,1)S(1)} %bitcast.84, bf16[768,3072]{1,0:T(8,128)(2,1)} %all-gather.8.cloned.1.call-done), kind=kOutput, calls=%fused_computation.8 | convolution fusion | flops 4834983936 | bytes 12582912 | tf_op jit(solution)/shard_map/dot_general | solution.py:72
  289.1 109.8 %reduce-scatter.2.cloned.1.call-done = bf16[256,3072]{1,0:T(8,128)(2,1)} async-done(((bf16[1024,3072]{1,0:T(8,128)(2,1)}), bf16[256,3072]{1,0:T(8,128)(2,1)}) %reduce-scatter.2.cloned.1.call-update) | async-done | bytes 1572880 | tf_op jit(solution)/shard_map/reduce_scatter | solution.py:71
  399.0 2.1 fusion.14
  401.1 0.8 multiply_reduce_fusion
  402.0 1.1 bitcast_add_fusion
  403.1 3.6 collective-permute-start
  406.7 1.9 collective-permute-start.2
  408.6 3.6 collective-permute-start.4
  412.3 1.9 collective-permute-start.6
  414.2 1.3 collective-permute-start.5
  415.5 1.6 collective-permute-done.6
  417.1 4.5 %collective-permute-start.7 = (bf16[256]{0:T(256)(128)(2,1)S(1)}, bf16[256]{0:T(256)(128)(2,1)S(1)}, u32[]{:S(2)}, u32[]{:S(2)}) collective-permute-start(bf16[256]{0:T(256)(128)(2,1)S(1)} %collective-permute-done.6), channel_id=1, source_target_pairs={{0,2},{1,3},{4,6},{5,7},{8,10},{9,11},{12,14},{13,15},{16,18},{17,... | collective-permute-start | bytes 1544 | tf_op jit(solution)/shard_map/ppermute | solution.py:15
  421.7 1.3 collective-permute-start.1
  423.0 4.9 %collective-permute-start.3 = (bf16[256,128]{0,1:T(8,128)(2,1)S(1)}, bf16[256,128]{0,1:T(8,128)(2,1)S(1)}, u32[]{:S(2)}, u32[]{:S(2)}) collective-permute-start(bf16[256,128]{0,1:T(8,128)(2,1)S(1)} %collective-permute-done.2), channel_id=1, source_target_pairs={{0,2},{1,3},{4,6},{5,7},{8,10},{9,11},{12,14},{13,15},{16,18},{17,... | collective-permute-start | bytes 196616 | tf_op jit(solution)/shard_map/ppermute | solution.py:15
  428.5 0.7 collective-permute-done.3
  (52 shorter events, 3.2 us)
Async XLA Ops:
  7.2 394.8 %copy-start = (bf16[3072,64]{0,1:T(8,128)(2,1)S(1)}, bf16[3072,64]{0,1:T(8,128)(2,1)}, u32[]{:S(2)}) copy-start(bf16[3072,64]{0,1:T(8,128)(2,1)} %param.12) | copy-start | bytes 1179652
  7.2 5.6 %copy-start.1 = (bf16[1,256,3072]{2,1,0:T(8,128)(2,1)S(1)}, bf16[1,256,3072]{2,1,0:T(8,128)(2,1)}, u32[]{:S(2)}) copy-start(bf16[1,256,3072]{2,1,0:T(8,128)(2,1)} %param.8) | copy-start | bytes 4718596
  7.2 125.4 %all-gather.4.cloned.1.call-start = ((), (), s32[]{:S(2)}) async-start(), calls=%async_computation.1 | async-start | bytes 7864320 | tf_op jit(solution)/shard_map/all_gather | solution.py:37
  14.8 208.9 %all-gather.6.cloned.1.call-start = ((), (), s32[]{:S(2)}) async-start(), calls=%async_computation.2 | async-start | bytes 17694720 | tf_op jit(solution)/shard_map/all_gather | solution.py:42
  15.5 263.3 %all-gather.8.cloned.1.call-start = ((), (), s32[]{:S(2)}) async-start(), calls=%async_computation.3 | async-start | bytes 5898240 | tf_op jit(solution)/shard_map/all_gather | solution.py:45
  16.3 382.7 %reduce-scatter.2.cloned.1.call-start = ((), (), s32[]{:S(2)}) async-start(), calls=%async_computation.4 | async-start | bytes 7864320 | tf_op jit(solution)/shard_map/reduce_scatter | solution.py:71
  243.2 3.6 copy-start.3
  252.4 5.3 %copy-start.2 = (f32[1024,6,1,128]{3,0,1,2:T(8,128)S(1)}, f32[1024,6,1,128]{3,0,1,2:T(8,128)}, u32[]{:S(2)}) copy-start(f32[1024,6,1,128]{3,0,1,2:T(8,128)} %copy.21) | copy-start | bytes 9437188
  257.7 9.2 %slice-start = ((s8[9437184]{0:T(1024)(128)(4,1)}), s8[4194304]{0:T(1024)(128)(4,1)S(1)}, s32[]{:S(2)}) async-start(s8[9437184]{0:T(1024)(128)(4,1)} %bitcast.79), calls=%async_computation.5 | async-start | bytes 8388608
  258.7 8.3 %slice-start.1 = ((s8[9437184]{0:T(1024)(128)(4,1)}), s8[4194304]{0:T(1024)(128)(4,1)S(1)}, s32[]{:S(2)}) async-start(s8[9437184]{0:T(1024)(128)(4,1)} %bitcast.79), calls=%async_computation.6 | async-start | bytes 8388608
  258.7 8.2 %slice-start.2 = ((s8[9437184]{0:T(1024)(128)(4,1)}), s8[1048576]{0:T(1024)(128)(4,1)S(1)}, s32[]{:S(2)}) async-start(s8[9437184]{0:T(1024)(128)(4,1)} %bitcast.79), calls=%async_computation.7 | async-start | bytes 2097152
  288.3 0.7 copy-start.7
  399.0 2.1 copy-start.4
  399.0 3.0 copy-start.5
  399.0 3.0 copy-start.6
  399.0 3.0 copy-start.8
  403.1 18.6 %collective-permute-start = (bf16[256,128]{0,1:T(8,128)(2,1)S(1)}, bf16[256,128]{0,1:T(8,128)(2,1)S(1)}, u32[]{:S(2)}, u32[]{:S(2)}) collective-permute-start(bf16[256,128]{0,1:T(8,128)(2,1)S(1)} %fusion.27), channel_id=1, source_target_pairs={{0,4},{4,8},{8,12},{1,5},{5,9},{9,13},{2,6},{6,10},{10,14},{3,7},{... | collective-permute-start | bytes 196616 | tf_op jit(solution)/shard_map/ppermute | solution.py:15
  406.7 16.3 %collective-permute-start.2 = (bf16[256,128]{0,1:T(8,128)(2,1)S(1)}, bf16[256,128]{0,1:T(8,128)(2,1)S(1)}, u32[]{:S(2)}, u32[]{:S(2)}) collective-permute-start(bf16[256,128]{0,1:T(8,128)(2,1)S(1)} %fusion.27), channel_id=1, source_target_pairs={{4,0},{8,4},{12,8},{5,1},{9,5},{13,9},{6,2},{10,6},{14,10},{7,3},{... | collective-permute-start | bytes 196616 | tf_op jit(solution)/shard_map/ppermute | solution.py:15
  408.6 5.6 %collective-permute-start.4 = (bf16[256]{0:T(256)(128)(2,1)S(1)}, bf16[256]{0:T(256)(128)(2,1)S(1)}, u32[]{:S(2)}, u32[]{:S(2)}) collective-permute-start(bf16[256]{0:T(256)(128)(2,1)S(1)} %convert_element_type.109), channel_id=1, source_target_pairs={{0,4},{4,8},{8,12},{1,5},{5,9},{9,13},{2,6},{6,10},{10,14},{3,7},{... | collective-permute-start | bytes 1544 | tf_op jit(solution)/shard_map/ppermute | solution.py:15
  412.3 4.9 %collective-permute-start.6 = (bf16[256]{0:T(256)(128)(2,1)S(1)}, bf16[256]{0:T(256)(128)(2,1)S(1)}, u32[]{:S(2)}, u32[]{:S(2)}) collective-permute-start(bf16[256]{0:T(256)(128)(2,1)S(1)} %convert_element_type.109), channel_id=1, source_target_pairs={{4,0},{8,4},{12,8},{5,1},{9,5},{13,9},{6,2},{10,6},{14,10},{7,3},{... | collective-permute-start | bytes 1544 | tf_op jit(solution)/shard_map/ppermute | solution.py:15
  414.2 13.7 %collective-permute-start.5 = (bf16[256]{0:T(256)(128)(2,1)S(1)}, bf16[256]{0:T(256)(128)(2,1)S(1)}, u32[]{:S(2)}, u32[]{:S(2)}) collective-permute-start(bf16[256]{0:T(256)(128)(2,1)S(1)} %collective-permute-done.4), channel_id=1, source_target_pairs={{2,0},{3,1},{6,4},{7,5},{10,8},{11,9},{14,12},{15,13},{18,16},{19,... | collective-permute-start | bytes 1544 | tf_op jit(solution)/shard_map/ppermute | solution.py:15
  417.1 10.8 %collective-permute-start.7 = (bf16[256]{0:T(256)(128)(2,1)S(1)}, bf16[256]{0:T(256)(128)(2,1)S(1)}, u32[]{:S(2)}, u32[]{:S(2)}) collective-permute-start(bf16[256]{0:T(256)(128)(2,1)S(1)} %collective-permute-done.6), channel_id=1, source_target_pairs={{0,2},{1,3},{4,6},{5,7},{8,10},{9,11},{12,14},{13,15},{16,18},{17,... | collective-permute-start | bytes 1544 | tf_op jit(solution)/shard_map/ppermute | solution.py:15
  421.7 6.8 %collective-permute-start.1 = (bf16[256,128]{0,1:T(8,128)(2,1)S(1)}, bf16[256,128]{0,1:T(8,128)(2,1)S(1)}, u32[]{:S(2)}, u32[]{:S(2)}) collective-permute-start(bf16[256,128]{0,1:T(8,128)(2,1)S(1)} %collective-permute-done), channel_id=1, source_target_pairs={{2,0},{3,1},{6,4},{7,5},{10,8},{11,9},{14,12},{15,13},{18,16},{19,... | collective-permute-start | bytes 196616 | tf_op jit(solution)/shard_map/ppermute | solution.py:15
  423.0 6.2 %collective-permute-start.3 = (bf16[256,128]{0,1:T(8,128)(2,1)S(1)}, bf16[256,128]{0,1:T(8,128)(2,1)S(1)}, u32[]{:S(2)}, u32[]{:S(2)}) collective-permute-start(bf16[256,128]{0,1:T(8,128)(2,1)S(1)} %collective-permute-done.2), channel_id=1, source_target_pairs={{0,2},{1,3},{4,6},{5,7},{8,10},{9,11},{12,14},{13,15},{16,18},{17,... | collective-permute-start | bytes 196616 | tf_op jit(solution)/shard_map/ppermute | solution.py:15
Sparse Core Ops, SparseCore 0:
  14.9 117.6 all-gather.3
  134.1 89.4 all-gather.5
  225.2 37.4 all-gather.7
  288.5 110.4 reduce-scatter.1
where the time goes:
time: 438 us; the launch traced here: 436 us
  waiting for transfers between devices  321 us (73%)
  matrix products  50 us (11%)
  starting transfers between devices  23.3 us (5%)
  other arithmetic  16.9 us (4%)
  between operations  14.9 us (3%)
  local copies, waits for them, and re-layouts  9.88 us (2%)
    all_gather x1, waiting for transfers between devices, shards(): gathered = lax.all_gather(norm_in, 'seq', axis=0, tiled=True)  116 us
    reduce_scatter x1, waiting for transfers between devices, shards(): lax.psum_scatter(jnp.dot(attended, full_out, preferred_element_type=jnp.f...  110 us
    all_gather x1, waiting for transfers between devices, shards(): lax.all_gather(w_qkv, 'tile', axis=0, tiled=True)  91.1 us
    ppermute x8, starting transfers between devices, shifted(): lax.ppermute(value, axis, [(source, source + steps) for source in range(l...  23.1 us
    dot_general x1, matrix products, shards(): jnp.dot(gathered, lax.all_gather(w_qkv, 'tile', axis=0, tiled=True), pref...  19.6 us
    dot_general x2, matrix products, shards(): jnp.einsum('qhe,khe->hqk', queries[first:first + block], keys, preferred_...  10.9 us
    dot_general x1, matrix products, shards(): jnp.dot(attended, full_out, preferred_element_type=jnp.float32)  9.54 us
    dot_general x2, matrix products, shards(): jnp.einsum('hqk,khe->qhe', probs, values, preferred_element_type=jnp.floa...  8.92 us
  transfers between devices with their start and end apart: 12, of which 6 were waited for; matrix products, arithmetic and copies ran while one was open for 12% of the time, Pallas kernels for 0%

commit v1 on v0

v1 whole, which is shorter than its diff:
```python
import functools
import math

import jax
import jax.numpy as jnp
from jax import lax
from jax.experimental import pallas as pl
from jax.experimental.pallas import tpu as pltpu
from jax.sharding import PartitionSpec as P

HD = 128
NSTEPS = 28
CHUNKS = 2
MIB = 1 << 20


def swap(value, axis, bit):
    count = lax.axis_size(axis)
    return lax.ppermute(value, axis, [(i, i ^ bit) for i in range(count)])


def bits_of(count):
    far = [1 << n for n in range(1, count.bit_length() - 1)]
    return far + [1]


def noise_level(index, steps):
    level = 1.0 - index / steps
    return 3.0 * level / (1.0 + 2.0 * level)


def layer_norm(values):
    mean = jnp.mean(values, axis=-1, keepdims=True)
    centred = values - mean
    spread = jnp.mean(centred * centred, axis=-1, keepdims=True)
    return centred * lax.rsqrt(spread + 1e-06)


def norm_kernel(blocks, starts_ref, hidden_ref, mod_ref, out_ref):
    local = hidden_ref[...].astype(jnp.float32)
    mean = jnp.mean(local, axis=-1, keepdims=True)
    centred = local - mean
    spread = jnp.mean(centred * centred, axis=-1, keepdims=True)
    scaling = lax.rsqrt(spread + 1e-06)
    width = hidden_ref.shape[1] // blocks
    for n in range(blocks):
        taken = pl.ds(pl.multiple_of(starts_ref[n], HD), width)
        values = (hidden_ref[:, taken].astype(jnp.float32) - mean) * scaling
        values = values * (1.0 + mod_ref[1:2, taken]) + mod_ref[0:1, taken]
        out_ref[:, n * width : (n + 1) * width] = values.astype(jnp.bfloat16)


def norm_rows(hidden, modulation, starts, chunk, rows):
    width = hidden.shape[1]
    block = math.gcd(rows, 64)
    steps = rows // block
    return pl.pallas_call(
        functools.partial(norm_kernel, starts.shape[0]),
        grid=(steps,),
        in_specs=[
            pl.BlockSpec(memory_space=pltpu.SMEM),
            pl.BlockSpec((block, width), lambda i: (chunk * steps + i, 0)),
            pl.BlockSpec(modulation.shape, lambda i: (0, 0)),
        ],
        out_specs=pl.BlockSpec((block, width), lambda i: (i, 0)),
        out_shape=jax.ShapeDtypeStruct((rows, width), jnp.bfloat16),
        name="norm_in",
    )(starts, hidden, modulation)


def qkv_kernel(blocks, x_ref, *refs):
    q_ref, k_ref, v_ref = refs[-3:]
    height = x_ref.shape[1] // blocks
    proj = 0.0
    for n in range(blocks):
        proj += jnp.dot(
            x_ref[:, n * height : (n + 1) * height],
            refs[n][...],
            preferred_element_type=jnp.float32,
        )
    shape = q_ref.shape

    def rooted(part):
        spread = jnp.mean(part * part, axis=-1, keepdims=True)
        return (part * lax.rsqrt(spread + 1e-06)).astype(jnp.bfloat16)

    q_ref[...] = rooted(proj[:, :HD]).reshape(shape)
    k_ref[...] = rooted(proj[:, HD : 2 * HD]).reshape(shape)
    v_ref[...] = proj[:, 2 * HD :].astype(jnp.bfloat16).reshape(shape)


def project(x, blocks, chunk, devices, before):
    length, width = x.shape
    rows = length // devices
    count = len(blocks)
    total = blocks[0].shape[1]
    heads = total // (3 * HD)
    out = jax.ShapeDtypeStruct((heads, devices, CHUNKS, rows, HD), jnp.bfloat16)
    spec = pl.BlockSpec((1, devices, 1, rows, HD), lambda h: (h, 0, chunk, 0, 0))
    return pl.pallas_call(
        functools.partial(qkv_kernel, count),
        grid=(heads,),
        in_specs=[pl.BlockSpec((length, width), lambda h: (0, 0))]
        + [pl.BlockSpec((width // count, 3 * HD), lambda h: (0, h))] * count
        + [pl.BlockSpec(memory_space=pl.ANY)] * len(before),
        out_specs=[spec] * 3,
        out_shape=[out] * 3,
        input_output_aliases={1 + count + i: i for i in range(len(before))},
        compiler_params=pltpu.CompilerParams(vmem_limit_bytes=40 * MIB),
        cost_estimate=pl.CostEstimate(
            flops=2 * length * width * total,
            bytes_accessed=2 * (length * width + width * total * 2),
            transcendentals=0,
        ),
        name="project",
    )(x, *blocks, *before)


def attend_kernel(dest_ref, q_ref, k_ref, v_ref, out_ref):
    scores = lax.dot_general(
        q_ref[0, 0], k_ref[0], (((1,), (1,)), ((), ())), preferred_element_type=jnp.float32
    )
    expo = jnp.exp(scores * (1.0 / math.sqrt(HD)))
    total = jnp.sum(expo, axis=-1, keepdims=True)
    mixed = jnp.dot(expo.astype(jnp.bfloat16), v_ref[0], preferred_element_type=jnp.float32)
    out_ref[...] = (mixed / total).astype(jnp.bfloat16)


def attend(dest, queries, keys, values):
    heads, devices, rows, _ = queries.shape
    length = devices * rows
    whole = pl.BlockSpec((1, length, HD), lambda h, dest: (h, 0, 0))
    return pl.pallas_call(
        attend_kernel,
        grid_spec=pltpu.PrefetchScalarGridSpec(
            num_scalar_prefetch=1,
            grid=(heads,),
            in_specs=[
                pl.BlockSpec((1, 1, rows, HD), lambda h, dest: (h, dest[0], 0, 0)),
                whole,
                whole,
            ],
            out_specs=pl.BlockSpec((rows, HD), lambda h, dest: (0, h)),
        ),
        out_shape=jax.ShapeDtypeStruct((rows, heads * HD), jnp.bfloat16),
        compiler_params=pltpu.CompilerParams(vmem_limit_bytes=40 * MIB),
        cost_estimate=pl.CostEstimate(
            flops=4 * rows * length * heads * HD,
            bytes_accessed=2 * heads * HD * 2 * (rows + length),
            transcendentals=rows * length * heads,
        ),
        name="attend",
    )(
        dest.reshape(1),
        queries,
        keys.reshape(heads, length, HD),
        values.reshape(heads, length, HD),
    )


def finish_kernel(devices, pieces, place_ref, coef_ref, *refs):
    parts = refs[:devices]
    sources = refs[devices : devices + pieces]
    hidden_ref, mod_ref, head_ref, latent_ref, weight_ref = refs[
        devices + pieces : devices + pieces + 5
    ]
    out_ref, sent_ref, weights, attended, mixed, sems = refs[devices + pieces + 5 :]
    copies = [
        pltpu.make_async_copy(sources[p], weights.at[p], sems.at[p]) for p in range(pieces)
    ]
    for copy in copies:
        copy.start()
    features = parts[0].shape[1]
    place = place_ref[0]
    for k in range(devices):
        origin = lax.rem(place - k + devices, devices)
        attended[:, pl.ds(pl.multiple_of(origin * features, HD), features)] = parts[k][...]
    width = weights.shape[2]
    for p in range(pieces):
        copies[p].wait()
        summed = jnp.dot(attended[...], weights[p], preferred_element_type=jnp.float32)
        cols = slice(p * width, (p + 1) * width)
        mixed[:, cols] = hidden_ref[:, cols].astype(jnp.float32) + mod_ref[2:3, cols] * summed
    normed = layer_norm(mixed[...]) * (1.0 + mod_ref[4:5, :]) + mod_ref[3:4, :]
    velocity = lax.dot_general(
        head_ref[...],
        normed.astype(jnp.bfloat16),
        (((1,), (1,)), ((), ())),
        preferred_element_type=jnp.float32,
    )
    channels = velocity.shape[0]
    base, weight = latent_ref[...], weight_ref[...]
    moved = (base + coef_ref[1] * velocity) * weight
    guess = (base - coef_ref[0] * velocity) * weight
    out_ref[:channels, :] = moved
    out_ref[channels:, :] = guess
    sent_ref[:channels, :] = moved.astype(jnp.bfloat16)
    sent_ref[channels:, :] = guess.astype(jnp.bfloat16)


def finish(place, coef, parts, pieces, hidden, modulation, head, latent, weight):
    devices, count = len(parts), len(pieces)
    rows, width = hidden.shape
    channels = head.shape[0]
    smem = pl.BlockSpec(memory_space=pltpu.SMEM)
    vmem = pl.BlockSpec(memory_space=pltpu.VMEM)
    hbm = pl.BlockSpec(memory_space=pl.ANY)
    return pl.pallas_call(
        functools.partial(finish_kernel, devices, count),
        in_specs=[smem, smem] + [vmem] * devices + [hbm] * count + [vmem] * 5,
        out_specs=[vmem, vmem],
        out_shape=[
            jax.ShapeDtypeStruct((2 * channels, rows), jnp.float32),
            jax.ShapeDtypeStruct((2 * channels, rows), jnp.bfloat16),
        ],
        scratch_shapes=[
            pltpu.VMEM((count,) + pieces[0].shape, jnp.bfloat16),
            pltpu.VMEM((rows, width), jnp.bfloat16),
            pltpu.VMEM((rows, width), jnp.float32),
            pltpu.SemaphoreType.DMA((count,)),
        ],
        compiler_params=pltpu.CompilerParams(vmem_limit_bytes=56 * MIB),
        cost_estimate=pl.CostEstimate(
            flops=2 * rows * width * width,
            bytes_accessed=2 * width * width,
            transcendentals=0,
        ),
        name="finish",
    )(place.reshape(1), coef, *parts, *pieces, hidden, modulation, head, latent, weight)


def shards(hidden, modulation, w_qkv, w_out, w_head, latent, weights_int, step_index):
    local = hidden[0]
    rows = local.shape[0]
    devices = lax.axis_size("seq")
    tiles = lax.axis_size("tile")
    groups = lax.axis_size("group")
    place, tile, group = lax.axis_index("seq"), lax.axis_index("tile"), lax.axis_index("group")

    weight = weights_int.astype(jnp.float32)
    joins = [
        (t * devices + s, (t + 1) * devices + s - (devices - 2))
        for t in range(tiles - 1)
        for s in range(devices - 2, devices)
    ]
    joins += [
        (t * devices + s, (t - 1) * devices + s + (devices - 2))
        for t in range(1, tiles)
        for s in range(2)
    ]
    norms = weight + lax.ppermute(
        weight.astype(jnp.bfloat16), ("tile", "seq"), joins
    ).astype(jnp.float32)

    part = w_out.shape[1] // groups
    share = lax.dynamic_slice_in_dim(w_out, group * part, part, axis=1)
    columns = {(0, 0): lax.all_gather(share, "seq", axis=0, tiled=True)}

    height = w_qkv.shape[0]
    blocks = {0: w_qkv}
    for bit in bits_of(tiles):
        blocks.update({d ^ bit: swap(blocks[d], "tile", bit) for d in list(blocks)})
    starts = jnp.stack([(tile ^ d) * height for d in range(tiles)]).astype(jnp.int32)
    if height % HD:
        full = jnp.zeros((tiles * height, w_qkv.shape[1]), w_qkv.dtype)
        for d in range(tiles):
            full = lax.dynamic_update_slice_in_dim(full, blocks[d], starts[d], axis=0)
        blocks = {0: full}
        starts = jnp.zeros((1,), jnp.int32)
    blocks = [blocks[d] for d in range(len(blocks))]

    count = rows // CHUNKS
    gathered = [
        lax.all_gather(norm_rows(local, modulation, starts, c, count), "seq", axis=0, tiled=True)
        for c in range(CHUNKS)
    ]

    far, near = bits_of(tiles)[:-1], bits_of(tiles)[-1]
    for bit in far:
        columns.update({(d ^ bit, g): swap(columns[d, g], "tile", bit) for d, g in list(columns)})
    if groups > 1:
        for turn in range(1, groups):
            pairs = [(g, (g + turn) % groups) for g in range(groups)]
            columns.update(
                {
                    (d, turn): lax.ppermute(columns[d, 0], "group", pairs)
                    for d, g in list(columns)
                    if g == 0
                }
            )
    columns.update({(d ^ near, g): swap(columns[d, g], "tile", near) for d, g in list(columns)})
    order = sorted(columns)

    def reorder(value, axis):
        return jnp.concatenate(
            [
                lax.dynamic_slice_in_dim(
                    value,
                    (tile ^ d) * (part * groups) + lax.rem(group - g + groups, groups) * part,
                    part,
                    axis=axis,
                )
                for d, g in order
            ],
            axis=axis,
        )

    hidden_by = reorder(local, 1)
    modulation_by = reorder(modulation, 1)
    head_by = reorder(w_head.T, 1)
    pieces = [columns[key] for key in order]
    if part % HD:
        pieces = [jnp.concatenate(pieces, axis=1)]

    state = ()
    for c in range(CHUNKS):
        state = project(gathered[c], blocks, c, devices, state)
    heads = w_qkv.shape[1] // (3 * HD)
    queries, keys, values = [value.reshape(heads, devices, rows, HD) for value in state]

    parts = {}
    for turn in list(range(1, devices)) + [0]:
        done = attend(lax.rem(place + turn, devices), queries, keys, values)
        if turn:
            done = lax.ppermute(done, "seq", [(s, (s + turn) % devices) for s in range(devices)])
        parts[turn] = done

    index = step_index[0].astype(jnp.float32)
    now = noise_level(index, NSTEPS)
    after = noise_level(index + 1.0, NSTEPS)
    weighted, sent = finish(
        place,
        jnp.stack([now, after - now]),
        [parts[turn] for turn in range(devices)],
        pieces,
        hidden_by,
        modulation_by,
        head_by,
        latent[0].T,
        weight,
    )
    other = lax.ppermute(sent, ("tile", "seq"), joins).astype(jnp.float32)
    joined = (weighted + other) / norms
    channels = w_head.shape[1]
    return (joined[:channels].T[None], joined[channels:].T[None])


def solution(mesh):
    in_specs = (
        P(("group", "tile"), "seq", None),
        P("group", None),
        P("tile", "seq"),
        P("seq", "tile"),
        P(),
        P(("group", "tile"), "seq", None),
        P(("group", "tile"), "seq"),
        P("group"),
    )
    out_specs = (P(("group", "tile"), "seq", None), P(("group", "tile"), "seq", None))
    return jax.shard_map(shards, mesh=mesh, in_specs=in_specs, out_specs=out_specs, check_vma=False)
```

time: 438 us -> 323 us (0.74)
  waiting for transfers between devices: 321 us -> 186 us
  Pallas kernels: 0 us -> 57.2 us
  matrix products: 50 us -> 0 us
  local copies, waits for them, and re-layouts: 9.88 us -> 36.3 us
  other arithmetic: 16.9 us -> 2.63 us
    all_gather x3, waiting for transfers between devices: 207 us -> 47.3 us  [the longest x1 47.3 us: shards(): columns = {(0, 0): lax.all_gather(share, 'seq', axis=0, tiled=True)}]
    ppermute x8 -> x15, waiting for transfers between devices: 2.91 us -> 139 us  [the longest x8 71.1 us: swap(): return lax.ppermute(value, axis, [(i, i ^ bit) for i in range(count)])]
    reduce_scatter x1 -> x0, waiting for transfers between devices: 110 us -> none  [shards(): lax.psum_scatter(jnp.dot(attended, full_out, preferred_element_type=jnp.f...]
    pallas_call x0 -> x9, Pallas kernels: none -> 57.2 us  [the longest x2 26.6 us: project(): pl.pallas_call(functools.partial(qkv_kernel, count), grid=(heads,), in_sp...]
    dot_general x7 -> x0, matrix products: 50 us -> none  [the longest x1 19.6 us: shards(): jnp.dot(gathered, lax.all_gather(w_qkv, 'tile', axis=0, tiled=True), pref...]
    unnamed x25 -> x69, local copies, waits for them, and re-layouts: 7.17 us -> 32.3 us
    reduce_sum x6 -> x0, other arithmetic: 11.8 us -> none  [the longest x2 5.21 us: root_norm(): jnp.mean(values * values, axis=-1, keepdims=True) + 1e-06]
    ppermute x8 -> x15, starting transfers between devices: 23.1 us -> 23.1 us  [the longest x8 9.38 us: swap(): return lax.ppermute(value, axis, [(i, i ^ bit) for i in range(count)])]
  transfers between devices with their start and end apart: 12 -> 18, of which waited for: 6 -> 6; matrix products, arithmetic and copies ran while one was open for 12% -> 4% of each run, Pallas kernels for 0% -> 18%
where the time goes in v1:
time: 323 us; the launch traced here: 320 us
  waiting for transfers between devices  186 us (58%)
  Pallas kernels  57.2 us (18%)
  local copies, waits for them, and re-layouts  36.3 us (11%)
  starting transfers between devices  23.2 us (7%)
  between operations  14.9 us (5%)
    ppermute x8, waiting for transfers between devices, swap(): return lax.ppermute(value, axis, [(i, i ^ bit) for i in range(count)])  71.1 us
    all_gather x1, waiting for transfers between devices, shards(): columns = {(0, 0): lax.all_gather(share, 'seq', axis=0, tiled=True)}  47.3 us
    ppermute x2, waiting for transfers between devices, shards(): lax.ppermute(columns[d, 0], 'group', pairs)  44.2 us
    unnamed x69, local copies, waits for them, and re-layouts  32.3 us
    pallas_call x2, Pallas kernels, project(): pl.pallas_call(functools.partial(qkv_kernel, count), grid=(heads,), in_sp...  26.6 us
    ppermute x3, waiting for transfers between devices, shards(): lax.ppermute(done, 'seq', [(s, (s + turn) % devices) for s in range(devic...  21.5 us
    pallas_call x1, Pallas kernels, finish(): pl.pallas_call(functools.partial(finish_kernel, devices, count), in_specs...  14.1 us
    pallas_call x4, Pallas kernels, attend(): pl.pallas_call(attend_kernel, grid_spec=pltpu.PrefetchScalarGridSpec(num_...  11.2 us
  transfers between devices with their start and end apart: 18, of which 6 were waited for; matrix products, arithmetic and copies ran while one was open for 4% of the time, Pallas kernels for 18%

profile of v1, /device:TPU:1, one launch (start us, length us, event | category | flops | bytes accessed | tf_op | source)
XLA Modules:
  0.0 320.5 jit_solution(825187581605113724)
XLA Ops:
  10.0 2.7 norm_in.3
  12.8 2.1 collective-permute-start.1
  14.9 47.3 %all-gather.8.cloned.1.call-done.refs_4_ = bf16[3072,384]{1,0:T(8,128)(2,1)} async-done(((bf16[768,384]{1,0:T(8,128)(2,1)}), bf16[3072,384]{1,0:T(8,128)(2,1)}) %all-gather.8.cloned.1.call-update) | async-done | bytes 2359312 | tf_op jit(solution)/shard_map/all_gather | solution.py:257
  63.3 2.7 norm_in.2
  67.1 24.4 %collective-permute-done.1.refs_2_ = bf16[768,2304]{1,0:T(8,128)(2,1)} collective-permute-done((bf16[768,2304]{1,0:T(8,128)(2,1)}, bf16[768,2304]{1,0:T(8,128)(2,1)}, u32[]{:S(2)}, u32[]{:S(2)}) %collective-permute-start.1) | collective-permute-done | bytes 3538976 | tf_op jit(solution)/shard_map/ppermute | solution.py:19
  91.4 2.1 collective-permute-start.2
  93.5 1.8 collective-permute-start.6
  95.3 46.7 %collective-permute-done.9.refs_8_ = bf16[3072,384]{1,0:T(8,128)(2,1)} collective-permute-done((bf16[3072,384]{1,0:T(8,128)(2,1)}, bf16[3072,384]{1,0:T(8,128)(2,1)}, u32[]{:S(2)}, u32[]{:S(2)}) %collective-permute-start.9) | collective-permute-done | bytes 2359328 | tf_op jit(solution)/shard_map/ppermute | solution.py:19
  149.9 1.9 collective-permute-start.7
  153.6 44.2 %collective-permute-done.10.refs_9_ = bf16[3072,384]{1,0:T(8,128)(2,1)} collective-permute-done((bf16[3072,384]{1,0:T(8,128)(2,1)}, bf16[3072,384]{1,0:T(8,128)(2,1)}, u32[]{:S(2)}, u32[]{:S(2)}) %collective-permute-start.10) | collective-permute-done | bytes 2359328 | tf_op jit(solution)/shard_map/ppermute | solution.py:286
  198.4 2.0 copy-done.12
  200.4 1.9 copy-done.14
  202.3 13.3 %project.2 = (bf16[6,4,2,128,128]{4,3,2,1,0:T(8,128)(2,1)S(1)}, bf16[6,4,2,128,128]{4,3,2,1,0:T(8,128)(2,1)S(1)}, bf16[6,4,2,128,128]{4,3,2,1,0:T(8,128)(2,1)S(1)}) custom-call(bf16[512,3072]{1,0:T(8,128)(2,1)S(1)} %copy-done.14, bf16[768,2304]{1,0:T(8,128)(2,1)S(1)} %copy-done.12, bf16[768,2304]{1,0:T(8,128)(2,1)} %collective-permute-done.refs_1_, ...), custom_call_target="tpu_custom_call" | custom-call | flops 7247757312 | bytes 31457280 | tf_op jit(solution)/shard_map/project/pallas_call | solution.py:100
  217.9 1.4 copy-done.2
  219.3 1.4 copy-done.7
  220.7 2.0 copy-done.13
  222.7 1.9 copy-done.15
  224.6 13.3 %project.3 = (bf16[6,4,2,128,128]{4,3,2,1,0:T(8,128)(2,1)S(1)}, bf16[6,4,2,128,128]{4,3,2,1,0:T(8,128)(2,1)S(1)}, bf16[6,4,2,128,128]{4,3,2,1,0:T(8,128)(2,1)S(1)}) custom-call(bf16[512,3072]{1,0:T(8,128)(2,1)S(1)} %copy-done.15, bf16[768,2304]{1,0:T(8,128)(2,1)S(1)} %copy-done.13, ...), custom_call_target="tpu_custom_call", output_to_operand_aliasing={{0}: (5, {}), {1}: (6, {}), {2}: (7, {})} | custom-call | flops 7247757312 | bytes 31457280 | tf_op jit(solution)/shard_map/project/pallas_call | solution.py:100
  240.3 1.4 copy-done.4
  241.7 1.4 copy-done.9
  243.1 2.8 attend.7
  245.9 3.6 %collective-permute-start.5 = (bf16[256,768]{1,0:T(8,128)(2,1)S(1)}, bf16[256,768]{1,0:T(8,128)(2,1)}, u32[]{:S(2)}, u32[]{:S(2)}) collective-permute-start(bf16[256,768]{1,0:T(8,128)(2,1)S(1)} %attend.7), channel_id=1, source_target_pairs={{0,3},{1,0},{2,1},{3,2},{4,7},{5,4},{6,5},{7,6},{8,11},{9,8},{10,9... | collective-permute-start | bytes 1179656 | tf_op jit(solution)/shard_map/ppermute | solution.py:325
  250.2 1.7 bitcast_dynamic-update-slice_fusion.1
  251.9 1.6 bitcast_dynamic-update-slice_fusion.refs_12_
  256.4 2.8 attend.6
  259.2 2.8 attend.5
  263.7 2.8 attend.4.refs_0_
  267.2 21.5 %collective-permute-done.4.refs_2_ = bf16[256,768]{1,0:T(8,128)(2,1)S(1)} collective-permute-done((bf16[256,768]{1,0:T(8,128)(2,1)S(1)}, bf16[256,768]{1,0:T(8,128)(2,1)S(1)}, u32[]{:S(2)}, u32[]{:S(2)}) %collective-permute-start.4) | collective-permute-done | bytes 393248 | tf_op jit(solution)/shard_map/ppermute | solution.py:325
  288.7 2.1 collective-permute-start.14
  291.6 14.1 %finish.1 = (f32[128,256]{1,0:T(8,128)}, bf16[128,256]{1,0:T(8,128)(2,1)}) custom-call(s32[1]{0:T(128)} %bitcast.place_ref, f32[2]{0:T(128)} %pad_maximum_fusion.coef_ref, bf16[256,768]{1,0:T(8,128)(2,1)} %copy-done.11, bf16[256,768]{1,0:T(8,128)(2,1)} %copy-done.21, bf16[256,768]{1,0:T(8,128)(2,1)} %copy-done.20, ...), custom_call_target="tpu_custom_call" | custom-call | flops 4831838208 | bytes 18874368 | tf_op jit(solution)/shard_map/finish/pallas_call | solution.py:208
  305.7 4.5 %collective-permute-start.13 = (bf16[128,256]{1,0:T(8,128)(2,1)}, bf16[128,256]{1,0:T(8,128)(2,1)S(1)}, u32[]{:S(2)}, u32[]{:S(2)}) collective-permute-start(bf16[128,256]{1,0:T(8,128)(2,1)} %get-tuple-element.17), channel_id=1, source_target_pairs={{2,4},{3,5},{6,8},{7,9},{10,12},{11,13},{4,2},{5,3},{8,6},{9,7},{1... | collective-permute-start | bytes 196616 | tf_op jit(solution)/shard_map/ppermute | solution.py:342
  310.3 2.1 collective-permute-done.13
  (95 shorter events, 27.5 us)
Async XLA Ops:
  7.2 55.0 %all-gather.8.cloned.1.call-start = ((), (), s32[]{:S(2)}) async-start(), calls=%async_computation.2 | async-start | bytes 2949120 | tf_op jit(solution)/shard_map/all_gather | solution.py:257
  9.4 189.0 %all-gather.6.cloned.1.call-start = ((), (), s32[]{:S(2)}) async-start(), calls=%async_computation.1 | async-start | bytes 3932160 | tf_op jit(solution)/shard_map/all_gather | solution.py:274
  12.7 130.5 %copy-start.18 = (f32[5,3072]{1,0:T(8,128)S(1)}, f32[5,3072]{1,0:T(8,128)}, u32[]{:S(2)}) copy-start(f32[5,3072]{1,0:T(8,128)} %mod_ref.3) | copy-start | bytes 184324
  12.7 137.0 %copy-start.16 = (bf16[1,256,3072]{2,1,0:T(8,128)(2,1)S(1)}, bf16[1,256,3072]{2,1,0:T(8,128)(2,1)}, u32[]{:S(2)}) copy-start(bf16[1,256,3072]{2,1,0:T(8,128)(2,1)} %param.8) | copy-start | bytes 4718596
  12.7 205.2 %all-gather.4.cloned.1.call-start = ((), (), s32[]{:S(2)}) async-start(), calls=%async_computation | async-start | bytes 3932160 | tf_op jit(solution)/shard_map/all_gather | solution.py:274
  12.8 78.7 %collective-permute-start.1 = (bf16[768,2304]{1,0:T(8,128)(2,1)}, bf16[768,2304]{1,0:T(8,128)(2,1)}, u32[]{:S(2)}, u32[]{:S(2)}) collective-permute-start(bf16[768,2304]{1,0:T(8,128)(2,1)} %refs_0_.3), channel_id=1, source_target_pairs={{0,8},{4,12},{8,0},{12,4},{1,9},{5,13},{9,1},{13,5},{2,10},{6,14},... | collective-permute-start | bytes 10616840 | tf_op jit(solution)/shard_map/ppermute | solution.py:19
  62.1 79.9 %collective-permute-start.9 = (bf16[3072,384]{1,0:T(8,128)(2,1)}, bf16[3072,384]{1,0:T(8,128)(2,1)}, u32[]{:S(2)}, u32[]{:S(2)}) collective-permute-start(bf16[3072,384]{1,0:T(8,128)(2,1)} %all-gather.8.cloned.1.call-done.refs_4_), channel_id=1, source_target_pairs={{0,8},{4,12},{8,0},{12,4},{1,9},{5,13},{9,1},{13,5},{2,10},{6,14},... | collective-permute-start | bytes 7077896 | tf_op jit(solution)/shard_map/ppermute | solution.py:19
  66.0 87.1 %collective-permute-start = (bf16[768,2304]{1,0:T(8,128)(2,1)}, bf16[768,2304]{1,0:T(8,128)(2,1)}, u32[]{:S(2)}, u32[]{:S(2)}) collective-permute-start(bf16[768,2304]{1,0:T(8,128)(2,1)} %refs_0_.3), channel_id=1, source_target_pairs={{0,4},{4,0},{8,12},{12,8},{1,5},{5,1},{9,13},{13,9},{2,6},{6,2},{1... | collective-permute-start | bytes 10616840 | tf_op jit(solution)/shard_map/ppermute | solution.py:19
  91.4 106.9 %collective-permute-start.2 = (bf16[768,2304]{1,0:T(8,128)(2,1)}, bf16[768,2304]{1,0:T(8,128)(2,1)}, u32[]{:S(2)}, u32[]{:S(2)}) collective-permute-start(bf16[768,2304]{1,0:T(8,128)(2,1)} %collective-permute-done.1.refs_2_), channel_id=1, source_target_pairs={{0,4},{4,0},{8,12},{12,8},{1,5},{5,1},{9,13},{13,9},{2,6},{6,2},{1... | collective-permute-start | bytes 10616840 | tf_op jit(solution)/shard_map/ppermute | solution.py:19
  93.5 59.6 %collective-permute-start.6 = (bf16[3072,384]{1,0:T(8,128)(2,1)}, bf16[3072,384]{1,0:T(8,128)(2,1)}, u32[]{:S(2)}, u32[]{:S(2)}) collective-permute-start(bf16[3072,384]{1,0:T(8,128)(2,1)} %all-gather.8.cloned.1.call-done.refs_4_), channel_id=1, source_target_pairs={{0,16},{16,0},{1,17},{17,1},{2,18},{18,2},{3,19},{19,3},{4,20},{20... | collective-permute-start | bytes 7077896 | tf_op jit(solution)/shard_map/ppermute | solution.py:286
  142.0 55.8 %collective-permute-start.10 = (bf16[3072,384]{1,0:T(8,128)(2,1)}, bf16[3072,384]{1,0:T(8,128)(2,1)}, u32[]{:S(2)}, u32[]{:S(2)}) collective-permute-start(bf16[3072,384]{1,0:T(8,128)(2,1)} %collective-permute-done.9.refs_8_), channel_id=1, source_target_pairs={{0,16},{16,0},{1,17},{17,1},{2,18},{18,2},{3,19},{19,3},{4,20},{20... | collective-permute-start | bytes 7077896 | tf_op jit(solution)/shard_map/ppermute | solution.py:286
  149.7 65.9 %copy-start.19 = (bf16[64,3072]{1,0:T(8,128)(2,1)}, bf16[64,3072]{1,0:T(8,128)(2,1)S(1)}, u32[]{:S(2)}) copy-start(bf16[64,3072]{1,0:T(8,128)(2,1)S(1)} %constant_dynamic-update-slice_fusion.8.refs_14_) | copy-start | bytes 1179652
  149.9 112.1 %collective-permute-start.7 = (bf16[3072,384]{1,0:T(8,128)(2,1)}, bf16[3072,384]{1,0:T(8,128)(2,1)}, u32[]{:S(2)}, u32[]{:S(2)}) collective-permute-start(bf16[3072,384]{1,0:T(8,128)(2,1)} %all-gather.8.cloned.1.call-done.refs_4_), channel_id=1, source_target_pairs={{0,4},{4,0},{8,12},{12,8},{1,5},{5,1},{9,13},{13,9},{2,6},{6,2},{1... | collective-permute-start | bytes 7077896 | tf_op jit(solution)/shard_map/ppermute | solution.py:19
  153.1 137.8 %collective-permute-start.11 = (bf16[3072,384]{1,0:T(8,128)(2,1)}, bf16[3072,384]{1,0:T(8,128)(2,1)}, u32[]{:S(2)}, u32[]{:S(2)}) collective-permute-start(bf16[3072,384]{1,0:T(8,128)(2,1)} %collective-permute-done.9.refs_8_), channel_id=1, source_target_pairs={{0,4},{4,0},{8,12},{12,8},{1,5},{5,1},{9,13},{13,9},{2,6},{6,2},{1... | collective-permute-start | bytes 7077896 | tf_op jit(solution)/shard_map/ppermute | solution.py:19
  153.1 137.7 %collective-permute-start.8 = (bf16[3072,384]{1,0:T(8,128)(2,1)}, bf16[3072,384]{1,0:T(8,128)(2,1)}, u32[]{:S(2)}, u32[]{:S(2)}) collective-permute-start(bf16[3072,384]{1,0:T(8,128)(2,1)} %collective-permute-done.6.refs_5_), channel_id=1, source_target_pairs={{0,4},{4,0},{8,12},{12,8},{1,5},{5,1},{9,13},{13,9},{2,6},{6,2},{1... | collective-permute-start | bytes 7077896 | tf_op jit(solution)/shard_map/ppermute | solution.py:19
  197.8 93.1 %collective-permute-start.12 = (bf16[3072,384]{1,0:T(8,128)(2,1)}, bf16[3072,384]{1,0:T(8,128)(2,1)}, u32[]{:S(2)}, u32[]{:S(2)}) collective-permute-start(bf16[3072,384]{1,0:T(8,128)(2,1)} %collective-permute-done.10.refs_9_), channel_id=1, source_target_pairs={{0,4},{4,0},{8,12},{12,8},{1,5},{5,1},{9,13},{13,9},{2,6},{6,2},{1... | collective-permute-start | bytes 7077896 | tf_op jit(solution)/shard_map/ppermute | solution.py:19
  198.4 2.0 copy-start.12
  200.4 1.9 copy-start.14
  217.9 1.4 copy-start.2
  220.7 2.0 copy-start.13
  222.7 1.9 copy-start.15
  240.3 1.4 copy-start.4
  241.7 1.4 copy-start.9
  245.9 16.2 %collective-permute-start.5 = (bf16[256,768]{1,0:T(8,128)(2,1)S(1)}, bf16[256,768]{1,0:T(8,128)(2,1)}, u32[]{:S(2)}, u32[]{:S(2)}) collective-permute-start(bf16[256,768]{1,0:T(8,128)(2,1)S(1)} %attend.7), channel_id=1, source_target_pairs={{0,3},{1,0},{2,1},{3,2},{4,7},{5,4},{6,5},{7,6},{8,11},{9,8},{10,9... | collective-permute-start | bytes 1179656 | tf_op jit(solution)/shard_map/ppermute | solution.py:325
  249.5 9.7 %copy-start.22 = (f32[5,3072]{1,0:T(8,128)}, f32[5,3072]{1,0:T(8,128)S(1)}, u32[]{:S(2)}) copy-start(f32[5,3072]{1,0:T(8,128)S(1)} %constant_dynamic-update-slice_fusion.refs_13_) | copy-start | bytes 184324
  253.5 1.4 copy-start.5
  259.2 3.9 %copy-start.23 = (s32[1,256]{1,0:T(1,128)S(1)}, s32[1,256]{1,0:T(1,128)}, u32[]{:S(2)}) copy-start(s32[1,256]{1,0:T(1,128)} %param.14) | copy-start | bytes 3076
  262.0 26.7 %collective-permute-start.4 = (bf16[256,768]{1,0:T(8,128)(2,1)S(1)}, bf16[256,768]{1,0:T(8,128)(2,1)S(1)}, u32[]{:S(2)}, u32[]{:S(2)}) collective-permute-start(bf16[256,768]{1,0:T(8,128)(2,1)S(1)} %attend.6), channel_id=1, source_target_pairs={{0,2},{1,3},{2,0},{3,1},{4,6},{5,7},{6,4},{7,5},{8,10},{9,11},{10,... | collective-permute-start | bytes 1179656 | tf_op jit(solution)/shard_map/ppermute | solution.py:325
  262.1 28.7 %collective-permute-start.3 = (bf16[256,768]{1,0:T(8,128)(2,1)S(1)}, bf16[256,768]{1,0:T(8,128)(2,1)S(1)}, u32[]{:S(2)}, u32[]{:S(2)}) collective-permute-start(bf16[256,768]{1,0:T(8,128)(2,1)S(1)} %attend.5), channel_id=1, source_target_pairs={{0,1},{1,2},{2,3},{3,0},{4,5},{5,6},{6,7},{7,4},{8,9},{9,10},{10,1... | collective-permute-start | bytes 1179656 | tf_op jit(solution)/shard_map/ppermute | solution.py:325
  288.7 2.2 copy-start.20
  288.7 21.5 %collective-permute-start.14 = (bf16[1,256]{1,0:T(2,128)(2,1)S(1)}, bf16[1,256]{1,0:T(2,128)(2,1)S(1)}, u32[]{:S(2)}, u32[]{:S(2)}) collective-permute-start(bf16[1,256]{1,0:T(2,128)(2,1)S(1)} %get-tuple-element.20), channel_id=1, source_target_pairs={{2,4},{3,5},{6,8},{7,9},{10,12},{11,13},{4,2},{5,3},{8,6},{9,7},{1... | collective-permute-start | bytes 1544 | tf_op jit(solution)/shard_map/ppermute | solution.py:251
  305.7 6.7 %collective-permute-start.13 = (bf16[128,256]{1,0:T(8,128)(2,1)}, bf16[128,256]{1,0:T(8,128)(2,1)S(1)}, u32[]{:S(2)}, u32[]{:S(2)}) collective-permute-start(bf16[128,256]{1,0:T(8,128)(2,1)} %get-tuple-element.17), channel_id=1, source_target_pairs={{2,4},{3,5},{6,8},{7,9},{10,12},{11,13},{4,2},{5,3},{8,6},{9,7},{1... | collective-permute-start | bytes 196616 | tf_op jit(solution)/shard_map/ppermute | solution.py:342
  (10 other events, 11.4 us)
Sparse Core Ops, SparseCore 0:
  9.6 52.5 all-gather.7
  63.7 62.2 all-gather.5
  127.6 62.1 all-gather.3

commit v2 on v1

--- a/solution.py
+++ b/solution.py
@@ -22,6 +22,23 @@
 def bits_of(count):
     far = [1 << n for n in range(1, count.bit_length() - 1)]
     return far + [1]
+
+
+def along(value, axis):
+    count = lax.axis_size(axis)
+    ups, downs = [value], [value]
+    for step in range(1, count):
+        ups.append(
+            lax.ppermute(ups[-1], axis, [(s, s + 1) for s in range(step - 1, count - 1)])
+        )
+        downs.append(
+            lax.ppermute(downs[-1], axis, [(s, s - 1) for s in range(1, count - step + 1)])
+        )
+    return [value] + [ups[m] + downs[count - m] for m in range(1, count)]
+
+
+def after(value, *others):
+    return lax.optimization_barrier((value,) + others)[0]
 
 
 def noise_level(index, steps):
@@ -78,15 +95,17 @@
             refs[n][...],
             preferred_element_type=jnp.float32,
         )
-    shape = q_ref.shape
+    shape = q_ref.shape[1:]
 
     def rooted(part):
         spread = jnp.mean(part * part, axis=-1, keepdims=True)
         return (part * lax.rsqrt(spread + 1e-06)).astype(jnp.bfloat16)
 
-    q_ref[...] = rooted(proj[:, :HD]).reshape(shape)
-    k_ref[...] = rooted(proj[:, HD : 2 * HD]).reshape(shape)
-    v_ref[...] = proj[:, 2 * HD :].astype(jnp.bfloat16).reshape(shape)
+    for h in range(q_ref.shape[0]):
+        query, key, value = (proj[:, (3 * h + i) * HD : (3 * h + i + 1) * HD] for i in range(3))
+        q_ref[h] = rooted(query).reshape(shape)
+        k_ref[h] = rooted(key).reshape(shape)
+        v_ref[h] = value.astype(jnp.bfloat16).reshape(shape)
 
 
 def project(x, blocks, chunk, devices, before):
@@ -95,18 +114,19 @@
     count = len(blocks)
     total = blocks[0].shape[1]
     heads = total // (3 * HD)
+    many = 2 if heads % 2 == 0 else 1
     out = jax.ShapeDtypeStruct((heads, devices, CHUNKS, rows, HD), jnp.bfloat16)
-    spec = pl.BlockSpec((1, devices, 1, rows, HD), lambda h: (h, 0, chunk, 0, 0))
+    spec = pl.BlockSpec((many, devices, 1, rows, HD), lambda h: (h, 0, chunk, 0, 0))
     return pl.pallas_call(
         functools.partial(qkv_kernel, count),
-        grid=(heads,),
+        grid=(heads // many,),
         in_specs=[pl.BlockSpec((length, width), lambda h: (0, 0))]
-        + [pl.BlockSpec((width // count, 3 * HD), lambda h: (0, h))] * count
+        + [pl.BlockSpec((width // count, many * 3 * HD), lambda h: (0, h))] * count
         + [pl.BlockSpec(memory_space=pl.ANY)] * len(before),
         out_specs=[spec] * 3,
         out_shape=[out] * 3,
         input_output_aliases={1 + count + i: i for i in range(len(before))},
-        compiler_params=pltpu.CompilerParams(vmem_limit_bytes=40 * MIB),
+        compiler_params=pltpu.CompilerParams(vmem_limit_bytes=60 * MIB),
         cost_estimate=pl.CostEstimate(
             flops=2 * length * width * total,
             bytes_accessed=2 * (length * width + width * total * 2),
@@ -143,7 +163,7 @@
             out_specs=pl.BlockSpec((rows, HD), lambda h, dest: (0, h)),
         ),
         out_shape=jax.ShapeDtypeStruct((rows, heads * HD), jnp.bfloat16),
-        compiler_params=pltpu.CompilerParams(vmem_limit_bytes=40 * MIB),
+        compiler_params=pltpu.CompilerParams(vmem_limit_bytes=60 * MIB),
         cost_estimate=pl.CostEstimate(
             flops=4 * rows * length * heads * HD,
             bytes_accessed=2 * heads * HD * 2 * (rows + length),
@@ -158,29 +178,68 @@
     )
 
 
-def finish_kernel(devices, pieces, place_ref, coef_ref, *refs):
-    parts = refs[:devices]
-    sources = refs[devices : devices + pieces]
-    hidden_ref, mod_ref, head_ref, latent_ref, weight_ref = refs[
-        devices + pieces : devices + pieces + 5
-    ]
-    out_ref, sent_ref, weights, attended, mixed, sems = refs[devices + pieces + 5 :]
-    copies = [
-        pltpu.make_async_copy(sources[p], weights.at[p], sems.at[p]) for p in range(pieces)
-    ]
-    for copy in copies:
-        copy.start()
-    features = parts[0].shape[1]
-    place = place_ref[0]
-    for k in range(devices):
-        origin = lax.rem(place - k + devices, devices)
-        attended[:, pl.ds(pl.multiple_of(origin * features, HD), features)] = parts[k][...]
+def add_kernel(count, part_ref, *refs):
+    pieces = refs[:count]
+    before_ref, mod_ref, out_ref = refs[count:]
+    width = pieces[0].shape[1]
+    for p in range(count):
+        cols = slice(p * width, (p + 1) * width)
+        summed = jnp.dot(part_ref[...], pieces[p][...], preferred_element_type=jnp.float32)
+        out_ref[:, cols] = before_ref[:, cols].astype(jnp.float32) + mod_ref[2:3, cols] * summed
+
+
+def add_part(part, turn, pieces, before, modulation):
+    rows, features = part.shape
+    width = before.shape[1]
+    count = len(pieces)
+    aliased = before.dtype == jnp.float32
+    return pl.pallas_call(
+        functools.partial(add_kernel, count),
+        grid=(1,),
+        in_specs=[pl.BlockSpec(part.shape, lambda i: (0, 0))]
+        + [pl.BlockSpec((features, pieces[0].shape[1]), lambda i: (turn, 0))] * count
+        + [
+            pl.BlockSpec(before.shape, lambda i: (0, 0)),
+            pl.BlockSpec(modulation.shape, lambda i: (0, 0)),
+        ],
+        out_specs=pl.BlockSpec((rows, width), lambda i: (0, 0)),
+        out_shape=jax.ShapeDtypeStruct((rows, width), jnp.float32),
+        input_output_aliases={1 + count: 0} if aliased else {},
+        compiler_params=pltpu.CompilerParams(vmem_limit_bytes=60 * MIB),
+        cost_estimate=pl.CostEstimate(
+            flops=2 * rows * width * features,
+            bytes_accessed=2 * width * features + 8 * rows * width,
+            transcendentals=0,
+        ),
+        name="add_part",
+    )(part, *pieces, before, modulation)
+
+
+def finish_kernel(turn, count, coef_ref, part_ref, *refs):
+    sources = refs[:count]
+    before_ref, mod_ref, head_ref, latent_ref, weight_ref = refs[count : count + 5]
+    out_ref, sent_ref, weights, mixed, sems = refs[count + 5 :]
+    features = part_ref.shape[1]
     width = weights.shape[2]
-    for p in range(pieces):
-        copies[p].wait()
-        summed = jnp.dot(attended[...], weights[p], preferred_element_type=jnp.float32)
+    copies = []
+    for p in range(count):
+        cols = pl.ds(p * width, width)
+        copies.append(
+            (
+                pltpu.make_async_copy(
+                    sources[p].at[pl.ds(turn * features, features)], weights.at[p], sems.at[0, p]
+                ),
+                pltpu.make_async_copy(before_ref.at[:, cols], mixed.at[:, cols], sems.at[1, p]),
+            )
+        )
+        copies[p][0].start()
+        copies[p][1].start()
+    for p in range(count):
+        copies[p][0].wait()
+        summed = jnp.dot(part_ref[...], weights[p], preferred_element_type=jnp.float32)
         cols = slice(p * width, (p + 1) * width)
-        mixed[:, cols] = hidden_ref[:, cols].astype(jnp.float32) + mod_ref[2:3, cols] * summed
+        copies[p][1].wait()
+        mixed[:, cols] += mod_ref[2:3, cols] * summed
     normed = layer_norm(mixed[...]) * (1.0 + mod_ref[4:5, :]) + mod_ref[3:4, :]
     velocity = lax.dot_general(
         head_ref[...],
@@ -198,35 +257,35 @@
     sent_ref[channels:, :] = guess.astype(jnp.bfloat16)
 
 
-def finish(place, coef, parts, pieces, hidden, modulation, head, latent, weight):
-    devices, count = len(parts), len(pieces)
-    rows, width = hidden.shape
+def finish(coef, part, turn, pieces, before, modulation, head, latent, weight):
+    rows, width = before.shape
+    features = part.shape[1]
+    count = len(pieces)
     channels = head.shape[0]
     smem = pl.BlockSpec(memory_space=pltpu.SMEM)
     vmem = pl.BlockSpec(memory_space=pltpu.VMEM)
     hbm = pl.BlockSpec(memory_space=pl.ANY)
     return pl.pallas_call(
-        functools.partial(finish_kernel, devices, count),
-        in_specs=[smem, smem] + [vmem] * devices + [hbm] * count + [vmem] * 5,
+        functools.partial(finish_kernel, turn, count),
+        in_specs=[smem, vmem] + [hbm] * count + [hbm] + [vmem] * 4,
         out_specs=[vmem, vmem],
         out_shape=[
             jax.ShapeDtypeStruct((2 * channels, rows), jnp.float32),
             jax.ShapeDtypeStruct((2 * channels, rows), jnp.bfloat16),
         ],
         scratch_shapes=[
-            pltpu.VMEM((count,) + pieces[0].shape, jnp.bfloat16),
-            pltpu.VMEM((rows, width), jnp.bfloat16),
+            pltpu.VMEM((count, features, pieces[0].shape[1]), jnp.bfloat16),
             pltpu.VMEM((rows, width), jnp.float32),
-            pltpu.SemaphoreType.DMA((count,)),
+            pltpu.SemaphoreType.DMA((2, count)),
         ],
-        compiler_params=pltpu.CompilerParams(vmem_limit_bytes=56 * MIB),
+        compiler_params=pltpu.CompilerParams(vmem_limit_bytes=60 * MIB),
         cost_estimate=pl.CostEstimate(
-            flops=2 * rows * width * width,
-            bytes_accessed=2 * width * width,
+            flops=2 * rows * width * features,
+            bytes_accessed=2 * width * features + 4 * rows * width,
             transcendentals=0,
         ),
         name="finish",
-    )(place.reshape(1), coef, *parts, *pieces, hidden, modulation, head, latent, weight)
+    )(coef, part, *pieces, before, modulation, head, latent, weight)
 
 
 def shards(hidden, modulation, w_qkv, w_out, w_head, latent, weights_int, step_index):
@@ -254,13 +313,14 @@
 
     part = w_out.shape[1] // groups
     share = lax.dynamic_slice_in_dim(w_out, group * part, part, axis=1)
-    columns = {(0, 0): lax.all_gather(share, "seq", axis=0, tiled=True)}
+    columns = {(0, 0): jnp.concatenate(along(share, "seq"), axis=0)}
 
     height = w_qkv.shape[0]
     blocks = {0: w_qkv}
     for bit in bits_of(tiles):
         blocks.update({d ^ bit: swap(blocks[d], "tile", bit) for d in list(blocks)})
     starts = jnp.stack([(tile ^ d) * height for d in range(tiles)]).astype(jnp.int32)
+    arrived = dict(blocks)
     if height % HD:
         full = jnp.zeros((tiles * height, w_qkv.shape[1]), w_qkv.dtype)
         for d in range(tiles):
@@ -275,20 +335,31 @@
         for c in range(CHUNKS)
     ]
 
+    state = ()
+    for c in range(CHUNKS):
+        state = project(gathered[c], blocks, c, devices, state)
+
     far, near = bits_of(tiles)[:-1], bits_of(tiles)[-1]
-    for bit in far:
+    if far:
+        first = far[0]
+        columns[first, 0] = swap(after(columns[0, 0], arrived[first]), "tile", first)
+    for bit in far[1:]:
         columns.update({(d ^ bit, g): swap(columns[d, g], "tile", bit) for d, g in list(columns)})
-    if groups > 1:
-        for turn in range(1, groups):
-            pairs = [(g, (g + turn) % groups) for g in range(groups)]
-            columns.update(
-                {
-                    (d, turn): lax.ppermute(columns[d, 0], "group", pairs)
-                    for d, g in list(columns)
-                    if g == 0
-                }
-            )
-    columns.update({(d ^ near, g): swap(columns[d, g], "tile", near) for d, g in list(columns)})
+    for turn in range(1, groups):
+        pairs = [(g, (g + turn) % groups) for g in range(groups)]
+        columns.update(
+            {
+                (d, turn): lax.ppermute(columns[d, 0], "group", pairs)
+                for d, g in list(columns)
+                if g == 0
+            }
+        )
+    columns.update(
+        {
+            (d ^ near, g): swap(after(columns[d, g], state[0]) if g else columns[d, g], "tile", near)
+            for d, g in list(columns)
+        }
+    )
     order = sorted(columns)
 
     def reorder(value, axis):
@@ -312,28 +383,29 @@
     if part % HD:
         pieces = [jnp.concatenate(pieces, axis=1)]
 
-    state = ()
-    for c in range(CHUNKS):
-        state = project(gathered[c], blocks, c, devices, state)
     heads = w_qkv.shape[1] // (3 * HD)
     queries, keys, values = [value.reshape(heads, devices, rows, HD) for value in state]
 
+    turns = sorted(range(1, devices), key=lambda turn: -min(turn, devices - turn))
     parts = {}
-    for turn in list(range(1, devices)) + [0]:
+    for turn in turns + [0]:
         done = attend(lax.rem(place + turn, devices), queries, keys, values)
         if turn:
             done = lax.ppermute(done, "seq", [(s, (s + turn) % devices) for s in range(devices)])
         parts[turn] = done
 
+    mixed = hidden_by
+    for turn in [0] + turns[:-1]:
+        mixed = add_part(parts[turn], turn, pieces, mixed, modulation_by)
     index = step_index[0].astype(jnp.float32)
     now = noise_level(index, NSTEPS)
-    after = noise_level(index + 1.0, NSTEPS)
+    later = noise_level(index + 1.0, NSTEPS)
     weighted, sent = finish(
-        place,
-        jnp.stack([now, after - now]),
-        [parts[turn] for turn in range(devices)],
+        jnp.stack([now, later - now]),
+        parts[turns[-1]],
+        turns[-1],
         pieces,
-        hidden_by,
+        mixed,
         modulation_by,
         head_by,
         latent[0].T,

time: 323 us -> 308 us (0.954)
  waiting for transfers between devices: 186 us -> 139 us
  Pallas kernels: 57.2 us -> 83 us
  starting transfers between devices: 23.2 us -> 42.3 us
  local copies, waits for them, and re-layouts: 36.3 us -> 19.6 us
  other arithmetic: 2.63 us -> 6.71 us
    ppermute x0 -> x6, waiting for transfers between devices: none -> 67.8 us  [the longest x3 51.6 us: along(): lax.ppermute(downs[-1], axis, [(s, s - 1) for s in range(1, count - step...]
    all_gather x1 -> x0, waiting for transfers between devices: 47.3 us -> none  [shards(): columns = {(0, 0): lax.all_gather(share, 'seq', axis=0, tiled=True)}]
    ppermute x2, waiting for transfers between devices: 44.2 us -> 15.7 us  [shards(): lax.ppermute(columns[d, 0], 'group', pairs)]
    ppermute x3, waiting for transfers between devices: 21.5 us -> 0.01 us  [shards(): lax.ppermute(done, 'seq', [(s, (s + turn) % devices) for s in range(devic...]
    ppermute x8, waiting for transfers between devices: 71.1 us -> 50.7 us  [swap(): return lax.ppermute(value, axis, [(i, i ^ bit) for i in range(count)])]
    unnamed x69 -> x43, local copies, waits for them, and re-layouts: 32.3 us -> 16.9 us
    pallas_call x3 -> x6, Pallas kernels: 40.7 us -> 54 us  [the longest x2 25.8 us: project(): pl.pallas_call(functools.partial(qkv_kernel, count), grid=(heads // many,...]
    pallas_call x4, Pallas kernels: 11.2 us -> 23.7 us  [attend(): pl.pallas_call(attend_kernel, grid_spec=pltpu.PrefetchScalarGridSpec(num_...]
  transfers between devices with their start and end apart: 18 -> 23, of which waited for: 6 -> 7; matrix products, arithmetic and copies ran while one was open for 4% -> 7% of each run, Pallas kernels for 18% -> 26%
where the time goes in v2:
time: 308 us; the launch traced here: 306 us
  waiting for transfers between devices  139 us (45%)
  Pallas kernels  83 us (27%)
  starting transfers between devices  42.3 us (14%)
  local copies, waits for them, and re-layouts  19.6 us (6%)
  between operations  15.2 us (5%)
  other arithmetic  6.71 us (2%)
    ppermute x3, waiting for transfers between devices, along(): lax.ppermute(downs[-1], axis, [(s, s - 1) for s in range(1, count - step...  51.6 us
    ppermute x8, waiting for transfers between devices, swap(): return lax.ppermute(value, axis, [(i, i ^ bit) for i in range(count)])  50.7 us
    pallas_call x2, Pallas kernels, project(): pl.pallas_call(functools.partial(qkv_kernel, count), grid=(heads // many,...  25.8 us
    pallas_call x4, Pallas kernels, attend(): pl.pallas_call(attend_kernel, grid_spec=pltpu.PrefetchScalarGridSpec(num_...  23.7 us
    ppermute x8, starting transfers between devices, swap(): return lax.ppermute(value, axis, [(i, i ^ bit) for i in range(count)])  20.4 us
    pallas_call x3, Pallas kernels, add_part(): pl.pallas_call(functools.partial(add_kernel, count), grid=(1,), in_specs=...  20.1 us
    unnamed x43, local copies, waits for them, and re-layouts  16.9 us
    ppermute x3, waiting for transfers between devices, along(): lax.ppermute(ups[-1], axis, [(s, s + 1) for s in range(step - 1, count -...  16.3 us
  transfers between devices with their start and end apart: 23, of which 7 were waited for; matrix products, arithmetic and copies ran while one was open for 7% of the time, Pallas kernels for 26%

profile of v2, /device:TPU:1, one launch (start us, length us, event | category | flops | bytes accessed | tf_op | source)
XLA Modules:
  0.0 306.1 jit_solution(10487315214703780461)
XLA Ops:
  7.8 2.7 norm_in.3
  10.6 2.1 collective-permute-start.1
  12.7 3.2 %collective-permute-start.4 = (bf16[768,384]{1,0:T(8,128)(2,1)S(1)}, bf16[768,384]{1,0:T(8,128)(2,1)S(1)}, u32[]{:S(2)}, u32[]{:S(2)}) collective-permute-start(bf16[768,384]{1,0:T(8,128)(2,1)S(1)} %constant_dynamic-slice_fusion), channel_id=1, source_target_pairs={{0,1},{1,2},{2,3},{4,5},{5,6},{6,7},{8,9},{9,10},{10,11},{12,13},{... | collective-permute-start | bytes 1769480 | tf_op jit(solution)/shard_map/ppermute | solution.py:32
  17.3 16.3 %collective-permute-done.4 = bf16[768,384]{1,0:T(8,128)(2,1)S(1)} collective-permute-done((bf16[768,384]{1,0:T(8,128)(2,1)S(1)}, bf16[768,384]{1,0:T(8,128)(2,1)S(1)}, u32[]{:S(2)}, u32[]{:S(2)}) %collective-permute-start.4) | collective-permute-done | bytes 589856 | tf_op jit(solution)/shard_map/ppermute | solution.py:32
  34.2 12.8 %collective-permute-done.5 = bf16[768,384]{1,0:T(8,128)(2,1)S(1)} collective-permute-done((bf16[768,384]{1,0:T(8,128)(2,1)S(1)}, bf16[768,384]{1,0:T(8,128)(2,1)S(1)}, u32[]{:S(2)}, u32[]{:S(2)}) %collective-permute-start.5) | collective-permute-done | bytes 589856 | tf_op jit(solution)/shard_map/ppermute | solution.py:35
  48.4 1.5 collective-permute-start.9
  49.9 34.2 %collective-permute-done.6 = bf16[768,384]{1,0:T(8,128)(2,1)} collective-permute-done((bf16[768,384]{1,0:T(8,128)(2,1)S(1)}, bf16[768,384]{1,0:T(8,128)(2,1)}, u32[]{:S(2)}, u32[]{:S(2)}) %collective-permute-start.6) | collective-permute-done | bytes 589856 | tf_op jit(solution)/shard_map/ppermute | solution.py:35
  85.3 2.7 norm_in.2
  88.0 10.5 %collective-permute-start = (bf16[768,2304]{1,0:T(8,128)(2,1)}, bf16[768,2304]{1,0:T(8,128)(2,1)}, u32[]{:S(2)}, u32[]{:S(2)}) collective-permute-start(bf16[768,2304]{1,0:T(8,128)(2,1)} %refs_0_.3), channel_id=1, source_target_pairs={{0,4},{4,0},{8,12},{12,8},{1,5},{5,1},{9,13},{13,9},{2,6},{6,2},{1... | collective-permute-start | bytes 10616840 | tf_op jit(solution)/shard_map/ppermute | solution.py:19
  101.1 4.6 %collective-permute-done.7 = bf16[768,384]{1,0:T(8,128)(2,1)} collective-permute-done((bf16[768,384]{1,0:T(8,128)(2,1)}, bf16[768,384]{1,0:T(8,128)(2,1)}, u32[]{:S(2)}, u32[]{:S(2)}) %collective-permute-start.7) | collective-permute-done | bytes 589856 | tf_op jit(solution)/shard_map/ppermute | solution.py:35
  106.9 4.3 %collective-permute-start.2 = (bf16[768,2304]{1,0:T(8,128)(2,1)}, bf16[768,2304]{1,0:T(8,128)(2,1)}, u32[]{:S(2)}, u32[]{:S(2)}) collective-permute-start(bf16[768,2304]{1,0:T(8,128)(2,1)} %collective-permute-done.1.refs_2_), channel_id=1, source_target_pairs={{0,4},{4,0},{8,12},{12,8},{1,5},{5,1},{9,13},{13,9},{2,6},{6,2},{1... | collective-permute-start | bytes 10616840 | tf_op jit(solution)/shard_map/ppermute | solution.py:19
  112.5 1.3 collective-permute-start.10
  113.8 50.7 %collective-permute-done.13.refs_4_ = bf16[3072,384]{1,0:T(8,128)(2,1)} collective-permute-done((bf16[3072,384]{1,0:T(8,128)(2,1)S(1)}, bf16[3072,384]{1,0:T(8,128)(2,1)}, u32[]{:S(2)}, u32[]{:S(2)}) %collective-permute-start.13) | collective-permute-done | bytes 2359328 | tf_op jit(solution)/shard_map/ppermute | solution.py:19
  170.7 1.5 constant_dynamic-update-slice_fusion.15
  172.2 1.4 constant_dynamic-update-slice_fusion.14
  174.7 12.9 %project.2 = (bf16[6,4,2,128,128]{4,3,2,1,0:T(8,128)(2,1)}, bf16[6,4,2,128,128]{4,3,2,1,0:T(8,128)(2,1)}, bf16[6,4,2,128,128]{4,3,2,1,0:T(8,128)(2,1)}) custom-call(bf16[512,3072]{1,0:T(8,128)(2,1)} %all-gather.5.cloned.1.call-done.x_ref, bf16[768,2304]{1,0:T(8,128)(2,1)} %refs_0_.3, bf16[768,2304]{1,0:T(8,128)(2,1)} %collective-permute-done.refs_1_, ...), custom_call_target="tpu_custom_call" | custom-call | flops 7247757312 | bytes 31457280 | tf_op jit(solution)/shard_map/project/pallas_call | solution.py:120
  187.6 12.9 %project.3 = (bf16[6,4,2,128,128]{4,3,2,1,0:T(8,128)(2,1)}, bf16[6,4,2,128,128]{4,3,2,1,0:T(8,128)(2,1)}, bf16[6,4,2,128,128]{4,3,2,1,0:T(8,128)(2,1)}) custom-call(bf16[512,3072]{1,0:T(8,128)(2,1)} %all-gather.3.cloned.1.call-done.x_ref, bf16[768,2304]{1,0:T(8,128)(2,1)} %refs_0_.3, ...), custom_call_target="tpu_custom_call", output_to_operand_aliasing={{0}: (5, {}), {1}: (6, {}), {2}: (7, {})} | custom-call | flops 7247757312 | bytes 31457280 | tf_op jit(solution)/shard_map/project/pallas_call | solution.py:120
  201.1 15.7 %collective-permute-done.14.refs_5_ = bf16[3072,384]{1,0:T(8,128)(2,1)} collective-permute-done((bf16[3072,384]{1,0:T(8,128)(2,1)}, bf16[3072,384]{1,0:T(8,128)(2,1)}, u32[]{:S(2)}, u32[]{:S(2)}) %collective-permute-start.14) | collective-permute-done | bytes 2359328 | tf_op jit(solution)/shard_map/ppermute | solution.py:352
  216.8 1.7 collective-permute-start.16
  218.5 1.3 constant_dynamic-update-slice_fusion.refs_9_
  228.5 5.9 %attend.6 = bf16[256,768]{1,0:T(8,128)(2,1)} custom-call(s32[1]{0:T(128)} %bitcast.10.dest_ref, bf16[6,4,256,128]{3,2,1,0:T(8,128)(2,1)} %bitcast.56, bf16[6,1024,128]{2,1,0:T(8,128)(2,1)} %bitcast.60, bf16[6,1024,128]{2,1,0:T(8,128)(2,1)} %bitcast.64), custom_call_target="tpu_custom_call" | custom-call | flops 805306368 | bytes 3932160 | tf_op jit(solution)/shard_map/attend/pallas_call | solution.py:153
  234.5 5.9 %attend.5 = bf16[256,768]{1,0:T(8,128)(2,1)} custom-call(s32[1]{0:T(128)} %bitcast.9.dest_ref, bf16[6,4,256,128]{3,2,1,0:T(8,128)(2,1)} %bitcast.57, bf16[6,1024,128]{2,1,0:T(8,128)(2,1)} %bitcast.61, bf16[6,1024,128]{2,1,0:T(8,128)(2,1)} %bitcast.65), custom_call_target="tpu_custom_call" | custom-call | flops 805306368 | bytes 3932160 | tf_op jit(solution)/shard_map/attend/pallas_call | solution.py:153
  242.3 5.9 %attend.4 = bf16[256,768]{1,0:T(8,128)(2,1)} custom-call(s32[1]{0:T(128)} %bitcast.dest_ref, bf16[6,4,256,128]{3,2,1,0:T(8,128)(2,1)} %bitcast.58, bf16[6,1024,128]{2,1,0:T(8,128)(2,1)} %bitcast.62, bf16[6,1024,128]{2,1,0:T(8,128)(2,1)} %bitcast.66), custom_call_target="tpu_custom_call" | custom-call | flops 805306368 | bytes 3932160 | tf_op jit(solution)/shard_map/attend/pallas_call | solution.py:153
  248.3 2.0 collective-permute-start.3
  250.3 5.9 %attend.7.part_ref = bf16[256,768]{1,0:T(8,128)(2,1)} custom-call(s32[1]{0:T(128)} %bitcast.11.dest_ref, bf16[6,4,256,128]{3,2,1,0:T(8,128)(2,1)} %bitcast.59, bf16[6,1024,128]{2,1,0:T(8,128)(2,1)} %bitcast.63, bf16[6,1024,128]{2,1,0:T(8,128)(2,1)} %bitcast.67), custom_call_target="tpu_custom_call" | custom-call | flops 805306368 | bytes 3932160 | tf_op jit(solution)/shard_map/attend/pallas_call | solution.py:153
  256.2 3.4 %collective-permute-start.20 = (bf16[1,256]{1,0:T(2,128)(2,1)S(1)}, bf16[1,256]{1,0:T(2,128)(2,1)S(1)}, u32[]{:S(2)}, u32[]{:S(2)}) collective-permute-start(bf16[1,256]{1,0:T(2,128)(2,1)S(1)} %get-tuple-element.26), channel_id=1, source_target_pairs={{2,4},{3,5},{6,8},{7,9},{10,12},{11,13},{4,2},{5,3},{8,6},{9,7},{1... | collective-permute-start | bytes 1544 | tf_op jit(solution)/shard_map/ppermute | solution.py:310
  259.6 6.3 %add_part.3.refs_8_ = f32[256,3072]{1,0:T(8,128)} custom-call(bf16[256,768]{1,0:T(8,128)(2,1)} %attend.7.part_ref, bf16[3072,384]{1,0:T(8,128)(2,1)} %copy-done.1, bf16[3072,384]{1,0:T(8,128)(2,1)} %collective-permute-done.10.refs_1_, bf16[3072,384]{1,0:T(8,128)(2,1)} %collective-permute-done.11.refs_2_, bf16[3072,384]{1,0:T(8,128)(2,1)} %collective-permute-done.12.refs_3_, ...), custom_call_target="tpu_custom_call" | custom-call | flops 1207959552 | bytes 11010048 | tf_op jit(solution)/shard_map/add_part/pallas_call | solution.py:196
  265.9 6.8 %add_part.4.refs_8_ = f32[256,3072]{1,0:T(8,128)} custom-call(bf16[256,768]{1,0:T(8,128)(2,1)} %collective-permute-done.18.part_ref, bf16[3072,384]{1,0:T(8,128)(2,1)} %copy-done.1, bf16[3072,384]{1,0:T(8,128)(2,1)} %collective-permute-done.10.refs_1_, bf16[3072,384]{1,0:T(8,128)(2,1)} %collective-permute-done.11.refs_2_, ...), custom_call_target="tpu_custom_call", output_to_operand_aliasing={{}: (9, {})} | custom-call | flops 1207959552 | bytes 11010048 | tf_op jit(solution)/shard_map/add_part/pallas_call | solution.py:196
  273.5 6.9 %add_part.5.refs_8_ = f32[256,3072]{1,0:T(8,128)} custom-call(bf16[256,768]{1,0:T(8,128)(2,1)} %copy-done.8, bf16[3072,384]{1,0:T(8,128)(2,1)} %copy-done.1, bf16[3072,384]{1,0:T(8,128)(2,1)} %collective-permute-done.10.refs_1_, bf16[3072,384]{1,0:T(8,128)(2,1)} %collective-permute-done.11.refs_2_, ...), custom_call_target="tpu_custom_call", output_to_operand_aliasing={{}: (9, {})} | custom-call | flops 1207959552 | bytes 11010048 | tf_op jit(solution)/shard_map/add_part/pallas_call | solution.py:196
  281.2 8.2 %finish.1 = (f32[128,256]{1,0:T(8,128)}, bf16[128,256]{1,0:T(8,128)(2,1)}) custom-call(f32[2]{0:T(128)} %pad_maximum_fusion.1.coef_ref, bf16[256,768]{1,0:T(8,128)(2,1)} %copy-done.9, bf16[3072,384]{1,0:T(8,128)(2,1)} %copy-done.1, bf16[3072,384]{1,0:T(8,128)(2,1)} %collective-permute-done.10.refs_1_, bf16[3072,384]{1,0:T(8,128)(2,1)} %collective-permute-done.11.refs_2_, ...), custom_call_target="tpu_custom_call" | custom-call | flops 1207959552 | bytes 7864320 | tf_op jit(solution)/shard_map/finish/pallas_call | solution.py:268
  289.4 3.3 %collective-permute-start.19 = (bf16[128,256]{1,0:T(8,128)(2,1)}, bf16[128,256]{1,0:T(8,128)(2,1)S(1)}, u32[]{:S(2)}, u32[]{:S(2)}) collective-permute-start(bf16[128,256]{1,0:T(8,128)(2,1)} %get-tuple-element.23), channel_id=1, source_target_pairs={{2,4},{3,5},{6,8},{7,9},{10,12},{11,13},{4,2},{5,3},{8,6},{9,7},{1... | collective-permute-start | bytes 196616 | tf_op jit(solution)/shard_map/ppermute | solution.py:414
  292.7 5.0 %collective-permute-done.19 = bf16[128,256]{1,0:T(8,128)(2,1)S(1)} collective-permute-done((bf16[128,256]{1,0:T(8,128)(2,1)}, bf16[128,256]{1,0:T(8,128)(2,1)S(1)}, u32[]{:S(2)}, u32[]{:S(2)}) %collective-permute-start.19) | collective-permute-done | bytes 65568 | tf_op jit(solution)/shard_map/ppermute | solution.py:414
  (85 shorter events, 31.1 us)
Async XLA Ops:
  7.2 5.5 %copy-start = (bf16[768,768]{1,0:T(8,128)(2,1)S(1)}, bf16[768,768]{1,0:T(8,128)(2,1)}, u32[]{:S(2)}) copy-start(bf16[768,768]{1,0:T(8,128)(2,1)} %param.11) | copy-start | bytes 3538948
  7.2 167.5 %all-gather.5.cloned.1.call-start = ((), (), s32[]{:S(2)}) async-start(), calls=%async_computation.1 | async-start | bytes 3932160 | tf_op jit(solution)/shard_map/all_gather | solution.py:334
  10.5 177.1 %all-gather.3.cloned.1.call-start = ((), (), s32[]{:S(2)}) async-start(), calls=%async_computation | async-start | bytes 3932160 | tf_op jit(solution)/shard_map/all_gather | solution.py:334
  10.6 96.3 %collective-permute-start.1 = (bf16[768,2304]{1,0:T(8,128)(2,1)}, bf16[768,2304]{1,0:T(8,128)(2,1)}, u32[]{:S(2)}, u32[]{:S(2)}) collective-permute-start(bf16[768,2304]{1,0:T(8,128)(2,1)} %refs_0_.3), channel_id=1, source_target_pairs={{0,8},{4,12},{8,0},{12,4},{1,9},{5,13},{9,1},{13,5},{2,10},{6,14},... | collective-permute-start | bytes 10616840 | tf_op jit(solution)/shard_map/ppermute | solution.py:19
  12.7 75.3 %copy-start.3 = (bf16[768,384]{1,0:T(8,128)(2,1)}, bf16[768,384]{1,0:T(8,128)(2,1)S(1)}, u32[]{:S(2)}) copy-start(bf16[768,384]{1,0:T(8,128)(2,1)S(1)} %constant_dynamic-slice_fusion) | copy-start | bytes 1769476
  12.7 20.8 %collective-permute-start.4 = (bf16[768,384]{1,0:T(8,128)(2,1)S(1)}, bf16[768,384]{1,0:T(8,128)(2,1)S(1)}, u32[]{:S(2)}, u32[]{:S(2)}) collective-permute-start(bf16[768,384]{1,0:T(8,128)(2,1)S(1)} %constant_dynamic-slice_fusion), channel_id=1, source_target_pairs={{0,1},{1,2},{2,3},{4,5},{5,6},{6,7},{8,9},{9,10},{10,11},{12,13},{... | collective-permute-start | bytes 1769480 | tf_op jit(solution)/shard_map/ppermute | solution.py:32
  16.0 31.1 %collective-permute-start.5 = (bf16[768,384]{1,0:T(8,128)(2,1)S(1)}, bf16[768,384]{1,0:T(8,128)(2,1)S(1)}, u32[]{:S(2)}, u32[]{:S(2)}) collective-permute-start(bf16[768,384]{1,0:T(8,128)(2,1)S(1)} %constant_dynamic-slice_fusion), channel_id=1, source_target_pairs={{1,0},{2,1},{3,2},{5,4},{6,5},{7,6},{9,8},{10,9},{11,10},{13,12},{... | collective-permute-start | bytes 1769480 | tf_op jit(solution)/shard_map/ppermute | solution.py:35
  33.5 14.8 %collective-permute-start.8 = (bf16[768,384]{1,0:T(8,128)(2,1)S(1)}, bf16[768,384]{1,0:T(8,128)(2,1)S(1)}, u32[]{:S(2)}, u32[]{:S(2)}) collective-permute-start(bf16[768,384]{1,0:T(8,128)(2,1)S(1)} %collective-permute-done.4), channel_id=1, source_target_pairs={{1,2},{2,3},{5,6},{6,7},{9,10},{10,11},{13,14},{14,15},{17,18},{18... | collective-permute-start | bytes 1769480 | tf_op jit(solution)/shard_map/ppermute | solution.py:32
  47.1 37.0 %collective-permute-start.6 = (bf16[768,384]{1,0:T(8,128)(2,1)S(1)}, bf16[768,384]{1,0:T(8,128)(2,1)}, u32[]{:S(2)}, u32[]{:S(2)}) collective-permute-start(bf16[768,384]{1,0:T(8,128)(2,1)S(1)} %collective-permute-done.5), channel_id=1, source_target_pairs={{1,0},{2,1},{5,4},{6,5},{9,8},{10,9},{13,12},{14,13},{17,16},{18,1... | collective-permute-start | bytes 1769480 | tf_op jit(solution)/shard_map/ppermute | solution.py:35
  48.4 51.4 %collective-permute-start.9 = (bf16[768,384]{1,0:T(8,128)(2,1)S(1)}, bf16[768,384]{1,0:T(8,128)(2,1)}, u32[]{:S(2)}, u32[]{:S(2)}) collective-permute-start(bf16[768,384]{1,0:T(8,128)(2,1)S(1)} %collective-permute-done.8), channel_id=1, source_target_pairs={{2,3},{6,7},{10,11},{14,15},{18,19},{22,23},{26,27},{30,31}} | collective-permute-start | bytes 1769480 | tf_op jit(solution)/shard_map/ppermute | solution.py:32
  84.1 21.6 %collective-permute-start.7 = (bf16[768,384]{1,0:T(8,128)(2,1)}, bf16[768,384]{1,0:T(8,128)(2,1)}, u32[]{:S(2)}, u32[]{:S(2)}) collective-permute-start(bf16[768,384]{1,0:T(8,128)(2,1)} %collective-permute-done.6), channel_id=1, source_target_pairs={{1,0},{5,4},{9,8},{13,12},{17,16},{21,20},{25,24},{29,28}} | collective-permute-start | bytes 1769480 | tf_op jit(solution)/shard_map/ppermute | solution.py:35
  88.0 86.6 %collective-permute-start = (bf16[768,2304]{1,0:T(8,128)(2,1)}, bf16[768,2304]{1,0:T(8,128)(2,1)}, u32[]{:S(2)}, u32[]{:S(2)}) collective-permute-start(bf16[768,2304]{1,0:T(8,128)(2,1)} %refs_0_.3), channel_id=1, source_target_pairs={{0,4},{4,0},{8,12},{12,8},{1,5},{5,1},{9,13},{13,9},{2,6},{6,2},{1... | collective-permute-start | bytes 10616840 | tf_op jit(solution)/shard_map/ppermute | solution.py:19
  99.8 11.5 %copy-start.4 = (bf16[768,384]{1,0:T(8,128)(2,1)S(1)}, bf16[768,384]{1,0:T(8,128)(2,1)}, u32[]{:S(2)}) copy-start(bf16[768,384]{1,0:T(8,128)(2,1)} %copy-done.3) | copy-start | bytes 1769476
  106.9 67.8 %collective-permute-start.2 = (bf16[768,2304]{1,0:T(8,128)(2,1)}, bf16[768,2304]{1,0:T(8,128)(2,1)}, u32[]{:S(2)}, u32[]{:S(2)}) collective-permute-start(bf16[768,2304]{1,0:T(8,128)(2,1)} %collective-permute-done.1.refs_2_), channel_id=1, source_target_pairs={{0,4},{4,0},{8,12},{12,8},{1,5},{5,1},{9,13},{13,9},{2,6},{6,2},{1... | collective-permute-start | bytes 10616840 | tf_op jit(solution)/shard_map/ppermute | solution.py:19
  111.5 76.1 %copy-start.1 = (bf16[3072,384]{1,0:T(8,128)(2,1)}, bf16[3072,384]{1,0:T(8,128)(2,1)S(1)}, u32[]{:S(2)}) copy-start(bf16[3072,384]{1,0:T(8,128)(2,1)S(1)} %pad_maximum_fusion.refs_0_) | copy-start | bytes 7077892
  111.5 53.0 %collective-permute-start.13 = (bf16[3072,384]{1,0:T(8,128)(2,1)S(1)}, bf16[3072,384]{1,0:T(8,128)(2,1)}, u32[]{:S(2)}, u32[]{:S(2)}) collective-permute-start(bf16[3072,384]{1,0:T(8,128)(2,1)S(1)} %pad_maximum_fusion.refs_0_), channel_id=1, source_target_pairs={{0,8},{4,12},{8,0},{12,4},{1,9},{5,13},{9,1},{13,5},{2,10},{6,14},... | collective-permute-start | bytes 7077896 | tf_op jit(solution)/shard_map/ppermute | solution.py:19
  112.5 88.1 %collective-permute-start.10 = (bf16[3072,384]{1,0:T(8,128)(2,1)S(1)}, bf16[3072,384]{1,0:T(8,128)(2,1)}, u32[]{:S(2)}, u32[]{:S(2)}) collective-permute-start(bf16[3072,384]{1,0:T(8,128)(2,1)S(1)} %pad_maximum_fusion.refs_0_), channel_id=1, source_target_pairs={{0,16},{16,0},{1,17},{17,1},{2,18},{18,2},{3,19},{19,3},{4,20},{20... | collective-permute-start | bytes 7077896 | tf_op jit(solution)/shard_map/ppermute | solution.py:352
  164.5 52.3 %collective-permute-start.14 = (bf16[3072,384]{1,0:T(8,128)(2,1)}, bf16[3072,384]{1,0:T(8,128)(2,1)}, u32[]{:S(2)}, u32[]{:S(2)}) collective-permute-start(bf16[3072,384]{1,0:T(8,128)(2,1)} %collective-permute-done.13.refs_4_), channel_id=1, source_target_pairs={{0,16},{16,0},{1,17},{17,1},{2,18},{18,2},{3,19},{19,3},{4,20},{20... | collective-permute-start | bytes 7077896 | tf_op jit(solution)/shard_map/ppermute | solution.py:352
  170.7 1.5 copy-start.6
  173.6 66.8 %collective-permute-start.11 = (bf16[3072,384]{1,0:T(8,128)(2,1)S(1)}, bf16[3072,384]{1,0:T(8,128)(2,1)}, u32[]{:S(2)}, u32[]{:S(2)}) collective-permute-start(bf16[3072,384]{1,0:T(8,128)(2,1)S(1)} %pad_maximum_fusion.refs_0_), channel_id=1, source_target_pairs={{0,4},{4,0},{8,12},{12,8},{1,5},{5,1},{9,13},{13,9},{2,6},{6,2},{1... | collective-permute-start | bytes 7077896 | tf_op jit(solution)/shard_map/ppermute | solution.py:19
  174.7 73.6 %collective-permute-start.15 = (bf16[3072,384]{1,0:T(8,128)(2,1)}, bf16[3072,384]{1,0:T(8,128)(2,1)}, u32[]{:S(2)}, u32[]{:S(2)}) collective-permute-start(bf16[3072,384]{1,0:T(8,128)(2,1)} %collective-permute-done.13.refs_4_), channel_id=1, source_target_pairs={{0,4},{4,0},{8,12},{12,8},{1,5},{5,1},{9,13},{13,9},{2,6},{6,2},{1... | collective-permute-start | bytes 7077896 | tf_op jit(solution)/shard_map/ppermute | solution.py:19
  187.6 32.2 %copy-start.7 = (bf16[3072,64]{0,1:T(8,128)(2,1)S(1)}, bf16[3072,64]{0,1:T(8,128)(2,1)}, u32[]{:S(2)}) copy-start(bf16[3072,64]{0,1:T(8,128)(2,1)} %param.12) | copy-start | bytes 1179652
  200.5 26.0 %copy-start.2 = (bf16[1,256,3072]{2,1,0:T(8,128)(2,1)S(1)}, bf16[1,256,3072]{2,1,0:T(8,128)(2,1)}, u32[]{:S(2)}) copy-start(bf16[1,256,3072]{2,1,0:T(8,128)(2,1)} %param.8) | copy-start | bytes 4718596
  200.5 55.6 %collective-permute-start.12 = (bf16[3072,384]{1,0:T(8,128)(2,1)}, bf16[3072,384]{1,0:T(8,128)(2,1)}, u32[]{:S(2)}, u32[]{:S(2)}) collective-permute-start(bf16[3072,384]{1,0:T(8,128)(2,1)} %collective-permute-done.10.refs_1_), channel_id=1, source_target_pairs={{0,4},{4,0},{8,12},{12,8},{1,5},{5,1},{9,13},{13,9},{2,6},{6,2},{1... | collective-permute-start | bytes 7077896 | tf_op jit(solution)/shard_map/ppermute | solution.py:19
  216.8 42.8 %collective-permute-start.16 = (bf16[3072,384]{1,0:T(8,128)(2,1)}, bf16[3072,384]{1,0:T(8,128)(2,1)}, u32[]{:S(2)}, u32[]{:S(2)}) collective-permute-start(bf16[3072,384]{1,0:T(8,128)(2,1)} %collective-permute-done.14.refs_5_), channel_id=1, source_target_pairs={{0,4},{4,0},{8,12},{12,8},{1,5},{5,1},{9,13},{13,9},{2,6},{6,2},{1... | collective-permute-start | bytes 7077896 | tf_op jit(solution)/shard_map/ppermute | solution.py:19
  223.6 4.4 %copy-start.10 = (s32[1,256]{1,0:T(1,128)S(1)}, s32[1,256]{1,0:T(1,128)}, u32[]{:S(2)}) copy-start(s32[1,256]{1,0:T(1,128)} %param.14) | copy-start | bytes 3076
  226.8 1.2 copy-start.5
  234.5 31.5 %collective-permute-start.18 = (bf16[256,768]{1,0:T(8,128)(2,1)}, bf16[256,768]{1,0:T(8,128)(2,1)}, u32[]{:S(2)}, u32[]{:S(2)}) collective-permute-start(bf16[256,768]{1,0:T(8,128)(2,1)} %attend.6), channel_id=1, source_target_pairs={{0,2},{1,3},{2,0},{3,1},{4,6},{5,7},{6,4},{7,5},{8,10},{9,11},{10,... | collective-permute-start | bytes 1179656 | tf_op jit(solution)/shard_map/ppermute | solution.py:394
  240.4 32.4 %collective-permute-start.17 = (bf16[256,768]{1,0:T(8,128)(2,1)}, bf16[256,768]{1,0:T(8,128)(2,1)S(1)}, u32[]{:S(2)}, u32[]{:S(2)}) collective-permute-start(bf16[256,768]{1,0:T(8,128)(2,1)} %attend.5), channel_id=1, source_target_pairs={{0,1},{1,2},{2,3},{3,0},{4,5},{5,6},{6,7},{7,4},{8,9},{9,10},{10,1... | collective-permute-start | bytes 1179656 | tf_op jit(solution)/shard_map/ppermute | solution.py:394
  248.3 32.2 %collective-permute-start.3 = (bf16[256,768]{1,0:T(8,128)(2,1)}, bf16[256,768]{1,0:T(8,128)(2,1)S(1)}, u32[]{:S(2)}, u32[]{:S(2)}) collective-permute-start(bf16[256,768]{1,0:T(8,128)(2,1)} %attend.4), channel_id=1, source_target_pairs={{0,3},{1,0},{2,1},{3,2},{4,7},{5,4},{6,5},{7,6},{8,11},{9,8},{10,9... | collective-permute-start | bytes 1179656 | tf_op jit(solution)/shard_map/ppermute | solution.py:394
  256.2 36.5 %collective-permute-start.20 = (bf16[1,256]{1,0:T(2,128)(2,1)S(1)}, bf16[1,256]{1,0:T(2,128)(2,1)S(1)}, u32[]{:S(2)}, u32[]{:S(2)}) collective-permute-start(bf16[1,256]{1,0:T(2,128)(2,1)S(1)} %get-tuple-element.26), channel_id=1, source_target_pairs={{2,4},{3,5},{6,8},{7,9},{10,12},{11,13},{4,2},{5,3},{8,6},{9,7},{1... | collective-permute-start | bytes 1544 | tf_op jit(solution)/shard_map/ppermute | solution.py:310
  289.4 8.2 %collective-permute-start.19 = (bf16[128,256]{1,0:T(8,128)(2,1)}, bf16[128,256]{1,0:T(8,128)(2,1)S(1)}, u32[]{:S(2)}, u32[]{:S(2)}) collective-permute-start(bf16[128,256]{1,0:T(8,128)(2,1)} %get-tuple-element.23), channel_id=1, source_target_pairs={{2,4},{3,5},{6,8},{7,9},{10,12},{11,13},{4,2},{5,3},{8,6},{9,7},{1... | collective-permute-start | bytes 196616 | tf_op jit(solution)/shard_map/ppermute | solution.py:414
  (2 other events, 1.6 us)
Sparse Core Ops, SparseCore 0:
  10.6 87.0 all-gather.4
  99.2 63.1 all-gather.2

commit v3 on v1

v3 whole, which is shorter than its diff:
```python
import functools
import math

import jax
import jax.numpy as jnp
from jax import lax
from jax.experimental import pallas as pl
from jax.experimental.pallas import tpu as pltpu
from jax.sharding import PartitionSpec as P

HD = 128
NSTEPS = 28
MIB = 1 << 20


def swap(value, axis, bit):
    count = lax.axis_size(axis)
    return lax.ppermute(value, axis, [(i, i ^ bit) for i in range(count)])


def bits_of(count):
    far = [1 << n for n in range(1, count.bit_length() - 1)]
    return far + [1]


def after(value, *others):
    return lax.optimization_barrier((value,) + others)[0]


def noise_level(index, steps):
    level = 1.0 - index / steps
    return 3.0 * level / (1.0 + 2.0 * level)


def turned(value, axis, turn):
    count = lax.axis_size(axis)
    return lax.ppermute(value, axis, [(i, (i + turn) % count) for i in range(count)])


def layer_norm(values):
    mean = jnp.mean(values, axis=-1, keepdims=True)
    centred = values - mean
    spread = jnp.mean(centred * centred, axis=-1, keepdims=True)
    return centred * lax.rsqrt(spread + 1e-06)


def root_norm(values):
    spread = jnp.mean(values * values, axis=-1, keepdims=True)
    return (values * lax.rsqrt(spread + 1e-06)).astype(jnp.bfloat16)


def norm_kernel(blocks, starts_ref, hidden_ref, mod_ref, out_ref):
    local = hidden_ref[...].astype(jnp.float32)
    mean = jnp.mean(local, axis=-1, keepdims=True)
    centred = local - mean
    spread = jnp.mean(centred * centred, axis=-1, keepdims=True)
    scaling = lax.rsqrt(spread + 1e-06)
    width = hidden_ref.shape[1] // blocks
    for n in range(blocks):
        taken = pl.ds(pl.multiple_of(starts_ref[n], HD), width)
        values = (hidden_ref[:, taken].astype(jnp.float32) - mean) * scaling
        values = values * (1.0 + mod_ref[1:2, taken]) + mod_ref[0:1, taken]
        out_ref[:, n * width : (n + 1) * width] = values.astype(jnp.bfloat16)


def norm_rows(hidden, modulation, starts, first, rows):
    width = hidden.shape[1]
    block = math.gcd(math.gcd(first, rows), 64)
    return pl.pallas_call(
        functools.partial(norm_kernel, starts.shape[0]),
        grid=(rows // block,),
        in_specs=[
            pl.BlockSpec(memory_space=pltpu.SMEM),
            pl.BlockSpec((block, width), lambda i: (first // block + i, 0)),
            pl.BlockSpec(modulation.shape, lambda i: (0, 0)),
        ],
        out_specs=pl.BlockSpec((block, width), lambda i: (i, 0)),
        out_shape=jax.ShapeDtypeStruct((rows, width), jnp.bfloat16),
        name="norm_in",
    )(starts, hidden, modulation)


def product(x_ref, blocks):
    height = x_ref.shape[1] // len(blocks)
    total = 0.0
    for n, block in enumerate(blocks):
        total += jnp.dot(
            x_ref[:, n * height : (n + 1) * height],
            block[...],
            preferred_element_type=jnp.float32,
        )
    return total


def project_kernel(sources, blocks, *refs):
    x_refs, w_refs = refs[:sources], refs[sources : sources + blocks]
    q_ref, k_ref, v_ref, x_all = refs[sources + blocks :]
    rows = x_refs[0].shape[0]

    @pl.when(pl.program_id(0) == 0)
    def _():
        for n in range(sources):
            x_all[n * rows : (n + 1) * rows] = x_refs[n][...]

    proj = product(x_all, w_refs)
    for h in range(q_ref.shape[0]):
        query, key, value = (proj[:, (3 * h + i) * HD : (3 * h + i + 1) * HD] for i in range(3))
        q_ref[h] = root_norm(query)
        k_ref[h] = root_norm(key)
        v_ref[h] = value.astype(jnp.bfloat16)


def project(sources, blocks):
    rows, width = sources[0].shape
    length = rows * len(sources)
    total = blocks[0].shape[1]
    heads = total // (3 * HD)
    many = 2 if heads % 2 == 0 else 1
    out = jax.ShapeDtypeStruct((heads, length, HD), jnp.bfloat16)
    return pl.pallas_call(
        functools.partial(project_kernel, len(sources), len(blocks)),
        grid=(heads // many,),
        in_specs=[pl.BlockSpec((rows, width), lambda h: (0, 0))] * len(sources)
        + [pl.BlockSpec((width // len(blocks), many * 3 * HD), lambda h: (0, h))] * len(blocks),
        out_specs=[pl.BlockSpec((many, length, HD), lambda h: (h, 0, 0))] * 3,
        out_shape=[out] * 3,
        scratch_shapes=[pltpu.VMEM((length, width), jnp.bfloat16)],
        compiler_params=pltpu.CompilerParams(vmem_limit_bytes=60 * MIB),
        cost_estimate=pl.CostEstimate(
            flops=2 * length * width * total,
            bytes_accessed=2 * (length * width + width * total * 2),
            transcendentals=0,
        ),
        name="project",
    )(*sources, *blocks)


def attend_kernel(blocks, devices, place_ref, x_ref, *refs):
    first, second = refs[0:3], refs[3:6]
    w_refs = refs[6 : 6 + blocks]
    outs = refs[6 + blocks : 6 + blocks + devices]
    queries, keys, values = refs[6 + blocks + devices :]
    proj = product(x_ref, w_refs)
    queries[...] = root_norm(proj[:, :HD])
    sets = (first[1].shape[1], second[1].shape[1], x_ref.shape[0])
    ends = (sets[0], sets[0] + sets[1], sum(sets))
    keys[: ends[0]] = first[1][0]
    keys[ends[0] : ends[1]] = second[1][0]
    keys[ends[1] :] = root_norm(proj[:, HD : 2 * HD])
    values[: ends[0], :HD] = first[2][0]
    values[ends[0] : ends[1], :HD] = second[2][0]
    values[ends[1] :, :HD] = proj[:, 2 * HD :].astype(jnp.bfloat16)
    values[:, HD:] = jnp.ones((ends[2], HD), jnp.bfloat16)
    rows = [count // devices for count in sets]
    for turn in range(devices):
        dest = lax.rem(place_ref[0] + turn, devices)
        slot = (devices - turn) % devices
        query = jnp.concatenate(
            [
                first[0][0, pl.ds(pl.multiple_of(dest * rows[0], rows[0]), rows[0])],
                second[0][0, slot * rows[1] : (slot + 1) * rows[1]],
                queries[pl.ds(pl.multiple_of(dest * rows[2], rows[2]), rows[2])],
            ],
            axis=0,
        )
        scores = lax.dot_general(
            query, keys[...], (((1,), (1,)), ((), ())), preferred_element_type=jnp.float32
        )
        expo = jnp.exp(scores * (1.0 / math.sqrt(HD))).astype(jnp.bfloat16)
        mixed = jnp.dot(expo, values[...], preferred_element_type=jnp.float32)
        outs[turn][...] = (mixed[:, :HD] / mixed[:, HD:]).astype(jnp.bfloat16)


def attend(place, devices, x, first, second, blocks, start, heads):
    last, width = x.shape
    length = last + first[0].shape[1] + second[0].shape[1]
    rows = length // devices
    head = lambda value: pl.BlockSpec((1, value.shape[1], HD), lambda h: (start + h, 0, 0))
    out = jax.ShapeDtypeStruct((rows, heads * HD), jnp.bfloat16)
    return pl.pallas_call(
        functools.partial(attend_kernel, len(blocks), devices),
        grid=(heads,),
        in_specs=[
            pl.BlockSpec(memory_space=pltpu.SMEM),
            pl.BlockSpec((last, width), lambda h: (0, 0)),
        ]
        + [head(value) for value in first + second]
        + [pl.BlockSpec((width // len(blocks), 3 * HD), lambda h: (0, start + h))] * len(blocks),
        out_specs=[pl.BlockSpec((rows, HD), lambda h: (0, h))] * devices,
        out_shape=[out] * devices,
        scratch_shapes=[
            pltpu.VMEM((last, HD), jnp.bfloat16),
            pltpu.VMEM((length, HD), jnp.bfloat16),
            pltpu.VMEM((length, 2 * HD), jnp.bfloat16),
        ],
        compiler_params=pltpu.CompilerParams(vmem_limit_bytes=60 * MIB),
        cost_estimate=pl.CostEstimate(
            flops=4 * length * length * heads * HD + 2 * last * width * 3 * HD * heads,
            bytes_accessed=2 * heads * HD * (4 * length + 3 * width),
            transcendentals=length * length * heads,
        ),
        name="attend",
    )(place.reshape(1), x, *first, *second, *blocks)


def multiply(parts, offsets, starts_ref, sources, weights, sems, wide, store):
    depth = [part.shape[1] for part in parts]
    width = weights.shape[2]
    copies = []
    for p, source in enumerate(sources):
        copies.append([])
        for n, offset in enumerate(offsets):
            to = sum(depth[:n])
            copies[p].append(
                pltpu.make_async_copy(
                    source.at[pl.ds(offset, depth[n])],
                    weights.at[p, pl.ds(to, depth[n])],
                    sems.at[p, n],
                )
            )
            copies[p][n].start()
    for n, part in enumerate(parts):
        wide[:, sum(depth[:n]) : sum(depth[: n + 1])] = part[...]
    for p in range(len(sources)):
        for copy in copies[p]:
            copy.wait()
        cols = pl.ds(pl.multiple_of(starts_ref[p], HD), width)
        store(p, cols, jnp.dot(wide[...], weights[p], preferred_element_type=jnp.float32))


def add_kernel(offsets, count, starts_ref, *refs):
    parts = refs[: len(offsets)]
    sources = refs[len(offsets) : len(offsets) + count]
    before_ref, mod_ref, out_ref, weights, wide, sems = refs[len(offsets) + count :]

    def store(p, cols, summed):
        out_ref[:, cols] = before_ref[:, cols].astype(jnp.float32) + mod_ref[2:3, cols] * summed

    multiply(parts, offsets, starts_ref, sources, weights, sems, wide, store)


def finish_kernel(offsets, count, starts_ref, coef_ref, *refs):
    parts = refs[: len(offsets)]
    sources = refs[len(offsets) : len(offsets) + count]
    before_ref, mod_ref, head_ref, latent_ref, weight_ref, out_ref, sent_ref = refs[
        len(offsets) + count : len(offsets) + count + 7
    ]
    weights, wide, sems, mixed, extra = refs[len(offsets) + count + 7 :]
    width = weights.shape[2]
    copies = []
    for p in range(count):
        cols = pl.ds(pl.multiple_of(starts_ref[p], HD), width)
        copies.append(
            pltpu.make_async_copy(before_ref.at[:, cols], mixed.at[:, cols], extra.at[p])
        )
        copies[p].start()

    def store(p, cols, summed):
        copies[p].wait()
        mixed[:, cols] += mod_ref[2:3, cols] * summed

    multiply(parts, offsets, starts_ref, sources, weights, sems, wide, store)
    normed = layer_norm(mixed[...]) * (1.0 + mod_ref[4:5, :]) + mod_ref[3:4, :]
    velocity = lax.dot_general(
        head_ref[...],
        normed.astype(jnp.bfloat16),
        (((1,), (1,)), ((), ())),
        preferred_element_type=jnp.float32,
    )
    channels = velocity.shape[0]
    base, weight = latent_ref[...], weight_ref[...]
    moved = (base + coef_ref[1] * velocity) * weight
    guess = (base - coef_ref[0] * velocity) * weight
    out_ref[:channels, :] = moved
    out_ref[channels:, :] = guess
    sent_ref[:channels, :] = moved.astype(jnp.bfloat16)
    sent_ref[channels:, :] = guess.astype(jnp.bfloat16)


def accumulate(parts, offsets, starts, pieces, before, modulation, last=None):
    rows, width = before.shape
    depth = sum(part.shape[1] for part in parts)
    count = len(pieces)
    smem = pl.BlockSpec(memory_space=pltpu.SMEM)
    vmem = pl.BlockSpec(memory_space=pltpu.VMEM)
    hbm = pl.BlockSpec(memory_space=pl.ANY)
    scratch = [
        pltpu.VMEM((count, depth, pieces[0].shape[1]), jnp.bfloat16),
        pltpu.VMEM((rows, depth), jnp.bfloat16),
        pltpu.SemaphoreType.DMA((count, len(parts))),
    ]
    params = dict(
        compiler_params=pltpu.CompilerParams(vmem_limit_bytes=60 * MIB),
        cost_estimate=pl.CostEstimate(
            flops=2 * rows * width * depth,
            bytes_accessed=2 * width * depth + 8 * rows * width,
            transcendentals=0,
        ),
    )
    if last is None:
        aliased = before.dtype == jnp.float32
        return pl.pallas_call(
            functools.partial(add_kernel, offsets, count),
            in_specs=[smem] + [vmem] * len(parts) + [hbm] * count + [vmem] * 2,
            out_specs=vmem,
            out_shape=jax.ShapeDtypeStruct((rows, width), jnp.float32),
            scratch_shapes=scratch,
            input_output_aliases={1 + len(parts) + count: 0} if aliased else {},
            name="add_parts",
            **params,
        )(starts, *parts, *pieces, before, modulation)
    coef, head, latent, weight = last
    channels = head.shape[0]
    return pl.pallas_call(
        functools.partial(finish_kernel, offsets, count),
        in_specs=[smem, smem] + [vmem] * len(parts) + [hbm] * (count + 1) + [vmem] * 4,
        out_specs=[vmem, vmem],
        out_shape=[
            jax.ShapeDtypeStruct((2 * channels, rows), jnp.float32),
            jax.ShapeDtypeStruct((2 * channels, rows), jnp.bfloat16),
        ],
        scratch_shapes=scratch
        + [pltpu.VMEM((rows, width), jnp.float32), pltpu.SemaphoreType.DMA((count,))],
        name="finish",
        **params,
    )(starts, coef, *parts, *pieces, before, modulation, head, latent, weight)


def shards(hidden, modulation, w_qkv, w_out, w_head, latent, weights_int, step_index):
    local = hidden[0]
    rows = local.shape[0]
    devices = lax.axis_size("seq")
    tiles = lax.axis_size("tile")
    groups = lax.axis_size("group")
    place, tile, group = lax.axis_index("seq"), lax.axis_index("tile"), lax.axis_index("group")
    far, near = bits_of(tiles)[:-1], bits_of(tiles)[-1]

    weight = weights_int.astype(jnp.float32)
    joins = [
        (t * devices + s, (t + 1) * devices + s - (devices - 2))
        for t in range(tiles - 1)
        for s in range(devices - 2, devices)
    ]
    joins += [
        (t * devices + s, (t - 1) * devices + s + (devices - 2))
        for t in range(1, tiles)
        for s in range(2)
    ]
    norms = weight + lax.ppermute(
        weight.astype(jnp.bfloat16), ("tile", "seq"), joins
    ).astype(jnp.float32)

    height = w_qkv.shape[0]
    blocks = {0: w_qkv}
    for bit in far + [near]:
        blocks.update({d ^ bit: swap(blocks[d], "tile", bit) for d in list(blocks)})
    arrived = dict(blocks)
    row_starts = jnp.stack([(tile ^ d) * height for d in range(tiles)]).astype(jnp.int32)
    if height % HD:
        full = jnp.zeros((tiles * height, w_qkv.shape[1]), w_qkv.dtype)
        for d in range(tiles):
            full = lax.dynamic_update_slice_in_dim(full, blocks[d], row_starts[d], axis=0)
        blocks = {0: full}
        row_starts = jnp.zeros((1,), jnp.int32)
    blocks = [blocks[d] for d in range(len(blocks))]

    counts = (rows // 2, rows // 4, rows // 4)
    normed = [
        norm_rows(local, modulation, row_starts, sum(counts[:n]), counts[n]) for n in range(3)
    ]
    gathered = lax.all_gather(normed[0], "seq", axis=0, tiled=True)

    part = w_out.shape[1] // groups
    share = lax.dynamic_slice_in_dim(w_out, group * part, part, axis=1)
    share = [share] + [turned(share, "seq", turn) for turn in range(1, devices)]
    passed = [normed[1]] + [turned(normed[1], "seq", turn) for turn in range(1, devices)]
    gathered_last = lax.all_gather(normed[2], "seq", axis=0, tiled=True)
    columns = {(0, 0): jnp.concatenate(share, axis=0)}
    if far:
        columns[far[0], 0] = swap(after(columns[0, 0], arrived[far[0]]), "tile", far[0])
    first = project([gathered], blocks)
    if far:
        columns[far[0], 0] = after(columns[far[0], 0], first[0])
    for bit in far[1:]:
        columns.update({(d ^ bit, g): swap(columns[d, g], "tile", bit) for d, g in list(columns)})
    for turn in range(1, groups):
        columns.update(
            {(d, turn): turned(columns[d, 0], "group", turn) for d, g in list(columns) if g == 0}
        )
    second = project(passed, blocks)
    heads = w_qkv.shape[1] // (3 * HD)
    halves = [(0, (heads + 1) // 2), ((heads + 1) // 2, heads // 2)]
    sent = []
    for start, count in halves:
        sent.append(
            attend(place, devices, gathered_last, first, second, blocks, start, count)
        )
    columns.update(
        {
            (d ^ near, g): swap(
                after(columns[d, g], sent[0][0]) if g else columns[d, g], "tile", near
            )
            for d, g in list(columns)
        }
    )
    order = sorted(columns)
    pieces = [columns[key] for key in order]
    starts = jnp.stack(
        [
            (tile ^ d) * (part * groups) + lax.rem(group - g + groups, groups) * part
            for d, g in order
        ]
    ).astype(jnp.int32)
    if part % HD:
        whole = jnp.zeros((w_out.shape[0] * devices, part * len(order)), w_out.dtype)
        for n, piece in enumerate(pieces):
            whole = lax.dynamic_update_slice_in_dim(whole, piece, starts[n], axis=1)
        pieces, starts = [whole], jnp.zeros((1,), jnp.int32)

    turns = sorted(range(1, devices), key=lambda turn: -min(turn, devices - turn))
    received = [
        [turned(half[turn], "seq", turn) for turn in turns] for half in sent
    ]
    features = w_out.shape[0]
    offsets = [[turn * features + start * HD for turn in turns] for start, _ in halves]
    mixed = accumulate(
        [half[0] for half in sent],
        [start * HD for start, _ in halves],
        starts,
        pieces,
        local,
        modulation,
    )
    mixed = accumulate(received[0], offsets[0], starts, pieces, mixed, modulation)
    index = step_index[0].astype(jnp.float32)
    now = noise_level(index, NSTEPS)
    later = noise_level(index + 1.0, NSTEPS)
    weighted, to_join = accumulate(
        received[1],
        offsets[1],
        starts,
        pieces,
        mixed,
        modulation,
        (jnp.stack([now, later - now]), w_head.T, latent[0].T, weight),
    )
    other = lax.ppermute(to_join, ("tile", "seq"), joins).astype(jnp.float32)
    joined = (weighted + other) / norms
    channels = w_head.shape[1]
    return (joined[:channels].T[None], joined[channels:].T[None])


def solution(mesh):
    in_specs = (
        P(("group", "tile"), "seq", None),
        P("group", None),
        P("tile", "seq"),
        P("seq", "tile"),
        P(),
        P(("group", "tile"), "seq", None),
        P(("group", "tile"), "seq"),
        P("group"),
    )
    out_specs = (P(("group", "tile"), "seq", None), P(("group", "tile"), "seq", None))
    return jax.shard_map(shards, mesh=mesh, in_specs=in_specs, out_specs=out_specs, check_vma=False)
```

time: 323 us -> 336 us (1.040)
  local copies, waits for them, and re-layouts: 36.3 us -> 2.8 us
  starting transfers between devices: 23.2 us -> 44.5 us
  Pallas kernels: 57.2 us -> 78.3 us
  waiting for transfers between devices: 186 us -> 192 us
    all_gather x3 -> x2, waiting for transfers between devices: 47.3 us -> 0.02 us  [the longest x1 0.02 us: shards(): gathered_last = lax.all_gather(normed[2], 'seq', axis=0, tiled=True)]
    ppermute x8, waiting for transfers between devices: 71.1 us -> 107 us  [swap(): return lax.ppermute(value, axis, [(i, i ^ bit) for i in range(count)])]
    unnamed x69 -> x18, local copies, waits for them, and re-layouts: 32.3 us -> 1.47 us
    pallas_call x9 -> x10, Pallas kernels: 57.2 us -> 78.3 us  [the longest x2 22.6 us: project(): pl.pallas_call(functools.partial(project_kernel, len(sources), len(blocks...]
    ppermute x6 -> x15, waiting for transfers between devices: 67.8 us -> 85 us  [the longest x14 79.2 us: turned(): lax.ppermute(value, axis, [(i, (i + turn) % count) for i in range(count)])]
    ppermute x6 -> x15, starting transfers between devices: 11.6 us -> 26.3 us  [the longest x14 23.5 us: turned(): lax.ppermute(value, axis, [(i, (i + turn) % count) for i in range(count)])]
    ppermute x8, starting transfers between devices: 9.38 us -> 14.5 us  [swap(): return lax.ppermute(value, axis, [(i, i ^ bit) for i in range(count)])]
  transfers between devices with their start and end apart: 18 -> 26, of which waited for: 6 -> 8; matrix products, arithmetic and copies ran while one was open for 4% -> 1% of each run, Pallas kernels for 18% -> 23%
where the time goes in v3:
time: 336 us; the launch traced here: 335 us
  waiting for transfers between devices  192 us (57%)
  Pallas kernels  78.3 us (23%)
  starting transfers between devices  44.5 us (13%)
  between operations  15 us (4%)
    ppermute x8, waiting for transfers between devices, swap(): return lax.ppermute(value, axis, [(i, i ^ bit) for i in range(count)])  107 us
    ppermute x14, waiting for transfers between devices, turned(): lax.ppermute(value, axis, [(i, (i + turn) % count) for i in range(count)])  79.2 us
    ppermute x14, starting transfers between devices, turned(): lax.ppermute(value, axis, [(i, (i + turn) % count) for i in range(count)])  23.5 us
    pallas_call x2, Pallas kernels, project(): pl.pallas_call(functools.partial(project_kernel, len(sources), len(blocks...  22.6 us
    pallas_call x2, Pallas kernels, attend(): pl.pallas_call(functools.partial(attend_kernel, len(blocks), devices), gr...  21.9 us
    pallas_call x2, Pallas kernels, accumulate(): pl.pallas_call(functools.partial(add_kernel, offsets, count), in_specs=[s...  16.6 us
    ppermute x8, starting transfers between devices, swap(): return lax.ppermute(value, axis, [(i, i ^ bit) for i in range(count)])  14.5 us
    pallas_call x1, Pallas kernels, accumulate(): pl.pallas_call(functools.partial(finish_kernel, offsets, count), in_specs...  10.2 us
  transfers between devices with their start and end apart: 26, of which 8 were waited for; matrix products, arithmetic and copies ran while one was open for 1% of the time, Pallas kernels for 23%

profile of v3, /device:TPU:1, one launch (start us, length us, event | category | flops | bytes accessed | tf_op | source)
XLA Modules:
  0.0 335.3 jit_solution(4099359394713236752)
XLA Ops:
  7.2 2.1 collective-permute-start.1
  9.9 2.6 norm_in.4
  13.6 72.3 %collective-permute-done.1.refs_3_.refs_6_.refs_8_ = bf16[768,2304]{1,0:T(8,128)(2,1)} collective-permute-done((bf16[768,2304]{1,0:T(8,128)(2,1)}, bf16[768,2304]{1,0:T(8,128)(2,1)}, u32[]{:S(2)}, u32[]{:S(2)}) %collective-permute-start.1) | collective-permute-done | bytes 3538976 | tf_op jit(solution)/shard_map/ppermute | solution.py:18
  87.2 3.6 %collective-permute-start.11 = (bf16[768,384]{1,0:T(8,128)(2,1)S(1)}, bf16[768,384]{1,0:T(8,128)(2,1)S(1)}, u32[]{:S(2)}, u32[]{:S(2)}) collective-permute-start(bf16[768,384]{1,0:T(8,128)(2,1)S(1)} %constant_dynamic-slice_fusion), channel_id=1, source_target_pairs={{0,3},{1,0},{2,1},{3,2},{4,7},{5,4},{6,5},{7,6},{8,11},{9,8},{10,9... | collective-permute-start | bytes 1769480 | tf_op jit(solution)/shard_map/ppermute | solution.py:37
  91.3 12.4 %collective-permute-done.11 = bf16[768,384]{1,0:T(8,128)(2,1)S(1)} collective-permute-done((bf16[768,384]{1,0:T(8,128)(2,1)S(1)}, bf16[768,384]{1,0:T(8,128)(2,1)S(1)}, u32[]{:S(2)}, u32[]{:S(2)}) %collective-permute-start.11) | collective-permute-done | bytes 589856 | tf_op jit(solution)/shard_map/ppermute | solution.py:37
  103.7 37.7 %collective-permute-done.10 = bf16[768,384]{1,0:T(8,128)(2,1)S(1)} collective-permute-done((bf16[768,384]{1,0:T(8,128)(2,1)S(1)}, bf16[768,384]{1,0:T(8,128)(2,1)S(1)}, u32[]{:S(2)}, u32[]{:S(2)}) %collective-permute-start.10) | collective-permute-done | bytes 589856 | tf_op jit(solution)/shard_map/ppermute | solution.py:37
  141.6 1.3 collective-permute-start.15
  142.9 2.2 norm_in.3
  145.1 1.3 collective-permute-start.12
  146.5 13.0 %project.2 = (bf16[6,512,128]{2,1,0:T(8,128)(2,1)}, bf16[6,512,128]{2,1,0:T(8,128)(2,1)}, bf16[6,512,128]{2,1,0:T(8,128)(2,1)}) custom-call(bf16[512,3072]{1,0:T(8,128)(2,1)} %all-gather.5.cloned.1.call-done.refs_0_, bf16[768,2304]{1,0:T(8,128)(2,1)} %refs_6_.3, bf16[768,2304]{1,0:T(8,128)(2,1)} %collective-permute-done.refs_2_.refs_5_.refs_7_, ...), custom_call_target="tpu_custom_call" | custom-call | flops 7247757312 | bytes 31457280 | tf_op jit(solution)/shard_map/project/pallas_call | solution.py:120
  159.4 34.4 %collective-permute-done.15.refs_6_.refs_7_ = bf16[3072,384]{1,0:T(8,128)(2,1)} collective-permute-done((bf16[3072,384]{1,0:T(8,128)(2,1)S(1)}, bf16[3072,384]{1,0:T(8,128)(2,1)}, u32[]{:S(2)}, u32[]{:S(2)}) %collective-permute-start.15) | collective-permute-done | bytes 2359328 | tf_op jit(solution)/shard_map/ppermute | solution.py:18
  195.0 2.2 norm_in.5.refs_0_
  197.2 1.9 collective-permute-start.4
  199.1 2.4 collective-permute-start.5
  201.5 6.7 %collective-permute-done.3.refs_1_ = bf16[64,3072]{1,0:T(8,128)(2,1)} collective-permute-done((bf16[64,3072]{1,0:T(8,128)(2,1)}, bf16[64,3072]{1,0:T(8,128)(2,1)}, u32[]{:S(2)}, u32[]{:S(2)}) %collective-permute-start.3) | collective-permute-done | bytes 393248 | tf_op jit(solution)/shard_map/ppermute | solution.py:37
  208.1 5.3 %collective-permute-start.13 = (bf16[3072,384]{1,0:T(8,128)(2,1)S(1)}, bf16[3072,384]{1,0:T(8,128)(2,1)}, u32[]{:S(2)}, u32[]{:S(2)}) collective-permute-start(bf16[3072,384]{1,0:T(8,128)(2,1)S(1)} %pad_maximum_fusion.refs_2_.refs_3_), channel_id=1, source_target_pairs={{0,4},{4,0},{8,12},{12,8},{1,5},{5,1},{9,13},{13,9},{2,6},{6,2},{1... | collective-permute-start | bytes 7077896 | tf_op jit(solution)/shard_map/ppermute | solution.py:18
  213.4 12.0 %collective-permute-done.4.refs_2_ = bf16[64,3072]{1,0:T(8,128)(2,1)} collective-permute-done((bf16[64,3072]{1,0:T(8,128)(2,1)}, bf16[64,3072]{1,0:T(8,128)(2,1)}, u32[]{:S(2)}, u32[]{:S(2)}) %collective-permute-start.4) | collective-permute-done | bytes 393248 | tf_op jit(solution)/shard_map/ppermute | solution.py:37
  225.4 9.6 %project.3 = (bf16[6,256,128]{2,1,0:T(8,128)(2,1)}, bf16[6,256,128]{2,1,0:T(8,128)(2,1)}, bf16[6,256,128]{2,1,0:T(8,128)(2,1)}) custom-call(bf16[64,3072]{1,0:T(8,128)(2,1)} %norm_in.5.refs_0_, bf16[64,3072]{1,0:T(8,128)(2,1)} %collective-permute-done.3.refs_1_, bf16[64,3072]{1,0:T(8,128)(2,1)} %collective-permute-done.4.refs_2_, ...), custom_call_target="tpu_custom_call" | custom-call | flops 3623878656 | bytes 29884416 | tf_op jit(solution)/shard_map/project/pallas_call | solution.py:120
  235.0 10.9 %attend.3 = (bf16[256,384]{1,0:T(8,128)(2,1)}, bf16[256,384]{1,0:T(8,128)(2,1)}, bf16[256,384]{1,0:T(8,128)(2,1)}, bf16[256,384]{1,0:T(8,128)(2,1)}) custom-call(s32[1]{0:T(128)} %bitcast.8.place_ref, bf16[256,3072]{1,0:T(8,128)(2,1)} %all-gather.3.cloned.1.call-done.x_ref, bf16[6,512,128]{2,1,0:T(8,128)(2,1)} %get-tuple-element.22.refs_0_, ...), custom_call_target="tpu_custom_call" | custom-call | flops 3422552064 | bytes 10223616 | tf_op jit(solution)/shard_map/attend/pallas_call | solution.py:180
  246.0 2.6 collective-permute-start.14
  251.5 6.2 %collective-permute-start.19 = (bf16[256,384]{1,0:T(8,128)(2,1)}, bf16[256,384]{1,0:T(8,128)(2,1)S(1)}, u32[]{:S(2)}, u32[]{:S(2)}) collective-permute-start(bf16[256,384]{1,0:T(8,128)(2,1)} %get-tuple-element.36), channel_id=1, source_target_pairs={{0,2},{1,3},{2,0},{3,1},{4,6},{5,7},{6,4},{7,5},{8,10},{9,11},{10,... | collective-permute-start | bytes 589832 | tf_op jit(solution)/shard_map/ppermute | solution.py:37
  258.2 2.9 collective-permute-start.20
  261.1 10.4 %collective-permute-done.19.refs_0_ = bf16[256,384]{1,0:T(8,128)(2,1)S(1)} collective-permute-done((bf16[256,384]{1,0:T(8,128)(2,1)}, bf16[256,384]{1,0:T(8,128)(2,1)S(1)}, u32[]{:S(2)}, u32[]{:S(2)}) %collective-permute-start.19) | collective-permute-done | bytes 196640 | tf_op jit(solution)/shard_map/ppermute | solution.py:37
  271.5 11.0 %attend.2 = (bf16[256,384]{1,0:T(8,128)(2,1)}, bf16[256,384]{1,0:T(8,128)(2,1)}, bf16[256,384]{1,0:T(8,128)(2,1)}, bf16[256,384]{1,0:T(8,128)(2,1)}) custom-call(s32[1]{0:T(128)} %bitcast.8.place_ref, bf16[256,3072]{1,0:T(8,128)(2,1)} %all-gather.3.cloned.1.call-done.x_ref, bf16[6,512,128]{2,1,0:T(8,128)(2,1)} %get-tuple-element.22.refs_0_, ...), custom_call_target="tpu_custom_call" | custom-call | flops 3422552064 | bytes 10223616 | tf_op jit(solution)/shard_map/attend/pallas_call | solution.py:180
  282.6 1.4 collective-permute-start.7
  284.0 2.1 collective-permute-start.8
  286.1 7.5 %add_parts.2.refs_11_ = f32[256,3072]{1,0:T(8,128)} custom-call(s32[8]{0:T(128)} %stack.59.starts_ref, bf16[256,384]{1,0:T(8,128)(2,1)} %get-tuple-element.31.refs_0_, bf16[256,384]{1,0:T(8,128)(2,1)} %get-tuple-element.39.refs_1_, bf16[3072,384]{1,0:T(8,128)(2,1)} %copy-done.1, bf16[3072,384]{1,0:T(8,128)(2,1)} %collective-permute-done.12.refs_3_.refs_4_, ...), custom_call_target="tpu_custom_call" | custom-call | flops 1207959552 | bytes 11010048 | tf_op jit(solution)/shard_map/add_parts/pallas_call | solution.py:302
  293.6 3.6 %collective-permute-start.23 = (bf16[1,256]{1,0:T(2,128)(2,1)S(1)}, bf16[1,256]{1,0:T(2,128)(2,1)S(1)}, u32[]{:S(2)}, u32[]{:S(2)}) collective-permute-start(bf16[1,256]{1,0:T(2,128)(2,1)S(1)} %get-tuple-element.44), channel_id=1, source_target_pairs={{2,4},{3,5},{6,8},{7,9},{10,12},{11,13},{4,2},{5,3},{8,6},{9,7},{1... | collective-permute-start | bytes 1544 | tf_op jit(solution)/shard_map/ppermute | solution.py:349
  297.9 9.1 %add_parts.3.refs_11_ = f32[256,3072]{1,0:T(8,128)} custom-call(s32[8]{0:T(128)} %stack.59.starts_ref, bf16[256,384]{1,0:T(8,128)(2,1)} %copy-done.2, bf16[256,384]{1,0:T(8,128)(2,1)} %copy-done.3, bf16[256,384]{1,0:T(8,128)(2,1)} %copy-done.5, bf16[3072,384]{1,0:T(8,128)(2,1)} %copy-done.1, ...), custom_call_target="tpu_custom_call", output_to_operand_aliasing={{}: (12, {})} | custom-call | flops 1811939328 | bytes 13369344 | tf_op jit(solution)/shard_map/add_parts/pallas_call | solution.py:302
  307.9 10.2 %finish.1 = (f32[128,256]{1,0:T(8,128)}, bf16[128,256]{1,0:T(8,128)(2,1)}) custom-call(s32[8]{0:T(128)} %stack.59.starts_ref, f32[2]{0:T(128)} %pad_maximum_fusion.1.coef_ref, bf16[256,384]{1,0:T(8,128)(2,1)} %copy-done.4, bf16[256,384]{1,0:T(8,128)(2,1)} %copy-done.6, bf16[256,384]{1,0:T(8,128)(2,1)} %copy-done.7, bf16[3072,384]{1,0:T(8,128)(2,1)} %copy-done.1, ...), custom_call_target="tpu_custom_call" | custom-call | flops 1811939328 | bytes 13369344 | tf_op jit(solution)/shard_map/finish/pallas_call | solution.py:314
  318.1 2.8 collective-permute-start.22
  321.0 5.9 %collective-permute-done.22 = bf16[128,256]{1,0:T(8,128)(2,1)S(1)} collective-permute-done((bf16[128,256]{1,0:T(8,128)(2,1)}, bf16[128,256]{1,0:T(8,128)(2,1)S(1)}, u32[]{:S(2)}, u32[]{:S(2)}) %collective-permute-start.22) | collective-permute-done | bytes 65568 | tf_op jit(solution)/shard_map/ppermute | solution.py:447
  (59 shorter events, 10.9 us)
Async XLA Ops:
  7.2 80.0 %copy-start = (bf16[768,768]{1,0:T(8,128)(2,1)S(1)}, bf16[768,768]{1,0:T(8,128)(2,1)}, u32[]{:S(2)}) copy-start(bf16[768,768]{1,0:T(8,128)(2,1)} %param.11) | copy-start | bytes 3538948
  7.2 139.3 %all-gather.5.cloned.1.call-start = ((), (), s32[]{:S(2)}) async-start(), calls=%async_computation.1 | async-start | bytes 3932160 | tf_op jit(solution)/shard_map/all_gather | solution.py:371
  7.2 78.7 %collective-permute-start.1 = (bf16[768,2304]{1,0:T(8,128)(2,1)}, bf16[768,2304]{1,0:T(8,128)(2,1)}, u32[]{:S(2)}, u32[]{:S(2)}) collective-permute-start(bf16[768,2304]{1,0:T(8,128)(2,1)} %refs_6_.3), channel_id=1, source_target_pairs={{0,8},{4,12},{8,0},{12,4},{1,9},{5,13},{9,1},{13,5},{2,10},{6,14},... | collective-permute-start | bytes 10616840 | tf_op jit(solution)/shard_map/ppermute | solution.py:18
  12.6 222.4 %all-gather.3.cloned.1.call-start = ((), (), s32[]{:S(2)}) async-start(), calls=%async_computation | async-start | bytes 1966080 | tf_op jit(solution)/shard_map/all_gather | solution.py:377
  12.6 133.8 %collective-permute-start = (bf16[768,2304]{1,0:T(8,128)(2,1)}, bf16[768,2304]{1,0:T(8,128)(2,1)}, u32[]{:S(2)}, u32[]{:S(2)}) collective-permute-start(bf16[768,2304]{1,0:T(8,128)(2,1)} %refs_6_.3), channel_id=1, source_target_pairs={{0,4},{4,0},{8,12},{12,8},{1,5},{5,1},{9,13},{13,9},{2,6},{6,2},{1... | collective-permute-start | bytes 10616840 | tf_op jit(solution)/shard_map/ppermute | solution.py:18
  85.9 60.5 %collective-permute-start.2 = (bf16[768,2304]{1,0:T(8,128)(2,1)}, bf16[768,2304]{1,0:T(8,128)(2,1)}, u32[]{:S(2)}, u32[]{:S(2)}) collective-permute-start(bf16[768,2304]{1,0:T(8,128)(2,1)} %collective-permute-done.1.refs_3_.refs_6_.refs_8_), channel_id=1, source_target_pairs={{0,4},{4,0},{8,12},{12,8},{1,5},{5,1},{9,13},{13,9},{2,6},{6,2},{1... | collective-permute-start | bytes 10616840 | tf_op jit(solution)/shard_map/ppermute | solution.py:18
  87.2 16.5 %collective-permute-start.11 = (bf16[768,384]{1,0:T(8,128)(2,1)S(1)}, bf16[768,384]{1,0:T(8,128)(2,1)S(1)}, u32[]{:S(2)}, u32[]{:S(2)}) collective-permute-start(bf16[768,384]{1,0:T(8,128)(2,1)S(1)} %constant_dynamic-slice_fusion), channel_id=1, source_target_pairs={{0,3},{1,0},{2,1},{3,2},{4,7},{5,4},{6,5},{7,6},{8,11},{9,8},{10,9... | collective-permute-start | bytes 1769480 | tf_op jit(solution)/shard_map/ppermute | solution.py:37
  90.8 50.6 %collective-permute-start.10 = (bf16[768,384]{1,0:T(8,128)(2,1)S(1)}, bf16[768,384]{1,0:T(8,128)(2,1)S(1)}, u32[]{:S(2)}, u32[]{:S(2)}) collective-permute-start(bf16[768,384]{1,0:T(8,128)(2,1)S(1)} %constant_dynamic-slice_fusion), channel_id=1, source_target_pairs={{0,2},{1,3},{2,0},{3,1},{4,6},{5,7},{6,4},{7,5},{8,10},{9,11},{10,... | collective-permute-start | bytes 1769480 | tf_op jit(solution)/shard_map/ppermute | solution.py:37
  90.8 50.6 %collective-permute-start.9 = (bf16[768,384]{1,0:T(8,128)(2,1)S(1)}, bf16[768,384]{1,0:T(8,128)(2,1)S(1)}, u32[]{:S(2)}, u32[]{:S(2)}) collective-permute-start(bf16[768,384]{1,0:T(8,128)(2,1)S(1)} %constant_dynamic-slice_fusion), channel_id=1, source_target_pairs={{0,1},{1,2},{2,3},{3,0},{4,5},{5,6},{6,7},{7,4},{8,9},{9,10},{10,1... | collective-permute-start | bytes 1769480 | tf_op jit(solution)/shard_map/ppermute | solution.py:37
  141.6 66.5 %copy-start.1 = (bf16[3072,384]{1,0:T(8,128)(2,1)}, bf16[3072,384]{1,0:T(8,128)(2,1)S(1)}, u32[]{:S(2)}) copy-start(bf16[3072,384]{1,0:T(8,128)(2,1)S(1)} %pad_maximum_fusion.refs_2_.refs_3_) | copy-start | bytes 7077892
  141.6 52.2 %collective-permute-start.15 = (bf16[3072,384]{1,0:T(8,128)(2,1)S(1)}, bf16[3072,384]{1,0:T(8,128)(2,1)}, u32[]{:S(2)}, u32[]{:S(2)}) collective-permute-start(bf16[3072,384]{1,0:T(8,128)(2,1)S(1)} %pad_maximum_fusion.refs_2_.refs_3_), channel_id=1, source_target_pairs={{0,8},{4,12},{8,0},{12,4},{1,9},{5,13},{9,1},{13,5},{2,10},{6,14},... | collective-permute-start | bytes 7077896 | tf_op jit(solution)/shard_map/ppermute | solution.py:18
  145.1 100.8 %collective-permute-start.12 = (bf16[3072,384]{1,0:T(8,128)(2,1)S(1)}, bf16[3072,384]{1,0:T(8,128)(2,1)}, u32[]{:S(2)}, u32[]{:S(2)}) collective-permute-start(bf16[3072,384]{1,0:T(8,128)(2,1)S(1)} %pad_maximum_fusion.refs_2_.refs_3_), channel_id=1, source_target_pairs={{0,16},{16,0},{1,17},{17,1},{2,18},{18,2},{3,19},{19,3},{4,20},{20... | collective-permute-start | bytes 7077896 | tf_op jit(solution)/shard_map/ppermute | solution.py:37
  193.8 54.8 %collective-permute-start.16 = (bf16[3072,384]{1,0:T(8,128)(2,1)}, bf16[3072,384]{1,0:T(8,128)(2,1)}, u32[]{:S(2)}, u32[]{:S(2)}) collective-permute-start(bf16[3072,384]{1,0:T(8,128)(2,1)} %collective-permute-done.15.refs_6_.refs_7_), channel_id=1, source_target_pairs={{0,16},{16,0},{1,17},{17,1},{2,18},{18,2},{3,19},{19,3},{4,20},{20... | collective-permute-start | bytes 7077896 | tf_op jit(solution)/shard_map/ppermute | solution.py:37
  197.2 10.9 %collective-permute-start.3 = (bf16[64,3072]{1,0:T(8,128)(2,1)}, bf16[64,3072]{1,0:T(8,128)(2,1)}, u32[]{:S(2)}, u32[]{:S(2)}) collective-permute-start(bf16[64,3072]{1,0:T(8,128)(2,1)} %norm_in.5.refs_0_), channel_id=1, source_target_pairs={{0,1},{1,2},{2,3},{3,0},{4,5},{5,6},{6,7},{7,4},{8,9},{9,10},{10,1... | collective-permute-start | bytes 1179656 | tf_op jit(solution)/shard_map/ppermute | solution.py:37
  197.2 28.2 %collective-permute-start.4 = (bf16[64,3072]{1,0:T(8,128)(2,1)}, bf16[64,3072]{1,0:T(8,128)(2,1)}, u32[]{:S(2)}, u32[]{:S(2)}) collective-permute-start(bf16[64,3072]{1,0:T(8,128)(2,1)} %norm_in.5.refs_0_), channel_id=1, source_target_pairs={{0,2},{1,3},{2,0},{3,1},{4,6},{5,7},{6,4},{7,5},{8,10},{9,11},{10,... | collective-permute-start | bytes 1179656 | tf_op jit(solution)/shard_map/ppermute | solution.py:37
  199.1 26.3 %collective-permute-start.5 = (bf16[64,3072]{1,0:T(8,128)(2,1)}, bf16[64,3072]{1,0:T(8,128)(2,1)}, u32[]{:S(2)}, u32[]{:S(2)}) collective-permute-start(bf16[64,3072]{1,0:T(8,128)(2,1)} %norm_in.5.refs_0_), channel_id=1, source_target_pairs={{0,3},{1,0},{2,1},{3,2},{4,7},{5,4},{6,5},{7,6},{8,11},{9,8},{10,9... | collective-permute-start | bytes 1179656 | tf_op jit(solution)/shard_map/ppermute | solution.py:37
  208.1 50.1 %collective-permute-start.13 = (bf16[3072,384]{1,0:T(8,128)(2,1)S(1)}, bf16[3072,384]{1,0:T(8,128)(2,1)}, u32[]{:S(2)}, u32[]{:S(2)}) collective-permute-start(bf16[3072,384]{1,0:T(8,128)(2,1)S(1)} %pad_maximum_fusion.refs_2_.refs_3_), channel_id=1, source_target_pairs={{0,4},{4,0},{8,12},{12,8},{1,5},{5,1},{9,13},{13,9},{2,6},{6,2},{1... | collective-permute-start | bytes 7077896 | tf_op jit(solution)/shard_map/ppermute | solution.py:18
  235.0 22.6 %copy-start.8 = (s32[1,256]{1,0:T(1,128)S(1)}, s32[1,256]{1,0:T(1,128)}, u32[]{:S(2)}) copy-start(s32[1,256]{1,0:T(1,128)} %param.14) | copy-start | bytes 3076
  246.0 36.5 %collective-permute-start.14 = (bf16[3072,384]{1,0:T(8,128)(2,1)}, bf16[3072,384]{1,0:T(8,128)(2,1)}, u32[]{:S(2)}, u32[]{:S(2)}) collective-permute-start(bf16[3072,384]{1,0:T(8,128)(2,1)} %collective-permute-done.12.refs_3_.refs_4_), channel_id=1, source_target_pairs={{0,4},{4,0},{8,12},{12,8},{1,5},{5,1},{9,13},{13,9},{2,6},{6,2},{1... | collective-permute-start | bytes 7077896 | tf_op jit(solution)/shard_map/ppermute | solution.py:18
  248.6 34.0 %collective-permute-start.17 = (bf16[3072,384]{1,0:T(8,128)(2,1)}, bf16[3072,384]{1,0:T(8,128)(2,1)}, u32[]{:S(2)}, u32[]{:S(2)}) collective-permute-start(bf16[3072,384]{1,0:T(8,128)(2,1)} %collective-permute-done.15.refs_6_.refs_7_), channel_id=1, source_target_pairs={{0,4},{4,0},{8,12},{12,8},{1,5},{5,1},{9,13},{13,9},{2,6},{6,2},{1... | collective-permute-start | bytes 7077896 | tf_op jit(solution)/shard_map/ppermute | solution.py:18
  248.6 35.4 %collective-permute-start.18 = (bf16[3072,384]{1,0:T(8,128)(2,1)}, bf16[3072,384]{1,0:T(8,128)(2,1)}, u32[]{:S(2)}, u32[]{:S(2)}) collective-permute-start(bf16[3072,384]{1,0:T(8,128)(2,1)} %collective-permute-done.16.refs_7_.refs_8_), channel_id=1, source_target_pairs={{0,4},{4,0},{8,12},{12,8},{1,5},{5,1},{9,13},{13,9},{2,6},{6,2},{1... | collective-permute-start | bytes 7077896 | tf_op jit(solution)/shard_map/ppermute | solution.py:18
  251.5 20.0 %collective-permute-start.19 = (bf16[256,384]{1,0:T(8,128)(2,1)}, bf16[256,384]{1,0:T(8,128)(2,1)S(1)}, u32[]{:S(2)}, u32[]{:S(2)}) collective-permute-start(bf16[256,384]{1,0:T(8,128)(2,1)} %get-tuple-element.36), channel_id=1, source_target_pairs={{0,2},{1,3},{2,0},{3,1},{4,6},{5,7},{6,4},{7,5},{8,10},{9,11},{10,... | collective-permute-start | bytes 589832 | tf_op jit(solution)/shard_map/ppermute | solution.py:37
  258.2 35.3 %collective-permute-start.20 = (bf16[256,384]{1,0:T(8,128)(2,1)}, bf16[256,384]{1,0:T(8,128)(2,1)S(1)}, u32[]{:S(2)}, u32[]{:S(2)}) collective-permute-start(bf16[256,384]{1,0:T(8,128)(2,1)} %get-tuple-element.37), channel_id=1, source_target_pairs={{0,1},{1,2},{2,3},{3,0},{4,5},{5,6},{6,7},{7,4},{8,9},{9,10},{10,1... | collective-permute-start | bytes 589832 | tf_op jit(solution)/shard_map/ppermute | solution.py:37
  271.5 11.0 %copy-start.2 = (bf16[256,384]{1,0:T(8,128)(2,1)}, bf16[256,384]{1,0:T(8,128)(2,1)S(1)}, u32[]{:S(2)}) copy-start(bf16[256,384]{1,0:T(8,128)(2,1)S(1)} %collective-permute-done.19.refs_0_) | copy-start | bytes 589828
  271.5 25.7 %collective-permute-start.21 = (bf16[256,384]{1,0:T(8,128)(2,1)}, bf16[256,384]{1,0:T(8,128)(2,1)S(1)}, u32[]{:S(2)}, u32[]{:S(2)}) collective-permute-start(bf16[256,384]{1,0:T(8,128)(2,1)} %get-tuple-element.38), channel_id=1, source_target_pairs={{0,3},{1,0},{2,1},{3,2},{4,7},{5,4},{6,5},{7,6},{8,11},{9,8},{10,9... | collective-permute-start | bytes 589832 | tf_op jit(solution)/shard_map/ppermute | solution.py:37
  282.5 24.6 %collective-permute-start.6 = (bf16[256,384]{1,0:T(8,128)(2,1)}, bf16[256,384]{1,0:T(8,128)(2,1)S(1)}, u32[]{:S(2)}, u32[]{:S(2)}) collective-permute-start(bf16[256,384]{1,0:T(8,128)(2,1)} %get-tuple-element.28), channel_id=1, source_target_pairs={{0,2},{1,3},{2,0},{3,1},{4,6},{5,7},{6,4},{7,5},{8,10},{9,11},{10,... | collective-permute-start | bytes 589832 | tf_op jit(solution)/shard_map/ppermute | solution.py:37
  282.6 24.5 %collective-permute-start.7 = (bf16[256,384]{1,0:T(8,128)(2,1)}, bf16[256,384]{1,0:T(8,128)(2,1)S(1)}, u32[]{:S(2)}, u32[]{:S(2)}) collective-permute-start(bf16[256,384]{1,0:T(8,128)(2,1)} %get-tuple-element.29), channel_id=1, source_target_pairs={{0,1},{1,2},{2,3},{3,0},{4,5},{5,6},{6,7},{7,4},{8,9},{9,10},{10,1... | collective-permute-start | bytes 589832 | tf_op jit(solution)/shard_map/ppermute | solution.py:37
  284.0 23.1 %collective-permute-start.8 = (bf16[256,384]{1,0:T(8,128)(2,1)}, bf16[256,384]{1,0:T(8,128)(2,1)S(1)}, u32[]{:S(2)}, u32[]{:S(2)}) collective-permute-start(bf16[256,384]{1,0:T(8,128)(2,1)} %get-tuple-element.30), channel_id=1, source_target_pairs={{0,3},{1,0},{2,1},{3,2},{4,7},{5,4},{6,5},{7,6},{8,11},{9,8},{10,9... | collective-permute-start | bytes 589832 | tf_op jit(solution)/shard_map/ppermute | solution.py:37
  293.6 3.6 %copy-start.3 = (bf16[256,384]{1,0:T(8,128)(2,1)}, bf16[256,384]{1,0:T(8,128)(2,1)S(1)}, u32[]{:S(2)}) copy-start(bf16[256,384]{1,0:T(8,128)(2,1)S(1)} %collective-permute-done.20.refs_1_) | copy-start | bytes 589828
  293.6 27.4 %collective-permute-start.23 = (bf16[1,256]{1,0:T(2,128)(2,1)S(1)}, bf16[1,256]{1,0:T(2,128)(2,1)S(1)}, u32[]{:S(2)}, u32[]{:S(2)}) collective-permute-start(bf16[1,256]{1,0:T(2,128)(2,1)S(1)} %get-tuple-element.44), channel_id=1, source_target_pairs={{2,4},{3,5},{6,8},{7,9},{10,12},{11,13},{4,2},{5,3},{8,6},{9,7},{1... | collective-permute-start | bytes 1544 | tf_op jit(solution)/shard_map/ppermute | solution.py:349
  307.1 0.8 copy-start.7
  318.1 8.8 %collective-permute-start.22 = (bf16[128,256]{1,0:T(8,128)(2,1)}, bf16[128,256]{1,0:T(8,128)(2,1)S(1)}, u32[]{:S(2)}, u32[]{:S(2)}) collective-permute-start(bf16[128,256]{1,0:T(8,128)(2,1)} %get-tuple-element.41), channel_id=1, source_target_pairs={{2,4},{3,5},{6,8},{7,9},{10,12},{11,13},{4,2},{5,3},{8,6},{9,7},{1... | collective-permute-start | bytes 196616 | tf_op jit(solution)/shard_map/ppermute | solution.py:447
  (3 other events, 2.1 us)
Sparse Core Ops, SparseCore 0:
  12.7 64.0 all-gather.4
  145.3 37.0 all-gather.2

commit v4 on v3

--- a/solution.py
+++ b/solution.py
@@ -21,10 +21,6 @@
 def bits_of(count):
     far = [1 << n for n in range(1, count.bit_length() - 1)]
     return far + [1]
-
-
-def after(value, *others):
-    return lax.optimization_barrier((value,) + others)[0]
 
 
 def noise_level(index, steps):
@@ -126,40 +122,46 @@
         out_shape=[out] * 3,
         scratch_shapes=[pltpu.VMEM((length, width), jnp.bfloat16)],
         compiler_params=pltpu.CompilerParams(vmem_limit_bytes=60 * MIB),
-        cost_estimate=pl.CostEstimate(
-            flops=2 * length * width * total,
-            bytes_accessed=2 * (length * width + width * total * 2),
-            transcendentals=0,
-        ),
         name="project",
     )(*sources, *blocks)
 
 
-def attend_kernel(blocks, devices, place_ref, x_ref, *refs):
-    first, second = refs[0:3], refs[3:6]
-    w_refs = refs[6 : 6 + blocks]
-    outs = refs[6 + blocks : 6 + blocks + devices]
-    queries, keys, values = refs[6 + blocks + devices :]
-    proj = product(x_ref, w_refs)
+def attend_kernel(blocks, devices, place_ref, gathered_ref, *refs):
+    passed, first = refs[:devices], refs[devices : devices + 3]
+    w_refs = refs[devices + 3 : devices + 3 + blocks]
+    outs = refs[devices + 3 + blocks : 2 * devices + 3 + blocks]
+    tokens, queries, keys, values, sems = refs[2 * devices + 3 + blocks :]
+    sets = (first[1].shape[1], gathered_ref.shape[0], passed[0].shape[0] * devices)
+    start, length = sets[0], sum(sets)
+    rows = [count // devices for count in sets]
+
+    @pl.when(pl.program_id(0) == 0)
+    def _():
+        copies = [pltpu.make_async_copy(gathered_ref, tokens.at[pl.ds(0, sets[1])], sems.at[0])]
+        for n in range(devices):
+            to = tokens.at[pl.ds(sets[1] + n * rows[2], rows[2])]
+            copies.append(pltpu.make_async_copy(passed[n], to, sems.at[n + 1]))
+        for copy in copies:
+            copy.start()
+        values[:, HD:] = jnp.ones((length, HD), jnp.bfloat16)
+        for copy in copies:
+            copy.wait()
+
+    proj = product(tokens, w_refs)
     queries[...] = root_norm(proj[:, :HD])
-    sets = (first[1].shape[1], second[1].shape[1], x_ref.shape[0])
-    ends = (sets[0], sets[0] + sets[1], sum(sets))
-    keys[: ends[0]] = first[1][0]
-    keys[ends[0] : ends[1]] = second[1][0]
-    keys[ends[1] :] = root_norm(proj[:, HD : 2 * HD])
-    values[: ends[0], :HD] = first[2][0]
-    values[ends[0] : ends[1], :HD] = second[2][0]
-    values[ends[1] :, :HD] = proj[:, 2 * HD :].astype(jnp.bfloat16)
-    values[:, HD:] = jnp.ones((ends[2], HD), jnp.bfloat16)
-    rows = [count // devices for count in sets]
+    keys[:start] = first[1][0]
+    keys[start:] = root_norm(proj[:, HD : 2 * HD])
+    values[:start, :HD] = first[2][0]
+    values[start:, :HD] = proj[:, 2 * HD :].astype(jnp.bfloat16)
     for turn in range(devices):
         dest = lax.rem(place_ref[0] + turn, devices)
         slot = (devices - turn) % devices
+        slot_start = sets[1] + slot * rows[2]
         query = jnp.concatenate(
             [
                 first[0][0, pl.ds(pl.multiple_of(dest * rows[0], rows[0]), rows[0])],
-                second[0][0, slot * rows[1] : (slot + 1) * rows[1]],
-                queries[pl.ds(pl.multiple_of(dest * rows[2], rows[2]), rows[2])],
+                queries[slot_start : slot_start + rows[2]],
+                queries[pl.ds(pl.multiple_of(dest * rows[1], rows[1]), rows[1])],
             ],
             axis=0,
         )
@@ -171,36 +173,34 @@
         outs[turn][...] = (mixed[:, :HD] / mixed[:, HD:]).astype(jnp.bfloat16)
 
 
-def attend(place, devices, x, first, second, blocks, start, heads):
-    last, width = x.shape
-    length = last + first[0].shape[1] + second[0].shape[1]
+def attend(place, gathered, passed, first, blocks, start, heads):
+    devices = len(passed)
+    last, width = gathered.shape
+    last += passed[0].shape[0] * devices
+    length = last + first[0].shape[1]
     rows = length // devices
-    head = lambda value: pl.BlockSpec((1, value.shape[1], HD), lambda h: (start + h, 0, 0))
+    hbm = pl.BlockSpec(memory_space=pl.ANY)
+    head = pl.BlockSpec((1, length - last, HD), lambda h: (start + h, 0, 0))
     out = jax.ShapeDtypeStruct((rows, heads * HD), jnp.bfloat16)
     return pl.pallas_call(
         functools.partial(attend_kernel, len(blocks), devices),
         grid=(heads,),
-        in_specs=[
-            pl.BlockSpec(memory_space=pltpu.SMEM),
-            pl.BlockSpec((last, width), lambda h: (0, 0)),
-        ]
-        + [head(value) for value in first + second]
+        in_specs=[pl.BlockSpec(memory_space=pltpu.SMEM), hbm]
+        + [hbm] * devices
+        + [head] * 3
         + [pl.BlockSpec((width // len(blocks), 3 * HD), lambda h: (0, start + h))] * len(blocks),
         out_specs=[pl.BlockSpec((rows, HD), lambda h: (0, h))] * devices,
         out_shape=[out] * devices,
         scratch_shapes=[
+            pltpu.VMEM((last, width), jnp.bfloat16),
             pltpu.VMEM((last, HD), jnp.bfloat16),
             pltpu.VMEM((length, HD), jnp.bfloat16),
             pltpu.VMEM((length, 2 * HD), jnp.bfloat16),
+            pltpu.SemaphoreType.DMA((devices + 1,)),
         ],
         compiler_params=pltpu.CompilerParams(vmem_limit_bytes=60 * MIB),
-        cost_estimate=pl.CostEstimate(
-            flops=4 * length * length * heads * HD + 2 * last * width * 3 * HD * heads,
-            bytes_accessed=2 * heads * HD * (4 * length + 3 * width),
-            transcendentals=length * length * heads,
-        ),
         name="attend",
-    )(place.reshape(1), x, *first, *second, *blocks)
+    )(place.reshape(1), gathered, *passed, *first, *blocks)
 
 
 def multiply(parts, offsets, starts_ref, sources, weights, sems, wide, store):
@@ -291,11 +291,6 @@
     ]
     params = dict(
         compiler_params=pltpu.CompilerParams(vmem_limit_bytes=60 * MIB),
-        cost_estimate=pl.CostEstimate(
-            flops=2 * rows * width * depth,
-            bytes_accessed=2 * width * depth + 8 * rows * width,
-            transcendentals=0,
-        ),
     )
     if last is None:
         aliased = before.dtype == jnp.float32
@@ -350,59 +345,77 @@
         weight.astype(jnp.bfloat16), ("tile", "seq"), joins
     ).astype(jnp.float32)
 
+    part = w_out.shape[1] // groups
+    share = lax.dynamic_slice_in_dim(w_out, group * part, part, axis=1)
+    narrow = part % HD != 0
+    if narrow:
+        share = share.T
+    share = [share] + [turned(share, "seq", turn) for turn in range(1, devices)]
+
     height = w_qkv.shape[0]
-    blocks = {0: w_qkv}
-    for bit in far + [near]:
-        blocks.update({d ^ bit: swap(blocks[d], "tile", bit) for d in list(blocks)})
-    arrived = dict(blocks)
     row_starts = jnp.stack([(tile ^ d) * height for d in range(tiles)]).astype(jnp.int32)
-    if height % HD:
-        full = jnp.zeros((tiles * height, w_qkv.shape[1]), w_qkv.dtype)
-        for d in range(tiles):
-            full = lax.dynamic_update_slice_in_dim(full, blocks[d], row_starts[d], axis=0)
-        blocks = {0: full}
+    if height % HD != 0:
         row_starts = jnp.zeros((1,), jnp.int32)
-    blocks = [blocks[d] for d in range(len(blocks))]
-
-    counts = (rows // 2, rows // 4, rows // 4)
+    counts = (3 * rows // 8, rows // 4, 3 * rows // 8)
     normed = [
         norm_rows(local, modulation, row_starts, sum(counts[:n]), counts[n]) for n in range(3)
     ]
     gathered = lax.all_gather(normed[0], "seq", axis=0, tiled=True)
 
-    part = w_out.shape[1] // groups
-    share = lax.dynamic_slice_in_dim(w_out, group * part, part, axis=1)
-    share = [share] + [turned(share, "seq", turn) for turn in range(1, devices)]
+    blocks = {0: w_qkv}
+    ragged = height % HD != 0
+    for bit in far if not ragged else []:
+        blocks.update({d ^ bit: swap(blocks[d], "tile", bit) for d in list(blocks)})
+    blocks, share, gathered = lax.optimization_barrier((blocks, share, gathered))
     passed = [normed[1]] + [turned(normed[1], "seq", turn) for turn in range(1, devices)]
     gathered_last = lax.all_gather(normed[2], "seq", axis=0, tiled=True)
-    columns = {(0, 0): jnp.concatenate(share, axis=0)}
-    if far:
-        columns[far[0], 0] = swap(after(columns[0, 0], arrived[far[0]]), "tile", far[0])
+    if ragged:
+        blocks[0] = lax.all_gather(blocks[0], "tile", axis=0, tiled=True)
+    else:
+        blocks.update({d ^ near: swap(blocks[d], "tile", near) for d in list(blocks)})
+    blocks = [blocks[d] for d in range(len(blocks))]
+
+    columns = {(0, 0): jnp.concatenate(share, axis=1 if narrow else 0)}
+    if narrow:
+        columns[0, 0] = lax.all_gather(columns[0, 0], ("tile", "group"), axis=0, tiled=True).T
+    else:
+        for bit in far:
+            columns.update({(d ^ bit, 0): swap(columns[d, 0], "tile", bit) for d, _ in list(columns)})
+        for turn in range(1, groups):
+            columns[0, turn] = turned(columns[0, 0], "group", turn)
     first = project([gathered], blocks)
-    if far:
-        columns[far[0], 0] = after(columns[far[0], 0], first[0])
-    for bit in far[1:]:
-        columns.update({(d ^ bit, g): swap(columns[d, g], "tile", bit) for d, g in list(columns)})
-    for turn in range(1, groups):
-        columns.update(
-            {(d, turn): turned(columns[d, 0], "group", turn) for d, g in list(columns) if g == 0}
+    passed, first, columns, gathered_last = lax.optimization_barrier(
+        (passed, first, columns, gathered_last)
+    )
+    late = {}
+    for turn in range(1, groups) if not narrow else []:
+        late.update(
+            {(d, turn): turned(columns[d, 0], "group", turn) for d, g in columns if d and not g}
         )
-    second = project(passed, blocks)
+    if groups == 2 and len(far) == 1 and not narrow:
+        bit, half = far[0], columns[0, 0].shape[0] // 2
+        late[bit, 1] = [
+            turned(columns[bit, 0][:half], "group", 1),
+            swap(columns[0, 1][half:], "tile", bit),
+        ]
+    if not narrow:
+        columns.update({(d ^ near, g): swap(columns[d, g], "tile", near) for d, g in list(columns)})
     heads = w_qkv.shape[1] // (3 * HD)
     halves = [(0, (heads + 1) // 2), ((heads + 1) // 2, heads // 2)]
-    sent = []
-    for start, count in halves:
-        sent.append(
-            attend(place, devices, gathered_last, first, second, blocks, start, count)
-        )
-    columns.update(
-        {
-            (d ^ near, g): swap(
-                after(columns[d, g], sent[0][0]) if g else columns[d, g], "tile", near
-            )
-            for d, g in list(columns)
-        }
-    )
+    turns = sorted(range(1, devices), key=lambda turn: -min(turn, devices - turn))
+    attended = attend(place, gathered_last, passed, first, blocks, *halves[0])
+    attended, columns, gathered_last = lax.optimization_barrier(
+        (attended, columns, gathered_last)
+    )
+    received = [[turned(attended[turn], "seq", turn) for turn in turns]]
+    own = [attended[0]]
+    attended = attend(place, gathered_last, passed, first, blocks, *halves[1])
+    attended, late, received = lax.optimization_barrier((attended, late, received))
+    for key, value in late.items():
+        columns[key] = jnp.concatenate(value, axis=0) if isinstance(value, list) else value
+    columns.update({(d ^ near, g): swap(columns[d, g], "tile", near) for d, g in late})
+    received.append([turned(attended[turn], "seq", turn) for turn in turns])
+    own.append(attended[0])
     order = sorted(columns)
     pieces = [columns[key] for key in order]
     starts = jnp.stack(
@@ -411,20 +424,13 @@
             for d, g in order
         ]
     ).astype(jnp.int32)
-    if part % HD:
-        whole = jnp.zeros((w_out.shape[0] * devices, part * len(order)), w_out.dtype)
-        for n, piece in enumerate(pieces):
-            whole = lax.dynamic_update_slice_in_dim(whole, piece, starts[n], axis=1)
-        pieces, starts = [whole], jnp.zeros((1,), jnp.int32)
-
-    turns = sorted(range(1, devices), key=lambda turn: -min(turn, devices - turn))
-    received = [
-        [turned(half[turn], "seq", turn) for turn in turns] for half in sent
-    ]
+    if narrow:
+        starts = jnp.zeros((1,), jnp.int32)
+
     features = w_out.shape[0]
     offsets = [[turn * features + start * HD for turn in turns] for start, _ in halves]
     mixed = accumulate(
-        [half[0] for half in sent],
+        own,
         [start * HD for start, _ in halves],
         starts,
         pieces,

time: 336 us -> 292 us (0.87)
  waiting for transfers between devices: 192 us -> 148 us
  local copies, waits for them, and re-layouts: 2.8 us -> 12.1 us
  starting transfers between devices: 44.5 us -> 35.3 us
    ppermute x8 -> x9, waiting for transfers between devices: 107 us -> 3.32 us  [swap(): return lax.ppermute(value, axis, [(i, i ^ bit) for i in range(count)])]
    all_gather x1, waiting for transfers between devices: 0.02 us -> 24.5 us  [shards(): gathered_last = lax.all_gather(normed[2], 'seq', axis=0, tiled=True)]
    ppermute x14, waiting for transfers between devices: 79.2 us -> 101 us  [turned(): lax.ppermute(value, axis, [(i, (i + turn) % count) for i in range(count)])]
    all_gather x1, waiting for transfers between devices: 0.01 us -> 14.6 us  [shards(): gathered = lax.all_gather(normed[0], 'seq', axis=0, tiled=True)]
    pallas_call x2 -> x1, Pallas kernels: 22.6 us -> 11.2 us  [project(): pl.pallas_call(functools.partial(project_kernel, len(sources), len(blocks...]
    pallas_call x2, Pallas kernels: 21.9 us -> 30.7 us  [attend(): pl.pallas_call(functools.partial(attend_kernel, len(blocks), devices), gr...]
    ppermute x8 -> x9, starting transfers between devices: 14.5 us -> 6.5 us  [swap(): return lax.ppermute(value, axis, [(i, i ^ bit) for i in range(count)])]
    slice x0 -> x2, local copies, waits for them, and re-layouts: none -> 3.55 us  [the longest x1 2.4 us: shards(): columns[bit, 0][:half]]
  transfers between devices with their start and end apart: 26 -> 27, of which waited for: 8 -> 9; matrix products, arithmetic and copies ran while one was open for 1% -> 3% of each run, Pallas kernels for 23% -> 27%
where the time goes in v4:
time: 292 us; the launch traced here: 291 us
  waiting for transfers between devices  148 us (51%)
  Pallas kernels  77.6 us (27%)
  starting transfers between devices  35.3 us (12%)
  between operations  15.1 us (5%)
  local copies, waits for them, and re-layouts  12.1 us (4%)
    ppermute x14, waiting for transfers between devices, turned(): lax.ppermute(value, axis, [(i, (i + turn) % count) for i in range(count)])  101 us
    pallas_call x2, Pallas kernels, attend(): pl.pallas_call(functools.partial(attend_kernel, len(blocks), devices), gr...  30.7 us
    all_gather x1, waiting for transfers between devices, shards(): gathered_last = lax.all_gather(normed[2], 'seq', axis=0, tiled=True)  24.5 us
    ppermute x14, starting transfers between devices, turned(): lax.ppermute(value, axis, [(i, (i + turn) % count) for i in range(count)])  22.1 us
    pallas_call x2, Pallas kernels, accumulate(): pl.pallas_call(functools.partial(add_kernel, offsets, count), in_specs=[s...  16.6 us
    all_gather x1, waiting for transfers between devices, shards(): gathered = lax.all_gather(normed[0], 'seq', axis=0, tiled=True)  14.6 us
    pallas_call x1, Pallas kernels, project(): pl.pallas_call(functools.partial(project_kernel, len(sources), len(blocks...  11.2 us
    pallas_call x1, Pallas kernels, accumulate(): pl.pallas_call(functools.partial(finish_kernel, offsets, count), in_specs...  10.3 us
  transfers between devices with their start and end apart: 27, of which 9 were waited for; matrix products, arithmetic and copies ran while one was open for 3% of the time, Pallas kernels for 27%

profile of v4, /device:TPU:1, one launch (start us, length us, event | category | flops | bytes accessed | tf_op | source)
XLA Modules:
  0.0 291.3 jit_solution(16744669528184607897)
XLA Ops:
  7.2 2.1 collective-permute-start.3
  9.9 3.3 %norm_in.4 = bf16[96,3072]{1,0:T(8,128)(2,1)} custom-call(s32[4]{0:T(128)} %pad_add_fusion.starts_ref, bf16[256,3072]{1,0:T(8,128)(2,1)} %bitcast.27, f32[5,3072]{1,0:T(8,128)} %refs_12_.3), custom_call_target="tpu_custom_call" | custom-call | tf_op jit(solution)/shard_map/norm_in/pallas_call | solution.py:65
  13.3 1.3 collective-permute-start.4
  14.7 2.3 collective-permute-start.5
  18.1 13.8 %collective-permute-done.4 = bf16[768,384]{1,0:T(8,128)(2,1)S(1)} collective-permute-done((bf16[768,384]{1,0:T(8,128)(2,1)S(1)}, bf16[768,384]{1,0:T(8,128)(2,1)S(1)}, u32[]{:S(2)}, u32[]{:S(2)}) %collective-permute-start.4) | collective-permute-done | bytes 589856 | tf_op jit(solution)/shard_map/ppermute | solution.py:33
  31.9 50.7 %collective-permute-done.5 = bf16[768,384]{1,0:T(8,128)(2,1)S(1)} collective-permute-done((bf16[768,384]{1,0:T(8,128)(2,1)S(1)}, bf16[768,384]{1,0:T(8,128)(2,1)S(1)}, u32[]{:S(2)}, u32[]{:S(2)}) %collective-permute-start.5) | collective-permute-done | bytes 589856 | tf_op jit(solution)/shard_map/ppermute | solution.py:33
  82.6 3.3 %collective-permute-done.3.refs_3_.refs_9_ = bf16[768,2304]{1,0:T(8,128)(2,1)} collective-permute-done((bf16[768,2304]{1,0:T(8,128)(2,1)}, bf16[768,2304]{1,0:T(8,128)(2,1)}, u32[]{:S(2)}, u32[]{:S(2)}) %collective-permute-start.3) | collective-permute-done | bytes 3538976 | tf_op jit(solution)/shard_map/ppermute | solution.py:18
  85.9 14.6 %all-gather.3.cloned.1.call-done.refs_0_ = bf16[384,3072]{1,0:T(8,128)(2,1)} async-done(((bf16[96,3072]{1,0:T(8,128)(2,1)}), bf16[384,3072]{1,0:T(8,128)(2,1)}) %all-gather.3.cloned.1.call-update) | async-done | bytes 2359312 | tf_op jit(solution)/shard_map/all_gather | solution.py:363
  101.1 3.3 %norm_in.5 = bf16[96,3072]{1,0:T(8,128)(2,1)} custom-call(s32[4]{0:T(128)} %pad_add_fusion.starts_ref, bf16[256,3072]{1,0:T(8,128)(2,1)} %bitcast.28, f32[5,3072]{1,0:T(8,128)} %refs_12_.3), custom_call_target="tpu_custom_call" | custom-call | tf_op jit(solution)/shard_map/norm_in/pallas_call | solution.py:65
  107.9 1.2 collective-permute-start.9
  109.4 2.3 norm_in.3.refs_0_
  111.7 6.2 %collective-permute-start = (bf16[64,3072]{1,0:T(8,128)(2,1)}, bf16[64,3072]{1,0:T(8,128)(2,1)}, u32[]{:S(2)}, u32[]{:S(2)}) collective-permute-start(bf16[64,3072]{1,0:T(8,128)(2,1)} %norm_in.3.refs_0_), channel_id=1, source_target_pairs={{0,1},{1,2},{2,3},{3,0},{4,5},{5,6},{6,7},{7,4},{8,9},{9,10},{10,1... | collective-permute-start | bytes 1179656 | tf_op jit(solution)/shard_map/ppermute | solution.py:33
  117.9 1.7 collective-permute-start.1
  120.0 11.2 %project.1 = (bf16[6,384,128]{2,1,0:T(8,128)(2,1)}, bf16[6,384,128]{2,1,0:T(8,128)(2,1)}, bf16[6,384,128]{2,1,0:T(8,128)(2,1)}) custom-call(bf16[384,3072]{1,0:T(8,128)(2,1)} %all-gather.3.cloned.1.call-done.refs_0_, bf16[768,2304]{1,0:T(8,128)(2,1)} %refs_7_.1, bf16[768,2304]{1,0:T(8,128)(2,1)} %collective-permute-done.7.refs_2_.refs_8_, ...), custom_call_target="tpu_custom_call" | custom-call | tf_op jit(solution)/shard_map/project/pallas_call | solution.py:116
  131.3 4.2 %collective-permute-done.refs_1_ = bf16[64,3072]{1,0:T(8,128)(2,1)} collective-permute-done((bf16[64,3072]{1,0:T(8,128)(2,1)}, bf16[64,3072]{1,0:T(8,128)(2,1)}, u32[]{:S(2)}, u32[]{:S(2)}) %collective-permute-start) | collective-permute-done | bytes 393248 | tf_op jit(solution)/shard_map/ppermute | solution.py:33
  135.5 30.0 %collective-permute-done.1.refs_2_ = bf16[64,3072]{1,0:T(8,128)(2,1)} collective-permute-done((bf16[64,3072]{1,0:T(8,128)(2,1)}, bf16[64,3072]{1,0:T(8,128)(2,1)}, u32[]{:S(2)}, u32[]{:S(2)}) %collective-permute-start.1) | collective-permute-done | bytes 393248 | tf_op jit(solution)/shard_map/ppermute | solution.py:33
  165.6 2.5 collective-permute-done.2.refs_3_
  168.1 24.5 %all-gather.5.cloned.1.call-done.gathered_ref = bf16[384,3072]{1,0:T(8,128)(2,1)} async-done(((bf16[96,3072]{1,0:T(8,128)(2,1)}), bf16[384,3072]{1,0:T(8,128)(2,1)}) %all-gather.5.cloned.1.call-update) | async-done | bytes 2359312 | tf_op jit(solution)/shard_map/all_gather | solution.py:371
  193.6 2.4 slice.12
  198.7 15.3 %attend.2 = (bf16[256,384]{1,0:T(8,128)(2,1)}, bf16[256,384]{1,0:T(8,128)(2,1)}, bf16[256,384]{1,0:T(8,128)(2,1)}, bf16[256,384]{1,0:T(8,128)(2,1)}) custom-call(s32[1]{0:T(128)} %bitcast.8.place_ref, bf16[384,3072]{1,0:T(8,128)(2,1)} %all-gather.5.cloned.1.call-done.gathered_ref, bf16[64,3072]{1,0:T(8,128)(2,1)} %norm_in.3.refs_0_, ...), custom_call_target="tpu_custom_call" | custom-call | tf_op jit(solution)/shard_map/attend/pallas_call | solution.py:185
  215.1 2.3 collective-permute-start.18
  217.5 15.4 %attend.3 = (bf16[256,384]{1,0:T(8,128)(2,1)}, bf16[256,384]{1,0:T(8,128)(2,1)}, bf16[256,384]{1,0:T(8,128)(2,1)}, bf16[256,384]{1,0:T(8,128)(2,1)}) custom-call(s32[1]{0:T(128)} %bitcast.8.place_ref, bf16[384,3072]{1,0:T(8,128)(2,1)} %all-gather.5.cloned.1.call-done.gathered_ref, bf16[64,3072]{1,0:T(8,128)(2,1)} %norm_in.3.refs_0_, ...), custom_call_target="tpu_custom_call" | custom-call | tf_op jit(solution)/shard_map/attend/pallas_call | solution.py:185
  233.7 1.4 constant_dynamic-update-slice_fusion.5
  235.1 1.5 constant_dynamic-update-slice_fusion.4.refs_7_.refs_8_
  236.6 1.4 collective-permute-start.22
  238.8 3.3 %collective-permute-start.21 = (bf16[256,384]{1,0:T(8,128)(2,1)}, bf16[256,384]{1,0:T(8,128)(2,1)}, u32[]{:S(2)}, u32[]{:S(2)}) collective-permute-start(bf16[256,384]{1,0:T(8,128)(2,1)} %get-tuple-element.88), channel_id=1, source_target_pairs={{0,3},{1,0},{2,1},{3,2},{4,7},{5,4},{6,5},{7,6},{8,11},{9,8},{10,9... | collective-permute-start | bytes 589832 | tf_op jit(solution)/shard_map/ppermute | solution.py:33
  242.7 2.7 collective-permute-start.24
  247.3 7.4 %add_parts.2.refs_11_ = f32[256,3072]{1,0:T(8,128)} custom-call(s32[8]{0:T(128)} %stack.59.starts_ref, bf16[256,384]{1,0:T(8,128)(2,1)} %get-tuple-element.100.refs_0_, bf16[256,384]{1,0:T(8,128)(2,1)} %get-tuple-element.101.refs_1_, bf16[3072,384]{1,0:T(8,128)(2,1)} %constant_dynamic-update-slice_fusion.refs_2_.refs_3_, bf16[3072,384]{1,0:T(8,128)(2,1)} %copy-done.1, ...), custom_call_target="tpu_custom_call" | custom-call | tf_op jit(solution)/shard_map/add_parts/pallas_call | solution.py:297
  254.8 9.1 %add_parts.3.refs_11_ = f32[256,3072]{1,0:T(8,128)} custom-call(s32[8]{0:T(128)} %stack.59.starts_ref, bf16[256,384]{1,0:T(8,128)(2,1)} %copy-done.3, bf16[256,384]{1,0:T(8,128)(2,1)} %copy-done.4, bf16[256,384]{1,0:T(8,128)(2,1)} %copy-done.5, bf16[3072,384]{1,0:T(8,128)(2,1)} %constant_dynamic-update-slice_fusion.refs_2_.refs_3_, ...), custom_call_target="tpu_custom_call", output_to_operand_aliasing={{}: (12, {})} | custom-call | tf_op jit(solution)/shard_map/add_parts/pallas_call | solution.py:297
  264.0 10.3 %finish.1 = (f32[128,256]{1,0:T(8,128)}, bf16[128,256]{1,0:T(8,128)(2,1)}) custom-call(s32[8]{0:T(128)} %stack.59.starts_ref, f32[2]{0:T(128)} %pad_maximum_fusion.coef_ref, bf16[256,384]{1,0:T(8,128)(2,1)} %collective-permute-done.19.refs_0_, bf16[256,384]{1,0:T(8,128)(2,1)} %collective-permute-done.20.refs_1_, ...), custom_call_target="tpu_custom_call" | custom-call | tf_op jit(solution)/shard_map/finish/pallas_call | solution.py:309
  274.2 4.0 %collective-permute-start.23 = (bf16[128,256]{1,0:T(8,128)(2,1)}, bf16[128,256]{1,0:T(8,128)(2,1)S(1)}, u32[]{:S(2)}, u32[]{:S(2)}) collective-permute-start(bf16[128,256]{1,0:T(8,128)(2,1)} %get-tuple-element.103), channel_id=1, source_target_pairs={{2,4},{3,5},{6,8},{7,9},{10,12},{11,13},{4,2},{5,3},{8,6},{9,7},{1... | collective-permute-start | bytes 196616 | tf_op jit(solution)/shard_map/ppermute | solution.py:453
  278.2 4.6 %collective-permute-done.23 = bf16[128,256]{1,0:T(8,128)(2,1)S(1)} collective-permute-done((bf16[128,256]{1,0:T(8,128)(2,1)}, bf16[128,256]{1,0:T(8,128)(2,1)S(1)}, u32[]{:S(2)}, u32[]{:S(2)}) %collective-permute-start.23) | collective-permute-done | bytes 65568 | tf_op jit(solution)/shard_map/ppermute | solution.py:453
  (63 shorter events, 16.4 us)
Async XLA Ops:
  7.2 6.1 %copy-start = (bf16[768,768]{1,0:T(8,128)(2,1)S(1)}, bf16[768,768]{1,0:T(8,128)(2,1)}, u32[]{:S(2)}) copy-start(bf16[768,768]{1,0:T(8,128)(2,1)} %param.11) | copy-start | bytes 3538948
  7.2 93.4 %all-gather.3.cloned.1.call-start = ((), (), s32[]{:S(2)}) async-start(), calls=%async_computation | async-start | bytes 2949120 | tf_op jit(solution)/shard_map/all_gather | solution.py:363
  7.2 78.7 %collective-permute-start.3 = (bf16[768,2304]{1,0:T(8,128)(2,1)}, bf16[768,2304]{1,0:T(8,128)(2,1)}, u32[]{:S(2)}, u32[]{:S(2)}) collective-permute-start(bf16[768,2304]{1,0:T(8,128)(2,1)} %refs_7_.1), channel_id=1, source_target_pairs={{0,8},{4,12},{8,0},{12,4},{1,9},{5,13},{9,1},{13,5},{2,10},{6,14},... | collective-permute-start | bytes 10616840 | tf_op jit(solution)/shard_map/ppermute | solution.py:18
  13.2 179.4 %all-gather.5.cloned.1.call-start = ((), (), s32[]{:S(2)}) async-start(), calls=%async_computation.1 | async-start | bytes 2949120 | tf_op jit(solution)/shard_map/all_gather | solution.py:371
  13.3 18.5 %collective-permute-start.4 = (bf16[768,384]{1,0:T(8,128)(2,1)S(1)}, bf16[768,384]{1,0:T(8,128)(2,1)S(1)}, u32[]{:S(2)}, u32[]{:S(2)}) collective-permute-start(bf16[768,384]{1,0:T(8,128)(2,1)S(1)} %constant_dynamic-slice_fusion), channel_id=1, source_target_pairs={{0,1},{1,2},{2,3},{3,0},{4,5},{5,6},{6,7},{7,4},{8,9},{9,10},{10,1... | collective-permute-start | bytes 1769480 | tf_op jit(solution)/shard_map/ppermute | solution.py:33
  14.7 67.9 %collective-permute-start.5 = (bf16[768,384]{1,0:T(8,128)(2,1)S(1)}, bf16[768,384]{1,0:T(8,128)(2,1)S(1)}, u32[]{:S(2)}, u32[]{:S(2)}) collective-permute-start(bf16[768,384]{1,0:T(8,128)(2,1)S(1)} %constant_dynamic-slice_fusion), channel_id=1, source_target_pairs={{0,2},{1,3},{2,0},{3,1},{4,6},{5,7},{6,4},{7,5},{8,10},{9,11},{10,... | collective-permute-start | bytes 1769480 | tf_op jit(solution)/shard_map/ppermute | solution.py:33
  17.0 65.6 %collective-permute-start.6 = (bf16[768,384]{1,0:T(8,128)(2,1)S(1)}, bf16[768,384]{1,0:T(8,128)(2,1)S(1)}, u32[]{:S(2)}, u32[]{:S(2)}) collective-permute-start(bf16[768,384]{1,0:T(8,128)(2,1)S(1)} %constant_dynamic-slice_fusion), channel_id=1, source_target_pairs={{0,3},{1,0},{2,1},{3,2},{4,7},{5,4},{6,5},{7,6},{8,11},{9,8},{10,9... | collective-permute-start | bytes 1769480 | tf_op jit(solution)/shard_map/ppermute | solution.py:33
  100.6 17.3 %collective-permute-start.7 = (bf16[768,2304]{1,0:T(8,128)(2,1)}, bf16[768,2304]{1,0:T(8,128)(2,1)}, u32[]{:S(2)}, u32[]{:S(2)}) collective-permute-start(bf16[768,2304]{1,0:T(8,128)(2,1)} %refs_7_.1), channel_id=1, source_target_pairs={{0,4},{4,0},{8,12},{12,8},{1,5},{5,1},{9,13},{13,9},{2,6},{6,2},{1... | collective-permute-start | bytes 10616840 | tf_op jit(solution)/shard_map/ppermute | solution.py:18
  101.0 18.5 %collective-permute-start.8 = (bf16[768,2304]{1,0:T(8,128)(2,1)}, bf16[768,2304]{1,0:T(8,128)(2,1)}, u32[]{:S(2)}, u32[]{:S(2)}) collective-permute-start(bf16[768,2304]{1,0:T(8,128)(2,1)} %collective-permute-done.3.refs_3_.refs_9_), channel_id=1, source_target_pairs={{0,4},{4,0},{8,12},{12,8},{1,5},{5,1},{9,13},{13,9},{2,6},{6,2},{1... | collective-permute-start | bytes 10616840 | tf_op jit(solution)/shard_map/ppermute | solution.py:18
  107.9 84.7 %collective-permute-start.9 = (bf16[3072,384]{1,0:T(8,128)(2,1)}, bf16[3072,384]{1,0:T(8,128)(2,1)S(1)}, u32[]{:S(2)}, u32[]{:S(2)}) collective-permute-start(bf16[3072,384]{1,0:T(8,128)(2,1)} %constant_dynamic-update-slice_fusion.refs_2_.refs_3_), channel_id=1, source_target_pairs={{0,16},{16,0},{1,17},{17,1},{2,18},{18,2},{3,19},{19,3},{4,20},{20... | collective-permute-start | bytes 7077896 | tf_op jit(solution)/shard_map/ppermute | solution.py:33
  109.2 83.5 %collective-permute-start.10 = (bf16[3072,384]{1,0:T(8,128)(2,1)}, bf16[3072,384]{1,0:T(8,128)(2,1)}, u32[]{:S(2)}, u32[]{:S(2)}) collective-permute-start(bf16[3072,384]{1,0:T(8,128)(2,1)} %constant_dynamic-update-slice_fusion.refs_2_.refs_3_), channel_id=1, source_target_pairs={{0,8},{4,12},{8,0},{12,4},{1,9},{5,13},{9,1},{13,5},{2,10},{6,14},... | collective-permute-start | bytes 7077896 | tf_op jit(solution)/shard_map/ppermute | solution.py:18
  111.7 23.8 %collective-permute-start = (bf16[64,3072]{1,0:T(8,128)(2,1)}, bf16[64,3072]{1,0:T(8,128)(2,1)}, u32[]{:S(2)}, u32[]{:S(2)}) collective-permute-start(bf16[64,3072]{1,0:T(8,128)(2,1)} %norm_in.3.refs_0_), channel_id=1, source_target_pairs={{0,1},{1,2},{2,3},{3,0},{4,5},{5,6},{6,7},{7,4},{8,9},{9,10},{10,1... | collective-permute-start | bytes 1179656 | tf_op jit(solution)/shard_map/ppermute | solution.py:33
  117.9 47.7 %collective-permute-start.1 = (bf16[64,3072]{1,0:T(8,128)(2,1)}, bf16[64,3072]{1,0:T(8,128)(2,1)}, u32[]{:S(2)}, u32[]{:S(2)}) collective-permute-start(bf16[64,3072]{1,0:T(8,128)(2,1)} %norm_in.3.refs_0_), channel_id=1, source_target_pairs={{0,2},{1,3},{2,0},{3,1},{4,6},{5,7},{6,4},{7,5},{8,10},{9,11},{10,... | collective-permute-start | bytes 1179656 | tf_op jit(solution)/shard_map/ppermute | solution.py:33
  119.5 48.5 %collective-permute-start.2 = (bf16[64,3072]{1,0:T(8,128)(2,1)}, bf16[64,3072]{1,0:T(8,128)(2,1)}, u32[]{:S(2)}, u32[]{:S(2)}) collective-permute-start(bf16[64,3072]{1,0:T(8,128)(2,1)} %norm_in.3.refs_0_), channel_id=1, source_target_pairs={{0,3},{1,0},{2,1},{3,2},{4,7},{5,4},{6,5},{7,6},{8,11},{9,8},{10,9... | collective-permute-start | bytes 1179656 | tf_op jit(solution)/shard_map/ppermute | solution.py:33
  192.6 4.6 %copy-start.1 = (bf16[3072,384]{1,0:T(8,128)(2,1)}, bf16[3072,384]{1,0:T(8,128)(2,1)S(1)}, u32[]{:S(2)}) copy-start(bf16[3072,384]{1,0:T(8,128)(2,1)S(1)} %collective-permute-done.9.refs_3_.refs_4_) | copy-start | bytes 7077892
  192.6 21.4 %collective-permute-start.11 = (bf16[3072,384]{1,0:T(8,128)(2,1)}, bf16[3072,384]{1,0:T(8,128)(2,1)}, u32[]{:S(2)}, u32[]{:S(2)}) collective-permute-start(bf16[3072,384]{1,0:T(8,128)(2,1)} %constant_dynamic-update-slice_fusion.refs_2_.refs_3_), channel_id=1, source_target_pairs={{0,4},{4,0},{8,12},{12,8},{1,5},{5,1},{9,13},{13,9},{2,6},{6,2},{1... | collective-permute-start | bytes 7077896 | tf_op jit(solution)/shard_map/ppermute | solution.py:18
  193.1 20.9 %collective-permute-start.12 = (bf16[3072,384]{1,0:T(8,128)(2,1)S(1)}, bf16[3072,384]{1,0:T(8,128)(2,1)}, u32[]{:S(2)}, u32[]{:S(2)}) collective-permute-start(bf16[3072,384]{1,0:T(8,128)(2,1)S(1)} %collective-permute-done.9.refs_3_.refs_4_), channel_id=1, source_target_pairs={{0,4},{4,0},{8,12},{12,8},{1,5},{5,1},{9,13},{13,9},{2,6},{6,2},{1... | collective-permute-start | bytes 7077896 | tf_op jit(solution)/shard_map/ppermute | solution.py:18
  193.2 20.9 %collective-permute-start.13 = (bf16[3072,384]{1,0:T(8,128)(2,1)}, bf16[3072,384]{1,0:T(8,128)(2,1)}, u32[]{:S(2)}, u32[]{:S(2)}) collective-permute-start(bf16[3072,384]{1,0:T(8,128)(2,1)} %collective-permute-done.10.refs_6_.refs_7_), channel_id=1, source_target_pairs={{0,4},{4,0},{8,12},{12,8},{1,5},{5,1},{9,13},{13,9},{2,6},{6,2},{1... | collective-permute-start | bytes 7077896 | tf_op jit(solution)/shard_map/ppermute | solution.py:18
  197.2 35.6 %collective-permute-start.14 = (bf16[1536,384]{1,0:T(8,128)(2,1)}, bf16[1536,384]{1,0:T(8,128)(2,1)}, u32[]{:S(2)}, u32[]{:S(2)}) collective-permute-start(bf16[1536,384]{1,0:T(8,128)(2,1)} %slice.12), channel_id=1, source_target_pairs={{0,16},{16,0},{1,17},{17,1},{2,18},{18,2},{3,19},{19,3},{4,20},{20... | collective-permute-start | bytes 3538952 | tf_op jit(solution)/shard_map/ppermute | solution.py:33
  197.5 35.3 %collective-permute-start.15 = (bf16[1536,384]{1,0:T(8,128)(2,1)}, bf16[1536,384]{1,0:T(8,128)(2,1)}, u32[]{:S(2)}, u32[]{:S(2)}) collective-permute-start(bf16[1536,384]{1,0:T(8,128)(2,1)} %slice.13), channel_id=1, source_target_pairs={{0,8},{4,12},{8,0},{12,4},{1,9},{5,13},{9,1},{13,5},{2,10},{6,14},... | collective-permute-start | bytes 3538952 | tf_op jit(solution)/shard_map/ppermute | solution.py:18
  214.1 18.8 %collective-permute-start.16 = (bf16[256,384]{1,0:T(8,128)(2,1)}, bf16[256,384]{1,0:T(8,128)(2,1)S(1)}, u32[]{:S(2)}, u32[]{:S(2)}) collective-permute-start(bf16[256,384]{1,0:T(8,128)(2,1)} %get-tuple-element.83), channel_id=1, source_target_pairs={{0,2},{1,3},{2,0},{3,1},{4,6},{5,7},{6,4},{7,5},{8,10},{9,11},{10,... | collective-permute-start | bytes 589832 | tf_op jit(solution)/shard_map/ppermute | solution.py:33
  214.2 18.7 %collective-permute-start.17 = (bf16[256,384]{1,0:T(8,128)(2,1)}, bf16[256,384]{1,0:T(8,128)(2,1)S(1)}, u32[]{:S(2)}, u32[]{:S(2)}) collective-permute-start(bf16[256,384]{1,0:T(8,128)(2,1)} %get-tuple-element.84), channel_id=1, source_target_pairs={{0,1},{1,2},{2,3},{3,0},{4,5},{5,6},{6,7},{7,4},{8,9},{9,10},{10,1... | collective-permute-start | bytes 589832 | tf_op jit(solution)/shard_map/ppermute | solution.py:33
  215.1 17.8 %collective-permute-start.18 = (bf16[256,384]{1,0:T(8,128)(2,1)}, bf16[256,384]{1,0:T(8,128)(2,1)S(1)}, u32[]{:S(2)}, u32[]{:S(2)}) collective-permute-start(bf16[256,384]{1,0:T(8,128)(2,1)} %get-tuple-element.85), channel_id=1, source_target_pairs={{0,3},{1,0},{2,1},{3,2},{4,7},{5,4},{6,5},{7,6},{8,11},{9,8},{10,9... | collective-permute-start | bytes 589832 | tf_op jit(solution)/shard_map/ppermute | solution.py:33
  232.9 3.7 %copy-start.3 = (bf16[256,384]{1,0:T(8,128)(2,1)}, bf16[256,384]{1,0:T(8,128)(2,1)S(1)}, u32[]{:S(2)}) copy-start(bf16[256,384]{1,0:T(8,128)(2,1)S(1)} %collective-permute-done.16.refs_0_) | copy-start | bytes 589828
  233.7 8.4 %copy-start.6 = (s32[1,256]{1,0:T(1,128)S(1)}, s32[1,256]{1,0:T(1,128)}, u32[]{:S(2)}) copy-start(s32[1,256]{1,0:T(1,128)} %param.14) | copy-start | bytes 3076
  236.6 10.7 %copy-start.2 = (bf16[3072,384]{1,0:T(8,128)(2,1)}, bf16[3072,384]{1,0:T(8,128)(2,1)S(1)}, u32[]{:S(2)}) copy-start(bf16[3072,384]{1,0:T(8,128)(2,1)S(1)} %constant_dynamic-update-slice_fusion.4.refs_7_.refs_8_) | copy-start | bytes 7077892
  236.6 10.7 %collective-permute-start.22 = (bf16[3072,384]{1,0:T(8,128)(2,1)S(1)}, bf16[3072,384]{1,0:T(8,128)(2,1)}, u32[]{:S(2)}, u32[]{:S(2)}) collective-permute-start(bf16[3072,384]{1,0:T(8,128)(2,1)S(1)} %constant_dynamic-update-slice_fusion.4.refs_7_.refs_8_), channel_id=1, source_target_pairs={{0,4},{4,0},{8,12},{12,8},{1,5},{5,1},{9,13},{13,9},{2,6},{6,2},{1... | collective-permute-start | bytes 7077896 | tf_op jit(solution)/shard_map/ppermute | solution.py:18
  238.0 25.9 %collective-permute-start.19 = (bf16[256,384]{1,0:T(8,128)(2,1)}, bf16[256,384]{1,0:T(8,128)(2,1)}, u32[]{:S(2)}, u32[]{:S(2)}) collective-permute-start(bf16[256,384]{1,0:T(8,128)(2,1)} %get-tuple-element.86), channel_id=1, source_target_pairs={{0,2},{1,3},{2,0},{3,1},{4,6},{5,7},{6,4},{7,5},{8,10},{9,11},{10,... | collective-permute-start | bytes 589832 | tf_op jit(solution)/shard_map/ppermute | solution.py:33
  238.8 25.1 %collective-permute-start.20 = (bf16[256,384]{1,0:T(8,128)(2,1)}, bf16[256,384]{1,0:T(8,128)(2,1)}, u32[]{:S(2)}, u32[]{:S(2)}) collective-permute-start(bf16[256,384]{1,0:T(8,128)(2,1)} %get-tuple-element.87), channel_id=1, source_target_pairs={{0,1},{1,2},{2,3},{3,0},{4,5},{5,6},{6,7},{7,4},{8,9},{9,10},{10,1... | collective-permute-start | bytes 589832 | tf_op jit(solution)/shard_map/ppermute | solution.py:33
  238.8 25.1 %collective-permute-start.21 = (bf16[256,384]{1,0:T(8,128)(2,1)}, bf16[256,384]{1,0:T(8,128)(2,1)}, u32[]{:S(2)}, u32[]{:S(2)}) collective-permute-start(bf16[256,384]{1,0:T(8,128)(2,1)} %get-tuple-element.88), channel_id=1, source_target_pairs={{0,3},{1,0},{2,1},{3,2},{4,7},{5,4},{6,5},{7,6},{8,11},{9,8},{10,9... | collective-permute-start | bytes 589832 | tf_op jit(solution)/shard_map/ppermute | solution.py:33
  242.7 35.6 %collective-permute-start.24 = (bf16[1,256]{1,0:T(2,128)(2,1)S(1)}, bf16[1,256]{1,0:T(2,128)(2,1)S(1)}, u32[]{:S(2)}, u32[]{:S(2)}) collective-permute-start(bf16[1,256]{1,0:T(2,128)(2,1)S(1)} %get-tuple-element.106), channel_id=1, source_target_pairs={{2,4},{3,5},{6,8},{7,9},{10,12},{11,13},{4,2},{5,3},{8,6},{9,7},{1... | collective-permute-start | bytes 1544 | tf_op jit(solution)/shard_map/ppermute | solution.py:344
  274.2 8.6 %collective-permute-start.23 = (bf16[128,256]{1,0:T(8,128)(2,1)}, bf16[128,256]{1,0:T(8,128)(2,1)S(1)}, u32[]{:S(2)}, u32[]{:S(2)}) collective-permute-start(bf16[128,256]{1,0:T(8,128)(2,1)} %get-tuple-element.103), channel_id=1, source_target_pairs={{2,4},{3,5},{6,8},{7,9},{10,12},{11,13},{4,2},{5,3},{8,6},{9,7},{1... | collective-permute-start | bytes 196616 | tf_op jit(solution)/shard_map/ppermute | solution.py:453
  (2 other events, 4.4 us)
Sparse Core Ops, SparseCore 0:
  13.3 87.1 all-gather.2
  104.5 88.0 all-gather.4

commit v5 on v4

v5 whole, which is shorter than its diff:
```python
import functools
import math

import jax
import jax.numpy as jnp
from jax import lax
from jax.experimental import pallas as pl
from jax.experimental.pallas import tpu as pltpu
from jax.sharding import PartitionSpec as P

HD = 128
NSTEPS = 28
MIB = 1 << 20


def swap(value, axis, bit):
    count = lax.axis_size(axis)
    return lax.ppermute(value, axis, [(i, i ^ bit) for i in range(count)])


def bits_of(count):
    far = [1 << n for n in range(1, count.bit_length() - 1)]
    return far + [1]


def noise_level(index, steps):
    level = 1.0 - index / steps
    return 3.0 * level / (1.0 + 2.0 * level)


def turned(value, axis, turn):
    count = lax.axis_size(axis)
    return lax.ppermute(value, axis, [(i, (i + turn) % count) for i in range(count)])


def step_pairs(count, step, way):
    if way > 0:
        return [(s, s + 1) for s in range(step - 1, count - 1)]
    return [(s, s - 1) for s in range(1, count - step + 1)]


def arrivals(count):
    return [
        sorted((s - home for home in range(count) if home != s), key=lambda hop: (abs(hop), -hop))
        for s in range(count)
    ]


def layer_norm(values):
    mean = jnp.mean(values, axis=-1, keepdims=True)
    centred = values - mean
    spread = jnp.mean(centred * centred, axis=-1, keepdims=True)
    return centred * lax.rsqrt(spread + 1e-06)


def root_norm(values):
    spread = jnp.mean(values * values, axis=-1, keepdims=True)
    return (values * lax.rsqrt(spread + 1e-06)).astype(jnp.bfloat16)


def norm_kernel(blocks, starts_ref, hidden_ref, mod_ref, out_ref):
    local = hidden_ref[...].astype(jnp.float32)
    mean = jnp.mean(local, axis=-1, keepdims=True)
    centred = local - mean
    spread = jnp.mean(centred * centred, axis=-1, keepdims=True)
    scaling = lax.rsqrt(spread + 1e-06)
    width = hidden_ref.shape[1] // blocks
    for n in range(blocks):
        taken = pl.ds(pl.multiple_of(starts_ref[n], HD), width)
        values = (hidden_ref[:, taken].astype(jnp.float32) - mean) * scaling
        values = values * (1.0 + mod_ref[1:2, taken]) + mod_ref[0:1, taken]
        out_ref[:, n * width : (n + 1) * width] = values.astype(jnp.bfloat16)


def norm_rows(hidden, modulation, starts, first, rows):
    width = hidden.shape[1]
    block = math.gcd(math.gcd(first, rows), 64)
    return pl.pallas_call(
        functools.partial(norm_kernel, starts.shape[0]),
        grid=(rows // block,),
        in_specs=[
            pl.BlockSpec(memory_space=pltpu.SMEM),
            pl.BlockSpec((block, width), lambda i: (first // block + i, 0)),
            pl.BlockSpec(modulation.shape, lambda i: (0, 0)),
        ],
        out_specs=pl.BlockSpec((block, width), lambda i: (i, 0)),
        out_shape=jax.ShapeDtypeStruct((rows, width), jnp.bfloat16),
        name="norm_in",
    )(starts, hidden, modulation)


def product(x_ref, blocks):
    height = x_ref.shape[1] // len(blocks)
    total = 0.0
    for n, block in enumerate(blocks):
        total += jnp.dot(
            x_ref[:, n * height : (n + 1) * height],
            block[...],
            preferred_element_type=jnp.float32,
        )
    return total


def load(place, choices, refs, to, sem):
    for n, ref in enumerate(refs):
        wanted = functools.reduce(
            jnp.logical_or, [place == s for s in range(len(choices)) if choices[s] == n]
        )

        @pl.when(wanted)
        def _():
            pltpu.make_async_copy(ref, to, sem).start()

    return pltpu.make_async_copy(refs[0], to, sem)


def load_all(place, plan, refs, tokens, sems):
    rows = tokens.shape[0] // len(plan)
    copies, used = [], 0
    for n, choices in enumerate(plan):
        many = max(choices) + 1
        to = tokens.at[pl.ds(n * rows, rows)]
        copies.append(load(place, choices, refs[used : used + many], to, sems.at[n]))
        used += many
    for copy in copies:
        copy.wait()


def project_kernel(plan, blocks, place_ref, *refs):
    w_refs = refs[:blocks]
    sources, (q_ref, k_ref, v_ref, tokens, sems) = refs[blocks:-5], refs[-5:]

    @pl.when(pl.program_id(0) == 0)
    def _():
        load_all(place_ref[0], plan, sources, tokens, sems)

    proj = product(tokens, w_refs)
    for h in range(q_ref.shape[0]):
        query, key, value = (proj[:, (3 * h + i) * HD : (3 * h + i + 1) * HD] for i in range(3))
        q_ref[h] = root_norm(query)
        k_ref[h] = root_norm(key)
        v_ref[h] = value.astype(jnp.bfloat16)


def project(place, plan, sources, blocks):
    rows, width = sources[0].shape
    length = rows * len(plan)
    total = blocks[0].shape[1]
    heads = total // (3 * HD)
    many = 2 if heads % 2 == 0 else 1
    out = jax.ShapeDtypeStruct((heads, length, HD), jnp.bfloat16)
    return pl.pallas_call(
        functools.partial(project_kernel, plan, len(blocks)),
        grid=(heads // many,),
        in_specs=[pl.BlockSpec(memory_space=pltpu.SMEM)]
        + [pl.BlockSpec((width // len(blocks), many * 3 * HD), lambda h: (0, h))] * len(blocks)
        + [pl.BlockSpec(memory_space=pl.ANY)] * len(sources),
        out_specs=[pl.BlockSpec((many, length, HD), lambda h: (h, 0, 0))] * 3,
        out_shape=[out] * 3,
        scratch_shapes=[
            pltpu.VMEM((length, width), jnp.bfloat16),
            pltpu.SemaphoreType.DMA((len(plan),)),
        ],
        compiler_params=pltpu.CompilerParams(vmem_limit_bytes=60 * MIB),
        name="project",
    )(place, *blocks, *sources)


def attend_kernel(plan, blocks, counts, place_ref, slots_ref, *refs):
    w_refs, refs = refs[:blocks], refs[blocks:]
    known, refs = refs[: 3 * len(counts)], refs[3 * len(counts) :]
    queries, keys, values, tokens, sems = refs[-5:]
    devices = slots_ref.shape[0]
    sources, outs = refs[: -5 - devices], refs[-5 - devices : -5]
    start, rows = sum(counts), tokens.shape[0]

    @pl.when(pl.program_id(0) == 0)
    def _():
        values[:, HD:] = jnp.ones((start + rows, HD), jnp.bfloat16)
        load_all(place_ref[0], plan, sources, tokens, sems)

    proj = product(tokens, w_refs)
    at = 0
    for n, count in enumerate(counts):
        queries[at : at + count] = known[3 * n][0]
        keys[at : at + count] = known[3 * n + 1][0]
        values[at : at + count, :HD] = known[3 * n + 2][0]
        at += count
    queries[start:] = root_norm(proj[:, :HD])
    keys[start:] = root_norm(proj[:, HD : 2 * HD])
    values[start:, :HD] = proj[:, 2 * HD :].astype(jnp.bfloat16)
    for turn in range(devices):
        first = pl.multiple_of(slots_ref[turn] * rows, rows)
        scores = lax.dot_general(
            queries[pl.ds(first, rows)],
            keys[...],
            (((1,), (1,)), ((), ())),
            preferred_element_type=jnp.float32,
        )
        expo = jnp.exp(scores * (1.0 / math.sqrt(HD))).astype(jnp.bfloat16)
        mixed = jnp.dot(expo, values[...], preferred_element_type=jnp.float32)
        outs[turn][...] = (mixed[:, :HD] / mixed[:, HD:]).astype(jnp.bfloat16)


def attend(place, slots, plan, sources, known, blocks, start, heads):
    devices = slots.shape[0]
    rows, width = sources[0].shape
    counts = [three[0].shape[1] for three in known]
    length = rows + sum(counts)
    smem = pl.BlockSpec(memory_space=pltpu.SMEM)
    out = jax.ShapeDtypeStruct((rows, heads * HD), jnp.bfloat16)
    return pl.pallas_call(
        functools.partial(attend_kernel, plan, len(blocks), counts),
        grid=(heads,),
        in_specs=[smem, smem]
        + [pl.BlockSpec((width // len(blocks), 3 * HD), lambda h: (0, start + h))] * len(blocks)
        + [
            pl.BlockSpec((1, count, HD), lambda h: (start + h, 0, 0))
            for count in counts
            for _ in range(3)
        ]
        + [pl.BlockSpec(memory_space=pl.ANY)] * len(sources),
        out_specs=[pl.BlockSpec((rows, HD), lambda h: (0, h))] * devices,
        out_shape=[out] * devices,
        scratch_shapes=[
            pltpu.VMEM((length, HD), jnp.bfloat16),
            pltpu.VMEM((length, HD), jnp.bfloat16),
            pltpu.VMEM((length, 2 * HD), jnp.bfloat16),
            pltpu.VMEM((rows, width), jnp.bfloat16),
            pltpu.SemaphoreType.DMA((1,)),
        ],
        compiler_params=pltpu.CompilerParams(vmem_limit_bytes=60 * MIB),
        name="attend",
    )(place, slots, *blocks, *(value for three in known for value in three), *sources)


def multiply(parts, offsets, starts_ref, rows_ref, sources, weights, sems, wide, store):
    depth = [part.shape[1] for part in parts]
    width = weights.shape[2]
    copies = []
    for p, source in enumerate(sources):
        copies.append([])
        for n, (turn, offset) in enumerate(offsets):
            to = sum(depth[:n])
            row = pl.multiple_of(rows_ref[turn] + offset, HD)
            copies[p].append(
                pltpu.make_async_copy(
                    source.at[pl.ds(row, depth[n])],
                    weights.at[p, pl.ds(to, depth[n])],
                    sems.at[p, n],
                )
            )
            copies[p][n].start()
    for n, part in enumerate(parts):
        wide[:, sum(depth[:n]) : sum(depth[: n + 1])] = part[...]
    for p in range(len(sources)):
        for copy in copies[p]:
            copy.wait()
        cols = pl.ds(pl.multiple_of(starts_ref[p], HD), width)
        store(p, cols, jnp.dot(wide[...], weights[p], preferred_element_type=jnp.float32))


def add_kernel(offsets, count, starts_ref, rows_ref, *refs):
    parts = refs[: len(offsets)]
    sources = refs[len(offsets) : len(offsets) + count]
    before_ref, mod_ref, out_ref, weights, wide, sems = refs[len(offsets) + count :]

    def store(p, cols, summed):
        out_ref[:, cols] = before_ref[:, cols].astype(jnp.float32) + mod_ref[2:3, cols] * summed

    multiply(parts, offsets, starts_ref, rows_ref, sources, weights, sems, wide, store)


def finish_kernel(offsets, count, starts_ref, rows_ref, coef_ref, *refs):
    parts = refs[: len(offsets)]
    sources = refs[len(offsets) : len(offsets) + count]
    before_ref, mod_ref, head_ref, latent_ref, weight_ref, out_ref, sent_ref = refs[
        len(offsets) + count : len(offsets) + count + 7
    ]
    weights, wide, sems, mixed, extra = refs[len(offsets) + count + 7 :]
    width = weights.shape[2]
    copies = []
    for p in range(count):
        cols = pl.ds(pl.multiple_of(starts_ref[p], HD), width)
        copies.append(
            pltpu.make_async_copy(before_ref.at[:, cols], mixed.at[:, cols], extra.at[p])
        )
        copies[p].start()

    def store(p, cols, summed):
        copies[p].wait()
        mixed[:, cols] += mod_ref[2:3, cols] * summed

    multiply(parts, offsets, starts_ref, rows_ref, sources, weights, sems, wide, store)
    normed = layer_norm(mixed[...]) * (1.0 + mod_ref[4:5, :]) + mod_ref[3:4, :]
    velocity = lax.dot_general(
        head_ref[...],
        normed.astype(jnp.bfloat16),
        (((1,), (1,)), ((), ())),
        preferred_element_type=jnp.float32,
    )
    channels = velocity.shape[0]
    base, weight = latent_ref[...], weight_ref[...]
    moved = (base + coef_ref[1] * velocity) * weight
    guess = (base - coef_ref[0] * velocity) * weight
    out_ref[:channels, :] = moved
    out_ref[channels:, :] = guess
    sent_ref[:channels, :] = moved.astype(jnp.bfloat16)
    sent_ref[channels:, :] = guess.astype(jnp.bfloat16)


def accumulate(parts, offsets, starts, firsts, pieces, before, modulation, last=None):
    rows, width = before.shape
    depth = sum(part.shape[1] for part in parts)
    count = len(pieces)
    smem = pl.BlockSpec(memory_space=pltpu.SMEM)
    vmem = pl.BlockSpec(memory_space=pltpu.VMEM)
    hbm = pl.BlockSpec(memory_space=pl.ANY)
    scratch = [
        pltpu.VMEM((count, depth, pieces[0].shape[1]), jnp.bfloat16),
        pltpu.VMEM((rows, depth), jnp.bfloat16),
        pltpu.SemaphoreType.DMA((count, len(parts))),
    ]
    params = dict(
        compiler_params=pltpu.CompilerParams(vmem_limit_bytes=60 * MIB),
    )
    if last is None:
        aliased = before.dtype == jnp.float32
        return pl.pallas_call(
            functools.partial(add_kernel, offsets, count),
            in_specs=[smem] * 2 + [vmem] * len(parts) + [hbm] * count + [vmem] * 2,
            out_specs=vmem,
            out_shape=jax.ShapeDtypeStruct((rows, width), jnp.float32),
            scratch_shapes=scratch,
            input_output_aliases={2 + len(parts) + count: 0} if aliased else {},
            name="add_parts",
            **params,
        )(starts, firsts, *parts, *pieces, before, modulation)
    coef, head, latent, weight = last
    channels = head.shape[0]
    return pl.pallas_call(
        functools.partial(finish_kernel, offsets, count),
        in_specs=[smem] * 3 + [vmem] * len(parts) + [hbm] * (count + 1) + [vmem] * 4,
        out_specs=[vmem, vmem],
        out_shape=[
            jax.ShapeDtypeStruct((2 * channels, rows), jnp.float32),
            jax.ShapeDtypeStruct((2 * channels, rows), jnp.bfloat16),
        ],
        scratch_shapes=scratch
        + [pltpu.VMEM((rows, width), jnp.float32), pltpu.SemaphoreType.DMA((count,))],
        name="finish",
        **params,
    )(starts, firsts, coef, *parts, *pieces, before, modulation, head, latent, weight)


def shards(hidden, modulation, w_qkv, w_out, w_head, latent, weights_int, step_index):
    local = hidden[0]
    rows = local.shape[0]
    devices = lax.axis_size("seq")
    tiles = lax.axis_size("tile")
    groups = lax.axis_size("group")
    place, tile, group = lax.axis_index("seq"), lax.axis_index("tile"), lax.axis_index("group")
    far, near = bits_of(tiles)[:-1], bits_of(tiles)[-1]

    weight = weights_int.astype(jnp.float32)
    joins = [
        (t * devices + s, (t + 1) * devices + s - (devices - 2))
        for t in range(tiles - 1)
        for s in range(devices - 2, devices)
    ]
    joins += [
        (t * devices + s, (t - 1) * devices + s + (devices - 2))
        for t in range(1, tiles)
        for s in range(2)
    ]
    norms = weight + lax.ppermute(
        weight.astype(jnp.bfloat16), ("tile", "seq"), joins
    ).astype(jnp.float32)

    height = w_qkv.shape[0]
    ragged = height % HD != 0
    row_starts = jnp.stack([(tile ^ d) * height for d in range(tiles)]).astype(jnp.int32)
    if ragged:
        row_starts = jnp.zeros((1,), jnp.int32)
    normed = norm_rows(local, modulation, row_starts, 0, rows)
    hops = arrivals(devices)
    blocks_by = {0: normed}

    def hop(step):
        for way in (1, -1):
            blocks_by[way * step] = lax.ppermute(
                blocks_by[way * (step - 1)], "seq", step_pairs(devices, step, way)
            )

    def arrival(number):
        wanted = [hops[s][number] for s in range(devices)]
        names = sorted(set(wanted))
        return [names.index(name) for name in wanted], [blocks_by[name] for name in names]

    part = w_out.shape[1] // groups
    share = lax.dynamic_slice_in_dim(w_out, group * part, part, axis=1)
    narrow = part % HD != 0
    columns = {(0, 0): lax.all_gather(share, "seq", axis=0, tiled=True)}

    blocks = {0: w_qkv}
    if not ragged:
        blocks[near] = swap(w_qkv, "tile", near)
        for bit in far:
            blocks.update(
                {d ^ bit: swap(blocks[d], "tile", bit) for d in list(blocks) if d != near}
            )
    hop(1)
    blocks, columns, blocks_by = lax.optimization_barrier((blocks, columns, blocks_by))
    if ragged:
        blocks[0] = lax.all_gather(blocks[0], "tile", axis=0, tiled=True)
    else:
        blocks.update(
            {d ^ near: swap(blocks[d], "tile", near) for d in list(blocks) if d not in (0, near)}
        )
    blocks = [blocks[d] for d in range(len(blocks))]
    if narrow:
        columns[0, 0] = lax.all_gather(columns[0, 0].T, ("tile", "group"), axis=0, tiled=True).T
    else:
        for bit in far:
            columns.update({(d ^ bit, 0): swap(columns[d, 0], "tile", bit) for d, _ in list(columns)})
        for turn in range(1, groups):
            columns[0, turn] = turned(columns[0, 0], "group", turn)

    at = place.reshape(1)
    known, plan, sources = [], [[0] * devices], [normed]
    for number in range(devices - 2):
        if number + 2 < devices:
            hop(number + 2)
        choices, found = arrival(number)
        plan, sources = plan + [choices], sources + found
        known.append(project(at, plan, sources, blocks))
        plan, sources = [], []
        if number + 3 < devices:
            blocks_by, known = lax.optimization_barrier((blocks_by, known))
    if not narrow:
        mine = lax.optimization_barrier((columns[0, 0], known[0]))[0]
        columns[near, 0] = swap(mine, "tile", near)
    blocks_by, known, columns = lax.optimization_barrier((blocks_by, known, columns))
    late = {}
    for turn in range(1, groups) if not narrow else []:
        late.update(
            {
                (d, turn): turned(columns[d, 0], "group", turn)
                for d, g in columns
                if d not in (0, near) and not g
            }
        )
    if groups == 2 and len(far) == 1 and not narrow:
        bit, half = far[0], columns[0, 0].shape[0] // 2
        late[bit, 1] = [
            turned(columns[bit, 0][:half], "group", 1),
            swap(columns[0, 1][half:], "tile", bit),
        ]
    if not narrow:
        columns.update(
            {
                (d ^ near, g): swap(columns[d, g], "tile", near)
                for d, g in list(columns)
                if (d ^ near, g) not in columns
            }
        )

    table = [
        [([s] + [s - hop for hop in hops[s]]).index((s + turn) % devices) for turn in range(devices)]
        for s in range(devices)
    ]
    slots = jnp.asarray(table, jnp.int32)[place]
    heads = w_qkv.shape[1] // (3 * HD)
    halves = [(0, (heads + 1) // 2), ((heads + 1) // 2, heads // 2)]
    turns = sorted(range(1, devices), key=lambda turn: -min(turn, devices - turn))
    choices, found = arrival(devices - 2)
    attended = attend(at, slots, [choices], found, known, blocks, *halves[0])
    attended, columns, found = lax.optimization_barrier((attended, columns, found))
    received = [[turned(attended[turn], "seq", turn) for turn in turns]]
    own = [attended[0]]
    attended = attend(at, slots, [choices], found, known, blocks, *halves[1])
    attended, late, received = lax.optimization_barrier((attended, late, received))
    for key, value in late.items():
        columns[key] = jnp.concatenate(value, axis=0) if isinstance(value, list) else value
    columns.update({(d ^ near, g): swap(columns[d, g], "tile", near) for d, g in late})
    received.append([turned(attended[turn], "seq", turn) for turn in turns])
    own.append(attended[0])
    order = sorted(columns)
    pieces = [columns[key] for key in order]
    starts = jnp.stack(
        [
            (tile ^ d) * (part * groups) + lax.rem(group - g + groups, groups) * part
            for d, g in order
        ]
    ).astype(jnp.int32)
    if narrow:
        starts = jnp.zeros((1,), jnp.int32)

    features = w_out.shape[0]
    firsts = jnp.stack(
        [lax.rem(place - turn + devices, devices) * features for turn in range(devices)]
    ).astype(jnp.int32)
    offsets = [[(turn, start * HD) for turn in turns] for start, _ in halves]
    mixed = accumulate(
        own + received[0],
        [(0, start * HD) for start, _ in halves] + offsets[0],
        starts,
        firsts,
        pieces,
        local,
        modulation,
    )
    index = step_index[0].astype(jnp.float32)
    now = noise_level(index, NSTEPS)
    later = noise_level(index + 1.0, NSTEPS)
    weighted, to_join = accumulate(
        received[1],
        offsets[1],
        starts,
        firsts,
        pieces,
        mixed,
        modulation,
        (jnp.stack([now, later - now]), w_head.T, latent[0].T, weight),
    )
    other = lax.ppermute(to_join, ("tile", "seq"), joins).astype(jnp.float32)
    joined = (weighted + other) / norms
    channels = w_head.shape[1]
    return (joined[:channels].T[None], joined[channels:].T[None])


def solution(mesh):
    in_specs = (
        P(("group", "tile"), "seq", None),
        P("group", None),
        P("tile", "seq"),
        P("seq", "tile"),
        P(),
        P(("group", "tile"), "seq", None),
        P(("group", "tile"), "seq"),
        P("group"),
    )
    out_specs = (P(("group", "tile"), "seq", None), P(("group", "tile"), "seq", None))
    return jax.shard_map(shards, mesh=mesh, in_specs=in_specs, out_specs=out_specs, check_vma=False)
```

time: 292 us -> 271 us (0.928)
  waiting for transfers between devices: 148 us -> 119 us
  starting transfers between devices: 35.3 us -> 47.3 us
  Pallas kernels: 77.6 us -> 73.8 us
    ppermute x0 -> x6, waiting for transfers between devices: none -> 110 us  [hop(): lax.ppermute(blocks_by[way * (step - 1)], 'seq', step_pairs(devices, step...]
    ppermute x14 -> x8, waiting for transfers between devices: 101 us -> 2.92 us  [turned(): lax.ppermute(value, axis, [(i, (i + turn) % count) for i in range(count)])]
    all_gather x2 -> x1, waiting for transfers between devices: 39.2 us -> 0.22 us  [shards(): columns = {(0, 0): lax.all_gather(share, 'seq', axis=0, tiled=True)}]
    ppermute x0 -> x6, starting transfers between devices: none -> 12.6 us  [hop(): lax.ppermute(blocks_by[way * (step - 1)], 'seq', step_pairs(devices, step...]
    ppermute x14 -> x8, starting transfers between devices: 22.1 us -> 13.1 us  [turned(): lax.ppermute(value, axis, [(i, (i + turn) % count) for i in range(count)])]
    pallas_call x3 -> x4, Pallas kernels: 42 us -> 48.3 us  [the longest x2 24.8 us: project(): pl.pallas_call(functools.partial(project_kernel, plan, len(blocks)), grid...]
    pallas_call x2 -> x1, Pallas kernels: 16.6 us -> 10.8 us  [accumulate(): pl.pallas_call(functools.partial(add_kernel, offsets, count), in_specs=[s...]
    pallas_call x3 -> x1, Pallas kernels: 8.78 us -> 4.42 us  [norm_rows(): pl.pallas_call(functools.partial(norm_kernel, starts.shape[0]), grid=(row...]
  transfers between devices with their start and end apart: 27 -> 26, of which waited for: 9 -> 8; matrix products, arithmetic and copies ran while one was open for 3% -> 3% of each run, Pallas kernels for 27% -> 27%
where the time goes in v5:
time: 271 us; the launch traced here: 270 us
  waiting for transfers between devices  119 us (44%)
  Pallas kernels  73.8 us (27%)
  starting transfers between devices  47.3 us (17%)
  between operations  15.1 us (6%)
  local copies, waits for them, and re-layouts  11.3 us (4%)
  other arithmetic  3.38 us (1%)
    ppermute x6, waiting for transfers between devices, hop(): lax.ppermute(blocks_by[way * (step - 1)], 'seq', step_pairs(devices, step...  110 us
    pallas_call x2, Pallas kernels, project(): pl.pallas_call(functools.partial(project_kernel, plan, len(blocks)), grid...  24.8 us
    pallas_call x2, Pallas kernels, attend(): pl.pallas_call(functools.partial(attend_kernel, plan, len(blocks), counts...  23.5 us
    ppermute x8, starting transfers between devices, turned(): lax.ppermute(value, axis, [(i, (i + turn) % count) for i in range(count)])  13.1 us
    ppermute x6, starting transfers between devices, hop(): lax.ppermute(blocks_by[way * (step - 1)], 'seq', step_pairs(devices, step...  12.6 us
    pallas_call x1, Pallas kernels, accumulate(): pl.pallas_call(functools.partial(add_kernel, offsets, count), in_specs=[s...  10.8 us
    pallas_call x1, Pallas kernels, accumulate(): pl.pallas_call(functools.partial(finish_kernel, offsets, count), in_specs...  10.3 us
    ppermute x9, starting transfers between devices, swap(): return lax.ppermute(value, axis, [(i, i ^ bit) for i in range(count)])  9.06 us
  transfers between devices with their start and end apart: 26, of which 8 were waited for; matrix products, arithmetic and copies ran while one was open for 3% of the time, Pallas kernels for 27%

profile of v5, /device:TPU:1, one launch (start us, length us, event | category | flops | bytes accessed | tf_op | source)
XLA Modules:
  0.0 270.0 jit_solution(15220758639248620025)
XLA Ops:
  7.3 2.7 collective-permute-start.1
  11.5 4.4 %norm_in.1.refs_4_ = bf16[256,3072]{1,0:T(8,128)(2,1)} custom-call(s32[4]{0:T(128)} %pad_add_fusion.1.starts_ref, bf16[256,3072]{1,0:T(8,128)(2,1)} %bitcast.33, f32[5,3072]{1,0:T(8,128)} %refs_12_.1), custom_call_target="tpu_custom_call" | custom-call | tf_op jit(solution)/shard_map/norm_in/pallas_call | solution.py:78
  15.9 1.3 collective-permute-start.2
  17.2 5.1 %collective-permute-start.3 = (bf16[256,3072]{1,0:T(8,128)(2,1)}, bf16[256,3072]{1,0:T(8,128)(2,1)}, u32[]{:S(2)}, u32[]{:S(2)}) collective-permute-start(bf16[256,3072]{1,0:T(8,128)(2,1)} %norm_in.1.refs_4_), channel_id=1, source_target_pairs={{0,1},{1,2},{2,3},{4,5},{5,6},{6,7},{8,9},{9,10},{10,11},{12,13},{... | collective-permute-start | bytes 4718600 | tf_op jit(solution)/shard_map/ppermute | solution.py:391
  22.4 69.3 %collective-permute-done.2.refs_5_ = bf16[256,3072]{1,0:T(8,128)(2,1)} collective-permute-done((bf16[256,3072]{1,0:T(8,128)(2,1)}, bf16[256,3072]{1,0:T(8,128)(2,1)}, u32[]{:S(2)}, u32[]{:S(2)}) %collective-permute-start.2) | collective-permute-done | bytes 1572896 | tf_op jit(solution)/shard_map/ppermute | solution.py:391
  93.0 1.3 collective-permute-start.5
  94.3 1.8 collective-permute-start.6
  96.1 1.2 collective-permute-start.9
  99.2 14.0 %project.2 = (bf16[6,512,128]{2,1,0:T(8,128)(2,1)}, bf16[6,512,128]{2,1,0:T(8,128)(2,1)}, bf16[6,512,128]{2,1,0:T(8,128)(2,1)}) custom-call(s32[1]{0:T(128)} %bitcast.12.place_ref, bf16[768,2304]{1,0:T(8,128)(2,1)} %refs_0_.3, bf16[768,2304]{1,0:T(8,128)(2,1)} %collective-permute-done.refs_1_, bf16[768,2304]{1,0:T(8,128)(2,1)} %collective-permute-done.1.refs_2_, ...), custom_call_target="tpu_custom_call" | custom-call | tf_op jit(solution)/shard_map/project/pallas_call | solution.py:152
  113.2 18.7 %collective-permute-done.5.refs_4_.refs_11_ = bf16[256,3072]{1,0:T(8,128)(2,1)} collective-permute-done((bf16[256,3072]{1,0:T(8,128)(2,1)}, bf16[256,3072]{1,0:T(8,128)(2,1)}, u32[]{:S(2)}, u32[]{:S(2)}) %collective-permute-start.5) | collective-permute-done | bytes 1572896 | tf_op jit(solution)/shard_map/ppermute | solution.py:391
  132.4 1.3 collective-permute-start.7
  133.7 1.8 collective-permute-start.8
  135.5 10.8 %project.3 = (bf16[6,256,128]{2,1,0:T(8,128)(2,1)}, bf16[6,256,128]{2,1,0:T(8,128)(2,1)}, bf16[6,256,128]{2,1,0:T(8,128)(2,1)}) custom-call(s32[1]{0:T(128)} %bitcast.12.place_ref, bf16[768,2304]{1,0:T(8,128)(2,1)} %refs_0_.3, bf16[768,2304]{1,0:T(8,128)(2,1)} %collective-permute-done.refs_1_, bf16[768,2304]{1,0:T(8,128)(2,1)} %collective-permute-done.1.refs_2_, ...), custom_call_target="tpu_custom_call" | custom-call | tf_op jit(solution)/shard_map/project/pallas_call | solution.py:152
  146.4 2.9 %collective-permute-done.9.refs_6_.refs_4_ = bf16[3072,384]{1,0:T(8,128)(2,1)S(1)} collective-permute-done((bf16[3072,384]{1,0:T(8,128)(2,1)}, bf16[3072,384]{1,0:T(8,128)(2,1)S(1)}, u32[]{:S(2)}, u32[]{:S(2)}) %collective-permute-start.9) | collective-permute-done | bytes 2359328 | tf_op jit(solution)/shard_map/ppermute | solution.py:33
  150.2 22.5 %collective-permute-done.7.refs_10_ = bf16[256,3072]{1,0:T(8,128)(2,1)} collective-permute-done((bf16[256,3072]{1,0:T(8,128)(2,1)}, bf16[256,3072]{1,0:T(8,128)(2,1)}, u32[]{:S(2)}, u32[]{:S(2)}) %collective-permute-start.7) | collective-permute-done | bytes 1572896 | tf_op jit(solution)/shard_map/ppermute | solution.py:391
  173.3 2.4 slice.12
  176.8 1.4 collective-permute-start.14
  178.3 1.2 collective-permute-start.15
  179.5 1.2 dynamic-slice_bitcast_fusion.slots_ref
  180.7 11.7 %attend.2 = (bf16[256,384]{1,0:T(8,128)(2,1)}, bf16[256,384]{1,0:T(8,128)(2,1)}, bf16[256,384]{1,0:T(8,128)(2,1)}, bf16[256,384]{1,0:T(8,128)(2,1)}) custom-call(s32[1]{0:T(128)} %bitcast.12.place_ref, s32[4]{0:T(128)} %dynamic-slice_bitcast_fusion.slots_ref, bf16[768,2304]{1,0:T(8,128)(2,1)} %refs_0_.3, bf16[768,2304]{1,0:T(8,128)(2,1)} %collective-permute-done.refs_1_, ...), custom_call_target="tpu_custom_call" | custom-call | tf_op jit(solution)/shard_map/attend/pallas_call | solution.py:212
  192.4 3.7 %collective-permute-start.16 = (bf16[256,384]{1,0:T(8,128)(2,1)}, bf16[256,384]{1,0:T(8,128)(2,1)S(1)}, u32[]{:S(2)}, u32[]{:S(2)}) collective-permute-start(bf16[256,384]{1,0:T(8,128)(2,1)} %get-tuple-element.113), channel_id=1, source_target_pairs={{0,2},{1,3},{2,0},{3,1},{4,6},{5,7},{6,4},{7,5},{8,10},{9,11},{10,... | collective-permute-start | bytes 589832 | tf_op jit(solution)/shard_map/ppermute | solution.py:33
  196.1 2.2 collective-permute-start.17
  199.4 11.7 %attend.3 = (bf16[256,384]{1,0:T(8,128)(2,1)}, bf16[256,384]{1,0:T(8,128)(2,1)}, bf16[256,384]{1,0:T(8,128)(2,1)}, bf16[256,384]{1,0:T(8,128)(2,1)}) custom-call(s32[1]{0:T(128)} %bitcast.12.place_ref, s32[4]{0:T(128)} %dynamic-slice_bitcast_fusion.slots_ref, bf16[768,2304]{1,0:T(8,128)(2,1)} %refs_0_.3, bf16[768,2304]{1,0:T(8,128)(2,1)} %collective-permute-done.refs_1_, ...), custom_call_target="tpu_custom_call" | custom-call | tf_op jit(solution)/shard_map/attend/pallas_call | solution.py:212
  212.0 1.4 constant_dynamic-update-slice_fusion.1
  213.4 1.5 constant_dynamic-update-slice_fusion.refs_10_.refs_8_
  214.9 2.0 collective-permute-start.22
  217.4 6.0 %collective-permute-start.24 = (bf16[1,256]{1,0:T(2,128)(2,1)S(1)}, bf16[1,256]{1,0:T(2,128)(2,1)S(1)}, u32[]{:S(2)}, u32[]{:S(2)}) collective-permute-start(bf16[1,256]{1,0:T(2,128)(2,1)S(1)} %get-tuple-element.136), channel_id=1, source_target_pairs={{2,4},{3,5},{6,8},{7,9},{10,12},{11,13},{4,2},{5,3},{8,6},{9,7},{1... | collective-permute-start | bytes 1544 | tf_op jit(solution)/shard_map/ppermute | solution.py:376
  225.4 2.9 %collective-permute-start.21 = (bf16[256,384]{1,0:T(8,128)(2,1)}, bf16[256,384]{1,0:T(8,128)(2,1)}, u32[]{:S(2)}, u32[]{:S(2)}) collective-permute-start(bf16[256,384]{1,0:T(8,128)(2,1)} %get-tuple-element.118), channel_id=1, source_target_pairs={{0,3},{1,0},{2,1},{3,2},{4,7},{5,4},{6,5},{7,6},{8,11},{9,8},{10,9... | collective-permute-start | bytes 589832 | tf_op jit(solution)/shard_map/ppermute | solution.py:33
  229.6 10.8 %add_parts.1.refs_11_ = f32[256,3072]{1,0:T(8,128)} custom-call(s32[8]{0:T(128)} %stack.74.starts_ref, s32[4]{0:T(128)} %pad_add_fusion.rows_ref, bf16[256,384]{1,0:T(8,128)(2,1)} %get-tuple-element.127.refs_0_, bf16[256,384]{1,0:T(8,128)(2,1)} %get-tuple-element.128.refs_1_, bf16[256,384]{1,0:T(8,128)(2,1)} %copy-done.3, bf16[256,384]{1,0:T(8,128)(2,1)} %copy-done.4, ...), custom_call_target="tpu_custom_call" | custom-call | tf_op jit(solution)/shard_map/add_parts/pallas_call | solution.py:329
  241.2 10.3 %finish.1 = (f32[128,256]{1,0:T(8,128)}, bf16[128,256]{1,0:T(8,128)(2,1)}) custom-call(s32[8]{0:T(128)} %stack.74.starts_ref, s32[4]{0:T(128)} %pad_add_fusion.rows_ref, f32[2]{0:T(128)} %pad_maximum_fusion.coef_ref, bf16[256,384]{1,0:T(8,128)(2,1)} %copy-done.6, bf16[256,384]{1,0:T(8,128)(2,1)} %copy-done.7, ...), custom_call_target="tpu_custom_call" | custom-call | tf_op jit(solution)/shard_map/finish/pallas_call | solution.py:341
  251.5 6.5 %collective-permute-start.23 = (bf16[128,256]{1,0:T(8,128)(2,1)}, bf16[128,256]{1,0:T(8,128)(2,1)S(1)}, u32[]{:S(2)}, u32[]{:S(2)}) collective-permute-start(bf16[128,256]{1,0:T(8,128)(2,1)} %get-tuple-element.133), channel_id=1, source_target_pairs={{2,4},{3,5},{6,8},{7,9},{10,12},{11,13},{4,2},{5,3},{8,6},{9,7},{1... | collective-permute-start | bytes 196616 | tf_op jit(solution)/shard_map/ppermute | solution.py:526
  258.1 3.5 %collective-permute-done.23 = bf16[128,256]{1,0:T(8,128)(2,1)S(1)} collective-permute-done((bf16[128,256]{1,0:T(8,128)(2,1)}, bf16[128,256]{1,0:T(8,128)(2,1)S(1)}, u32[]{:S(2)}, u32[]{:S(2)}) %collective-permute-start.23) | collective-permute-done | bytes 65568 | tf_op jit(solution)/shard_map/ppermute | solution.py:526
  (60 shorter events, 15.3 us)
Async XLA Ops:
  7.2 2.9 %copy-start = (bf16[768,768]{1,0:T(8,128)(2,1)S(1)}, bf16[768,768]{1,0:T(8,128)(2,1)}, u32[]{:S(2)}) copy-start(bf16[768,768]{1,0:T(8,128)(2,1)} %param.12) | copy-start | bytes 3538948
  7.2 84.7 %all-gather.2.cloned.1.call-start = ((), (), s32[]{:S(2)}) async-start(), calls=%async_computation | async-start | bytes 2949120 | tf_op jit(solution)/shard_map/all_gather | solution.py:403
  7.2 84.5 %collective-permute-start = (bf16[768,2304]{1,0:T(8,128)(2,1)}, bf16[768,2304]{1,0:T(8,128)(2,1)}, u32[]{:S(2)}, u32[]{:S(2)}) collective-permute-start(bf16[768,2304]{1,0:T(8,128)(2,1)} %refs_0_.3), channel_id=1, source_target_pairs={{0,4},{4,0},{8,12},{12,8},{1,5},{5,1},{9,13},{13,9},{2,6},{6,2},{1... | collective-permute-start | bytes 10616840 | tf_op jit(solution)/shard_map/ppermute | solution.py:18
  7.3 84.4 %collective-permute-start.1 = (bf16[768,2304]{1,0:T(8,128)(2,1)}, bf16[768,2304]{1,0:T(8,128)(2,1)}, u32[]{:S(2)}, u32[]{:S(2)}) collective-permute-start(bf16[768,2304]{1,0:T(8,128)(2,1)} %refs_0_.3), channel_id=1, source_target_pairs={{0,8},{4,12},{8,0},{12,4},{1,9},{5,13},{9,1},{13,5},{2,10},{6,14},... | collective-permute-start | bytes 10616840 | tf_op jit(solution)/shard_map/ppermute | solution.py:18
  15.9 75.8 %collective-permute-start.2 = (bf16[256,3072]{1,0:T(8,128)(2,1)}, bf16[256,3072]{1,0:T(8,128)(2,1)}, u32[]{:S(2)}, u32[]{:S(2)}) collective-permute-start(bf16[256,3072]{1,0:T(8,128)(2,1)} %norm_in.1.refs_4_), channel_id=1, source_target_pairs={{1,0},{2,1},{3,2},{5,4},{6,5},{7,6},{9,8},{10,9},{11,10},{13,12},{... | collective-permute-start | bytes 4718600 | tf_op jit(solution)/shard_map/ppermute | solution.py:391
  17.2 74.5 %collective-permute-start.3 = (bf16[256,3072]{1,0:T(8,128)(2,1)}, bf16[256,3072]{1,0:T(8,128)(2,1)}, u32[]{:S(2)}, u32[]{:S(2)}) collective-permute-start(bf16[256,3072]{1,0:T(8,128)(2,1)} %norm_in.1.refs_4_), channel_id=1, source_target_pairs={{0,1},{1,2},{2,3},{4,5},{5,6},{6,7},{8,9},{9,10},{10,11},{12,13},{... | collective-permute-start | bytes 4718600 | tf_op jit(solution)/shard_map/ppermute | solution.py:391
  91.9 7.2 %collective-permute-start.4 = (bf16[768,2304]{1,0:T(8,128)(2,1)}, bf16[768,2304]{1,0:T(8,128)(2,1)}, u32[]{:S(2)}, u32[]{:S(2)}) collective-permute-start(bf16[768,2304]{1,0:T(8,128)(2,1)} %collective-permute-done.1.refs_2_), channel_id=1, source_target_pairs={{0,4},{4,0},{8,12},{12,8},{1,5},{5,1},{9,13},{13,9},{2,6},{6,2},{1... | collective-permute-start | bytes 10616840 | tf_op jit(solution)/shard_map/ppermute | solution.py:18
  93.0 38.9 %collective-permute-start.5 = (bf16[256,3072]{1,0:T(8,128)(2,1)}, bf16[256,3072]{1,0:T(8,128)(2,1)}, u32[]{:S(2)}, u32[]{:S(2)}) collective-permute-start(bf16[256,3072]{1,0:T(8,128)(2,1)} %collective-permute-done.2.refs_5_), channel_id=1, source_target_pairs={{1,0},{2,1},{5,4},{6,5},{9,8},{10,9},{13,12},{14,13},{17,16},{18,1... | collective-permute-start | bytes 4718600 | tf_op jit(solution)/shard_map/ppermute | solution.py:391
  94.3 37.6 %collective-permute-start.6 = (bf16[256,3072]{1,0:T(8,128)(2,1)}, bf16[256,3072]{1,0:T(8,128)(2,1)}, u32[]{:S(2)}, u32[]{:S(2)}) collective-permute-start(bf16[256,3072]{1,0:T(8,128)(2,1)} %collective-permute-done.3.refs_6_), channel_id=1, source_target_pairs={{1,2},{2,3},{5,6},{6,7},{9,10},{10,11},{13,14},{14,15},{17,18},{18... | collective-permute-start | bytes 4718600 | tf_op jit(solution)/shard_map/ppermute | solution.py:391
  96.1 53.2 %collective-permute-start.9 = (bf16[3072,384]{1,0:T(8,128)(2,1)}, bf16[3072,384]{1,0:T(8,128)(2,1)S(1)}, u32[]{:S(2)}, u32[]{:S(2)}) collective-permute-start(bf16[3072,384]{1,0:T(8,128)(2,1)} %all-gather.2.cloned.1.call-done.refs_5_.refs_3_), channel_id=1, source_target_pairs={{0,16},{16,0},{1,17},{17,1},{2,18},{18,2},{3,19},{19,3},{4,20},{20... | collective-permute-start | bytes 7077896 | tf_op jit(solution)/shard_map/ppermute | solution.py:33
  97.3 52.8 %collective-permute-start.11 = (bf16[3072,384]{1,0:T(8,128)(2,1)}, bf16[3072,384]{1,0:T(8,128)(2,1)}, u32[]{:S(2)}, u32[]{:S(2)}) collective-permute-start(bf16[3072,384]{1,0:T(8,128)(2,1)} %all-gather.2.cloned.1.call-done.refs_5_.refs_3_), channel_id=1, source_target_pairs={{0,8},{4,12},{8,0},{12,4},{1,9},{5,13},{9,1},{13,5},{2,10},{6,14},... | collective-permute-start | bytes 7077896 | tf_op jit(solution)/shard_map/ppermute | solution.py:18
  131.9 40.8 %collective-permute-start.10 = (bf16[3072,384]{1,0:T(8,128)(2,1)}, bf16[3072,384]{1,0:T(8,128)(2,1)}, u32[]{:S(2)}, u32[]{:S(2)}) collective-permute-start(bf16[3072,384]{1,0:T(8,128)(2,1)} %all-gather.2.cloned.1.call-done.refs_5_.refs_3_), channel_id=1, source_target_pairs={{0,4},{4,0},{8,12},{12,8},{1,5},{5,1},{9,13},{13,9},{2,6},{6,2},{1... | collective-permute-start | bytes 7077896 | tf_op jit(solution)/shard_map/ppermute | solution.py:18
  132.4 40.2 %collective-permute-start.7 = (bf16[256,3072]{1,0:T(8,128)(2,1)}, bf16[256,3072]{1,0:T(8,128)(2,1)}, u32[]{:S(2)}, u32[]{:S(2)}) collective-permute-start(bf16[256,3072]{1,0:T(8,128)(2,1)} %collective-permute-done.5.refs_4_.refs_11_), channel_id=1, source_target_pairs={{1,0},{5,4},{9,8},{13,12},{17,16},{21,20},{25,24},{29,28}} | collective-permute-start | bytes 4718600 | tf_op jit(solution)/shard_map/ppermute | solution.py:391
  133.7 38.9 %collective-permute-start.8 = (bf16[256,3072]{1,0:T(8,128)(2,1)}, bf16[256,3072]{1,0:T(8,128)(2,1)}, u32[]{:S(2)}, u32[]{:S(2)}) collective-permute-start(bf16[256,3072]{1,0:T(8,128)(2,1)} %collective-permute-done.6.refs_6_.refs_12_), channel_id=1, source_target_pairs={{2,3},{6,7},{10,11},{14,15},{18,19},{22,23},{26,27},{30,31}} | collective-permute-start | bytes 4718600 | tf_op jit(solution)/shard_map/ppermute | solution.py:391
  149.3 27.6 %copy-start.1 = (bf16[3072,384]{1,0:T(8,128)(2,1)}, bf16[3072,384]{1,0:T(8,128)(2,1)S(1)}, u32[]{:S(2)}) copy-start(bf16[3072,384]{1,0:T(8,128)(2,1)S(1)} %collective-permute-done.9.refs_6_.refs_4_) | copy-start | bytes 7077892
  172.6 19.8 %collective-permute-start.12 = (bf16[3072,384]{1,0:T(8,128)(2,1)S(1)}, bf16[3072,384]{1,0:T(8,128)(2,1)}, u32[]{:S(2)}, u32[]{:S(2)}) collective-permute-start(bf16[3072,384]{1,0:T(8,128)(2,1)S(1)} %collective-permute-done.9.refs_6_.refs_4_), channel_id=1, source_target_pairs={{0,4},{4,0},{8,12},{12,8},{1,5},{5,1},{9,13},{13,9},{2,6},{6,2},{1... | collective-permute-start | bytes 7077896 | tf_op jit(solution)/shard_map/ppermute | solution.py:18
  173.2 19.2 %collective-permute-start.13 = (bf16[3072,384]{1,0:T(8,128)(2,1)}, bf16[3072,384]{1,0:T(8,128)(2,1)}, u32[]{:S(2)}, u32[]{:S(2)}) collective-permute-start(bf16[3072,384]{1,0:T(8,128)(2,1)} %collective-permute-done.11.refs_9_.refs_7_), channel_id=1, source_target_pairs={{0,4},{4,0},{8,12},{12,8},{1,5},{5,1},{9,13},{13,9},{2,6},{6,2},{1... | collective-permute-start | bytes 7077896 | tf_op jit(solution)/shard_map/ppermute | solution.py:18
  176.8 34.3 %collective-permute-start.14 = (bf16[1536,384]{1,0:T(8,128)(2,1)}, bf16[1536,384]{1,0:T(8,128)(2,1)}, u32[]{:S(2)}, u32[]{:S(2)}) collective-permute-start(bf16[1536,384]{1,0:T(8,128)(2,1)} %slice.12), channel_id=1, source_target_pairs={{0,16},{16,0},{1,17},{17,1},{2,18},{18,2},{3,19},{19,3},{4,20},{20... | collective-permute-start | bytes 3538952 | tf_op jit(solution)/shard_map/ppermute | solution.py:33
  178.3 32.9 %collective-permute-start.15 = (bf16[1536,384]{1,0:T(8,128)(2,1)}, bf16[1536,384]{1,0:T(8,128)(2,1)}, u32[]{:S(2)}, u32[]{:S(2)}) collective-permute-start(bf16[1536,384]{1,0:T(8,128)(2,1)} %slice.13), channel_id=1, source_target_pairs={{0,8},{4,12},{8,0},{12,4},{1,9},{5,13},{9,1},{13,5},{2,10},{6,14},... | collective-permute-start | bytes 3538952 | tf_op jit(solution)/shard_map/ppermute | solution.py:18
  192.4 18.8 %collective-permute-start.16 = (bf16[256,384]{1,0:T(8,128)(2,1)}, bf16[256,384]{1,0:T(8,128)(2,1)S(1)}, u32[]{:S(2)}, u32[]{:S(2)}) collective-permute-start(bf16[256,384]{1,0:T(8,128)(2,1)} %get-tuple-element.113), channel_id=1, source_target_pairs={{0,2},{1,3},{2,0},{3,1},{4,6},{5,7},{6,4},{7,5},{8,10},{9,11},{10,... | collective-permute-start | bytes 589832 | tf_op jit(solution)/shard_map/ppermute | solution.py:33
  196.1 15.1 %collective-permute-start.17 = (bf16[256,384]{1,0:T(8,128)(2,1)}, bf16[256,384]{1,0:T(8,128)(2,1)S(1)}, u32[]{:S(2)}, u32[]{:S(2)}) collective-permute-start(bf16[256,384]{1,0:T(8,128)(2,1)} %get-tuple-element.114), channel_id=1, source_target_pairs={{0,1},{1,2},{2,3},{3,0},{4,5},{5,6},{6,7},{7,4},{8,9},{9,10},{10,1... | collective-permute-start | bytes 589832 | tf_op jit(solution)/shard_map/ppermute | solution.py:33
  198.3 12.9 %collective-permute-start.18 = (bf16[256,384]{1,0:T(8,128)(2,1)}, bf16[256,384]{1,0:T(8,128)(2,1)S(1)}, u32[]{:S(2)}, u32[]{:S(2)}) collective-permute-start(bf16[256,384]{1,0:T(8,128)(2,1)} %get-tuple-element.115), channel_id=1, source_target_pairs={{0,3},{1,0},{2,1},{3,2},{4,7},{5,4},{6,5},{7,6},{8,11},{9,8},{10,9... | collective-permute-start | bytes 589832 | tf_op jit(solution)/shard_map/ppermute | solution.py:33
  211.2 3.7 %copy-start.3 = (bf16[256,384]{1,0:T(8,128)(2,1)}, bf16[256,384]{1,0:T(8,128)(2,1)S(1)}, u32[]{:S(2)}) copy-start(bf16[256,384]{1,0:T(8,128)(2,1)S(1)} %collective-permute-done.16.refs_2_) | copy-start | bytes 589828
  211.2 3.7 %copy-start.4 = (bf16[256,384]{1,0:T(8,128)(2,1)}, bf16[256,384]{1,0:T(8,128)(2,1)S(1)}, u32[]{:S(2)}) copy-start(bf16[256,384]{1,0:T(8,128)(2,1)S(1)} %collective-permute-done.17.refs_3_) | copy-start | bytes 589828
  212.0 4.9 %copy-start.8 = (s32[1,256]{1,0:T(1,128)S(1)}, s32[1,256]{1,0:T(1,128)}, u32[]{:S(2)}) copy-start(s32[1,256]{1,0:T(1,128)} %param.15) | copy-start | bytes 3076
  214.9 14.8 %copy-start.2 = (bf16[3072,384]{1,0:T(8,128)(2,1)}, bf16[3072,384]{1,0:T(8,128)(2,1)S(1)}, u32[]{:S(2)}) copy-start(bf16[3072,384]{1,0:T(8,128)(2,1)S(1)} %constant_dynamic-update-slice_fusion.refs_10_.refs_8_) | copy-start | bytes 7077892
  214.9 14.7 %collective-permute-start.22 = (bf16[3072,384]{1,0:T(8,128)(2,1)S(1)}, bf16[3072,384]{1,0:T(8,128)(2,1)}, u32[]{:S(2)}, u32[]{:S(2)}) collective-permute-start(bf16[3072,384]{1,0:T(8,128)(2,1)S(1)} %constant_dynamic-update-slice_fusion.refs_10_.refs_8_), channel_id=1, source_target_pairs={{0,4},{4,0},{8,12},{12,8},{1,5},{5,1},{9,13},{13,9},{2,6},{6,2},{1... | collective-permute-start | bytes 7077896 | tf_op jit(solution)/shard_map/ppermute | solution.py:18
  217.4 40.6 %collective-permute-start.24 = (bf16[1,256]{1,0:T(2,128)(2,1)S(1)}, bf16[1,256]{1,0:T(2,128)(2,1)S(1)}, u32[]{:S(2)}, u32[]{:S(2)}) collective-permute-start(bf16[1,256]{1,0:T(2,128)(2,1)S(1)} %get-tuple-element.136), channel_id=1, source_target_pairs={{2,4},{3,5},{6,8},{7,9},{10,12},{11,13},{4,2},{5,3},{8,6},{9,7},{1... | collective-permute-start | bytes 1544 | tf_op jit(solution)/shard_map/ppermute | solution.py:376
  224.9 15.6 %collective-permute-start.19 = (bf16[256,384]{1,0:T(8,128)(2,1)}, bf16[256,384]{1,0:T(8,128)(2,1)S(1)}, u32[]{:S(2)}, u32[]{:S(2)}) collective-permute-start(bf16[256,384]{1,0:T(8,128)(2,1)} %get-tuple-element.116), channel_id=1, source_target_pairs={{0,2},{1,3},{2,0},{3,1},{4,6},{5,7},{6,4},{7,5},{8,10},{9,11},{10,... | collective-permute-start | bytes 589832 | tf_op jit(solution)/shard_map/ppermute | solution.py:33
  225.1 15.4 %collective-permute-start.20 = (bf16[256,384]{1,0:T(8,128)(2,1)}, bf16[256,384]{1,0:T(8,128)(2,1)S(1)}, u32[]{:S(2)}, u32[]{:S(2)}) collective-permute-start(bf16[256,384]{1,0:T(8,128)(2,1)} %get-tuple-element.117), channel_id=1, source_target_pairs={{0,1},{1,2},{2,3},{3,0},{4,5},{5,6},{6,7},{7,4},{8,9},{9,10},{10,1... | collective-permute-start | bytes 589832 | tf_op jit(solution)/shard_map/ppermute | solution.py:33
  225.4 15.1 %collective-permute-start.21 = (bf16[256,384]{1,0:T(8,128)(2,1)}, bf16[256,384]{1,0:T(8,128)(2,1)}, u32[]{:S(2)}, u32[]{:S(2)}) collective-permute-start(bf16[256,384]{1,0:T(8,128)(2,1)} %get-tuple-element.118), channel_id=1, source_target_pairs={{0,3},{1,0},{2,1},{3,2},{4,7},{5,4},{6,5},{7,6},{8,11},{9,8},{10,9... | collective-permute-start | bytes 589832 | tf_op jit(solution)/shard_map/ppermute | solution.py:33
  251.5 10.1 %collective-permute-start.23 = (bf16[128,256]{1,0:T(8,128)(2,1)}, bf16[128,256]{1,0:T(8,128)(2,1)S(1)}, u32[]{:S(2)}, u32[]{:S(2)}) collective-permute-start(bf16[128,256]{1,0:T(8,128)(2,1)} %get-tuple-element.133), channel_id=1, source_target_pairs={{2,4},{3,5},{6,8},{7,9},{10,12},{11,13},{4,2},{5,3},{8,6},{9,7},{1... | collective-permute-start | bytes 196616 | tf_op jit(solution)/shard_map/ppermute | solution.py:526
  (3 other events, 2.2 us)
Sparse Core Ops, SparseCore 0:
  11.0 80.8 all-gather.1

commit v6 on v5

--- a/solution.py
+++ b/solution.py
@@ -161,7 +161,7 @@
             pltpu.VMEM((length, width), jnp.bfloat16),
             pltpu.SemaphoreType.DMA((len(plan),)),
         ],
-        compiler_params=pltpu.CompilerParams(vmem_limit_bytes=60 * MIB),
+        compiler_params=pltpu.CompilerParams(vmem_limit_bytes=28 * MIB),
         name="project",
     )(place, *blocks, *sources)
 
@@ -229,7 +229,7 @@
             pltpu.VMEM((rows, width), jnp.bfloat16),
             pltpu.SemaphoreType.DMA((1,)),
         ],
-        compiler_params=pltpu.CompilerParams(vmem_limit_bytes=60 * MIB),
+        compiler_params=pltpu.CompilerParams(vmem_limit_bytes=28 * MIB),
         name="attend",
     )(place, slots, *blocks, *(value for three in known for value in three), *sources)
 
@@ -238,19 +238,25 @@
     depth = [part.shape[1] for part in parts]
     width = weights.shape[2]
     copies = []
-    for p, source in enumerate(sources):
+    for p, split in enumerate(sources):
         copies.append([])
         for n, (turn, offset) in enumerate(offsets):
-            to = sum(depth[:n])
-            row = pl.multiple_of(rows_ref[turn] + offset, HD)
-            copies[p].append(
-                pltpu.make_async_copy(
-                    source.at[pl.ds(row, depth[n])],
-                    weights.at[p, pl.ds(to, depth[n])],
-                    sems.at[p, n],
-                )
-            )
-            copies[p][n].start()
+            to = weights.at[p, pl.ds(sum(depth[:n]), depth[n])]
+            row = rows_ref[turn] + offset
+            size = split[0].shape[0]
+            for i, source in enumerate(split):
+                if len(split) == 1:
+                    rows = source.at[pl.ds(pl.multiple_of(row, HD), depth[n])]
+                    pltpu.make_async_copy(rows, to, sems.at[p, n]).start()
+                    continue
+
+                @pl.when(jnp.logical_and(row >= i * size, row < (i + 1) * size))
+                def _():
+                    rows = source.at[pl.ds(pl.multiple_of(row - i * size, HD), depth[n])]
+                    pltpu.make_async_copy(rows, to, sems.at[p, n]).start()
+
+            rows = split[0].at[pl.ds(0, depth[n])]
+            copies[p].append(pltpu.make_async_copy(rows, to, sems.at[p, n]))
     for n, part in enumerate(parts):
         wide[:, sum(depth[:n]) : sum(depth[: n + 1])] = part[...]
     for p in range(len(sources)):
@@ -260,10 +266,18 @@
         store(p, cols, jnp.dot(wide[...], weights[p], preferred_element_type=jnp.float32))
 
 
-def add_kernel(offsets, count, starts_ref, rows_ref, *refs):
+def split_refs(refs, splits):
+    grouped = []
+    for split in splits:
+        grouped.append(refs[:split])
+        refs = refs[split:]
+    return grouped, refs
+
+
+def add_kernel(offsets, splits, starts_ref, rows_ref, *refs):
     parts = refs[: len(offsets)]
-    sources = refs[len(offsets) : len(offsets) + count]
-    before_ref, mod_ref, out_ref, weights, wide, sems = refs[len(offsets) + count :]
+    sources, refs = split_refs(refs[len(offsets) :], splits)
+    before_ref, mod_ref, out_ref, weights, wide, sems = refs
 
     def store(p, cols, summed):
         out_ref[:, cols] = before_ref[:, cols].astype(jnp.float32) + mod_ref[2:3, cols] * summed
@@ -271,13 +285,12 @@
     multiply(parts, offsets, starts_ref, rows_ref, sources, weights, sems, wide, store)
 
 
-def finish_kernel(offsets, count, starts_ref, rows_ref, coef_ref, *refs):
+def finish_kernel(offsets, splits, starts_ref, rows_ref, coef_ref, *refs):
     parts = refs[: len(offsets)]
-    sources = refs[len(offsets) : len(offsets) + count]
-    before_ref, mod_ref, head_ref, latent_ref, weight_ref, out_ref, sent_ref = refs[
-        len(offsets) + count : len(offsets) + count + 7
-    ]
-    weights, wide, sems, mixed, extra = refs[len(offsets) + count + 7 :]
+    sources, refs = split_refs(refs[len(offsets) :], splits)
+    before_ref, mod_ref, head_ref, latent_ref, weight_ref, out_ref, sent_ref = refs[:7]
+    weights, wide, sems, mixed, extra = refs[7:]
+    count = len(splits)
     width = weights.shape[2]
     copies = []
     for p in range(count):
@@ -313,6 +326,8 @@
     rows, width = before.shape
     depth = sum(part.shape[1] for part in parts)
     count = len(pieces)
+    splits = [len(piece) for piece in pieces]
+    pieces = [array for piece in pieces for array in piece]
     smem = pl.BlockSpec(memory_space=pltpu.SMEM)
     vmem = pl.BlockSpec(memory_space=pltpu.VMEM)
     hbm = pl.BlockSpec(memory_space=pl.ANY)
@@ -322,25 +337,25 @@
         pltpu.SemaphoreType.DMA((count, len(parts))),
     ]
     params = dict(
-        compiler_params=pltpu.CompilerParams(vmem_limit_bytes=60 * MIB),
+        compiler_params=pltpu.CompilerParams(vmem_limit_bytes=36 * MIB),
     )
     if last is None:
         aliased = before.dtype == jnp.float32
         return pl.pallas_call(
-            functools.partial(add_kernel, offsets, count),
-            in_specs=[smem] * 2 + [vmem] * len(parts) + [hbm] * count + [vmem] * 2,
+            functools.partial(add_kernel, offsets, splits),
+            in_specs=[smem] * 2 + [vmem] * len(parts) + [hbm] * len(pieces) + [vmem] * 2,
             out_specs=vmem,
             out_shape=jax.ShapeDtypeStruct((rows, width), jnp.float32),
             scratch_shapes=scratch,
-            input_output_aliases={2 + len(parts) + count: 0} if aliased else {},
+            input_output_aliases={2 + len(parts) + len(pieces): 0} if aliased else {},
             name="add_parts",
             **params,
         )(starts, firsts, *parts, *pieces, before, modulation)
     coef, head, latent, weight = last
     channels = head.shape[0]
     return pl.pallas_call(
-        functools.partial(finish_kernel, offsets, count),
-        in_specs=[smem] * 3 + [vmem] * len(parts) + [hbm] * (count + 1) + [vmem] * 4,
+        functools.partial(finish_kernel, offsets, splits),
+        in_specs=[smem] * 3 + [vmem] * len(parts) + [hbm] * (len(pieces) + 1) + [vmem] * 4,
         out_specs=[vmem, vmem],
         out_shape=[
             jax.ShapeDtypeStruct((2 * channels, rows), jnp.float32),
@@ -410,7 +425,31 @@
                 {d ^ bit: swap(blocks[d], "tile", bit) for d in list(blocks) if d != near}
             )
     hop(1)
-    blocks, columns, blocks_by = lax.optimization_barrier((blocks, columns, blocks_by))
+
+    table = [
+        [([s] + [s - hop for hop in hops[s]]).index((s + turn) % devices) for turn in range(devices)]
+        for s in range(devices)
+    ]
+    slots = jnp.asarray(table, jnp.int32)[place]
+    order = [(d, g) for d in range(tiles) for g in range(groups)]
+    starts = jnp.stack(
+        [
+            (tile ^ d) * (part * groups) + lax.rem(group - g + groups, groups) * part
+            for d, g in order
+        ]
+    ).astype(jnp.int32)
+    if narrow:
+        order, starts = [(0, 0)], jnp.zeros((1,), jnp.int32)
+    features = w_out.shape[0]
+    firsts = jnp.stack(
+        [lax.rem(place - turn + devices, devices) * features for turn in range(devices)]
+    ).astype(jnp.int32)
+    index = step_index[0].astype(jnp.float32)
+    now = noise_level(index, NSTEPS)
+    coef = jnp.stack([now, noise_level(index + 1.0, NSTEPS) - now])
+    blocks, columns, blocks_by, slots, starts, firsts, coef, norms = lax.optimization_barrier(
+        (blocks, columns, blocks_by, slots, starts, firsts, coef, norms)
+    )
     if ragged:
         blocks[0] = lax.all_gather(blocks[0], "tile", axis=0, tiled=True)
     else:
@@ -440,38 +479,33 @@
     if not narrow:
         mine = lax.optimization_barrier((columns[0, 0], known[0]))[0]
         columns[near, 0] = swap(mine, "tile", near)
+    columns = {key: [value] for key, value in columns.items()}
+    for turn in range(1, groups) if not narrow else []:
+        columns.update(
+            {
+                (d, turn): [turned(columns[d, 0][0], "group", turn)]
+                for d in range(1, tiles)
+                if d & near == 0 and (groups != 2 or len(far) != 1)
+            }
+        )
+    if groups == 2 and len(far) == 1 and not narrow:
+        bit, half = far[0], columns[0, 0][0].shape[0] // 2
+        columns[bit, 1] = [
+            turned(columns[bit, 0][0][:half], "group", 1),
+            swap(columns[0, 1][0][half:], "tile", bit),
+        ]
     blocks_by, known, columns = lax.optimization_barrier((blocks_by, known, columns))
-    late = {}
-    for turn in range(1, groups) if not narrow else []:
-        late.update(
-            {
-                (d, turn): turned(columns[d, 0], "group", turn)
-                for d, g in columns
-                if d not in (0, near) and not g
-            }
-        )
-    if groups == 2 and len(far) == 1 and not narrow:
-        bit, half = far[0], columns[0, 0].shape[0] // 2
-        late[bit, 1] = [
-            turned(columns[bit, 0][:half], "group", 1),
-            swap(columns[0, 1][half:], "tile", bit),
-        ]
     if not narrow:
         columns.update(
             {
-                (d ^ near, g): swap(columns[d, g], "tile", near)
+                (d ^ near, g): [swap(array, "tile", near) for array in columns[d, g]]
                 for d, g in list(columns)
                 if (d ^ near, g) not in columns
             }
         )
-
-    table = [
-        [([s] + [s - hop for hop in hops[s]]).index((s + turn) % devices) for turn in range(devices)]
-        for s in range(devices)
-    ]
-    slots = jnp.asarray(table, jnp.int32)[place]
     heads = w_qkv.shape[1] // (3 * HD)
-    halves = [(0, (heads + 1) // 2), ((heads + 1) // 2, heads // 2)]
+    many = heads - heads // 3
+    halves = [(0, many), (many, heads - many)]
     turns = sorted(range(1, devices), key=lambda turn: -min(turn, devices - turn))
     choices, found = arrival(devices - 2)
     attended = attend(at, slots, [choices], found, known, blocks, *halves[0])
@@ -479,27 +513,10 @@
     received = [[turned(attended[turn], "seq", turn) for turn in turns]]
     own = [attended[0]]
     attended = attend(at, slots, [choices], found, known, blocks, *halves[1])
-    attended, late, received = lax.optimization_barrier((attended, late, received))
-    for key, value in late.items():
-        columns[key] = jnp.concatenate(value, axis=0) if isinstance(value, list) else value
-    columns.update({(d ^ near, g): swap(columns[d, g], "tile", near) for d, g in late})
+    attended, received = lax.optimization_barrier((attended, received))
     received.append([turned(attended[turn], "seq", turn) for turn in turns])
     own.append(attended[0])
-    order = sorted(columns)
     pieces = [columns[key] for key in order]
-    starts = jnp.stack(
-        [
-            (tile ^ d) * (part * groups) + lax.rem(group - g + groups, groups) * part
-            for d, g in order
-        ]
-    ).astype(jnp.int32)
-    if narrow:
-        starts = jnp.zeros((1,), jnp.int32)
-
-    features = w_out.shape[0]
-    firsts = jnp.stack(
-        [lax.rem(place - turn + devices, devices) * features for turn in range(devices)]
-    ).astype(jnp.int32)
     offsets = [[(turn, start * HD) for turn in turns] for start, _ in halves]
     mixed = accumulate(
         own + received[0],
@@ -510,9 +527,6 @@
         local,
         modulation,
     )
-    index = step_index[0].astype(jnp.float32)
-    now = noise_level(index, NSTEPS)
-    later = noise_level(index + 1.0, NSTEPS)
     weighted, to_join = accumulate(
         received[1],
         offsets[1],
@@ -521,7 +535,7 @@
         pieces,
         mixed,
         modulation,
-        (jnp.stack([now, later - now]), w_head.T, latent[0].T, weight),
+        (coef, w_head.T, latent[0].T, weight),
     )
     other = lax.ppermute(to_join, ("tile", "seq"), joins).astype(jnp.float32)
     joined = (weighted + other) / norms

time: 271 us -> 278 us (1.026)
  local copies, waits for them, and re-layouts: 11.3 us -> 21 us
  waiting for transfers between devices: 119 us -> 128 us
  Pallas kernels: 73.8 us -> 65.6 us
    ppermute x6, waiting for transfers between devices: 110 us -> 16.2 us  [hop(): lax.ppermute(blocks_by[way * (step - 1)], 'seq', step_pairs(devices, step...]
    ppermute x1, waiting for transfers between devices: 0.01 us -> 65.9 us  [shards(): lax.ppermute(weight.astype(jnp.bfloat16), ('tile', 'seq'), joins)]
    ppermute x8, waiting for transfers between devices: 2.92 us -> 22 us  [turned(): lax.ppermute(value, axis, [(i, (i + turn) % count) for i in range(count)])]
    ppermute x9 -> x10, waiting for transfers between devices: 1.94 us -> 18.4 us  [swap(): return lax.ppermute(value, axis, [(i, i ^ bit) for i in range(count)])]
    unnamed x19 -> x50, local copies, waits for them, and re-layouts: 2.9 us -> 16.2 us
    pallas_call x2, Pallas kernels: 24.8 us -> 17 us  [project(): pl.pallas_call(functools.partial(project_kernel, plan, len(blocks)), grid...]
    ppermute x8, starting transfers between devices: 13.1 us -> 19.7 us  [turned(): lax.ppermute(value, axis, [(i, (i + turn) % count) for i in range(count)])]
    ppermute x1, starting transfers between devices: 6.52 us -> 1.92 us  [shards(): other = lax.ppermute(to_join, ('tile', 'seq'), joins).astype(jnp.float32)]
  transfers between devices with their start and end apart: 26 -> 27, of which waited for: 8 -> 8; matrix products, arithmetic and copies ran while one was open for 3% -> 1% of each run, Pallas kernels for 27% -> 20%
where the time goes in v6:
time: 278 us; the launch traced here: 276 us
  waiting for transfers between devices  128 us (46%)
  Pallas kernels  65.6 us (24%)
  starting transfers between devices  46.2 us (17%)
  local copies, waits for them, and re-layouts  21 us (8%)
  between operations  15.1 us (5%)
    ppermute x1, waiting for transfers between devices, shards(): lax.ppermute(weight.astype(jnp.bfloat16), ('tile', 'seq'), joins)  65.9 us
    ppermute x8, waiting for transfers between devices, turned(): lax.ppermute(value, axis, [(i, (i + turn) % count) for i in range(count)])  22 us
    pallas_call x2, Pallas kernels, attend(): pl.pallas_call(functools.partial(attend_kernel, plan, len(blocks), counts...  19.9 us
    ppermute x8, starting transfers between devices, turned(): lax.ppermute(value, axis, [(i, (i + turn) % count) for i in range(count)])  19.7 us
    ppermute x10, waiting for transfers between devices, swap(): return lax.ppermute(value, axis, [(i, i ^ bit) for i in range(count)])  18.4 us
    pallas_call x2, Pallas kernels, project(): pl.pallas_call(functools.partial(project_kernel, plan, len(blocks)), grid...  17 us
    ppermute x6, waiting for transfers between devices, hop(): lax.ppermute(blocks_by[way * (step - 1)], 'seq', step_pairs(devices, step...  16.2 us
    unnamed x50, local copies, waits for them, and re-layouts  16.2 us
  transfers between devices with their start and end apart: 27, of which 8 were waited for; matrix products, arithmetic and copies ran while one was open for 1% of the time, Pallas kernels for 20%

profile of v6, /device:TPU:1, one launch (start us, length us, event | category | flops | bytes accessed | tf_op | source)
XLA Modules:
  0.0 276.3 jit_solution(16417397733905740731)
XLA Ops:
  9.4 2.7 collective-permute-start.1
  12.7 4.4 %norm_in.1.refs_4_ = bf16[256,3072]{1,0:T(8,128)(2,1)} custom-call(s32[4]{0:T(128)} %pad_add_fusion.starts_ref, bf16[256,3072]{1,0:T(8,128)(2,1)} %bitcast.33, f32[5,3072]{1,0:T(8,128)} %refs_14_.1), custom_call_target="tpu_custom_call" | custom-call | tf_op jit(solution)/shard_map/norm_in/pallas_call | solution.py:78
  17.2 4.3 %collective-permute-start.3 = (bf16[256,3072]{1,0:T(8,128)(2,1)}, bf16[256,3072]{1,0:T(8,128)(2,1)}, u32[]{:S(2)}, u32[]{:S(2)}) collective-permute-start(bf16[256,3072]{1,0:T(8,128)(2,1)} %norm_in.1.refs_4_), channel_id=1, source_target_pairs={{0,1},{1,2},{2,3},{4,5},{5,6},{6,7},{8,9},{9,10},{10,11},{12,13},{... | collective-permute-start | bytes 4718600 | tf_op jit(solution)/shard_map/ppermute | solution.py:406
  22.8 4.7 %collective-permute-start.4 = (bf16[1,256]{1,0:T(2,128)(2,1)S(1)}, bf16[1,256]{1,0:T(2,128)(2,1)S(1)}, u32[]{:S(2)}, u32[]{:S(2)}) collective-permute-start(bf16[1,256]{1,0:T(2,128)(2,1)S(1)} %get-tuple-element.155), channel_id=1, source_target_pairs={{2,4},{3,5},{6,8},{7,9},{10,12},{11,13},{4,2},{5,3},{8,6},{9,7},{1... | collective-permute-start | bytes 1544 | tf_op jit(solution)/shard_map/ppermute | solution.py:391
  29.2 65.9 %collective-permute-done.4 = bf16[1,256]{1,0:T(2,128)(2,1)S(1)} collective-permute-done((bf16[1,256]{1,0:T(2,128)(2,1)S(1)}, bf16[1,256]{1,0:T(2,128)(2,1)S(1)}, u32[]{:S(2)}, u32[]{:S(2)}) %collective-permute-start.4) | collective-permute-done | bytes 544 | tf_op jit(solution)/shard_map/ppermute | solution.py:391
  97.3 1.5 collective-permute-start.12
  100.0 1.6 collective-permute-done.5.refs_3_
  101.7 2.0 copy-done.1
  103.7 1.4 copy-done.12
  105.1 10.4 %project.2 = (bf16[6,512,128]{2,1,0:T(8,128)(2,1)S(1)}, bf16[6,512,128]{2,1,0:T(8,128)(2,1)S(1)}, bf16[6,512,128]{2,1,0:T(8,128)(2,1)S(1)}) custom-call(s32[1]{0:T(128)} %bitcast.18.place_ref, bf16[768,2304]{1,0:T(8,128)(2,1)S(1)} %copy-done.1, bf16[768,2304]{1,0:T(8,128)(2,1)} %collective-permute-done.refs_1_, ...), custom_call_target="tpu_custom_call" | custom-call | tf_op jit(solution)/shard_map/project/pallas_call | solution.py:152
  116.4 16.2 %collective-permute-done.6.refs_4_.refs_11_ = bf16[256,3072]{1,0:T(8,128)(2,1)S(1)} collective-permute-done((bf16[256,3072]{1,0:T(8,128)(2,1)S(1)}, bf16[256,3072]{1,0:T(8,128)(2,1)S(1)}, u32[]{:S(2)}, u32[]{:S(2)}) %collective-permute-start.6) | collective-permute-done | bytes 1572896 | tf_op jit(solution)/shard_map/ppermute | solution.py:406
  136.0 13.9 %collective-permute-done.12.refs_9_.refs_7_ = bf16[3072,384]{1,0:T(8,128)(2,1)S(1)} collective-permute-done((bf16[3072,384]{1,0:T(8,128)(2,1)}, bf16[3072,384]{1,0:T(8,128)(2,1)S(1)}, u32[]{:S(2)}, u32[]{:S(2)}) %collective-permute-start.12) | collective-permute-done | bytes 2359328 | tf_op jit(solution)/shard_map/ppermute | solution.py:18
  153.7 1.8 collective-permute-start.14
  155.5 6.6 %project.3 = (bf16[6,256,128]{2,1,0:T(8,128)(2,1)S(1)}, bf16[6,256,128]{2,1,0:T(8,128)(2,1)S(1)}, bf16[6,256,128]{2,1,0:T(8,128)(2,1)S(1)}) custom-call(s32[1]{0:T(128)} %bitcast.18.place_ref, bf16[768,2304]{1,0:T(8,128)(2,1)S(1)} %copy-done.1, bf16[768,2304]{1,0:T(8,128)(2,1)} %collective-permute-done.refs_1_, ...), custom_call_target="tpu_custom_call" | custom-call | tf_op jit(solution)/shard_map/project/pallas_call | solution.py:152
  162.1 15.6 %collective-permute-done.13.refs_10_.refs_8_ = bf16[1536,384]{1,0:T(8,128)(2,1)} collective-permute-done((bf16[1536,384]{1,0:T(8,128)(2,1)}, bf16[1536,384]{1,0:T(8,128)(2,1)}, u32[]{:S(2)}, u32[]{:S(2)}) %collective-permute-start.13) | collective-permute-done | bytes 1179680 | tf_op jit(solution)/shard_map/ppermute | solution.py:33
  177.7 2.8 %collective-permute-done.14.refs_11_.refs_9_ = bf16[1536,384]{1,0:T(8,128)(2,1)} collective-permute-done((bf16[1536,384]{1,0:T(8,128)(2,1)}, bf16[1536,384]{1,0:T(8,128)(2,1)}, u32[]{:S(2)}, u32[]{:S(2)}) %collective-permute-start.14) | collective-permute-done | bytes 1179680 | tf_op jit(solution)/shard_map/ppermute | solution.py:18
  182.9 1.4 copy-done.5
  184.3 2.2 collective-permute-start.15
  187.0 1.4 copy-done.8
  188.4 1.4 copy-done.10
  190.9 12.6 %attend.2 = (bf16[256,512]{1,0:T(8,128)(2,1)S(1)}, bf16[256,512]{1,0:T(8,128)(2,1)}, bf16[256,512]{1,0:T(8,128)(2,1)}, bf16[256,512]{1,0:T(8,128)(2,1)}) custom-call(s32[1]{0:T(128)} %bitcast.18.place_ref, s32[4]{0:T(128)S(1)} %dynamic-slice_bitcast_fusion.slots_ref, bf16[768,2304]{1,0:T(8,128)(2,1)S(1)} %copy-done.1, ...), custom_call_target="tpu_custom_call" | custom-call | tf_op jit(solution)/shard_map/attend/pallas_call | solution.py:212
  203.6 3.8 %collective-permute-start.19 = (bf16[256,512]{1,0:T(8,128)(2,1)}, bf16[256,512]{1,0:T(8,128)(2,1)S(1)}, u32[]{:S(2)}, u32[]{:S(2)}) collective-permute-start(bf16[256,512]{1,0:T(8,128)(2,1)} %get-tuple-element.128), channel_id=1, source_target_pairs={{0,2},{1,3},{2,0},{3,1},{4,6},{5,7},{6,4},{7,5},{8,10},{9,11},{10,... | collective-permute-start | bytes 786440 | tf_op jit(solution)/shard_map/ppermute | solution.py:33
  207.6 3.1 %collective-permute-start.21 = (bf16[256,512]{1,0:T(8,128)(2,1)}, bf16[256,512]{1,0:T(8,128)(2,1)S(1)}, u32[]{:S(2)}, u32[]{:S(2)}) collective-permute-start(bf16[256,512]{1,0:T(8,128)(2,1)} %get-tuple-element.130), channel_id=1, source_target_pairs={{0,3},{1,0},{2,1},{3,2},{4,7},{5,4},{6,5},{7,6},{8,11},{9,8},{10,9... | collective-permute-start | bytes 786440 | tf_op jit(solution)/shard_map/ppermute | solution.py:33
  210.7 7.3 %attend.3 = (bf16[256,256]{1,0:T(8,128)(2,1)S(1)}, bf16[256,256]{1,0:T(8,128)(2,1)}, bf16[256,256]{1,0:T(8,128)(2,1)S(1)}, bf16[256,256]{1,0:T(8,128)(2,1)S(1)}) custom-call(s32[1]{0:T(128)} %bitcast.18.place_ref, s32[4]{0:T(128)S(1)} %dynamic-slice_bitcast_fusion.slots_ref, bf16[768,2304]{1,0:T(8,128)(2,1)S(1)} %copy-done.1, ...), custom_call_target="tpu_custom_call" | custom-call | tf_op jit(solution)/shard_map/attend/pallas_call | solution.py:212
  218.7 6.4 %collective-permute-done.19.refs_2_ = bf16[256,512]{1,0:T(8,128)(2,1)S(1)} collective-permute-done((bf16[256,512]{1,0:T(8,128)(2,1)}, bf16[256,512]{1,0:T(8,128)(2,1)S(1)}, u32[]{:S(2)}, u32[]{:S(2)}) %collective-permute-start.19) | collective-permute-done | bytes 262176 | tf_op jit(solution)/shard_map/ppermute | solution.py:33
  225.1 6.9 %collective-permute-start.22 = (bf16[256,256]{1,0:T(8,128)(2,1)S(1)}, bf16[256,256]{1,0:T(8,128)(2,1)S(1)}, u32[]{:S(2)}, u32[]{:S(2)}) collective-permute-start(bf16[256,256]{1,0:T(8,128)(2,1)S(1)} %get-tuple-element.131), channel_id=1, source_target_pairs={{0,2},{1,3},{2,0},{3,1},{4,6},{5,7},{6,4},{7,5},{8,10},{9,11},{10,... | collective-permute-start | bytes 393224 | tf_op jit(solution)/shard_map/ppermute | solution.py:33
  232.0 3.3 %collective-permute-start.24 = (bf16[256,256]{1,0:T(8,128)(2,1)S(1)}, bf16[256,256]{1,0:T(8,128)(2,1)S(1)}, u32[]{:S(2)}, u32[]{:S(2)}) collective-permute-start(bf16[256,256]{1,0:T(8,128)(2,1)S(1)} %get-tuple-element.133), channel_id=1, source_target_pairs={{0,3},{1,0},{2,1},{3,2},{4,7},{5,4},{6,5},{7,6},{8,11},{9,8},{10,9... | collective-permute-start | bytes 393224 | tf_op jit(solution)/shard_map/ppermute | solution.py:33
  235.3 1.4 copy-done.11
  237.6 13.7 %add_parts.1.refs_13_ = f32[256,3072]{1,0:T(8,128)} custom-call(s32[8]{0:T(128)S(1)} %stack.79.starts_ref, s32[4]{0:T(128)S(1)} %pad_add_fusion.1.rows_ref, bf16[256,512]{1,0:T(8,128)(2,1)S(1)} %get-tuple-element.144.refs_0_, bf16[256,256]{1,0:T(8,128)(2,1)S(1)} %copy-done.22, bf16[256,512]{1,0:T(8,128)(2,1)S(1)} %collective-permute-done.19.refs_2_, ...), custom_call_target="tpu_custom_call" | custom-call | tf_op jit(solution)/shard_map/add_parts/pallas_call | solution.py:344
  251.4 10.5 %finish.1 = (f32[128,256]{1,0:T(8,128)S(1)}, bf16[128,256]{1,0:T(8,128)(2,1)S(1)}) custom-call(s32[8]{0:T(128)S(1)} %stack.79.starts_ref, s32[4]{0:T(128)S(1)} %pad_add_fusion.1.rows_ref, f32[2]{0:T(128)S(1)} %pad_maximum_fusion.coef_ref, bf16[256,256]{1,0:T(8,128)(2,1)S(1)} %collective-permute-done.22.refs_0_, ...), custom_call_target="tpu_custom_call" | custom-call | tf_op jit(solution)/shard_map/finish/pallas_call | solution.py:356
  261.9 1.9 collective-permute-start.25
  263.8 5.0 %collective-permute-done.25 = bf16[128,256]{1,0:T(8,128)(2,1)S(1)} collective-permute-done((bf16[128,256]{1,0:T(8,128)(2,1)S(1)}, bf16[128,256]{1,0:T(8,128)(2,1)S(1)}, u32[]{:S(2)}, u32[]{:S(2)}) %collective-permute-start.25) | collective-permute-done | bytes 65568 | tf_op jit(solution)/shard_map/ppermute | solution.py:540
  (92 shorter events, 22.8 us)
Async XLA Ops:
  7.2 87.9 %all-gather.2.cloned.1.call-start = ((), (), s32[]{:S(2)}) async-start(), calls=%async_computation | async-start | bytes 2949120 | tf_op jit(solution)/shard_map/all_gather | solution.py:418
  9.3 85.8 %collective-permute-start = (bf16[768,2304]{1,0:T(8,128)(2,1)}, bf16[768,2304]{1,0:T(8,128)(2,1)}, u32[]{:S(2)}, u32[]{:S(2)}) collective-permute-start(bf16[768,2304]{1,0:T(8,128)(2,1)} %refs_0_.3), channel_id=1, source_target_pairs={{0,4},{4,0},{8,12},{12,8},{1,5},{5,1},{9,13},{13,9},{2,6},{6,2},{1... | collective-permute-start | bytes 10616840 | tf_op jit(solution)/shard_map/ppermute | solution.py:18
  9.4 85.7 %collective-permute-start.1 = (bf16[768,2304]{1,0:T(8,128)(2,1)}, bf16[768,2304]{1,0:T(8,128)(2,1)}, u32[]{:S(2)}, u32[]{:S(2)}) collective-permute-start(bf16[768,2304]{1,0:T(8,128)(2,1)} %refs_0_.3), channel_id=1, source_target_pairs={{0,8},{4,12},{8,0},{12,4},{1,9},{5,13},{9,1},{13,5},{2,10},{6,14},... | collective-permute-start | bytes 10616840 | tf_op jit(solution)/shard_map/ppermute | solution.py:18
  17.2 77.9 %collective-permute-start.3 = (bf16[256,3072]{1,0:T(8,128)(2,1)}, bf16[256,3072]{1,0:T(8,128)(2,1)}, u32[]{:S(2)}, u32[]{:S(2)}) collective-permute-start(bf16[256,3072]{1,0:T(8,128)(2,1)} %norm_in.1.refs_4_), channel_id=1, source_target_pairs={{0,1},{1,2},{2,3},{4,5},{5,6},{6,7},{8,9},{9,10},{10,11},{12,13},{... | collective-permute-start | bytes 4718600 | tf_op jit(solution)/shard_map/ppermute | solution.py:406
  21.5 73.6 %collective-permute-start.2 = (bf16[256,3072]{1,0:T(8,128)(2,1)}, bf16[256,3072]{1,0:T(8,128)(2,1)S(1)}, u32[]{:S(2)}, u32[]{:S(2)}) collective-permute-start(bf16[256,3072]{1,0:T(8,128)(2,1)} %norm_in.1.refs_4_), channel_id=1, source_target_pairs={{1,0},{2,1},{3,2},{5,4},{6,5},{7,6},{9,8},{10,9},{11,10},{13,12},{... | collective-permute-start | bytes 4718600 | tf_op jit(solution)/shard_map/ppermute | solution.py:406
  22.8 72.3 %collective-permute-start.4 = (bf16[1,256]{1,0:T(2,128)(2,1)S(1)}, bf16[1,256]{1,0:T(2,128)(2,1)S(1)}, u32[]{:S(2)}, u32[]{:S(2)}) collective-permute-start(bf16[1,256]{1,0:T(2,128)(2,1)S(1)} %get-tuple-element.155), channel_id=1, source_target_pairs={{2,4},{3,5},{6,8},{7,9},{10,12},{11,13},{4,2},{5,3},{8,6},{9,7},{1... | collective-permute-start | bytes 1544 | tf_op jit(solution)/shard_map/ppermute | solution.py:391
  95.2 6.5 %collective-permute-start.5 = (bf16[768,2304]{1,0:T(8,128)(2,1)}, bf16[768,2304]{1,0:T(8,128)(2,1)S(1)}, u32[]{:S(2)}, u32[]{:S(2)}) collective-permute-start(bf16[768,2304]{1,0:T(8,128)(2,1)} %collective-permute-done.1.refs_2_), channel_id=1, source_target_pairs={{0,4},{4,0},{8,12},{12,8},{1,5},{5,1},{9,13},{13,9},{2,6},{6,2},{1... | collective-permute-start | bytes 10616840 | tf_op jit(solution)/shard_map/ppermute | solution.py:18
  95.2 37.4 %collective-permute-start.6 = (bf16[256,3072]{1,0:T(8,128)(2,1)S(1)}, bf16[256,3072]{1,0:T(8,128)(2,1)S(1)}, u32[]{:S(2)}, u32[]{:S(2)}) collective-permute-start(bf16[256,3072]{1,0:T(8,128)(2,1)S(1)} %collective-permute-done.2.refs_5_), channel_id=1, source_target_pairs={{1,0},{2,1},{5,4},{6,5},{9,8},{10,9},{13,12},{14,13},{17,16},{18,1... | collective-permute-start | bytes 4718600 | tf_op jit(solution)/shard_map/ppermute | solution.py:406
  96.5 36.1 %collective-permute-start.7 = (bf16[256,3072]{1,0:T(8,128)(2,1)}, bf16[256,3072]{1,0:T(8,128)(2,1)S(1)}, u32[]{:S(2)}, u32[]{:S(2)}) collective-permute-start(bf16[256,3072]{1,0:T(8,128)(2,1)} %collective-permute-done.3.refs_6_), channel_id=1, source_target_pairs={{1,2},{2,3},{5,6},{6,7},{9,10},{10,11},{13,14},{14,15},{17,18},{18... | collective-permute-start | bytes 4718600 | tf_op jit(solution)/shard_map/ppermute | solution.py:406
  97.3 52.6 %collective-permute-start.12 = (bf16[3072,384]{1,0:T(8,128)(2,1)}, bf16[3072,384]{1,0:T(8,128)(2,1)S(1)}, u32[]{:S(2)}, u32[]{:S(2)}) collective-permute-start(bf16[3072,384]{1,0:T(8,128)(2,1)} %all-gather.2.cloned.1.call-done.refs_5_.refs_3_), channel_id=1, source_target_pairs={{0,8},{4,12},{8,0},{12,4},{1,9},{5,13},{9,1},{13,5},{2,10},{6,14},... | collective-permute-start | bytes 7077896 | tf_op jit(solution)/shard_map/ppermute | solution.py:18
  98.8 53.6 %collective-permute-start.10 = (bf16[3072,384]{1,0:T(8,128)(2,1)}, bf16[3072,384]{1,0:T(8,128)(2,1)S(1)}, u32[]{:S(2)}, u32[]{:S(2)}) collective-permute-start(bf16[3072,384]{1,0:T(8,128)(2,1)} %all-gather.2.cloned.1.call-done.refs_5_.refs_3_), channel_id=1, source_target_pairs={{0,16},{16,0},{1,17},{17,1},{2,18},{18,2},{3,19},{19,3},{4,20},{20... | collective-permute-start | bytes 7077896 | tf_op jit(solution)/shard_map/ppermute | solution.py:33
  116.4 37.3 %copy-start.13 = (bf16[6,512,128]{2,1,0:T(8,128)(2,1)}, bf16[6,512,128]{2,1,0:T(8,128)(2,1)S(1)}, u32[]{:S(2)}) copy-start(bf16[6,512,128]{2,1,0:T(8,128)(2,1)S(1)} %get-tuple-element.100.refs_4_) | copy-start | bytes 2359300
  116.4 37.3 %copy-start.15 = (bf16[6,512,128]{2,1,0:T(8,128)(2,1)}, bf16[6,512,128]{2,1,0:T(8,128)(2,1)S(1)}, u32[]{:S(2)}) copy-start(bf16[6,512,128]{2,1,0:T(8,128)(2,1)S(1)} %get-tuple-element.101.refs_5_) | copy-start | bytes 2359300
  132.6 50.3 %collective-permute-start.11 = (bf16[3072,384]{1,0:T(8,128)(2,1)S(1)}, bf16[3072,384]{1,0:T(8,128)(2,1)S(1)}, u32[]{:S(2)}, u32[]{:S(2)}) collective-permute-start(bf16[3072,384]{1,0:T(8,128)(2,1)S(1)} %copy-done.4), channel_id=1, source_target_pairs={{0,4},{4,0},{8,12},{12,8},{1,5},{5,1},{9,13},{13,9},{2,6},{6,2},{1... | collective-permute-start | bytes 7077896 | tf_op jit(solution)/shard_map/ppermute | solution.py:18
  133.9 46.6 %collective-permute-start.8 = (bf16[256,3072]{1,0:T(8,128)(2,1)S(1)}, bf16[256,3072]{1,0:T(8,128)(2,1)S(1)}, u32[]{:S(2)}, u32[]{:S(2)}) collective-permute-start(bf16[256,3072]{1,0:T(8,128)(2,1)S(1)} %collective-permute-done.6.refs_4_.refs_11_), channel_id=1, source_target_pairs={{1,0},{5,4},{9,8},{13,12},{17,16},{21,20},{25,24},{29,28}} | collective-permute-start | bytes 4718600 | tf_op jit(solution)/shard_map/ppermute | solution.py:406
  135.2 46.5 %collective-permute-start.9 = (bf16[256,3072]{1,0:T(8,128)(2,1)S(1)}, bf16[256,3072]{1,0:T(8,128)(2,1)S(1)}, u32[]{:S(2)}, u32[]{:S(2)}) collective-permute-start(bf16[256,3072]{1,0:T(8,128)(2,1)S(1)} %collective-permute-done.7.refs_6_.refs_12_), channel_id=1, source_target_pairs={{2,3},{6,7},{10,11},{14,15},{18,19},{22,23},{26,27},{30,31}} | collective-permute-start | bytes 4718600 | tf_op jit(solution)/shard_map/ppermute | solution.py:406
  149.9 36.5 %copy-start.2 = (bf16[3072,384]{1,0:T(8,128)(2,1)}, bf16[3072,384]{1,0:T(8,128)(2,1)S(1)}, u32[]{:S(2)}) copy-start(bf16[3072,384]{1,0:T(8,128)(2,1)S(1)} %collective-permute-done.12.refs_9_.refs_7_) | copy-start | bytes 7077892
  151.2 26.5 %collective-permute-start.13 = (bf16[1536,384]{1,0:T(8,128)(2,1)}, bf16[1536,384]{1,0:T(8,128)(2,1)}, u32[]{:S(2)}, u32[]{:S(2)}) collective-permute-start(bf16[1536,384]{1,0:T(8,128)(2,1)} %slice.16), channel_id=1, source_target_pairs={{0,16},{16,0},{1,17},{17,1},{2,18},{18,2},{3,19},{19,3},{4,20},{20... | collective-permute-start | bytes 3538952 | tf_op jit(solution)/shard_map/ppermute | solution.py:33
  153.7 26.8 %collective-permute-start.14 = (bf16[1536,384]{1,0:T(8,128)(2,1)}, bf16[1536,384]{1,0:T(8,128)(2,1)}, u32[]{:S(2)}, u32[]{:S(2)}) collective-permute-start(bf16[1536,384]{1,0:T(8,128)(2,1)} %slice.17), channel_id=1, source_target_pairs={{0,8},{4,12},{8,0},{12,4},{1,9},{5,13},{9,1},{13,5},{2,10},{6,14},... | collective-permute-start | bytes 3538952 | tf_op jit(solution)/shard_map/ppermute | solution.py:18
  155.5 31.5 %copy-start.16 = (bf16[6,512,128]{2,1,0:T(8,128)(2,1)S(1)}, bf16[6,512,128]{2,1,0:T(8,128)(2,1)}, u32[]{:S(2)}) copy-start(bf16[6,512,128]{2,1,0:T(8,128)(2,1)} %copy-done.15) | copy-start | bytes 2359300
  184.3 19.3 %collective-permute-start.15 = (bf16[3072,384]{1,0:T(8,128)(2,1)S(1)}, bf16[3072,384]{1,0:T(8,128)(2,1)S(1)}, u32[]{:S(2)}, u32[]{:S(2)}) collective-permute-start(bf16[3072,384]{1,0:T(8,128)(2,1)S(1)} %collective-permute-done.10.refs_6_.refs_4_), channel_id=1, source_target_pairs={{0,4},{4,0},{8,12},{12,8},{1,5},{5,1},{9,13},{13,9},{2,6},{6,2},{1... | collective-permute-start | bytes 7077896 | tf_op jit(solution)/shard_map/ppermute | solution.py:18
  186.5 17.1 %collective-permute-start.16 = (bf16[3072,384]{1,0:T(8,128)(2,1)S(1)}, bf16[3072,384]{1,0:T(8,128)(2,1)}, u32[]{:S(2)}, u32[]{:S(2)}) collective-permute-start(bf16[3072,384]{1,0:T(8,128)(2,1)S(1)} %collective-permute-done.12.refs_9_.refs_7_), channel_id=1, source_target_pairs={{0,4},{4,0},{8,12},{12,8},{1,5},{5,1},{9,13},{13,9},{2,6},{6,2},{1... | collective-permute-start | bytes 7077896 | tf_op jit(solution)/shard_map/ppermute | solution.py:18
  186.5 17.1 %collective-permute-start.17 = (bf16[1536,384]{1,0:T(8,128)(2,1)}, bf16[1536,384]{1,0:T(8,128)(2,1)S(1)}, u32[]{:S(2)}, u32[]{:S(2)}) collective-permute-start(bf16[1536,384]{1,0:T(8,128)(2,1)} %collective-permute-done.13.refs_10_.refs_8_), channel_id=1, source_target_pairs={{0,4},{4,0},{8,12},{12,8},{1,5},{5,1},{9,13},{13,9},{2,6},{6,2},{1... | collective-permute-start | bytes 3538952 | tf_op jit(solution)/shard_map/ppermute | solution.py:18
  187.0 16.6 %collective-permute-start.18 = (bf16[1536,384]{1,0:T(8,128)(2,1)}, bf16[1536,384]{1,0:T(8,128)(2,1)}, u32[]{:S(2)}, u32[]{:S(2)}) collective-permute-start(bf16[1536,384]{1,0:T(8,128)(2,1)} %collective-permute-done.14.refs_11_.refs_9_), channel_id=1, source_target_pairs={{0,4},{4,0},{8,12},{12,8},{1,5},{5,1},{9,13},{13,9},{2,6},{6,2},{1... | collective-permute-start | bytes 3538952 | tf_op jit(solution)/shard_map/ppermute | solution.py:18
  203.6 31.7 %copy-start.19 = (f32[5,3072]{1,0:T(8,128)S(1)}, f32[5,3072]{1,0:T(8,128)}, u32[]{:S(2)}) copy-start(f32[5,3072]{1,0:T(8,128)} %refs_14_.1) | copy-start | bytes 184324
  203.6 21.5 %collective-permute-start.19 = (bf16[256,512]{1,0:T(8,128)(2,1)}, bf16[256,512]{1,0:T(8,128)(2,1)S(1)}, u32[]{:S(2)}, u32[]{:S(2)}) collective-permute-start(bf16[256,512]{1,0:T(8,128)(2,1)} %get-tuple-element.128), channel_id=1, source_target_pairs={{0,2},{1,3},{2,0},{3,1},{4,6},{5,7},{6,4},{7,5},{8,10},{9,11},{10,... | collective-permute-start | bytes 786440 | tf_op jit(solution)/shard_map/ppermute | solution.py:33
  207.4 17.7 %collective-permute-start.20 = (bf16[256,512]{1,0:T(8,128)(2,1)}, bf16[256,512]{1,0:T(8,128)(2,1)S(1)}, u32[]{:S(2)}, u32[]{:S(2)}) collective-permute-start(bf16[256,512]{1,0:T(8,128)(2,1)} %get-tuple-element.129), channel_id=1, source_target_pairs={{0,1},{1,2},{2,3},{3,0},{4,5},{5,6},{6,7},{7,4},{8,9},{9,10},{10,1... | collective-permute-start | bytes 786440 | tf_op jit(solution)/shard_map/ppermute | solution.py:33
  207.6 17.6 %collective-permute-start.21 = (bf16[256,512]{1,0:T(8,128)(2,1)}, bf16[256,512]{1,0:T(8,128)(2,1)S(1)}, u32[]{:S(2)}, u32[]{:S(2)}) collective-permute-start(bf16[256,512]{1,0:T(8,128)(2,1)} %get-tuple-element.130), channel_id=1, source_target_pairs={{0,3},{1,0},{2,1},{3,2},{4,7},{5,4},{6,5},{7,6},{8,11},{9,8},{10,9... | collective-permute-start | bytes 786440 | tf_op jit(solution)/shard_map/ppermute | solution.py:33
  225.1 26.2 %collective-permute-start.22 = (bf16[256,256]{1,0:T(8,128)(2,1)S(1)}, bf16[256,256]{1,0:T(8,128)(2,1)S(1)}, u32[]{:S(2)}, u32[]{:S(2)}) collective-permute-start(bf16[256,256]{1,0:T(8,128)(2,1)S(1)} %get-tuple-element.131), channel_id=1, source_target_pairs={{0,2},{1,3},{2,0},{3,1},{4,6},{5,7},{6,4},{7,5},{8,10},{9,11},{10,... | collective-permute-start | bytes 393224 | tf_op jit(solution)/shard_map/ppermute | solution.py:33
  232.0 19.3 %collective-permute-start.23 = (bf16[256,256]{1,0:T(8,128)(2,1)}, bf16[256,256]{1,0:T(8,128)(2,1)S(1)}, u32[]{:S(2)}, u32[]{:S(2)}) collective-permute-start(bf16[256,256]{1,0:T(8,128)(2,1)} %get-tuple-element.132), channel_id=1, source_target_pairs={{0,1},{1,2},{2,3},{3,0},{4,5},{5,6},{6,7},{7,4},{8,9},{9,10},{10,1... | collective-permute-start | bytes 393224 | tf_op jit(solution)/shard_map/ppermute | solution.py:33
  232.0 19.3 %collective-permute-start.24 = (bf16[256,256]{1,0:T(8,128)(2,1)S(1)}, bf16[256,256]{1,0:T(8,128)(2,1)S(1)}, u32[]{:S(2)}, u32[]{:S(2)}) collective-permute-start(bf16[256,256]{1,0:T(8,128)(2,1)S(1)} %get-tuple-element.133), channel_id=1, source_target_pairs={{0,3},{1,0},{2,1},{3,2},{4,7},{5,4},{6,5},{7,6},{8,11},{9,8},{10,9... | collective-permute-start | bytes 393224 | tf_op jit(solution)/shard_map/ppermute | solution.py:33
  261.9 6.9 %collective-permute-start.25 = (bf16[128,256]{1,0:T(8,128)(2,1)S(1)}, bf16[128,256]{1,0:T(8,128)(2,1)S(1)}, u32[]{:S(2)}, u32[]{:S(2)}) collective-permute-start(bf16[128,256]{1,0:T(8,128)(2,1)S(1)} %get-tuple-element.150), channel_id=1, source_target_pairs={{2,4},{3,5},{6,8},{7,9},{10,12},{11,13},{4,2},{5,3},{8,6},{9,7},{1... | collective-permute-start | bytes 196616 | tf_op jit(solution)/shard_map/ppermute | solution.py:540
  (20 other events, 151.3 us)
Sparse Core Ops, SparseCore 0:
  9.6 82.3 all-gather.1

commit v7 on v6

--- a/solution.py
+++ b/solution.py
@@ -161,48 +161,89 @@
             pltpu.VMEM((length, width), jnp.bfloat16),
             pltpu.SemaphoreType.DMA((len(plan),)),
         ],
-        compiler_params=pltpu.CompilerParams(vmem_limit_bytes=28 * MIB),
+        compiler_params=pltpu.CompilerParams(vmem_limit_bytes=42 * MIB),
         name="project",
     )(place, *blocks, *sources)
 
 
-def attend_kernel(plan, blocks, counts, place_ref, slots_ref, *refs):
-    w_refs, refs = refs[:blocks], refs[blocks:]
-    known, refs = refs[: 3 * len(counts)], refs[3 * len(counts) :]
-    queries, keys, values, tokens, sems = refs[-5:]
-    devices = slots_ref.shape[0]
-    sources, outs = refs[: -5 - devices], refs[-5 - devices : -5]
-    start, rows = sum(counts), tokens.shape[0]
-
-    @pl.when(pl.program_id(0) == 0)
-    def _():
-        values[:, HD:] = jnp.ones((start + rows, HD), jnp.bfloat16)
-        load_all(place_ref[0], plan, sources, tokens, sems)
-
-    proj = product(tokens, w_refs)
+def weigh(query, key, values):
+    scores = lax.dot_general(
+        query, key, (((1,), (1,)), ((), ())), preferred_element_type=jnp.float32
+    )
+    expo = jnp.exp(scores * (1.0 / math.sqrt(HD))).astype(jnp.bfloat16)
+    return jnp.dot(expo, values, preferred_element_type=jnp.float32)
+
+
+def gather_known(known, counts, queries, keys, values):
     at = 0
     for n, count in enumerate(counts):
         queries[at : at + count] = known[3 * n][0]
         keys[at : at + count] = known[3 * n + 1][0]
         values[at : at + count, :HD] = known[3 * n + 2][0]
         at += count
+
+
+def early_kernel(counts, rows, *refs):
+    known, (out_ref, queries, keys, values) = refs[:-4], refs[-4:]
+
+    @pl.when(pl.program_id(0) == 0)
+    def _():
+        values[:, HD:] = jnp.ones((sum(counts), HD), jnp.bfloat16)
+
+    gather_known(known, counts, queries, keys, values)
+    for first in range(0, sum(counts), rows):
+        part = slice(first, first + rows)
+        out_ref[0, part] = weigh(queries[part], keys[...], values[...])
+
+
+def early(known, rows):
+    counts = [three[0].shape[1] for three in known]
+    heads, length = known[0][0].shape[0], sum(counts)
+    return pl.pallas_call(
+        functools.partial(early_kernel, counts, rows),
+        grid=(heads,),
+        in_specs=[
+            pl.BlockSpec((1, count, HD), lambda h: (h, 0, 0)) for count in counts for _ in range(3)
+        ],
+        out_specs=pl.BlockSpec((1, length, 2 * HD), lambda h: (h, 0, 0)),
+        out_shape=jax.ShapeDtypeStruct((heads, length, 2 * HD), jnp.float32),
+        scratch_shapes=[
+            pltpu.VMEM((length, HD), jnp.bfloat16),
+            pltpu.VMEM((length, HD), jnp.bfloat16),
+            pltpu.VMEM((length, 2 * HD), jnp.bfloat16),
+        ],
+        compiler_params=pltpu.CompilerParams(vmem_limit_bytes=42 * MIB),
+        name="early",
+    )(*(value for three in known for value in three))
+
+
+def attend_kernel(plan, blocks, counts, place_ref, slots_ref, *refs):
+    w_refs, before_ref, refs = refs[:blocks], refs[blocks], refs[blocks + 1 :]
+    known, refs = refs[: 3 * len(counts)], refs[3 * len(counts) :]
+    queries, keys, values, sums, tokens, sems = refs[-6:]
+    devices = slots_ref.shape[0]
+    sources, outs = refs[: -6 - devices], refs[-6 - devices : -6]
+    start, rows = sum(counts), tokens.shape[0]
+
+    @pl.when(pl.program_id(0) == 0)
+    def _():
+        values[:, HD:] = jnp.ones((start + rows, HD), jnp.bfloat16)
+        load_all(place_ref[0], plan, sources, tokens, sems)
+
+    proj = product(tokens, w_refs)
+    gather_known(known, counts, queries, keys, values)
     queries[start:] = root_norm(proj[:, :HD])
     keys[start:] = root_norm(proj[:, HD : 2 * HD])
     values[start:, :HD] = proj[:, 2 * HD :].astype(jnp.bfloat16)
+    sums[:start] = before_ref[0]
+    sums[start:] = weigh(queries[start:], keys[:start], values[:start])
     for turn in range(devices):
-        first = pl.multiple_of(slots_ref[turn] * rows, rows)
-        scores = lax.dot_general(
-            queries[pl.ds(first, rows)],
-            keys[...],
-            (((1,), (1,)), ((), ())),
-            preferred_element_type=jnp.float32,
-        )
-        expo = jnp.exp(scores * (1.0 / math.sqrt(HD))).astype(jnp.bfloat16)
-        mixed = jnp.dot(expo, values[...], preferred_element_type=jnp.float32)
+        part = pl.ds(pl.multiple_of(slots_ref[turn] * rows, rows), rows)
+        mixed = sums[part] + weigh(queries[part], keys[start:], values[start:])
         outs[turn][...] = (mixed[:, :HD] / mixed[:, HD:]).astype(jnp.bfloat16)
 
 
-def attend(place, slots, plan, sources, known, blocks, start, heads):
+def attend(place, slots, plan, sources, known, before, blocks, start, heads):
     devices = slots.shape[0]
     rows, width = sources[0].shape
     counts = [three[0].shape[1] for three in known]
@@ -214,6 +255,7 @@
         grid=(heads,),
         in_specs=[smem, smem]
         + [pl.BlockSpec((width // len(blocks), 3 * HD), lambda h: (0, start + h))] * len(blocks)
+        + [pl.BlockSpec((1, length - rows, 2 * HD), lambda h: (start + h, 0, 0))]
         + [
             pl.BlockSpec((1, count, HD), lambda h: (start + h, 0, 0))
             for count in counts
@@ -226,12 +268,13 @@
             pltpu.VMEM((length, HD), jnp.bfloat16),
             pltpu.VMEM((length, HD), jnp.bfloat16),
             pltpu.VMEM((length, 2 * HD), jnp.bfloat16),
+            pltpu.VMEM((length, 2 * HD), jnp.float32),
             pltpu.VMEM((rows, width), jnp.bfloat16),
             pltpu.SemaphoreType.DMA((1,)),
         ],
-        compiler_params=pltpu.CompilerParams(vmem_limit_bytes=28 * MIB),
+        compiler_params=pltpu.CompilerParams(vmem_limit_bytes=42 * MIB),
         name="attend",
-    )(place, slots, *blocks, *(value for three in known for value in three), *sources)
+    )(place, slots, *blocks, before, *(value for three in known for value in three), *sources)
 
 
 def multiply(parts, offsets, starts_ref, rows_ref, sources, weights, sems, wide, store):
@@ -307,11 +350,11 @@
     multiply(parts, offsets, starts_ref, rows_ref, sources, weights, sems, wide, store)
     normed = layer_norm(mixed[...]) * (1.0 + mod_ref[4:5, :]) + mod_ref[3:4, :]
     velocity = lax.dot_general(
+        normed.astype(jnp.bfloat16),
         head_ref[...],
-        normed.astype(jnp.bfloat16),
         (((1,), (1,)), ((), ())),
         preferred_element_type=jnp.float32,
-    )
+    ).T
     channels = velocity.shape[0]
     base, weight = latent_ref[...], weight_ref[...]
     moved = (base + coef_ref[1] * velocity) * weight
@@ -337,7 +380,7 @@
         pltpu.SemaphoreType.DMA((count, len(parts))),
     ]
     params = dict(
-        compiler_params=pltpu.CompilerParams(vmem_limit_bytes=36 * MIB),
+        compiler_params=pltpu.CompilerParams(vmem_limit_bytes=60 * MIB),
     )
     if last is None:
         aliased = before.dtype == jnp.float32
@@ -479,22 +522,24 @@
     if not narrow:
         mine = lax.optimization_barrier((columns[0, 0], known[0]))[0]
         columns[near, 0] = swap(mine, "tile", near)
+    before = early(known, rows)
     columns = {key: [value] for key, value in columns.items()}
-    for turn in range(1, groups) if not narrow else []:
-        columns.update(
-            {
-                (d, turn): [turned(columns[d, 0][0], "group", turn)]
-                for d in range(1, tiles)
-                if d & near == 0 and (groups != 2 or len(far) != 1)
-            }
-        )
-    if groups == 2 and len(far) == 1 and not narrow:
+    diagonal = groups == 2 and len(far) == 1 and not narrow
+    crossing = ()
+    if diagonal:
         bit, half = far[0], columns[0, 0][0].shape[0] // 2
-        columns[bit, 1] = [
-            turned(columns[bit, 0][0][:half], "group", 1),
-            swap(columns[0, 1][0][half:], "tile", bit),
-        ]
-    blocks_by, known, columns = lax.optimization_barrier((blocks_by, known, columns))
+        crossing = (columns[bit, 0][0][:half], columns[0, 1][0][half:])
+    blocks_by, known, before, columns, crossing = lax.optimization_barrier(
+        (blocks_by, known, before, columns, crossing)
+    )
+    late = {}
+    if diagonal:
+        late[bit, 1] = [turned(crossing[0], "group", 1), swap(crossing[1], "tile", bit)]
+    elif not narrow:
+        for turn in range(1, groups):
+            for d in range(1, tiles):
+                if d & near == 0:
+                    late[d, turn] = [turned(columns[d, 0][0], "group", turn)]
     if not narrow:
         columns.update(
             {
@@ -504,16 +549,20 @@
             }
         )
     heads = w_qkv.shape[1] // (3 * HD)
-    many = heads - heads // 3
+    many = heads - heads // 2
     halves = [(0, many), (many, heads - many)]
     turns = sorted(range(1, devices), key=lambda turn: -min(turn, devices - turn))
     choices, found = arrival(devices - 2)
-    attended = attend(at, slots, [choices], found, known, blocks, *halves[0])
+    attended = attend(at, slots, [choices], found, known, before, blocks, *halves[0])
     attended, columns, found = lax.optimization_barrier((attended, columns, found))
     received = [[turned(attended[turn], "seq", turn) for turn in turns]]
     own = [attended[0]]
-    attended = attend(at, slots, [choices], found, known, blocks, *halves[1])
-    attended, received = lax.optimization_barrier((attended, received))
+    attended = attend(at, slots, [choices], found, known, before, blocks, *halves[1])
+    attended, received, late = lax.optimization_barrier((attended, received, late))
+    columns.update(late)
+    columns.update(
+        {(d ^ near, g): [swap(array, "tile", near) for array in late[d, g]] for d, g in late}
+    )
     received.append([turned(attended[turn], "seq", turn) for turn in turns])
     own.append(attended[0])
     pieces = [columns[key] for key in order]

time: 278 us -> 253 us (0.910)
  waiting for transfers between devices: 128 us -> 104 us
    ppermute x8, waiting for transfers between devices: 22 us -> 2.58 us  [turned(): lax.ppermute(value, axis, [(i, (i + turn) % count) for i in range(count)])]
    pallas_call x0 -> x1, Pallas kernels: none -> 5.54 us  [early(): pl.pallas_call(functools.partial(early_kernel, counts, rows), grid=(heads...]
    unnamed x50 -> x38, local copies, waits for them, and re-layouts: 16.2 us -> 11 us
    ppermute x1, starting transfers between devices: 1.92 us -> 6.95 us  [shards(): other = lax.ppermute(to_join, ('tile', 'seq'), joins).astype(jnp.float32)]
    ppermute x8, starting transfers between devices: 19.7 us -> 15.3 us  [turned(): lax.ppermute(value, axis, [(i, (i + turn) % count) for i in range(count)])]
    pallas_call x2, Pallas kernels: 19.9 us -> 15.9 us  [attend(): pl.pallas_call(functools.partial(attend_kernel, plan, len(blocks), counts...]
    pallas_call x1, Pallas kernels: 13.7 us -> 10.8 us  [accumulate(): pl.pallas_call(functools.partial(add_kernel, offsets, splits), in_specs=[...]
  transfers between devices with their start and end apart: 27 -> 27, of which waited for: 8 -> 8; matrix products, arithmetic and copies ran while one was open for 1% -> 3% of each run, Pallas kernels for 20% -> 22%
where the time goes in v7:
time: 253 us; the launch traced here: 252 us
  waiting for transfers between devices  104 us (41%)
  Pallas kernels  65.1 us (26%)
  starting transfers between devices  45.8 us (18%)
  local copies, waits for them, and re-layouts  18.7 us (7%)
  between operations  15.2 us (6%)
  other arithmetic  3.42 us (1%)
    ppermute x1, waiting for transfers between devices, shards(): lax.ppermute(weight.astype(jnp.bfloat16), ('tile', 'seq'), joins)  63.6 us
    pallas_call x2, Pallas kernels, project(): pl.pallas_call(functools.partial(project_kernel, plan, len(blocks)), grid...  17.9 us
    ppermute x6, waiting for transfers between devices, hop(): lax.ppermute(blocks_by[way * (step - 1)], 'seq', step_pairs(devices, step...  17.8 us
    ppermute x10, waiting for transfers between devices, swap(): return lax.ppermute(value, axis, [(i, i ^ bit) for i in range(count)])  16.5 us
    pallas_call x2, Pallas kernels, attend(): pl.pallas_call(functools.partial(attend_kernel, plan, len(blocks), counts...  15.9 us
    ppermute x8, starting transfers between devices, turned(): lax.ppermute(value, axis, [(i, (i + turn) % count) for i in range(count)])  15.3 us
    unnamed x38, local copies, waits for them, and re-layouts  11 us
    pallas_call x1, Pallas kernels, accumulate(): pl.pallas_call(functools.partial(add_kernel, offsets, splits), in_specs=[...  10.8 us
  transfers between devices with their start and end apart: 27, of which 8 were waited for; matrix products, arithmetic and copies ran while one was open for 3% of the time, Pallas kernels for 22%

profile of v7, /device:TPU:1, one launch (start us, length us, event | category | flops | bytes accessed | tf_op | source)
XLA Modules:
  0.0 251.9 jit_solution(11732699623816354550)
XLA Ops:
  9.4 2.7 %collective-permute-start.1 = (bf16[768,2304]{1,0:T(8,128)(2,1)}, bf16[768,2304]{1,0:T(8,128)(2,1)}, u32[]{:S(2)}, u32[]{:S(2)}) collective-permute-start(bf16[768,2304]{1,0:T(8,128)(2,1)} %refs_0_.3), channel_id=1, source_target_pairs={{0,8},{4,12},{8,0},{12,4},{1,9},{5,13},{9,1},{13,5},{2,10},{6,14},... | collective-permute-start | bytes 10616840 | tf_op jit(solution)/shard_map/ppermute | solution.py:18
  12.7 4.5 %norm_in.1.refs_4_ = bf16[256,3072]{1,0:T(8,128)(2,1)} custom-call(s32[4]{0:T(128)} %pad_add_fusion.starts_ref, bf16[256,3072]{1,0:T(8,128)(2,1)} %bitcast.33, f32[5,3072]{1,0:T(8,128)} %refs_14_.1), custom_call_target="tpu_custom_call" | custom-call | tf_op jit(solution)/shard_map/norm_in/pallas_call | solution.py:78
  17.2 4.3 %collective-permute-start.3 = (bf16[256,3072]{1,0:T(8,128)(2,1)}, bf16[256,3072]{1,0:T(8,128)(2,1)}, u32[]{:S(2)}, u32[]{:S(2)}) collective-permute-start(bf16[256,3072]{1,0:T(8,128)(2,1)} %norm_in.1.refs_4_), channel_id=1, source_target_pairs={{0,1},{1,2},{2,3},{4,5},{5,6},{6,7},{8,9},{9,10},{10,11},{12,13},{... | collective-permute-start | bytes 4718600 | tf_op jit(solution)/shard_map/ppermute | solution.py:449
  23.4 4.6 %collective-permute-start.4 = (bf16[1,256]{1,0:T(2,128)(2,1)S(1)}, bf16[1,256]{1,0:T(2,128)(2,1)S(1)}, u32[]{:S(2)}, u32[]{:S(2)}) collective-permute-start(bf16[1,256]{1,0:T(2,128)(2,1)S(1)} %get-tuple-element.153), channel_id=1, source_target_pairs={{2,4},{3,5},{6,8},{7,9},{10,12},{11,13},{4,2},{5,3},{8,6},{9,7},{1... | collective-permute-start | bytes 1544 | tf_op jit(solution)/shard_map/ppermute | solution.py:434
  31.5 63.6 %collective-permute-done.4 = bf16[1,256]{1,0:T(2,128)(2,1)S(1)} collective-permute-done((bf16[1,256]{1,0:T(2,128)(2,1)S(1)}, bf16[1,256]{1,0:T(2,128)(2,1)S(1)}, u32[]{:S(2)}, u32[]{:S(2)}) %collective-permute-start.4) | collective-permute-done | bytes 544 | tf_op jit(solution)/shard_map/ppermute | solution.py:434
  95.2 1.3 collective-permute-start.6
  97.3 1.5 collective-permute-start.12
  100.0 1.6 collective-permute-done.5.refs_3_
  101.7 1.8 copy-done.6
  103.4 2.0 copy-done.1
  105.4 1.4 copy-done.3
  106.8 10.7 %project.2 = (bf16[6,512,128]{2,1,0:T(8,128)(2,1)S(1)}, bf16[6,512,128]{2,1,0:T(8,128)(2,1)S(1)}, bf16[6,512,128]{2,1,0:T(8,128)(2,1)S(1)}) custom-call(s32[1]{0:T(128)} %bitcast.18.place_ref, bf16[768,2304]{1,0:T(8,128)(2,1)S(1)} %copy-done.1, bf16[768,2304]{1,0:T(8,128)(2,1)} %collective-permute-done.refs_1_, ...), custom_call_target="tpu_custom_call" | custom-call | tf_op jit(solution)/shard_map/project/pallas_call | solution.py:152
  117.5 15.2 %collective-permute-done.6.refs_4_.refs_12_ = bf16[256,3072]{1,0:T(8,128)(2,1)S(1)} collective-permute-done((bf16[256,3072]{1,0:T(8,128)(2,1)S(1)}, bf16[256,3072]{1,0:T(8,128)(2,1)S(1)}, u32[]{:S(2)}, u32[]{:S(2)}) %collective-permute-start.6) | collective-permute-done | bytes 1572896 | tf_op jit(solution)/shard_map/ppermute | solution.py:449
  136.0 14.0 %collective-permute-done.12.refs_9_.refs_7_ = bf16[3072,384]{1,0:T(8,128)(2,1)} collective-permute-done((bf16[3072,384]{1,0:T(8,128)(2,1)}, bf16[3072,384]{1,0:T(8,128)(2,1)}, u32[]{:S(2)}, u32[]{:S(2)}) %collective-permute-start.12) | collective-permute-done | bytes 2359328 | tf_op jit(solution)/shard_map/ppermute | solution.py:18
  150.0 2.4 slice.16
  152.5 2.4 slice.17
  154.9 7.2 %project.3 = (bf16[6,256,128]{2,1,0:T(8,128)(2,1)S(1)}, bf16[6,256,128]{2,1,0:T(8,128)(2,1)S(1)}, bf16[6,256,128]{2,1,0:T(8,128)(2,1)S(1)}) custom-call(s32[1]{0:T(128)} %bitcast.18.place_ref, bf16[768,2304]{1,0:T(8,128)(2,1)S(1)} %copy-done.1, bf16[768,2304]{1,0:T(8,128)(2,1)} %collective-permute-done.refs_1_, ...), custom_call_target="tpu_custom_call" | custom-call | tf_op jit(solution)/shard_map/project/pallas_call | solution.py:152
  162.1 5.5 %early.1.refs_4_ = f32[6,768,256]{2,1,0:T(8,128)S(1)} custom-call(bf16[6,512,128]{2,1,0:T(8,128)(2,1)S(1)} %get-tuple-element.100.refs_0_.refs_5_, bf16[6,512,128]{2,1,0:T(8,128)(2,1)S(1)} %get-tuple-element.101.refs_1_.refs_6_, bf16[6,512,128]{2,1,0:T(8,128)(2,1)S(1)} %get-tuple-element.102.refs_2_.refs_7_, ...), custom_call_target="tpu_custom_call" | custom-call | tf_op jit(solution)/shard_map/early/pallas_call | solution.py:202
  167.7 2.2 copy-done.2
  169.8 2.6 %collective-permute-done.8.refs_11_ = bf16[256,3072]{1,0:T(8,128)(2,1)S(1)} collective-permute-done((bf16[256,3072]{1,0:T(8,128)(2,1)S(1)}, bf16[256,3072]{1,0:T(8,128)(2,1)S(1)}, u32[]{:S(2)}, u32[]{:S(2)}) %collective-permute-start.8) | collective-permute-done | bytes 1572896 | tf_op jit(solution)/shard_map/ppermute | solution.py:449
  175.5 7.9 %attend.2 = (bf16[256,384]{1,0:T(8,128)(2,1)S(1)}, bf16[256,384]{1,0:T(8,128)(2,1)S(1)}, bf16[256,384]{1,0:T(8,128)(2,1)S(1)}, bf16[256,384]{1,0:T(8,128)(2,1)S(1)}) custom-call(s32[1]{0:T(128)} %bitcast.18.place_ref, s32[4]{0:T(128)S(1)} %dynamic-slice_bitcast_fusion.slots_ref, bf16[768,2304]{1,0:T(8,128)(2,1)} %refs_0_.3, ...), custom_call_target="tpu_custom_call" | custom-call | tf_op jit(solution)/shard_map/attend/pallas_call | solution.py:253
  183.5 2.5 collective-permute-start.15
  185.9 2.2 collective-permute-start.16
  189.2 8.0 %attend.3 = (bf16[256,384]{1,0:T(8,128)(2,1)S(1)}, bf16[256,384]{1,0:T(8,128)(2,1)S(1)}, bf16[256,384]{1,0:T(8,128)(2,1)S(1)}, bf16[256,384]{1,0:T(8,128)(2,1)S(1)}) custom-call(s32[1]{0:T(128)} %bitcast.18.place_ref, s32[4]{0:T(128)S(1)} %dynamic-slice_bitcast_fusion.slots_ref, bf16[768,2304]{1,0:T(8,128)(2,1)} %refs_0_.3, ...), custom_call_target="tpu_custom_call" | custom-call | tf_op jit(solution)/shard_map/attend/pallas_call | solution.py:253
  197.9 2.6 %collective-permute-done.18.refs_10_.refs_8_ = bf16[1536,384]{1,0:T(8,128)(2,1)S(1)} collective-permute-done((bf16[1536,384]{1,0:T(8,128)(2,1)}, bf16[1536,384]{1,0:T(8,128)(2,1)S(1)}, u32[]{:S(2)}, u32[]{:S(2)}) %collective-permute-start.18) | collective-permute-done | bytes 1179680 | tf_op jit(solution)/shard_map/ppermute | solution.py:33
  201.3 1.7 collective-permute-start.23
  203.1 3.9 %collective-permute-start.20 = (bf16[256,384]{1,0:T(8,128)(2,1)S(1)}, bf16[256,384]{1,0:T(8,128)(2,1)S(1)}, u32[]{:S(2)}, u32[]{:S(2)}) collective-permute-start(bf16[256,384]{1,0:T(8,128)(2,1)S(1)} %get-tuple-element.131), channel_id=1, source_target_pairs={{0,2},{1,3},{2,0},{3,1},{4,6},{5,7},{6,4},{7,5},{8,10},{9,11},{10,... | collective-permute-start | bytes 589832 | tf_op jit(solution)/shard_map/ppermute | solution.py:33
  207.7 2.6 %collective-permute-start.22 = (bf16[256,384]{1,0:T(8,128)(2,1)S(1)}, bf16[256,384]{1,0:T(8,128)(2,1)}, u32[]{:S(2)}, u32[]{:S(2)}) collective-permute-start(bf16[256,384]{1,0:T(8,128)(2,1)S(1)} %get-tuple-element.133), channel_id=1, source_target_pairs={{0,3},{1,0},{2,1},{3,2},{4,7},{5,4},{6,5},{7,6},{8,11},{9,8},{10,9... | collective-permute-start | bytes 589832 | tf_op jit(solution)/shard_map/ppermute | solution.py:33
  211.3 10.8 %add_parts.1.refs_13_ = f32[256,3072]{1,0:T(8,128)} custom-call(s32[8]{0:T(128)} %stack.79.starts_ref, s32[4]{0:T(128)} %pad_add_fusion.1.rows_ref, bf16[256,384]{1,0:T(8,128)(2,1)} %copy-done.4, bf16[256,384]{1,0:T(8,128)(2,1)} %copy-done.5, bf16[256,384]{1,0:T(8,128)(2,1)} %copy-done.13, bf16[256,384]{1,0:T(8,128)(2,1)} %copy-done.14, ...), custom_call_target="tpu_custom_call" | custom-call | tf_op jit(solution)/shard_map/add_parts/pallas_call | solution.py:387
  222.9 10.5 %finish.1 = (f32[128,256]{1,0:T(8,128)}, bf16[128,256]{1,0:T(8,128)(2,1)}) custom-call(s32[8]{0:T(128)} %stack.79.starts_ref, s32[4]{0:T(128)} %pad_add_fusion.1.rows_ref, f32[2]{0:T(128)} %pad_maximum_fusion.coef_ref, bf16[256,384]{1,0:T(8,128)(2,1)} %copy-done.16, bf16[256,384]{1,0:T(8,128)(2,1)} %copy-done.17, ...), custom_call_target="tpu_custom_call" | custom-call | tf_op jit(solution)/shard_map/finish/pallas_call | solution.py:399
  233.4 7.0 %collective-permute-start.25 = (bf16[128,256]{1,0:T(8,128)(2,1)}, bf16[128,256]{1,0:T(8,128)(2,1)S(1)}, u32[]{:S(2)}, u32[]{:S(2)}) collective-permute-start(bf16[128,256]{1,0:T(8,128)(2,1)} %get-tuple-element.148), channel_id=1, source_target_pairs={{2,4},{3,5},{6,8},{7,9},{10,12},{11,13},{4,2},{5,3},{8,6},{9,7},{1... | collective-permute-start | bytes 196616 | tf_op jit(solution)/shard_map/ppermute | solution.py:589
  240.4 3.2 %collective-permute-done.25 = bf16[128,256]{1,0:T(8,128)(2,1)S(1)} collective-permute-done((bf16[128,256]{1,0:T(8,128)(2,1)}, bf16[128,256]{1,0:T(8,128)(2,1)S(1)}, u32[]{:S(2)}, u32[]{:S(2)}) %collective-permute-start.25) | collective-permute-done | bytes 65568 | tf_op jit(solution)/shard_map/ppermute | solution.py:589
  (81 shorter events, 22.5 us)
Async XLA Ops:
  7.2 87.9 %all-gather.2.cloned.1.call-start = ((), (), s32[]{:S(2)}) async-start(), calls=%async_computation | async-start | bytes 2949120 | tf_op jit(solution)/shard_map/all_gather | solution.py:461
  9.3 85.8 %collective-permute-start = (bf16[768,2304]{1,0:T(8,128)(2,1)}, bf16[768,2304]{1,0:T(8,128)(2,1)}, u32[]{:S(2)}, u32[]{:S(2)}) collective-permute-start(bf16[768,2304]{1,0:T(8,128)(2,1)} %refs_0_.3), channel_id=1, source_target_pairs={{0,4},{4,0},{8,12},{12,8},{1,5},{5,1},{9,13},{13,9},{2,6},{6,2},{1... | collective-permute-start | bytes 10616840 | tf_op jit(solution)/shard_map/ppermute | solution.py:18
  9.4 85.7 %collective-permute-start.1 = (bf16[768,2304]{1,0:T(8,128)(2,1)}, bf16[768,2304]{1,0:T(8,128)(2,1)}, u32[]{:S(2)}, u32[]{:S(2)}) collective-permute-start(bf16[768,2304]{1,0:T(8,128)(2,1)} %refs_0_.3), channel_id=1, source_target_pairs={{0,8},{4,12},{8,0},{12,4},{1,9},{5,13},{9,1},{13,5},{2,10},{6,14},... | collective-permute-start | bytes 10616840 | tf_op jit(solution)/shard_map/ppermute | solution.py:18
  12.7 10.1 %copy-start.18 = (s32[1,256]{1,0:T(1,128)S(1)}, s32[1,256]{1,0:T(1,128)}, u32[]{:S(2)}) copy-start(s32[1,256]{1,0:T(1,128)} %param.15) | copy-start | bytes 3076
  17.2 77.9 %collective-permute-start.3 = (bf16[256,3072]{1,0:T(8,128)(2,1)}, bf16[256,3072]{1,0:T(8,128)(2,1)}, u32[]{:S(2)}, u32[]{:S(2)}) collective-permute-start(bf16[256,3072]{1,0:T(8,128)(2,1)} %norm_in.1.refs_4_), channel_id=1, source_target_pairs={{0,1},{1,2},{2,3},{4,5},{5,6},{6,7},{8,9},{9,10},{10,11},{12,13},{... | collective-permute-start | bytes 4718600 | tf_op jit(solution)/shard_map/ppermute | solution.py:449
  21.5 73.6 %collective-permute-start.2 = (bf16[256,3072]{1,0:T(8,128)(2,1)}, bf16[256,3072]{1,0:T(8,128)(2,1)S(1)}, u32[]{:S(2)}, u32[]{:S(2)}) collective-permute-start(bf16[256,3072]{1,0:T(8,128)(2,1)} %norm_in.1.refs_4_), channel_id=1, source_target_pairs={{1,0},{2,1},{3,2},{5,4},{6,5},{7,6},{9,8},{10,9},{11,10},{13,12},{... | collective-permute-start | bytes 4718600 | tf_op jit(solution)/shard_map/ppermute | solution.py:449
  23.4 71.7 %collective-permute-start.4 = (bf16[1,256]{1,0:T(2,128)(2,1)S(1)}, bf16[1,256]{1,0:T(2,128)(2,1)S(1)}, u32[]{:S(2)}, u32[]{:S(2)}) collective-permute-start(bf16[1,256]{1,0:T(2,128)(2,1)S(1)} %get-tuple-element.153), channel_id=1, source_target_pairs={{2,4},{3,5},{6,8},{7,9},{10,12},{11,13},{4,2},{5,3},{8,6},{9,7},{1... | collective-permute-start | bytes 1544 | tf_op jit(solution)/shard_map/ppermute | solution.py:434
  95.2 6.5 %collective-permute-start.5 = (bf16[768,2304]{1,0:T(8,128)(2,1)}, bf16[768,2304]{1,0:T(8,128)(2,1)S(1)}, u32[]{:S(2)}, u32[]{:S(2)}) collective-permute-start(bf16[768,2304]{1,0:T(8,128)(2,1)} %collective-permute-done.1.refs_2_), channel_id=1, source_target_pairs={{0,4},{4,0},{8,12},{12,8},{1,5},{5,1},{9,13},{13,9},{2,6},{6,2},{1... | collective-permute-start | bytes 10616840 | tf_op jit(solution)/shard_map/ppermute | solution.py:18
  95.2 37.5 %collective-permute-start.6 = (bf16[256,3072]{1,0:T(8,128)(2,1)S(1)}, bf16[256,3072]{1,0:T(8,128)(2,1)S(1)}, u32[]{:S(2)}, u32[]{:S(2)}) collective-permute-start(bf16[256,3072]{1,0:T(8,128)(2,1)S(1)} %collective-permute-done.2.refs_5_), channel_id=1, source_target_pairs={{1,0},{2,1},{5,4},{6,5},{9,8},{10,9},{13,12},{14,13},{17,16},{18,1... | collective-permute-start | bytes 4718600 | tf_op jit(solution)/shard_map/ppermute | solution.py:449
  96.5 36.2 %collective-permute-start.7 = (bf16[256,3072]{1,0:T(8,128)(2,1)}, bf16[256,3072]{1,0:T(8,128)(2,1)S(1)}, u32[]{:S(2)}, u32[]{:S(2)}) collective-permute-start(bf16[256,3072]{1,0:T(8,128)(2,1)} %collective-permute-done.3.refs_6_), channel_id=1, source_target_pairs={{1,2},{2,3},{5,6},{6,7},{9,10},{10,11},{13,14},{14,15},{17,18},{18... | collective-permute-start | bytes 4718600 | tf_op jit(solution)/shard_map/ppermute | solution.py:449
  97.3 52.7 %collective-permute-start.12 = (bf16[3072,384]{1,0:T(8,128)(2,1)}, bf16[3072,384]{1,0:T(8,128)(2,1)}, u32[]{:S(2)}, u32[]{:S(2)}) collective-permute-start(bf16[3072,384]{1,0:T(8,128)(2,1)} %all-gather.2.cloned.1.call-done.refs_5_.refs_3_), channel_id=1, source_target_pairs={{0,8},{4,12},{8,0},{12,4},{1,9},{5,13},{9,1},{13,5},{2,10},{6,14},... | collective-permute-start | bytes 7077896 | tf_op jit(solution)/shard_map/ppermute | solution.py:18
  98.8 53.6 %collective-permute-start.10 = (bf16[3072,384]{1,0:T(8,128)(2,1)}, bf16[3072,384]{1,0:T(8,128)(2,1)}, u32[]{:S(2)}, u32[]{:S(2)}) collective-permute-start(bf16[3072,384]{1,0:T(8,128)(2,1)} %all-gather.2.cloned.1.call-done.refs_5_.refs_3_), channel_id=1, source_target_pairs={{0,16},{16,0},{1,17},{17,1},{2,18},{18,2},{3,19},{19,3},{4,20},{20... | collective-permute-start | bytes 7077896 | tf_op jit(solution)/shard_map/ppermute | solution.py:33
  106.8 25.9 %copy-start.7 = (bf16[3072,384]{1,0:T(8,128)(2,1)S(1)}, bf16[3072,384]{1,0:T(8,128)(2,1)}, u32[]{:S(2)}) copy-start(bf16[3072,384]{1,0:T(8,128)(2,1)} %all-gather.2.cloned.1.call-done.refs_5_.refs_3_) | copy-start | bytes 7077892
  132.7 39.7 %collective-permute-start.11 = (bf16[3072,384]{1,0:T(8,128)(2,1)S(1)}, bf16[3072,384]{1,0:T(8,128)(2,1)}, u32[]{:S(2)}, u32[]{:S(2)}) collective-permute-start(bf16[3072,384]{1,0:T(8,128)(2,1)S(1)} %copy-done.7), channel_id=1, source_target_pairs={{0,4},{4,0},{8,12},{12,8},{1,5},{5,1},{9,13},{13,9},{2,6},{6,2},{1... | collective-permute-start | bytes 7077896 | tf_op jit(solution)/shard_map/ppermute | solution.py:18
  133.9 38.5 %collective-permute-start.8 = (bf16[256,3072]{1,0:T(8,128)(2,1)S(1)}, bf16[256,3072]{1,0:T(8,128)(2,1)S(1)}, u32[]{:S(2)}, u32[]{:S(2)}) collective-permute-start(bf16[256,3072]{1,0:T(8,128)(2,1)S(1)} %collective-permute-done.6.refs_4_.refs_12_), channel_id=1, source_target_pairs={{1,0},{5,4},{9,8},{13,12},{17,16},{21,20},{25,24},{29,28}} | collective-permute-start | bytes 4718600 | tf_op jit(solution)/shard_map/ppermute | solution.py:449
  135.2 37.2 %collective-permute-start.9 = (bf16[256,3072]{1,0:T(8,128)(2,1)S(1)}, bf16[256,3072]{1,0:T(8,128)(2,1)S(1)}, u32[]{:S(2)}, u32[]{:S(2)}) collective-permute-start(bf16[256,3072]{1,0:T(8,128)(2,1)S(1)} %collective-permute-done.7.refs_6_.refs_13_), channel_id=1, source_target_pairs={{2,3},{6,7},{10,11},{14,15},{18,19},{22,23},{26,27},{30,31}} | collective-permute-start | bytes 4718600 | tf_op jit(solution)/shard_map/ppermute | solution.py:449
  172.5 11.0 %collective-permute-start.13 = (bf16[3072,384]{1,0:T(8,128)(2,1)}, bf16[3072,384]{1,0:T(8,128)(2,1)S(1)}, u32[]{:S(2)}, u32[]{:S(2)}) collective-permute-start(bf16[3072,384]{1,0:T(8,128)(2,1)} %collective-permute-done.10.refs_6_.refs_4_), channel_id=1, source_target_pairs={{0,4},{4,0},{8,12},{12,8},{1,5},{5,1},{9,13},{13,9},{2,6},{6,2},{1... | collective-permute-start | bytes 7077896 | tf_op jit(solution)/shard_map/ppermute | solution.py:18
  173.0 10.4 %collective-permute-start.14 = (bf16[3072,384]{1,0:T(8,128)(2,1)}, bf16[3072,384]{1,0:T(8,128)(2,1)S(1)}, u32[]{:S(2)}, u32[]{:S(2)}) collective-permute-start(bf16[3072,384]{1,0:T(8,128)(2,1)} %collective-permute-done.12.refs_9_.refs_7_), channel_id=1, source_target_pairs={{0,4},{4,0},{8,12},{12,8},{1,5},{5,1},{9,13},{13,9},{2,6},{6,2},{1... | collective-permute-start | bytes 7077896 | tf_op jit(solution)/shard_map/ppermute | solution.py:18
  173.1 27.3 %collective-permute-start.18 = (bf16[1536,384]{1,0:T(8,128)(2,1)}, bf16[1536,384]{1,0:T(8,128)(2,1)S(1)}, u32[]{:S(2)}, u32[]{:S(2)}) collective-permute-start(bf16[1536,384]{1,0:T(8,128)(2,1)} %slice.16), channel_id=1, source_target_pairs={{0,16},{16,0},{1,17},{17,1},{2,18},{18,2},{3,19},{19,3},{4,20},{20... | collective-permute-start | bytes 3538952 | tf_op jit(solution)/shard_map/ppermute | solution.py:33
  174.3 27.0 %collective-permute-start.19 = (bf16[1536,384]{1,0:T(8,128)(2,1)}, bf16[1536,384]{1,0:T(8,128)(2,1)S(1)}, u32[]{:S(2)}, u32[]{:S(2)}) collective-permute-start(bf16[1536,384]{1,0:T(8,128)(2,1)} %slice.17), channel_id=1, source_target_pairs={{0,8},{4,12},{8,0},{12,4},{1,9},{5,13},{9,1},{13,5},{2,10},{6,14},... | collective-permute-start | bytes 3538952 | tf_op jit(solution)/shard_map/ppermute | solution.py:18
  183.4 13.7 %copy-start.4 = (bf16[256,384]{1,0:T(8,128)(2,1)}, bf16[256,384]{1,0:T(8,128)(2,1)S(1)}, u32[]{:S(2)}) copy-start(bf16[256,384]{1,0:T(8,128)(2,1)S(1)} %get-tuple-element.142.refs_0_) | copy-start | bytes 589828
  183.4 13.7 %copy-start.8 = (bf16[3072,384]{1,0:T(8,128)(2,1)}, bf16[3072,384]{1,0:T(8,128)(2,1)S(1)}, u32[]{:S(2)}) copy-start(bf16[3072,384]{1,0:T(8,128)(2,1)S(1)} %collective-permute-done.13.refs_8_.refs_6_) | copy-start | bytes 7077892
  183.5 13.7 %copy-start.9 = (bf16[3072,384]{1,0:T(8,128)(2,1)}, bf16[3072,384]{1,0:T(8,128)(2,1)S(1)}, u32[]{:S(2)}) copy-start(bf16[3072,384]{1,0:T(8,128)(2,1)S(1)} %collective-permute-done.14.refs_12_.refs_10_) | copy-start | bytes 7077892
  183.5 17.8 %collective-permute-start.15 = (bf16[256,384]{1,0:T(8,128)(2,1)S(1)}, bf16[256,384]{1,0:T(8,128)(2,1)S(1)}, u32[]{:S(2)}, u32[]{:S(2)}) collective-permute-start(bf16[256,384]{1,0:T(8,128)(2,1)S(1)} %get-tuple-element.126), channel_id=1, source_target_pairs={{0,2},{1,3},{2,0},{3,1},{4,6},{5,7},{6,4},{7,5},{8,10},{9,11},{10,... | collective-permute-start | bytes 589832 | tf_op jit(solution)/shard_map/ppermute | solution.py:33
  185.9 15.4 %collective-permute-start.16 = (bf16[256,384]{1,0:T(8,128)(2,1)S(1)}, bf16[256,384]{1,0:T(8,128)(2,1)S(1)}, u32[]{:S(2)}, u32[]{:S(2)}) collective-permute-start(bf16[256,384]{1,0:T(8,128)(2,1)S(1)} %get-tuple-element.127), channel_id=1, source_target_pairs={{0,1},{1,2},{2,3},{3,0},{4,5},{5,6},{6,7},{7,4},{8,9},{9,10},{10,1... | collective-permute-start | bytes 589832 | tf_op jit(solution)/shard_map/ppermute | solution.py:33
  188.1 13.2 %collective-permute-start.17 = (bf16[256,384]{1,0:T(8,128)(2,1)S(1)}, bf16[256,384]{1,0:T(8,128)(2,1)S(1)}, u32[]{:S(2)}, u32[]{:S(2)}) collective-permute-start(bf16[256,384]{1,0:T(8,128)(2,1)S(1)} %get-tuple-element.128), channel_id=1, source_target_pairs={{0,3},{1,0},{2,1},{3,2},{4,7},{5,4},{6,5},{7,6},{8,11},{9,8},{10,9... | collective-permute-start | bytes 589832 | tf_op jit(solution)/shard_map/ppermute | solution.py:33
  201.3 8.9 %collective-permute-start.23 = (bf16[1536,384]{1,0:T(8,128)(2,1)S(1)}, bf16[1536,384]{1,0:T(8,128)(2,1)S(1)}, u32[]{:S(2)}, u32[]{:S(2)}) collective-permute-start(bf16[1536,384]{1,0:T(8,128)(2,1)S(1)} %collective-permute-done.18.refs_10_.refs_8_), channel_id=1, source_target_pairs={{0,4},{4,0},{8,12},{12,8},{1,5},{5,1},{9,13},{13,9},{2,6},{6,2},{1... | collective-permute-start | bytes 3538952 | tf_op jit(solution)/shard_map/ppermute | solution.py:18
  203.0 7.3 %collective-permute-start.24 = (bf16[1536,384]{1,0:T(8,128)(2,1)S(1)}, bf16[1536,384]{1,0:T(8,128)(2,1)}, u32[]{:S(2)}, u32[]{:S(2)}) collective-permute-start(bf16[1536,384]{1,0:T(8,128)(2,1)S(1)} %collective-permute-done.19.refs_11_.refs_9_), channel_id=1, source_target_pairs={{0,4},{4,0},{8,12},{12,8},{1,5},{5,1},{9,13},{13,9},{2,6},{6,2},{1... | collective-permute-start | bytes 3538952 | tf_op jit(solution)/shard_map/ppermute | solution.py:18
  203.1 19.0 %collective-permute-start.20 = (bf16[256,384]{1,0:T(8,128)(2,1)S(1)}, bf16[256,384]{1,0:T(8,128)(2,1)S(1)}, u32[]{:S(2)}, u32[]{:S(2)}) collective-permute-start(bf16[256,384]{1,0:T(8,128)(2,1)S(1)} %get-tuple-element.131), channel_id=1, source_target_pairs={{0,2},{1,3},{2,0},{3,1},{4,6},{5,7},{6,4},{7,5},{8,10},{9,11},{10,... | collective-permute-start | bytes 589832 | tf_op jit(solution)/shard_map/ppermute | solution.py:33
  207.0 15.1 %collective-permute-start.21 = (bf16[256,384]{1,0:T(8,128)(2,1)S(1)}, bf16[256,384]{1,0:T(8,128)(2,1)S(1)}, u32[]{:S(2)}, u32[]{:S(2)}) collective-permute-start(bf16[256,384]{1,0:T(8,128)(2,1)S(1)} %get-tuple-element.132), channel_id=1, source_target_pairs={{0,1},{1,2},{2,3},{3,0},{4,5},{5,6},{6,7},{7,4},{8,9},{9,10},{10,1... | collective-permute-start | bytes 589832 | tf_op jit(solution)/shard_map/ppermute | solution.py:33
  207.7 14.4 %collective-permute-start.22 = (bf16[256,384]{1,0:T(8,128)(2,1)S(1)}, bf16[256,384]{1,0:T(8,128)(2,1)}, u32[]{:S(2)}, u32[]{:S(2)}) collective-permute-start(bf16[256,384]{1,0:T(8,128)(2,1)S(1)} %get-tuple-element.133), channel_id=1, source_target_pairs={{0,3},{1,0},{2,1},{3,2},{4,7},{5,4},{6,5},{7,6},{8,11},{9,8},{10,9... | collective-permute-start | bytes 589832 | tf_op jit(solution)/shard_map/ppermute | solution.py:33
  233.4 10.1 %collective-permute-start.25 = (bf16[128,256]{1,0:T(8,128)(2,1)}, bf16[128,256]{1,0:T(8,128)(2,1)S(1)}, u32[]{:S(2)}, u32[]{:S(2)}) collective-permute-start(bf16[128,256]{1,0:T(8,128)(2,1)} %get-tuple-element.148), channel_id=1, source_target_pairs={{2,4},{3,5},{6,8},{7,9},{10,12},{11,13},{4,2},{5,3},{8,6},{9,7},{1... | collective-permute-start | bytes 196616 | tf_op jit(solution)/shard_map/ppermute | solution.py:589
  (14 other events, 57.5 us)
Sparse Core Ops, SparseCore 0:
  9.6 82.3 all-gather.1

commit v8 on v7

--- a/solution.py
+++ b/solution.py
@@ -220,7 +220,7 @@
 def attend_kernel(plan, blocks, counts, place_ref, slots_ref, *refs):
     w_refs, before_ref, refs = refs[:blocks], refs[blocks], refs[blocks + 1 :]
     known, refs = refs[: 3 * len(counts)], refs[3 * len(counts) :]
-    queries, keys, values, sums, tokens, sems = refs[-6:]
+    queries, keys, values, done, tokens, sems = refs[-6:]
     devices = slots_ref.shape[0]
     sources, outs = refs[: -6 - devices], refs[-6 - devices : -6]
     start, rows = sum(counts), tokens.shape[0]
@@ -235,12 +235,13 @@
     queries[start:] = root_norm(proj[:, :HD])
     keys[start:] = root_norm(proj[:, HD : 2 * HD])
     values[start:, :HD] = proj[:, 2 * HD :].astype(jnp.bfloat16)
-    sums[:start] = before_ref[0]
-    sums[start:] = weigh(queries[start:], keys[:start], values[:start])
+    mixed = before_ref[0] + weigh(queries[:start], keys[start:], values[start:])
+    done[:start] = (mixed[:, :HD] / mixed[:, HD:]).astype(jnp.bfloat16)
+    mixed = weigh(queries[start:], keys[...], values[...])
+    done[start:] = (mixed[:, :HD] / mixed[:, HD:]).astype(jnp.bfloat16)
     for turn in range(devices):
         part = pl.ds(pl.multiple_of(slots_ref[turn] * rows, rows), rows)
-        mixed = sums[part] + weigh(queries[part], keys[start:], values[start:])
-        outs[turn][...] = (mixed[:, :HD] / mixed[:, HD:]).astype(jnp.bfloat16)
+        outs[turn][...] = done[part]
 
 
 def attend(place, slots, plan, sources, known, before, blocks, start, heads):
@@ -268,7 +269,7 @@
             pltpu.VMEM((length, HD), jnp.bfloat16),
             pltpu.VMEM((length, HD), jnp.bfloat16),
             pltpu.VMEM((length, 2 * HD), jnp.bfloat16),
-            pltpu.VMEM((length, 2 * HD), jnp.float32),
+            pltpu.VMEM((length, HD), jnp.bfloat16),
             pltpu.VMEM((rows, width), jnp.bfloat16),
             pltpu.SemaphoreType.DMA((1,)),
         ],
@@ -343,18 +344,38 @@
         )
         copies[p].start()
 
+    held = {}
+
     def store(p, cols, summed):
         copies[p].wait()
-        mixed[:, cols] += mod_ref[2:3, cols] * summed
+        values = mixed[:, cols] + mod_ref[2:3, cols] * summed
+        mixed[:, cols] = values
+        if p == 0:
+            held["base"] = jnp.mean(values, axis=-1, keepdims=True)
+        away = values - held["base"]
+        sums = (
+            jnp.sum(away, axis=-1, keepdims=True),
+            jnp.sum(away * away, axis=-1, keepdims=True),
+        )
+        held["sums"] = [a + b for a, b in zip(held.get("sums", (0.0, 0.0)), sums)]
 
     multiply(parts, offsets, starts_ref, rows_ref, sources, weights, sems, wide, store)
-    normed = layer_norm(mixed[...]) * (1.0 + mod_ref[4:5, :]) + mod_ref[3:4, :]
-    velocity = lax.dot_general(
-        normed.astype(jnp.bfloat16),
-        head_ref[...],
-        (((1,), (1,)), ((), ())),
-        preferred_element_type=jnp.float32,
-    ).T
+    total = width * count
+    shift = held["sums"][0] / total
+    scaling = lax.rsqrt(held["sums"][1] / total - shift * shift + 1e-06)
+    mean = held["base"] + shift
+    velocity = 0.0
+    for p in range(count):
+        cols = slice(p * width, (p + 1) * width)
+        normed = (mixed[:, cols] - mean) * scaling
+        normed = normed * (1.0 + mod_ref[4:5, cols]) + mod_ref[3:4, cols]
+        velocity += lax.dot_general(
+            normed.astype(jnp.bfloat16),
+            head_ref[:, cols],
+            (((1,), (1,)), ((), ())),
+            preferred_element_type=jnp.float32,
+        )
+    velocity = velocity.T
     channels = velocity.shape[0]
     base, weight = latent_ref[...], weight_ref[...]
     moved = (base + coef_ref[1] * velocity) * weight
@@ -522,20 +543,21 @@
     if not narrow:
         mine = lax.optimization_barrier((columns[0, 0], known[0]))[0]
         columns[near, 0] = swap(mine, "tile", near)
-    before = early(known, rows)
     columns = {key: [value] for key, value in columns.items()}
     diagonal = groups == 2 and len(far) == 1 and not narrow
     crossing = ()
     if diagonal:
         bit, half = far[0], columns[0, 0][0].shape[0] // 2
         crossing = (columns[bit, 0][0][:half], columns[0, 1][0][half:])
-    blocks_by, known, before, columns, crossing = lax.optimization_barrier(
-        (blocks_by, known, before, columns, crossing)
-    )
+    known, crossing = lax.optimization_barrier((known, crossing))
     late = {}
     if diagonal:
         late[bit, 1] = [turned(crossing[0], "group", 1), swap(crossing[1], "tile", bit)]
-    elif not narrow:
+    before = early(known, rows)
+    blocks_by, known, before, columns = lax.optimization_barrier(
+        (blocks_by, known, before, columns)
+    )
+    if not narrow and not diagonal:
         for turn in range(1, groups):
             for d in range(1, tiles):
                 if d & near == 0:

time: 253 us -> 253 us (level)
    ppermute x10, waiting for transfers between devices: 16.5 us -> 2.5 us  [swap(): return lax.ppermute(value, axis, [(i, i ^ bit) for i in range(count)])]
    ppermute x8, waiting for transfers between devices: 2.58 us -> 16.2 us  [turned(): lax.ppermute(value, axis, [(i, (i + turn) % count) for i in range(count)])]
where the time goes in v8:
time: 253 us; the launch traced here: 252 us
  waiting for transfers between devices  103 us (41%)
  Pallas kernels  65.8 us (26%)
  starting transfers between devices  45.9 us (18%)
  local copies, waits for them, and re-layouts  18.7 us (7%)
  between operations  15.2 us (6%)
  other arithmetic  3.42 us (1%)
    ppermute x1, waiting for transfers between devices, shards(): lax.ppermute(weight.astype(jnp.bfloat16), ('tile', 'seq'), joins)  63.6 us
    pallas_call x2, Pallas kernels, project(): pl.pallas_call(functools.partial(project_kernel, plan, len(blocks)), grid...  17.9 us
    ppermute x6, waiting for transfers between devices, hop(): lax.ppermute(blocks_by[way * (step - 1)], 'seq', step_pairs(devices, step...  17.8 us
    pallas_call x2, Pallas kernels, attend(): pl.pallas_call(functools.partial(attend_kernel, plan, len(blocks), counts...  16.3 us
    ppermute x8, waiting for transfers between devices, turned(): lax.ppermute(value, axis, [(i, (i + turn) % count) for i in range(count)])  16.2 us
    ppermute x8, starting transfers between devices, turned(): lax.ppermute(value, axis, [(i, (i + turn) % count) for i in range(count)])  15.6 us
    unnamed x38, local copies, waits for them, and re-layouts  11 us
    pallas_call x1, Pallas kernels, accumulate(): pl.pallas_call(functools.partial(finish_kernel, offsets, splits), in_spec...  10.8 us
  transfers between devices with their start and end apart: 27, of which 8 were waited for; matrix products, arithmetic and copies ran while one was open for 3% of the time, Pallas kernels for 22%

profile of v8, /device:TPU:1, one launch (start us, length us, event | category | flops | bytes accessed | tf_op | source)
XLA Modules:
  0.0 252.3 jit_solution(6758601208424631844)
XLA Ops:
  9.4 2.7 %collective-permute-start.1 = (bf16[768,2304]{1,0:T(8,128)(2,1)}, bf16[768,2304]{1,0:T(8,128)(2,1)}, u32[]{:S(2)}, u32[]{:S(2)}) collective-permute-start(bf16[768,2304]{1,0:T(8,128)(2,1)} %refs_0_.3), channel_id=1, source_target_pairs={{0,8},{4,12},{8,0},{12,4},{1,9},{5,13},{9,1},{13,5},{2,10},{6,14},... | collective-permute-start | bytes 10616840 | tf_op jit(solution)/shard_map/ppermute | solution.py:18
  12.7 4.5 %norm_in.1.refs_4_ = bf16[256,3072]{1,0:T(8,128)(2,1)} custom-call(s32[4]{0:T(128)} %pad_add_fusion.starts_ref, bf16[256,3072]{1,0:T(8,128)(2,1)} %bitcast.33, f32[5,3072]{1,0:T(8,128)} %refs_14_.1), custom_call_target="tpu_custom_call" | custom-call | tf_op jit(solution)/shard_map/norm_in/pallas_call | solution.py:78
  17.2 4.3 %collective-permute-start.3 = (bf16[256,3072]{1,0:T(8,128)(2,1)}, bf16[256,3072]{1,0:T(8,128)(2,1)}, u32[]{:S(2)}, u32[]{:S(2)}) collective-permute-start(bf16[256,3072]{1,0:T(8,128)(2,1)} %norm_in.1.refs_4_), channel_id=1, source_target_pairs={{0,1},{1,2},{2,3},{4,5},{5,6},{6,7},{8,9},{9,10},{10,11},{12,13},{... | collective-permute-start | bytes 4718600 | tf_op jit(solution)/shard_map/ppermute | solution.py:470
  23.4 4.6 %collective-permute-start.4 = (bf16[1,256]{1,0:T(2,128)(2,1)S(1)}, bf16[1,256]{1,0:T(2,128)(2,1)S(1)}, u32[]{:S(2)}, u32[]{:S(2)}) collective-permute-start(bf16[1,256]{1,0:T(2,128)(2,1)S(1)} %get-tuple-element.165), channel_id=1, source_target_pairs={{2,4},{3,5},{6,8},{7,9},{10,12},{11,13},{4,2},{5,3},{8,6},{9,7},{1... | collective-permute-start | bytes 1544 | tf_op jit(solution)/shard_map/ppermute | solution.py:455
  31.5 63.6 %collective-permute-done.4 = bf16[1,256]{1,0:T(2,128)(2,1)S(1)} collective-permute-done((bf16[1,256]{1,0:T(2,128)(2,1)S(1)}, bf16[1,256]{1,0:T(2,128)(2,1)S(1)}, u32[]{:S(2)}, u32[]{:S(2)}) %collective-permute-start.4) | collective-permute-done | bytes 544 | tf_op jit(solution)/shard_map/ppermute | solution.py:455
  95.2 1.3 collective-permute-start.6
  98.6 1.5 collective-permute-start.10
  100.0 1.6 collective-permute-done.5.refs_3_
  101.7 1.8 copy-done.6
  103.4 2.0 copy-done.1
  105.4 1.4 copy-done.3
  106.8 10.7 %project.2 = (bf16[6,512,128]{2,1,0:T(8,128)(2,1)S(1)}, bf16[6,512,128]{2,1,0:T(8,128)(2,1)S(1)}, bf16[6,512,128]{2,1,0:T(8,128)(2,1)S(1)}) custom-call(s32[1]{0:T(128)} %bitcast.18.place_ref, bf16[768,2304]{1,0:T(8,128)(2,1)S(1)} %copy-done.1, bf16[768,2304]{1,0:T(8,128)(2,1)} %collective-permute-done.refs_1_, ...), custom_call_target="tpu_custom_call" | custom-call | tf_op jit(solution)/shard_map/project/pallas_call | solution.py:152
  117.5 15.2 %collective-permute-done.6.refs_4_.refs_12_ = bf16[256,3072]{1,0:T(8,128)(2,1)S(1)} collective-permute-done((bf16[256,3072]{1,0:T(8,128)(2,1)S(1)}, bf16[256,3072]{1,0:T(8,128)(2,1)S(1)}, u32[]{:S(2)}, u32[]{:S(2)}) %collective-permute-start.6) | collective-permute-done | bytes 1572896 | tf_op jit(solution)/shard_map/ppermute | solution.py:470
  136.0 14.0 %collective-permute-done.11.refs_6_.refs_4_ = bf16[3072,384]{1,0:T(8,128)(2,1)} collective-permute-done((bf16[3072,384]{1,0:T(8,128)(2,1)}, bf16[3072,384]{1,0:T(8,128)(2,1)}, u32[]{:S(2)}, u32[]{:S(2)}) %collective-permute-start.11) | collective-permute-done | bytes 2359328 | tf_op jit(solution)/shard_map/ppermute | solution.py:33
  150.0 2.4 slice.17
  152.4 2.4 slice.16
  154.8 7.2 %project.3 = (bf16[6,256,128]{2,1,0:T(8,128)(2,1)S(1)}, bf16[6,256,128]{2,1,0:T(8,128)(2,1)S(1)}, bf16[6,256,128]{2,1,0:T(8,128)(2,1)S(1)}) custom-call(s32[1]{0:T(128)} %bitcast.18.place_ref, bf16[768,2304]{1,0:T(8,128)(2,1)S(1)} %copy-done.1, bf16[768,2304]{1,0:T(8,128)(2,1)} %collective-permute-done.refs_1_, ...), custom_call_target="tpu_custom_call" | custom-call | tf_op jit(solution)/shard_map/project/pallas_call | solution.py:152
  162.1 5.5 %early.1.refs_4_ = f32[6,768,256]{2,1,0:T(8,128)S(1)} custom-call(bf16[6,512,128]{2,1,0:T(8,128)(2,1)S(1)} %get-tuple-element.112.refs_0_.refs_5_, bf16[6,512,128]{2,1,0:T(8,128)(2,1)S(1)} %get-tuple-element.113.refs_1_.refs_6_, bf16[6,512,128]{2,1,0:T(8,128)(2,1)S(1)} %get-tuple-element.114.refs_2_.refs_7_, ...), custom_call_target="tpu_custom_call" | custom-call | tf_op jit(solution)/shard_map/early/pallas_call | solution.py:202
  167.6 2.2 copy-done.2
  169.8 2.6 %collective-permute-done.8.refs_11_ = bf16[256,3072]{1,0:T(8,128)(2,1)S(1)} collective-permute-done((bf16[256,3072]{1,0:T(8,128)(2,1)S(1)}, bf16[256,3072]{1,0:T(8,128)(2,1)S(1)}, u32[]{:S(2)}, u32[]{:S(2)}) %collective-permute-start.8) | collective-permute-done | bytes 1572896 | tf_op jit(solution)/shard_map/ppermute | solution.py:470
  175.5 8.1 %attend.2 = (bf16[256,384]{1,0:T(8,128)(2,1)S(1)}, bf16[256,384]{1,0:T(8,128)(2,1)S(1)}, bf16[256,384]{1,0:T(8,128)(2,1)S(1)}, bf16[256,384]{1,0:T(8,128)(2,1)S(1)}) custom-call(s32[1]{0:T(128)} %bitcast.18.place_ref, s32[4]{0:T(128)S(1)} %dynamic-slice_bitcast_fusion.slots_ref, bf16[768,2304]{1,0:T(8,128)(2,1)} %refs_0_.3, ...), custom_call_target="tpu_custom_call" | custom-call | tf_op jit(solution)/shard_map/attend/pallas_call | solution.py:254
  183.7 2.5 collective-permute-start.15
  186.1 2.2 collective-permute-start.16
  189.4 8.2 %attend.3 = (bf16[256,384]{1,0:T(8,128)(2,1)S(1)}, bf16[256,384]{1,0:T(8,128)(2,1)S(1)}, bf16[256,384]{1,0:T(8,128)(2,1)S(1)}, bf16[256,384]{1,0:T(8,128)(2,1)S(1)}) custom-call(s32[1]{0:T(128)} %bitcast.18.place_ref, s32[4]{0:T(128)S(1)} %dynamic-slice_bitcast_fusion.slots_ref, bf16[768,2304]{1,0:T(8,128)(2,1)} %refs_0_.3, ...), custom_call_target="tpu_custom_call" | custom-call | tf_op jit(solution)/shard_map/attend/pallas_call | solution.py:254
  198.3 2.1 collective-permute-done.18.refs_10_.refs_8_
  201.3 1.7 collective-permute-start.23
  203.1 4.1 %collective-permute-start.20 = (bf16[256,384]{1,0:T(8,128)(2,1)S(1)}, bf16[256,384]{1,0:T(8,128)(2,1)S(1)}, u32[]{:S(2)}, u32[]{:S(2)}) collective-permute-start(bf16[256,384]{1,0:T(8,128)(2,1)S(1)} %get-tuple-element.143), channel_id=1, source_target_pairs={{0,2},{1,3},{2,0},{3,1},{4,6},{5,7},{6,4},{7,5},{8,10},{9,11},{10,... | collective-permute-start | bytes 589832 | tf_op jit(solution)/shard_map/ppermute | solution.py:33
  207.7 2.8 %collective-permute-start.22 = (bf16[256,384]{1,0:T(8,128)(2,1)S(1)}, bf16[256,384]{1,0:T(8,128)(2,1)}, u32[]{:S(2)}, u32[]{:S(2)}) collective-permute-start(bf16[256,384]{1,0:T(8,128)(2,1)S(1)} %get-tuple-element.145), channel_id=1, source_target_pairs={{0,3},{1,0},{2,1},{3,2},{4,7},{5,4},{6,5},{7,6},{8,11},{9,8},{10,9... | collective-permute-start | bytes 589832 | tf_op jit(solution)/shard_map/ppermute | solution.py:33
  211.5 10.8 %add_parts.1.refs_13_ = f32[256,3072]{1,0:T(8,128)} custom-call(s32[8]{0:T(128)} %stack.79.starts_ref, s32[4]{0:T(128)} %pad_add_fusion.1.rows_ref, bf16[256,384]{1,0:T(8,128)(2,1)} %copy-done.4, bf16[256,384]{1,0:T(8,128)(2,1)} %copy-done.5, bf16[256,384]{1,0:T(8,128)(2,1)} %copy-done.13, bf16[256,384]{1,0:T(8,128)(2,1)} %copy-done.14, ...), custom_call_target="tpu_custom_call" | custom-call | tf_op jit(solution)/shard_map/add_parts/pallas_call | solution.py:408
  223.1 10.8 %finish.1 = (f32[128,256]{1,0:T(8,128)}, bf16[128,256]{1,0:T(8,128)(2,1)}) custom-call(s32[8]{0:T(128)} %stack.79.starts_ref, s32[4]{0:T(128)} %pad_add_fusion.1.rows_ref, f32[2]{0:T(128)} %pad_maximum_fusion.coef_ref, bf16[256,384]{1,0:T(8,128)(2,1)} %copy-done.16, bf16[256,384]{1,0:T(8,128)(2,1)} %copy-done.17, ...), custom_call_target="tpu_custom_call" | custom-call | tf_op jit(solution)/shard_map/finish/pallas_call | solution.py:420
  233.9 6.8 %collective-permute-start.25 = (bf16[128,256]{1,0:T(8,128)(2,1)}, bf16[128,256]{1,0:T(8,128)(2,1)S(1)}, u32[]{:S(2)}, u32[]{:S(2)}) collective-permute-start(bf16[128,256]{1,0:T(8,128)(2,1)} %get-tuple-element.160), channel_id=1, source_target_pairs={{2,4},{3,5},{6,8},{7,9},{10,12},{11,13},{4,2},{5,3},{8,6},{9,7},{1... | collective-permute-start | bytes 196616 | tf_op jit(solution)/shard_map/ppermute | solution.py:611
  240.6 3.2 %collective-permute-done.25 = bf16[128,256]{1,0:T(8,128)(2,1)S(1)} collective-permute-done((bf16[128,256]{1,0:T(8,128)(2,1)}, bf16[128,256]{1,0:T(8,128)(2,1)S(1)}, u32[]{:S(2)}, u32[]{:S(2)}) %collective-permute-start.25) | collective-permute-done | bytes 65568 | tf_op jit(solution)/shard_map/ppermute | solution.py:611
  (81 shorter events, 22.4 us)
Async XLA Ops:
  7.2 87.9 %all-gather.2.cloned.1.call-start = ((), (), s32[]{:S(2)}) async-start(), calls=%async_computation | async-start | bytes 2949120 | tf_op jit(solution)/shard_map/all_gather | solution.py:482
  9.3 85.8 %collective-permute-start = (bf16[768,2304]{1,0:T(8,128)(2,1)}, bf16[768,2304]{1,0:T(8,128)(2,1)}, u32[]{:S(2)}, u32[]{:S(2)}) collective-permute-start(bf16[768,2304]{1,0:T(8,128)(2,1)} %refs_0_.3), channel_id=1, source_target_pairs={{0,4},{4,0},{8,12},{12,8},{1,5},{5,1},{9,13},{13,9},{2,6},{6,2},{1... | collective-permute-start | bytes 10616840 | tf_op jit(solution)/shard_map/ppermute | solution.py:18
  9.4 85.7 %collective-permute-start.1 = (bf16[768,2304]{1,0:T(8,128)(2,1)}, bf16[768,2304]{1,0:T(8,128)(2,1)}, u32[]{:S(2)}, u32[]{:S(2)}) collective-permute-start(bf16[768,2304]{1,0:T(8,128)(2,1)} %refs_0_.3), channel_id=1, source_target_pairs={{0,8},{4,12},{8,0},{12,4},{1,9},{5,13},{9,1},{13,5},{2,10},{6,14},... | collective-permute-start | bytes 10616840 | tf_op jit(solution)/shard_map/ppermute | solution.py:18
  12.7 10.1 %copy-start.18 = (s32[1,256]{1,0:T(1,128)S(1)}, s32[1,256]{1,0:T(1,128)}, u32[]{:S(2)}) copy-start(s32[1,256]{1,0:T(1,128)} %param.15) | copy-start | bytes 3076
  17.2 77.9 %collective-permute-start.3 = (bf16[256,3072]{1,0:T(8,128)(2,1)}, bf16[256,3072]{1,0:T(8,128)(2,1)}, u32[]{:S(2)}, u32[]{:S(2)}) collective-permute-start(bf16[256,3072]{1,0:T(8,128)(2,1)} %norm_in.1.refs_4_), channel_id=1, source_target_pairs={{0,1},{1,2},{2,3},{4,5},{5,6},{6,7},{8,9},{9,10},{10,11},{12,13},{... | collective-permute-start | bytes 4718600 | tf_op jit(solution)/shard_map/ppermute | solution.py:470
  21.5 73.6 %collective-permute-start.2 = (bf16[256,3072]{1,0:T(8,128)(2,1)}, bf16[256,3072]{1,0:T(8,128)(2,1)S(1)}, u32[]{:S(2)}, u32[]{:S(2)}) collective-permute-start(bf16[256,3072]{1,0:T(8,128)(2,1)} %norm_in.1.refs_4_), channel_id=1, source_target_pairs={{1,0},{2,1},{3,2},{5,4},{6,5},{7,6},{9,8},{10,9},{11,10},{13,12},{... | collective-permute-start | bytes 4718600 | tf_op jit(solution)/shard_map/ppermute | solution.py:470
  23.4 71.7 %collective-permute-start.4 = (bf16[1,256]{1,0:T(2,128)(2,1)S(1)}, bf16[1,256]{1,0:T(2,128)(2,1)S(1)}, u32[]{:S(2)}, u32[]{:S(2)}) collective-permute-start(bf16[1,256]{1,0:T(2,128)(2,1)S(1)} %get-tuple-element.165), channel_id=1, source_target_pairs={{2,4},{3,5},{6,8},{7,9},{10,12},{11,13},{4,2},{5,3},{8,6},{9,7},{1... | collective-permute-start | bytes 1544 | tf_op jit(solution)/shard_map/ppermute | solution.py:455
  95.2 6.5 %collective-permute-start.5 = (bf16[768,2304]{1,0:T(8,128)(2,1)}, bf16[768,2304]{1,0:T(8,128)(2,1)S(1)}, u32[]{:S(2)}, u32[]{:S(2)}) collective-permute-start(bf16[768,2304]{1,0:T(8,128)(2,1)} %collective-permute-done.1.refs_2_), channel_id=1, source_target_pairs={{0,4},{4,0},{8,12},{12,8},{1,5},{5,1},{9,13},{13,9},{2,6},{6,2},{1... | collective-permute-start | bytes 10616840 | tf_op jit(solution)/shard_map/ppermute | solution.py:18
  95.2 37.5 %collective-permute-start.6 = (bf16[256,3072]{1,0:T(8,128)(2,1)S(1)}, bf16[256,3072]{1,0:T(8,128)(2,1)S(1)}, u32[]{:S(2)}, u32[]{:S(2)}) collective-permute-start(bf16[256,3072]{1,0:T(8,128)(2,1)S(1)} %collective-permute-done.2.refs_5_), channel_id=1, source_target_pairs={{1,0},{2,1},{5,4},{6,5},{9,8},{10,9},{13,12},{14,13},{17,16},{18,1... | collective-permute-start | bytes 4718600 | tf_op jit(solution)/shard_map/ppermute | solution.py:470
  96.5 36.2 %collective-permute-start.7 = (bf16[256,3072]{1,0:T(8,128)(2,1)}, bf16[256,3072]{1,0:T(8,128)(2,1)S(1)}, u32[]{:S(2)}, u32[]{:S(2)}) collective-permute-start(bf16[256,3072]{1,0:T(8,128)(2,1)} %collective-permute-done.3.refs_6_), channel_id=1, source_target_pairs={{1,2},{2,3},{5,6},{6,7},{9,10},{10,11},{13,14},{14,15},{17,18},{18... | collective-permute-start | bytes 4718600 | tf_op jit(solution)/shard_map/ppermute | solution.py:470
  97.3 52.7 %collective-permute-start.11 = (bf16[3072,384]{1,0:T(8,128)(2,1)}, bf16[3072,384]{1,0:T(8,128)(2,1)}, u32[]{:S(2)}, u32[]{:S(2)}) collective-permute-start(bf16[3072,384]{1,0:T(8,128)(2,1)} %all-gather.2.cloned.1.call-done.refs_5_.refs_3_), channel_id=1, source_target_pairs={{0,16},{16,0},{1,17},{17,1},{2,18},{18,2},{3,19},{19,3},{4,20},{20... | collective-permute-start | bytes 7077896 | tf_op jit(solution)/shard_map/ppermute | solution.py:33
  98.6 53.9 %collective-permute-start.10 = (bf16[3072,384]{1,0:T(8,128)(2,1)}, bf16[3072,384]{1,0:T(8,128)(2,1)}, u32[]{:S(2)}, u32[]{:S(2)}) collective-permute-start(bf16[3072,384]{1,0:T(8,128)(2,1)} %all-gather.2.cloned.1.call-done.refs_5_.refs_3_), channel_id=1, source_target_pairs={{0,8},{4,12},{8,0},{12,4},{1,9},{5,13},{9,1},{13,5},{2,10},{6,14},... | collective-permute-start | bytes 7077896 | tf_op jit(solution)/shard_map/ppermute | solution.py:18
  106.8 25.9 %copy-start.7 = (bf16[3072,384]{1,0:T(8,128)(2,1)S(1)}, bf16[3072,384]{1,0:T(8,128)(2,1)}, u32[]{:S(2)}) copy-start(bf16[3072,384]{1,0:T(8,128)(2,1)} %all-gather.2.cloned.1.call-done.refs_5_.refs_3_) | copy-start | bytes 7077892
  132.7 39.7 %collective-permute-start.12 = (bf16[3072,384]{1,0:T(8,128)(2,1)S(1)}, bf16[3072,384]{1,0:T(8,128)(2,1)}, u32[]{:S(2)}, u32[]{:S(2)}) collective-permute-start(bf16[3072,384]{1,0:T(8,128)(2,1)S(1)} %copy-done.7), channel_id=1, source_target_pairs={{0,4},{4,0},{8,12},{12,8},{1,5},{5,1},{9,13},{13,9},{2,6},{6,2},{1... | collective-permute-start | bytes 7077896 | tf_op jit(solution)/shard_map/ppermute | solution.py:18
  133.9 38.5 %collective-permute-start.8 = (bf16[256,3072]{1,0:T(8,128)(2,1)S(1)}, bf16[256,3072]{1,0:T(8,128)(2,1)S(1)}, u32[]{:S(2)}, u32[]{:S(2)}) collective-permute-start(bf16[256,3072]{1,0:T(8,128)(2,1)S(1)} %collective-permute-done.6.refs_4_.refs_12_), channel_id=1, source_target_pairs={{1,0},{5,4},{9,8},{13,12},{17,16},{21,20},{25,24},{29,28}} | collective-permute-start | bytes 4718600 | tf_op jit(solution)/shard_map/ppermute | solution.py:470
  135.2 37.2 %collective-permute-start.9 = (bf16[256,3072]{1,0:T(8,128)(2,1)S(1)}, bf16[256,3072]{1,0:T(8,128)(2,1)S(1)}, u32[]{:S(2)}, u32[]{:S(2)}) collective-permute-start(bf16[256,3072]{1,0:T(8,128)(2,1)S(1)} %collective-permute-done.7.refs_6_.refs_13_), channel_id=1, source_target_pairs={{2,3},{6,7},{10,11},{14,15},{18,19},{22,23},{26,27},{30,31}} | collective-permute-start | bytes 4718600 | tf_op jit(solution)/shard_map/ppermute | solution.py:470
  172.5 11.2 %collective-permute-start.13 = (bf16[3072,384]{1,0:T(8,128)(2,1)}, bf16[3072,384]{1,0:T(8,128)(2,1)S(1)}, u32[]{:S(2)}, u32[]{:S(2)}) collective-permute-start(bf16[3072,384]{1,0:T(8,128)(2,1)} %collective-permute-done.11.refs_6_.refs_4_), channel_id=1, source_target_pairs={{0,4},{4,0},{8,12},{12,8},{1,5},{5,1},{9,13},{13,9},{2,6},{6,2},{1... | collective-permute-start | bytes 7077896 | tf_op jit(solution)/shard_map/ppermute | solution.py:18
  173.0 10.6 %collective-permute-start.14 = (bf16[3072,384]{1,0:T(8,128)(2,1)}, bf16[3072,384]{1,0:T(8,128)(2,1)S(1)}, u32[]{:S(2)}, u32[]{:S(2)}) collective-permute-start(bf16[3072,384]{1,0:T(8,128)(2,1)} %collective-permute-done.10.refs_9_.refs_7_), channel_id=1, source_target_pairs={{0,4},{4,0},{8,12},{12,8},{1,5},{5,1},{9,13},{13,9},{2,6},{6,2},{1... | collective-permute-start | bytes 7077896 | tf_op jit(solution)/shard_map/ppermute | solution.py:18
  173.1 27.3 %collective-permute-start.18 = (bf16[1536,384]{1,0:T(8,128)(2,1)}, bf16[1536,384]{1,0:T(8,128)(2,1)S(1)}, u32[]{:S(2)}, u32[]{:S(2)}) collective-permute-start(bf16[1536,384]{1,0:T(8,128)(2,1)} %slice.16), channel_id=1, source_target_pairs={{0,16},{16,0},{1,17},{17,1},{2,18},{18,2},{3,19},{19,3},{4,20},{20... | collective-permute-start | bytes 3538952 | tf_op jit(solution)/shard_map/ppermute | solution.py:33
  174.3 27.0 %collective-permute-start.19 = (bf16[1536,384]{1,0:T(8,128)(2,1)}, bf16[1536,384]{1,0:T(8,128)(2,1)S(1)}, u32[]{:S(2)}, u32[]{:S(2)}) collective-permute-start(bf16[1536,384]{1,0:T(8,128)(2,1)} %slice.17), channel_id=1, source_target_pairs={{0,8},{4,12},{8,0},{12,4},{1,9},{5,13},{9,1},{13,5},{2,10},{6,14},... | collective-permute-start | bytes 3538952 | tf_op jit(solution)/shard_map/ppermute | solution.py:18
  183.6 14.0 %copy-start.4 = (bf16[256,384]{1,0:T(8,128)(2,1)}, bf16[256,384]{1,0:T(8,128)(2,1)S(1)}, u32[]{:S(2)}) copy-start(bf16[256,384]{1,0:T(8,128)(2,1)S(1)} %get-tuple-element.154.refs_0_) | copy-start | bytes 589828
  183.6 14.0 %copy-start.8 = (bf16[3072,384]{1,0:T(8,128)(2,1)}, bf16[3072,384]{1,0:T(8,128)(2,1)S(1)}, u32[]{:S(2)}) copy-start(bf16[3072,384]{1,0:T(8,128)(2,1)S(1)} %collective-permute-done.13.refs_8_.refs_6_) | copy-start | bytes 7077892
  183.6 13.9 %copy-start.9 = (bf16[3072,384]{1,0:T(8,128)(2,1)}, bf16[3072,384]{1,0:T(8,128)(2,1)S(1)}, u32[]{:S(2)}) copy-start(bf16[3072,384]{1,0:T(8,128)(2,1)S(1)} %collective-permute-done.14.refs_12_.refs_10_) | copy-start | bytes 7077892
  183.7 17.7 %collective-permute-start.15 = (bf16[256,384]{1,0:T(8,128)(2,1)S(1)}, bf16[256,384]{1,0:T(8,128)(2,1)S(1)}, u32[]{:S(2)}, u32[]{:S(2)}) collective-permute-start(bf16[256,384]{1,0:T(8,128)(2,1)S(1)} %get-tuple-element.138), channel_id=1, source_target_pairs={{0,2},{1,3},{2,0},{3,1},{4,6},{5,7},{6,4},{7,5},{8,10},{9,11},{10,... | collective-permute-start | bytes 589832 | tf_op jit(solution)/shard_map/ppermute | solution.py:33
  186.1 15.2 %collective-permute-start.16 = (bf16[256,384]{1,0:T(8,128)(2,1)S(1)}, bf16[256,384]{1,0:T(8,128)(2,1)S(1)}, u32[]{:S(2)}, u32[]{:S(2)}) collective-permute-start(bf16[256,384]{1,0:T(8,128)(2,1)S(1)} %get-tuple-element.139), channel_id=1, source_target_pairs={{0,1},{1,2},{2,3},{3,0},{4,5},{5,6},{6,7},{7,4},{8,9},{9,10},{10,1... | collective-permute-start | bytes 589832 | tf_op jit(solution)/shard_map/ppermute | solution.py:33
  188.3 13.0 %collective-permute-start.17 = (bf16[256,384]{1,0:T(8,128)(2,1)S(1)}, bf16[256,384]{1,0:T(8,128)(2,1)S(1)}, u32[]{:S(2)}, u32[]{:S(2)}) collective-permute-start(bf16[256,384]{1,0:T(8,128)(2,1)S(1)} %get-tuple-element.140), channel_id=1, source_target_pairs={{0,3},{1,0},{2,1},{3,2},{4,7},{5,4},{6,5},{7,6},{8,11},{9,8},{10,9... | collective-permute-start | bytes 589832 | tf_op jit(solution)/shard_map/ppermute | solution.py:33
  201.3 9.1 %collective-permute-start.23 = (bf16[1536,384]{1,0:T(8,128)(2,1)S(1)}, bf16[1536,384]{1,0:T(8,128)(2,1)S(1)}, u32[]{:S(2)}, u32[]{:S(2)}) collective-permute-start(bf16[1536,384]{1,0:T(8,128)(2,1)S(1)} %collective-permute-done.18.refs_10_.refs_8_), channel_id=1, source_target_pairs={{0,4},{4,0},{8,12},{12,8},{1,5},{5,1},{9,13},{13,9},{2,6},{6,2},{1... | collective-permute-start | bytes 3538952 | tf_op jit(solution)/shard_map/ppermute | solution.py:18
  203.0 7.5 %collective-permute-start.24 = (bf16[1536,384]{1,0:T(8,128)(2,1)S(1)}, bf16[1536,384]{1,0:T(8,128)(2,1)}, u32[]{:S(2)}, u32[]{:S(2)}) collective-permute-start(bf16[1536,384]{1,0:T(8,128)(2,1)S(1)} %collective-permute-done.19.refs_11_.refs_9_), channel_id=1, source_target_pairs={{0,4},{4,0},{8,12},{12,8},{1,5},{5,1},{9,13},{13,9},{2,6},{6,2},{1... | collective-permute-start | bytes 3538952 | tf_op jit(solution)/shard_map/ppermute | solution.py:18
  203.1 19.2 %collective-permute-start.20 = (bf16[256,384]{1,0:T(8,128)(2,1)S(1)}, bf16[256,384]{1,0:T(8,128)(2,1)S(1)}, u32[]{:S(2)}, u32[]{:S(2)}) collective-permute-start(bf16[256,384]{1,0:T(8,128)(2,1)S(1)} %get-tuple-element.143), channel_id=1, source_target_pairs={{0,2},{1,3},{2,0},{3,1},{4,6},{5,7},{6,4},{7,5},{8,10},{9,11},{10,... | collective-permute-start | bytes 589832 | tf_op jit(solution)/shard_map/ppermute | solution.py:33
  207.2 15.1 %collective-permute-start.21 = (bf16[256,384]{1,0:T(8,128)(2,1)S(1)}, bf16[256,384]{1,0:T(8,128)(2,1)S(1)}, u32[]{:S(2)}, u32[]{:S(2)}) collective-permute-start(bf16[256,384]{1,0:T(8,128)(2,1)S(1)} %get-tuple-element.144), channel_id=1, source_target_pairs={{0,1},{1,2},{2,3},{3,0},{4,5},{5,6},{6,7},{7,4},{8,9},{9,10},{10,1... | collective-permute-start | bytes 589832 | tf_op jit(solution)/shard_map/ppermute | solution.py:33
  207.7 14.7 %collective-permute-start.22 = (bf16[256,384]{1,0:T(8,128)(2,1)S(1)}, bf16[256,384]{1,0:T(8,128)(2,1)}, u32[]{:S(2)}, u32[]{:S(2)}) collective-permute-start(bf16[256,384]{1,0:T(8,128)(2,1)S(1)} %get-tuple-element.145), channel_id=1, source_target_pairs={{0,3},{1,0},{2,1},{3,2},{4,7},{5,4},{6,5},{7,6},{8,11},{9,8},{10,9... | collective-permute-start | bytes 589832 | tf_op jit(solution)/shard_map/ppermute | solution.py:33
  233.9 10.0 %collective-permute-start.25 = (bf16[128,256]{1,0:T(8,128)(2,1)}, bf16[128,256]{1,0:T(8,128)(2,1)S(1)}, u32[]{:S(2)}, u32[]{:S(2)}) collective-permute-start(bf16[128,256]{1,0:T(8,128)(2,1)} %get-tuple-element.160), channel_id=1, source_target_pairs={{2,4},{3,5},{6,8},{7,9},{10,12},{11,13},{4,2},{5,3},{8,6},{9,7},{1... | collective-permute-start | bytes 196616 | tf_op jit(solution)/shard_map/ppermute | solution.py:611
  (14 other events, 58.5 us)
Sparse Core Ops, SparseCore 0:
  9.6 82.3 all-gather.1

commit v9 on v8

--- a/solution.py
+++ b/solution.py
@@ -217,31 +217,34 @@
     )(*(value for three in known for value in three))
 
 
-def attend_kernel(plan, blocks, counts, place_ref, slots_ref, *refs):
+def attend_kernel(plan, blocks, counts, head, heads, place_ref, slots_ref, *refs):
     w_refs, before_ref, refs = refs[:blocks], refs[blocks], refs[blocks + 1 :]
     known, refs = refs[: 3 * len(counts)], refs[3 * len(counts) :]
     queries, keys, values, done, tokens, sems = refs[-6:]
     devices = slots_ref.shape[0]
     sources, outs = refs[: -6 - devices], refs[-6 - devices : -6]
     start, rows = sum(counts), tokens.shape[0]
-
-    @pl.when(pl.program_id(0) == 0)
-    def _():
-        values[:, HD:] = jnp.ones((start + rows, HD), jnp.bfloat16)
-        load_all(place_ref[0], plan, sources, tokens, sems)
-
-    proj = product(tokens, w_refs)
-    gather_known(known, counts, queries, keys, values)
-    queries[start:] = root_norm(proj[:, :HD])
-    keys[start:] = root_norm(proj[:, HD : 2 * HD])
-    values[start:, :HD] = proj[:, 2 * HD :].astype(jnp.bfloat16)
-    mixed = before_ref[0] + weigh(queries[:start], keys[start:], values[start:])
-    done[:start] = (mixed[:, :HD] / mixed[:, HD:]).astype(jnp.bfloat16)
-    mixed = weigh(queries[start:], keys[...], values[...])
-    done[start:] = (mixed[:, :HD] / mixed[:, HD:]).astype(jnp.bfloat16)
-    for turn in range(devices):
-        part = pl.ds(pl.multiple_of(slots_ref[turn] * rows, rows), rows)
-        outs[turn][...] = done[part]
+    values[:, HD:] = jnp.ones((start + rows, HD), jnp.bfloat16)
+    load_all(place_ref[0], plan, sources, tokens, sems)
+    for h in range(heads):
+        cols = slice((head + h) * 3 * HD, (head + h + 1) * 3 * HD)
+        proj = product(tokens, [w_ref.at[:, cols] for w_ref in w_refs])
+        at = 0
+        for n, count in enumerate(counts):
+            queries[at : at + count] = known[3 * n][head + h]
+            keys[at : at + count] = known[3 * n + 1][head + h]
+            values[at : at + count, :HD] = known[3 * n + 2][head + h]
+            at += count
+        queries[start:] = root_norm(proj[:, :HD])
+        keys[start:] = root_norm(proj[:, HD : 2 * HD])
+        values[start:, :HD] = proj[:, 2 * HD :].astype(jnp.bfloat16)
+        mixed = before_ref[head + h] + weigh(queries[:start], keys[start:], values[start:])
+        done[:start] = (mixed[:, :HD] / mixed[:, HD:]).astype(jnp.bfloat16)
+        mixed = weigh(queries[start:], keys[...], values[...])
+        done[start:] = (mixed[:, :HD] / mixed[:, HD:]).astype(jnp.bfloat16)
+        for turn in range(devices):
+            part = pl.ds(pl.multiple_of(slots_ref[turn] * rows, rows), rows)
+            outs[turn][:, h * HD : (h + 1) * HD] = done[part]
 
 
 def attend(place, slots, plan, sources, known, before, blocks, start, heads):
@@ -250,20 +253,14 @@
     counts = [three[0].shape[1] for three in known]
     length = rows + sum(counts)
     smem = pl.BlockSpec(memory_space=pltpu.SMEM)
+    vmem = pl.BlockSpec(memory_space=pltpu.VMEM)
     out = jax.ShapeDtypeStruct((rows, heads * HD), jnp.bfloat16)
     return pl.pallas_call(
-        functools.partial(attend_kernel, plan, len(blocks), counts),
-        grid=(heads,),
+        functools.partial(attend_kernel, plan, len(blocks), counts, start, heads),
         in_specs=[smem, smem]
-        + [pl.BlockSpec((width // len(blocks), 3 * HD), lambda h: (0, start + h))] * len(blocks)
-        + [pl.BlockSpec((1, length - rows, 2 * HD), lambda h: (start + h, 0, 0))]
-        + [
-            pl.BlockSpec((1, count, HD), lambda h: (start + h, 0, 0))
-            for count in counts
-            for _ in range(3)
-        ]
+        + [vmem] * (len(blocks) + 1 + 3 * len(counts))
         + [pl.BlockSpec(memory_space=pl.ANY)] * len(sources),
-        out_specs=[pl.BlockSpec((rows, HD), lambda h: (0, h))] * devices,
+        out_specs=[vmem] * devices,
         out_shape=[out] * devices,
         scratch_shapes=[
             pltpu.VMEM((length, HD), jnp.bfloat16),
@@ -273,7 +270,7 @@
             pltpu.VMEM((rows, width), jnp.bfloat16),
             pltpu.SemaphoreType.DMA((1,)),
         ],
-        compiler_params=pltpu.CompilerParams(vmem_limit_bytes=42 * MIB),
+        compiler_params=pltpu.CompilerParams(vmem_limit_bytes=36 * MIB),
         name="attend",
     )(place, slots, *blocks, before, *(value for three in known for value in three), *sources)
 
@@ -333,22 +330,13 @@
     parts = refs[: len(offsets)]
     sources, refs = split_refs(refs[len(offsets) :], splits)
     before_ref, mod_ref, head_ref, latent_ref, weight_ref, out_ref, sent_ref = refs[:7]
-    weights, wide, sems, mixed, extra = refs[7:]
+    weights, wide, sems, mixed = refs[7:]
     count = len(splits)
     width = weights.shape[2]
-    copies = []
-    for p in range(count):
-        cols = pl.ds(pl.multiple_of(starts_ref[p], HD), width)
-        copies.append(
-            pltpu.make_async_copy(before_ref.at[:, cols], mixed.at[:, cols], extra.at[p])
-        )
-        copies[p].start()
-
     held = {}
 
     def store(p, cols, summed):
-        copies[p].wait()
-        values = mixed[:, cols] + mod_ref[2:3, cols] * summed
+        values = before_ref[:, cols] + mod_ref[2:3, cols] * summed
         mixed[:, cols] = values
         if p == 0:
             held["base"] = jnp.mean(values, axis=-1, keepdims=True)
@@ -401,7 +389,7 @@
         pltpu.SemaphoreType.DMA((count, len(parts))),
     ]
     params = dict(
-        compiler_params=pltpu.CompilerParams(vmem_limit_bytes=60 * MIB),
+        compiler_params=pltpu.CompilerParams(vmem_limit_bytes=52 * MIB),
     )
     if last is None:
         aliased = before.dtype == jnp.float32
@@ -419,14 +407,14 @@
     channels = head.shape[0]
     return pl.pallas_call(
         functools.partial(finish_kernel, offsets, splits),
-        in_specs=[smem] * 3 + [vmem] * len(parts) + [hbm] * (len(pieces) + 1) + [vmem] * 4,
+        in_specs=[smem] * 3 + [vmem] * len(parts) + [hbm] * len(pieces) + [vmem] * 5,
         out_specs=[vmem, vmem],
         out_shape=[
             jax.ShapeDtypeStruct((2 * channels, rows), jnp.float32),
             jax.ShapeDtypeStruct((2 * channels, rows), jnp.bfloat16),
         ],
         scratch_shapes=scratch
-        + [pltpu.VMEM((rows, width), jnp.float32), pltpu.SemaphoreType.DMA((count,))],
+        + [pltpu.VMEM((rows, width), jnp.float32)],
         name="finish",
         **params,
     )(starts, firsts, coef, *parts, *pieces, before, modulation, head, latent, weight)

time: 253 us -> 255 us (level)
  local copies, waits for them, and re-layouts: 18.7 us -> 23 us
  Pallas kernels: 65.8 us -> 69.4 us
  starting transfers between devices: 45.9 us -> 43.2 us
  other arithmetic: 3.42 us -> 0.77 us
    pallas_call x2, Pallas kernels: 16.3 us -> 22.3 us  [attend(): pl.pallas_call(functools.partial(attend_kernel, plan, len(blocks), counts...]
    unnamed x38 -> x40, local copies, waits for them, and re-layouts: 11 us -> 15.9 us
    ppermute x1, starting transfers between devices: 6.75 us -> 3.63 us  [shards(): other = lax.ppermute(to_join, ('tile', 'seq'), joins).astype(jnp.float32)]
  transfers between devices with their start and end apart: 27 -> 27, of which waited for: 8 -> 6; matrix products, arithmetic and copies ran while one was open for 3% -> 3% of each run, Pallas kernels for 22% -> 24%
where the time goes in v9:
time: 255 us; the launch traced here: 254 us
  waiting for transfers between devices  103 us (40%)
  Pallas kernels  69.4 us (27%)
  starting transfers between devices  43.2 us (17%)
  local copies, waits for them, and re-layouts  23 us (9%)
  between operations  15.2 us (6%)
    ppermute x1, waiting for transfers between devices, shards(): lax.ppermute(weight.astype(jnp.bfloat16), ('tile', 'seq'), joins)  65.9 us
    pallas_call x2, Pallas kernels, attend(): pl.pallas_call(functools.partial(attend_kernel, plan, len(blocks), counts...  22.3 us
    ppermute x6, waiting for transfers between devices, hop(): lax.ppermute(blocks_by[way * (step - 1)], 'seq', step_pairs(devices, step...  17.9 us
    pallas_call x2, Pallas kernels, project(): pl.pallas_call(functools.partial(project_kernel, plan, len(blocks)), grid...  17.8 us
    unnamed x40, local copies, waits for them, and re-layouts  15.9 us
    ppermute x8, starting transfers between devices, turned(): lax.ppermute(value, axis, [(i, (i + turn) % count) for i in range(count)])  15.7 us
    ppermute x8, waiting for transfers between devices, turned(): lax.ppermute(value, axis, [(i, (i + turn) % count) for i in range(count)])  14 us
    pallas_call x1, Pallas kernels, accumulate(): pl.pallas_call(functools.partial(add_kernel, offsets, splits), in_specs=[...  10.5 us
  transfers between devices with their start and end apart: 27, of which 6 were waited for; matrix products, arithmetic and copies ran while one was open for 3% of the time, Pallas kernels for 24%

profile of v9, /device:TPU:1, one launch (start us, length us, event | category | flops | bytes accessed | tf_op | source)
XLA Modules:
  0.0 254.1 jit_solution(7321606909701057744)
XLA Ops:
  9.5 2.7 %collective-permute-start.1 = (bf16[768,2304]{1,0:T(8,128)(2,1)}, bf16[768,2304]{1,0:T(8,128)(2,1)}, u32[]{:S(2)}, u32[]{:S(2)}) collective-permute-start(bf16[768,2304]{1,0:T(8,128)(2,1)} %refs_0_.3), channel_id=1, source_target_pairs={{0,8},{4,12},{8,0},{12,4},{1,9},{5,13},{9,1},{13,5},{2,10},{6,14},... | collective-permute-start | bytes 10616840 | tf_op jit(solution)/shard_map/ppermute | solution.py:18
  12.7 4.4 %norm_in.1.refs_4_ = bf16[256,3072]{1,0:T(8,128)(2,1)} custom-call(s32[4]{0:T(128)} %pad_add_fusion.starts_ref, bf16[256,3072]{1,0:T(8,128)(2,1)} %bitcast.35, f32[5,3072]{1,0:T(8,128)} %refs_14_.1), custom_call_target="tpu_custom_call" | custom-call | tf_op jit(solution)/shard_map/norm_in/pallas_call | solution.py:78
  17.2 4.3 %collective-permute-start.3 = (bf16[256,3072]{1,0:T(8,128)(2,1)}, bf16[256,3072]{1,0:T(8,128)(2,1)}, u32[]{:S(2)}, u32[]{:S(2)}) collective-permute-start(bf16[256,3072]{1,0:T(8,128)(2,1)} %norm_in.1.refs_4_), channel_id=1, source_target_pairs={{0,1},{1,2},{2,3},{4,5},{5,6},{6,7},{8,9},{9,10},{10,11},{12,13},{... | collective-permute-start | bytes 4718600 | tf_op jit(solution)/shard_map/ppermute | solution.py:458
  22.8 4.7 %collective-permute-start.4 = (bf16[1,256]{1,0:T(2,128)(2,1)S(1)}, bf16[1,256]{1,0:T(2,128)(2,1)S(1)}, u32[]{:S(2)}, u32[]{:S(2)}) collective-permute-start(bf16[1,256]{1,0:T(2,128)(2,1)S(1)} %get-tuple-element.165), channel_id=1, source_target_pairs={{2,4},{3,5},{6,8},{7,9},{10,12},{11,13},{4,2},{5,3},{8,6},{9,7},{1... | collective-permute-start | bytes 1544 | tf_op jit(solution)/shard_map/ppermute | solution.py:443
  29.2 65.9 %collective-permute-done.4 = bf16[1,256]{1,0:T(2,128)(2,1)S(1)} collective-permute-done((bf16[1,256]{1,0:T(2,128)(2,1)S(1)}, bf16[1,256]{1,0:T(2,128)(2,1)S(1)}, u32[]{:S(2)}, u32[]{:S(2)}) %collective-permute-start.4) | collective-permute-done | bytes 544 | tf_op jit(solution)/shard_map/ppermute | solution.py:443
  98.6 1.5 collective-permute-start.10
  100.0 1.6 collective-permute-done.5.refs_3_
  101.7 1.8 copy-done.12
  103.4 2.0 copy-done.1
  105.4 1.4 copy-done.8
  106.8 10.5 %project.2 = (bf16[6,512,128]{2,1,0:T(8,128)(2,1)S(1)}, bf16[6,512,128]{2,1,0:T(8,128)(2,1)S(1)}, bf16[6,512,128]{2,1,0:T(8,128)(2,1)S(1)}) custom-call(s32[1]{0:T(128)} %bitcast.18.place_ref, bf16[768,2304]{1,0:T(8,128)(2,1)S(1)} %copy-done.1, bf16[768,2304]{1,0:T(8,128)(2,1)} %collective-permute-done.refs_1_, ...), custom_call_target="tpu_custom_call" | custom-call | tf_op jit(solution)/shard_map/project/pallas_call | solution.py:152
  117.4 15.3 %collective-permute-done.6.refs_4_.refs_12_ = bf16[256,3072]{1,0:T(8,128)(2,1)S(1)} collective-permute-done((bf16[256,3072]{1,0:T(8,128)(2,1)S(1)}, bf16[256,3072]{1,0:T(8,128)(2,1)S(1)}, u32[]{:S(2)}, u32[]{:S(2)}) %collective-permute-start.6) | collective-permute-done | bytes 1572896 | tf_op jit(solution)/shard_map/ppermute | solution.py:458
  136.0 14.0 %collective-permute-done.11.refs_6_.refs_4_ = bf16[3072,384]{1,0:T(8,128)(2,1)} collective-permute-done((bf16[3072,384]{1,0:T(8,128)(2,1)}, bf16[3072,384]{1,0:T(8,128)(2,1)}, u32[]{:S(2)}, u32[]{:S(2)}) %collective-permute-start.11) | collective-permute-done | bytes 2359328 | tf_op jit(solution)/shard_map/ppermute | solution.py:33
  150.0 2.4 slice.17
  152.4 2.4 slice.16
  154.9 7.2 %project.3 = (bf16[6,256,128]{2,1,0:T(8,128)(2,1)S(1)}, bf16[6,256,128]{2,1,0:T(8,128)(2,1)S(1)}, bf16[6,256,128]{2,1,0:T(8,128)(2,1)S(1)}) custom-call(s32[1]{0:T(128)} %bitcast.18.place_ref, bf16[768,2304]{1,0:T(8,128)(2,1)S(1)} %copy-done.1, bf16[768,2304]{1,0:T(8,128)(2,1)} %collective-permute-done.refs_1_, ...), custom_call_target="tpu_custom_call" | custom-call | tf_op jit(solution)/shard_map/project/pallas_call | solution.py:152
  162.1 5.6 %early.1.refs_4_ = f32[6,768,256]{2,1,0:T(8,128)S(1)} custom-call(bf16[6,512,128]{2,1,0:T(8,128)(2,1)S(1)} %get-tuple-element.112.refs_0_.refs_5_, bf16[6,512,128]{2,1,0:T(8,128)(2,1)S(1)} %get-tuple-element.113.refs_1_.refs_6_, bf16[6,512,128]{2,1,0:T(8,128)(2,1)S(1)} %get-tuple-element.114.refs_2_.refs_7_, ...), custom_call_target="tpu_custom_call" | custom-call | tf_op jit(solution)/shard_map/early/pallas_call | solution.py:202
  167.7 2.2 copy-done.3
  169.9 2.6 %collective-permute-done.8.refs_11_ = bf16[256,3072]{1,0:T(8,128)(2,1)S(1)} collective-permute-done((bf16[256,3072]{1,0:T(8,128)(2,1)S(1)}, bf16[256,3072]{1,0:T(8,128)(2,1)S(1)}, u32[]{:S(2)}, u32[]{:S(2)}) %collective-permute-start.8) | collective-permute-done | bytes 1572896 | tf_op jit(solution)/shard_map/ppermute | solution.py:458
  177.8 1.4 copy-done.5
  179.2 1.4 copy-done.7
  180.6 11.2 %attend.2 = (bf16[256,384]{1,0:T(8,128)(2,1)S(1)}, bf16[256,384]{1,0:T(8,128)(2,1)S(1)}, bf16[256,384]{1,0:T(8,128)(2,1)S(1)}, bf16[256,384]{1,0:T(8,128)(2,1)S(1)}) custom-call(s32[1]{0:T(128)} %bitcast.18.place_ref, s32[4]{0:T(128)S(1)} %dynamic-slice_bitcast_fusion.slots_ref, bf16[768,2304]{1,0:T(8,128)(2,1)S(1)} %copy-done.2, ...), custom_call_target="tpu_custom_call" | custom-call | tf_op jit(solution)/shard_map/attend/pallas_call | solution.py:258
  191.9 2.2 collective-permute-start.15
  195.4 1.9 collective-permute-start.17
  197.3 11.0 %attend.3 = (bf16[256,384]{1,0:T(8,128)(2,1)S(1)}, bf16[256,384]{1,0:T(8,128)(2,1)S(1)}, bf16[256,384]{1,0:T(8,128)(2,1)S(1)}, bf16[256,384]{1,0:T(8,128)(2,1)S(1)}) custom-call(s32[1]{0:T(128)} %bitcast.18.place_ref, s32[4]{0:T(128)S(1)} %dynamic-slice_bitcast_fusion.slots_ref, bf16[768,2304]{1,0:T(8,128)(2,1)S(1)} %copy-done.2, ...), custom_call_target="tpu_custom_call" | custom-call | tf_op jit(solution)/shard_map/attend/pallas_call | solution.py:258
  208.5 2.0 collective-permute-start.23
  210.5 4.6 %collective-permute-start.20 = (bf16[256,384]{1,0:T(8,128)(2,1)S(1)}, bf16[256,384]{1,0:T(8,128)(2,1)S(1)}, u32[]{:S(2)}, u32[]{:S(2)}) collective-permute-start(bf16[256,384]{1,0:T(8,128)(2,1)S(1)} %get-tuple-element.143), channel_id=1, source_target_pairs={{0,2},{1,3},{2,0},{3,1},{4,6},{5,7},{6,4},{7,5},{8,10},{9,11},{10,... | collective-permute-start | bytes 589832 | tf_op jit(solution)/shard_map/ppermute | solution.py:33
  215.1 3.3 %collective-permute-start.22 = (bf16[256,384]{1,0:T(8,128)(2,1)S(1)}, bf16[256,384]{1,0:T(8,128)(2,1)S(1)}, u32[]{:S(2)}, u32[]{:S(2)}) collective-permute-start(bf16[256,384]{1,0:T(8,128)(2,1)S(1)} %get-tuple-element.145), channel_id=1, source_target_pairs={{0,3},{1,0},{2,1},{3,2},{4,7},{5,4},{6,5},{7,6},{8,11},{9,8},{10,9... | collective-permute-start | bytes 589832 | tf_op jit(solution)/shard_map/ppermute | solution.py:33
  220.5 10.5 %add_parts.1.refs_13_ = f32[256,3072]{1,0:T(8,128)} custom-call(s32[8]{0:T(128)S(1)} %stack.79.starts_ref, s32[4]{0:T(128)S(1)} %pad_add_fusion.1.rows_ref, bf16[256,384]{1,0:T(8,128)(2,1)S(1)} %get-tuple-element.154.refs_0_, bf16[256,384]{1,0:T(8,128)(2,1)S(1)} %get-tuple-element.155.refs_1_, bf16[256,384]{1,0:T(8,128)(2,1)S(1)} %collective-permute-done.15.refs_2_, ...), custom_call_target="tpu_custom_call" | custom-call | tf_op jit(solution)/shard_map/add_parts/pallas_call | solution.py:396
  231.1 8.9 %finish.1 = (f32[128,256]{1,0:T(8,128)S(1)}, bf16[128,256]{1,0:T(8,128)(2,1)S(1)}) custom-call(s32[8]{0:T(128)S(1)} %stack.79.starts_ref, s32[4]{0:T(128)S(1)} %pad_add_fusion.1.rows_ref, f32[2]{0:T(128)S(1)} %pad_maximum_fusion.coef_ref, bf16[256,384]{1,0:T(8,128)(2,1)S(1)} %collective-permute-done.20.refs_0_, ...), custom_call_target="tpu_custom_call" | custom-call | tf_op jit(solution)/shard_map/finish/pallas_call | solution.py:408
  239.9 3.6 %collective-permute-start.25 = (bf16[128,256]{1,0:T(8,128)(2,1)S(1)}, bf16[128,256]{1,0:T(8,128)(2,1)S(1)}, u32[]{:S(2)}, u32[]{:S(2)}) collective-permute-start(bf16[128,256]{1,0:T(8,128)(2,1)S(1)} %get-tuple-element.160), channel_id=1, source_target_pairs={{2,4},{3,5},{6,8},{7,9},{10,12},{11,13},{4,2},{5,3},{8,6},{9,7},{1... | collective-permute-start | bytes 196616 | tf_op jit(solution)/shard_map/ppermute | solution.py:599
  243.6 3.0 %collective-permute-done.25 = bf16[128,256]{1,0:T(8,128)(2,1)S(1)} collective-permute-done((bf16[128,256]{1,0:T(8,128)(2,1)S(1)}, bf16[128,256]{1,0:T(8,128)(2,1)S(1)}, u32[]{:S(2)}, u32[]{:S(2)}) %collective-permute-start.25) | collective-permute-done | bytes 65568 | tf_op jit(solution)/shard_map/ppermute | solution.py:599
  (83 shorter events, 21.4 us)
Async XLA Ops:
  7.2 87.9 %all-gather.2.cloned.1.call-start = ((), (), s32[]{:S(2)}) async-start(), calls=%async_computation | async-start | bytes 2949120 | tf_op jit(solution)/shard_map/all_gather | solution.py:470
  9.3 85.8 %collective-permute-start = (bf16[768,2304]{1,0:T(8,128)(2,1)}, bf16[768,2304]{1,0:T(8,128)(2,1)}, u32[]{:S(2)}, u32[]{:S(2)}) collective-permute-start(bf16[768,2304]{1,0:T(8,128)(2,1)} %refs_0_.3), channel_id=1, source_target_pairs={{0,4},{4,0},{8,12},{12,8},{1,5},{5,1},{9,13},{13,9},{2,6},{6,2},{1... | collective-permute-start | bytes 10616840 | tf_op jit(solution)/shard_map/ppermute | solution.py:18
  9.5 85.7 %collective-permute-start.1 = (bf16[768,2304]{1,0:T(8,128)(2,1)}, bf16[768,2304]{1,0:T(8,128)(2,1)}, u32[]{:S(2)}, u32[]{:S(2)}) collective-permute-start(bf16[768,2304]{1,0:T(8,128)(2,1)} %refs_0_.3), channel_id=1, source_target_pairs={{0,8},{4,12},{8,0},{12,4},{1,9},{5,13},{9,1},{13,5},{2,10},{6,14},... | collective-permute-start | bytes 10616840 | tf_op jit(solution)/shard_map/ppermute | solution.py:18
  17.2 77.9 %collective-permute-start.3 = (bf16[256,3072]{1,0:T(8,128)(2,1)}, bf16[256,3072]{1,0:T(8,128)(2,1)}, u32[]{:S(2)}, u32[]{:S(2)}) collective-permute-start(bf16[256,3072]{1,0:T(8,128)(2,1)} %norm_in.1.refs_4_), channel_id=1, source_target_pairs={{0,1},{1,2},{2,3},{4,5},{5,6},{6,7},{8,9},{9,10},{10,11},{12,13},{... | collective-permute-start | bytes 4718600 | tf_op jit(solution)/shard_map/ppermute | solution.py:458
  21.5 73.6 %collective-permute-start.2 = (bf16[256,3072]{1,0:T(8,128)(2,1)}, bf16[256,3072]{1,0:T(8,128)(2,1)S(1)}, u32[]{:S(2)}, u32[]{:S(2)}) collective-permute-start(bf16[256,3072]{1,0:T(8,128)(2,1)} %norm_in.1.refs_4_), channel_id=1, source_target_pairs={{1,0},{2,1},{3,2},{5,4},{6,5},{7,6},{9,8},{10,9},{11,10},{13,12},{... | collective-permute-start | bytes 4718600 | tf_op jit(solution)/shard_map/ppermute | solution.py:458
  22.8 72.3 %collective-permute-start.4 = (bf16[1,256]{1,0:T(2,128)(2,1)S(1)}, bf16[1,256]{1,0:T(2,128)(2,1)S(1)}, u32[]{:S(2)}, u32[]{:S(2)}) collective-permute-start(bf16[1,256]{1,0:T(2,128)(2,1)S(1)} %get-tuple-element.165), channel_id=1, source_target_pairs={{2,4},{3,5},{6,8},{7,9},{10,12},{11,13},{4,2},{5,3},{8,6},{9,7},{1... | collective-permute-start | bytes 1544 | tf_op jit(solution)/shard_map/ppermute | solution.py:443
  95.2 6.5 %collective-permute-start.5 = (bf16[768,2304]{1,0:T(8,128)(2,1)}, bf16[768,2304]{1,0:T(8,128)(2,1)S(1)}, u32[]{:S(2)}, u32[]{:S(2)}) collective-permute-start(bf16[768,2304]{1,0:T(8,128)(2,1)} %collective-permute-done.1.refs_2_), channel_id=1, source_target_pairs={{0,4},{4,0},{8,12},{12,8},{1,5},{5,1},{9,13},{13,9},{2,6},{6,2},{1... | collective-permute-start | bytes 10616840 | tf_op jit(solution)/shard_map/ppermute | solution.py:18
  95.2 37.5 %collective-permute-start.6 = (bf16[256,3072]{1,0:T(8,128)(2,1)S(1)}, bf16[256,3072]{1,0:T(8,128)(2,1)S(1)}, u32[]{:S(2)}, u32[]{:S(2)}) collective-permute-start(bf16[256,3072]{1,0:T(8,128)(2,1)S(1)} %collective-permute-done.2.refs_5_), channel_id=1, source_target_pairs={{1,0},{2,1},{5,4},{6,5},{9,8},{10,9},{13,12},{14,13},{17,16},{18,1... | collective-permute-start | bytes 4718600 | tf_op jit(solution)/shard_map/ppermute | solution.py:458
  96.5 36.2 %collective-permute-start.7 = (bf16[256,3072]{1,0:T(8,128)(2,1)}, bf16[256,3072]{1,0:T(8,128)(2,1)S(1)}, u32[]{:S(2)}, u32[]{:S(2)}) collective-permute-start(bf16[256,3072]{1,0:T(8,128)(2,1)} %collective-permute-done.3.refs_6_), channel_id=1, source_target_pairs={{1,2},{2,3},{5,6},{6,7},{9,10},{10,11},{13,14},{14,15},{17,18},{18... | collective-permute-start | bytes 4718600 | tf_op jit(solution)/shard_map/ppermute | solution.py:458
  97.3 52.7 %collective-permute-start.11 = (bf16[3072,384]{1,0:T(8,128)(2,1)}, bf16[3072,384]{1,0:T(8,128)(2,1)}, u32[]{:S(2)}, u32[]{:S(2)}) collective-permute-start(bf16[3072,384]{1,0:T(8,128)(2,1)} %all-gather.2.cloned.1.call-done.refs_5_.refs_3_), channel_id=1, source_target_pairs={{0,16},{16,0},{1,17},{17,1},{2,18},{18,2},{3,19},{19,3},{4,20},{20... | collective-permute-start | bytes 7077896 | tf_op jit(solution)/shard_map/ppermute | solution.py:33
  98.6 53.9 %collective-permute-start.10 = (bf16[3072,384]{1,0:T(8,128)(2,1)}, bf16[3072,384]{1,0:T(8,128)(2,1)}, u32[]{:S(2)}, u32[]{:S(2)}) collective-permute-start(bf16[3072,384]{1,0:T(8,128)(2,1)} %all-gather.2.cloned.1.call-done.refs_5_.refs_3_), channel_id=1, source_target_pairs={{0,8},{4,12},{8,0},{12,4},{1,9},{5,13},{9,1},{13,5},{2,10},{6,14},... | collective-permute-start | bytes 7077896 | tf_op jit(solution)/shard_map/ppermute | solution.py:18
  132.7 42.1 %collective-permute-start.12 = (bf16[3072,384]{1,0:T(8,128)(2,1)}, bf16[3072,384]{1,0:T(8,128)(2,1)}, u32[]{:S(2)}, u32[]{:S(2)}) collective-permute-start(bf16[3072,384]{1,0:T(8,128)(2,1)} %all-gather.2.cloned.1.call-done.refs_5_.refs_3_), channel_id=1, source_target_pairs={{0,4},{4,0},{8,12},{12,8},{1,5},{5,1},{9,13},{13,9},{2,6},{6,2},{1... | collective-permute-start | bytes 7077896 | tf_op jit(solution)/shard_map/ppermute | solution.py:18
  133.9 38.5 %collective-permute-start.8 = (bf16[256,3072]{1,0:T(8,128)(2,1)S(1)}, bf16[256,3072]{1,0:T(8,128)(2,1)S(1)}, u32[]{:S(2)}, u32[]{:S(2)}) collective-permute-start(bf16[256,3072]{1,0:T(8,128)(2,1)S(1)} %collective-permute-done.6.refs_4_.refs_12_), channel_id=1, source_target_pairs={{1,0},{5,4},{9,8},{13,12},{17,16},{21,20},{25,24},{29,28}} | collective-permute-start | bytes 4718600 | tf_op jit(solution)/shard_map/ppermute | solution.py:458
  135.2 38.4 %collective-permute-start.9 = (bf16[256,3072]{1,0:T(8,128)(2,1)S(1)}, bf16[256,3072]{1,0:T(8,128)(2,1)S(1)}, u32[]{:S(2)}, u32[]{:S(2)}) collective-permute-start(bf16[256,3072]{1,0:T(8,128)(2,1)S(1)} %collective-permute-done.7.refs_6_.refs_13_), channel_id=1, source_target_pairs={{2,3},{6,7},{10,11},{14,15},{18,19},{22,23},{26,27},{30,31}} | collective-permute-start | bytes 4718600 | tf_op jit(solution)/shard_map/ppermute | solution.py:458
  174.8 17.0 %collective-permute-start.13 = (bf16[3072,384]{1,0:T(8,128)(2,1)}, bf16[3072,384]{1,0:T(8,128)(2,1)S(1)}, u32[]{:S(2)}, u32[]{:S(2)}) collective-permute-start(bf16[3072,384]{1,0:T(8,128)(2,1)} %collective-permute-done.11.refs_6_.refs_4_), channel_id=1, source_target_pairs={{0,4},{4,0},{8,12},{12,8},{1,5},{5,1},{9,13},{13,9},{2,6},{6,2},{1... | collective-permute-start | bytes 7077896 | tf_op jit(solution)/shard_map/ppermute | solution.py:18
  175.4 16.4 %collective-permute-start.14 = (bf16[3072,384]{1,0:T(8,128)(2,1)}, bf16[3072,384]{1,0:T(8,128)(2,1)S(1)}, u32[]{:S(2)}, u32[]{:S(2)}) collective-permute-start(bf16[3072,384]{1,0:T(8,128)(2,1)} %collective-permute-done.10.refs_9_.refs_7_), channel_id=1, source_target_pairs={{0,4},{4,0},{8,12},{12,8},{1,5},{5,1},{9,13},{13,9},{2,6},{6,2},{1... | collective-permute-start | bytes 7077896 | tf_op jit(solution)/shard_map/ppermute | solution.py:18
  175.4 33.0 %collective-permute-start.18 = (bf16[1536,384]{1,0:T(8,128)(2,1)}, bf16[1536,384]{1,0:T(8,128)(2,1)S(1)}, u32[]{:S(2)}, u32[]{:S(2)}) collective-permute-start(bf16[1536,384]{1,0:T(8,128)(2,1)} %slice.16), channel_id=1, source_target_pairs={{0,16},{16,0},{1,17},{17,1},{2,18},{18,2},{3,19},{19,3},{4,20},{20... | collective-permute-start | bytes 3538952 | tf_op jit(solution)/shard_map/ppermute | solution.py:33
  176.6 31.8 %collective-permute-start.19 = (bf16[1536,384]{1,0:T(8,128)(2,1)}, bf16[1536,384]{1,0:T(8,128)(2,1)S(1)}, u32[]{:S(2)}, u32[]{:S(2)}) collective-permute-start(bf16[1536,384]{1,0:T(8,128)(2,1)} %slice.17), channel_id=1, source_target_pairs={{0,8},{4,12},{8,0},{12,4},{1,9},{5,13},{9,1},{13,5},{2,10},{6,14},... | collective-permute-start | bytes 3538952 | tf_op jit(solution)/shard_map/ppermute | solution.py:18
  191.8 16.6 %copy-start.13 = (bf16[3072,384]{1,0:T(8,128)(2,1)}, bf16[3072,384]{1,0:T(8,128)(2,1)S(1)}, u32[]{:S(2)}) copy-start(bf16[3072,384]{1,0:T(8,128)(2,1)S(1)} %collective-permute-done.13.refs_8_.refs_6_) | copy-start | bytes 7077892
  191.8 16.5 %copy-start.14 = (bf16[3072,384]{1,0:T(8,128)(2,1)}, bf16[3072,384]{1,0:T(8,128)(2,1)S(1)}, u32[]{:S(2)}) copy-start(bf16[3072,384]{1,0:T(8,128)(2,1)S(1)} %collective-permute-done.14.refs_12_.refs_10_) | copy-start | bytes 7077892
  191.8 28.7 %copy-start.9 = (f32[5,3072]{1,0:T(8,128)S(1)}, f32[5,3072]{1,0:T(8,128)}, u32[]{:S(2)}) copy-start(f32[5,3072]{1,0:T(8,128)} %refs_14_.1) | copy-start | bytes 184324
  191.9 16.6 %collective-permute-start.15 = (bf16[256,384]{1,0:T(8,128)(2,1)S(1)}, bf16[256,384]{1,0:T(8,128)(2,1)S(1)}, u32[]{:S(2)}, u32[]{:S(2)}) collective-permute-start(bf16[256,384]{1,0:T(8,128)(2,1)S(1)} %get-tuple-element.138), channel_id=1, source_target_pairs={{0,2},{1,3},{2,0},{3,1},{4,6},{5,7},{6,4},{7,5},{8,10},{9,11},{10,... | collective-permute-start | bytes 589832 | tf_op jit(solution)/shard_map/ppermute | solution.py:33
  194.0 14.4 %collective-permute-start.16 = (bf16[256,384]{1,0:T(8,128)(2,1)S(1)}, bf16[256,384]{1,0:T(8,128)(2,1)S(1)}, u32[]{:S(2)}, u32[]{:S(2)}) collective-permute-start(bf16[256,384]{1,0:T(8,128)(2,1)S(1)} %get-tuple-element.139), channel_id=1, source_target_pairs={{0,1},{1,2},{2,3},{3,0},{4,5},{5,6},{6,7},{7,4},{8,9},{9,10},{10,1... | collective-permute-start | bytes 589832 | tf_op jit(solution)/shard_map/ppermute | solution.py:33
  195.4 13.1 %collective-permute-start.17 = (bf16[256,384]{1,0:T(8,128)(2,1)S(1)}, bf16[256,384]{1,0:T(8,128)(2,1)S(1)}, u32[]{:S(2)}, u32[]{:S(2)}) collective-permute-start(bf16[256,384]{1,0:T(8,128)(2,1)S(1)} %get-tuple-element.140), channel_id=1, source_target_pairs={{0,3},{1,0},{2,1},{3,2},{4,7},{5,4},{6,5},{7,6},{8,11},{9,8},{10,9... | collective-permute-start | bytes 589832 | tf_op jit(solution)/shard_map/ppermute | solution.py:33
  208.5 22.6 %copy-start.10 = (bf16[3072,64]{0,1:T(8,128)(2,1)S(1)}, bf16[3072,64]{0,1:T(8,128)(2,1)}, u32[]{:S(2)}) copy-start(bf16[3072,64]{0,1:T(8,128)(2,1)} %param.13) | copy-start | bytes 1179652
  208.5 22.6 %copy-start.11 = (f32[1,256,64]{1,2,0:T(8,128)S(1)}, f32[1,256,64]{1,2,0:T(8,128)}, u32[]{:S(2)}) copy-start(f32[1,256,64]{1,2,0:T(8,128)} %param.14) | copy-start | bytes 196612
  208.5 9.9 %collective-permute-start.23 = (bf16[1536,384]{1,0:T(8,128)(2,1)S(1)}, bf16[1536,384]{1,0:T(8,128)(2,1)S(1)}, u32[]{:S(2)}, u32[]{:S(2)}) collective-permute-start(bf16[1536,384]{1,0:T(8,128)(2,1)S(1)} %collective-permute-done.18.refs_10_.refs_8_), channel_id=1, source_target_pairs={{0,4},{4,0},{8,12},{12,8},{1,5},{5,1},{9,13},{13,9},{2,6},{6,2},{1... | collective-permute-start | bytes 3538952 | tf_op jit(solution)/shard_map/ppermute | solution.py:18
  210.4 7.9 %collective-permute-start.24 = (bf16[1536,384]{1,0:T(8,128)(2,1)S(1)}, bf16[1536,384]{1,0:T(8,128)(2,1)S(1)}, u32[]{:S(2)}, u32[]{:S(2)}) collective-permute-start(bf16[1536,384]{1,0:T(8,128)(2,1)S(1)} %collective-permute-done.19.refs_11_.refs_9_), channel_id=1, source_target_pairs={{0,4},{4,0},{8,12},{12,8},{1,5},{5,1},{9,13},{13,9},{2,6},{6,2},{1... | collective-permute-start | bytes 3538952 | tf_op jit(solution)/shard_map/ppermute | solution.py:18
  210.5 20.5 %collective-permute-start.20 = (bf16[256,384]{1,0:T(8,128)(2,1)S(1)}, bf16[256,384]{1,0:T(8,128)(2,1)S(1)}, u32[]{:S(2)}, u32[]{:S(2)}) collective-permute-start(bf16[256,384]{1,0:T(8,128)(2,1)S(1)} %get-tuple-element.143), channel_id=1, source_target_pairs={{0,2},{1,3},{2,0},{3,1},{4,6},{5,7},{6,4},{7,5},{8,10},{9,11},{10,... | collective-permute-start | bytes 589832 | tf_op jit(solution)/shard_map/ppermute | solution.py:33
  215.1 15.9 %collective-permute-start.21 = (bf16[256,384]{1,0:T(8,128)(2,1)S(1)}, bf16[256,384]{1,0:T(8,128)(2,1)S(1)}, u32[]{:S(2)}, u32[]{:S(2)}) collective-permute-start(bf16[256,384]{1,0:T(8,128)(2,1)S(1)} %get-tuple-element.144), channel_id=1, source_target_pairs={{0,1},{1,2},{2,3},{3,0},{4,5},{5,6},{6,7},{7,4},{8,9},{9,10},{10,1... | collective-permute-start | bytes 589832 | tf_op jit(solution)/shard_map/ppermute | solution.py:33
  215.1 15.9 %collective-permute-start.22 = (bf16[256,384]{1,0:T(8,128)(2,1)S(1)}, bf16[256,384]{1,0:T(8,128)(2,1)S(1)}, u32[]{:S(2)}, u32[]{:S(2)}) collective-permute-start(bf16[256,384]{1,0:T(8,128)(2,1)S(1)} %get-tuple-element.145), channel_id=1, source_target_pairs={{0,3},{1,0},{2,1},{3,2},{4,7},{5,4},{6,5},{7,6},{8,11},{9,8},{10,9... | collective-permute-start | bytes 589832 | tf_op jit(solution)/shard_map/ppermute | solution.py:33
  239.9 6.6 %collective-permute-start.25 = (bf16[128,256]{1,0:T(8,128)(2,1)S(1)}, bf16[128,256]{1,0:T(8,128)(2,1)S(1)}, u32[]{:S(2)}, u32[]{:S(2)}) collective-permute-start(bf16[128,256]{1,0:T(8,128)(2,1)S(1)} %get-tuple-element.160), channel_id=1, source_target_pairs={{2,4},{3,5},{6,8},{7,9},{10,12},{11,13},{4,2},{5,3},{8,6},{9,7},{1... | collective-permute-start | bytes 196616 | tf_op jit(solution)/shard_map/ppermute | solution.py:599
  (15 other events, 61.6 us)
Sparse Core Ops, SparseCore 0:
  9.6 82.3 all-gather.1

commit v10 on v8

--- a/solution.py
+++ b/solution.py
@@ -333,22 +333,13 @@
     parts = refs[: len(offsets)]
     sources, refs = split_refs(refs[len(offsets) :], splits)
     before_ref, mod_ref, head_ref, latent_ref, weight_ref, out_ref, sent_ref = refs[:7]
-    weights, wide, sems, mixed, extra = refs[7:]
+    weights, wide, sems, mixed = refs[7:]
     count = len(splits)
     width = weights.shape[2]
-    copies = []
-    for p in range(count):
-        cols = pl.ds(pl.multiple_of(starts_ref[p], HD), width)
-        copies.append(
-            pltpu.make_async_copy(before_ref.at[:, cols], mixed.at[:, cols], extra.at[p])
-        )
-        copies[p].start()
-
     held = {}
 
     def store(p, cols, summed):
-        copies[p].wait()
-        values = mixed[:, cols] + mod_ref[2:3, cols] * summed
+        values = before_ref[:, cols] + mod_ref[2:3, cols] * summed
         mixed[:, cols] = values
         if p == 0:
             held["base"] = jnp.mean(values, axis=-1, keepdims=True)
@@ -401,7 +392,7 @@
         pltpu.SemaphoreType.DMA((count, len(parts))),
     ]
     params = dict(
-        compiler_params=pltpu.CompilerParams(vmem_limit_bytes=60 * MIB),
+        compiler_params=pltpu.CompilerParams(vmem_limit_bytes=52 * MIB),
     )
     if last is None:
         aliased = before.dtype == jnp.float32
@@ -419,14 +410,14 @@
     channels = head.shape[0]
     return pl.pallas_call(
         functools.partial(finish_kernel, offsets, splits),
-        in_specs=[smem] * 3 + [vmem] * len(parts) + [hbm] * (len(pieces) + 1) + [vmem] * 4,
+        in_specs=[smem] * 3 + [vmem] * len(parts) + [hbm] * len(pieces) + [vmem] * 5,
         out_specs=[vmem, vmem],
         out_shape=[
             jax.ShapeDtypeStruct((2 * channels, rows), jnp.float32),
             jax.ShapeDtypeStruct((2 * channels, rows), jnp.bfloat16),
         ],
         scratch_shapes=scratch
-        + [pltpu.VMEM((rows, width), jnp.float32), pltpu.SemaphoreType.DMA((count,))],
+        + [pltpu.VMEM((rows, width), jnp.float32)],
         name="finish",
         **params,
     )(starts, firsts, coef, *parts, *pieces, before, modulation, head, latent, weight)

time: 253 us -> 250 us (0.988)
  waiting for transfers between devices: 103 us -> 106 us
  other arithmetic: 3.42 us -> 0.77 us
    unnamed x38 -> x32, local copies, waits for them, and re-layouts: 11 us -> 10.7 us
where the time goes in v10:
time: 250 us; the launch traced here: 249 us
  waiting for transfers between devices  106 us (42%)
  Pallas kernels  63.7 us (25%)
  starting transfers between devices  45.2 us (18%)
  local copies, waits for them, and re-layouts  17.8 us (7%)
  between operations  15.1 us (6%)
    ppermute x1, waiting for transfers between devices, shards(): lax.ppermute(weight.astype(jnp.bfloat16), ('tile', 'seq'), joins)  65.9 us
    pallas_call x2, Pallas kernels, project(): pl.pallas_call(functools.partial(project_kernel, plan, len(blocks)), grid...  17.9 us
    ppermute x6, waiting for transfers between devices, hop(): lax.ppermute(blocks_by[way * (step - 1)], 'seq', step_pairs(devices, step...  17.8 us
    ppermute x8, waiting for transfers between devices, turned(): lax.ppermute(value, axis, [(i, (i + turn) % count) for i in range(count)])  16.8 us
    pallas_call x2, Pallas kernels, attend(): pl.pallas_call(functools.partial(attend_kernel, plan, len(blocks), counts...  16.4 us
    ppermute x8, starting transfers between devices, turned(): lax.ppermute(value, axis, [(i, (i + turn) % count) for i in range(count)])  15.6 us
    unnamed x32, local copies, waits for them, and re-layouts  10.7 us
    pallas_call x1, Pallas kernels, accumulate(): pl.pallas_call(functools.partial(add_kernel, offsets, splits), in_specs=[...  10.5 us
  transfers between devices with their start and end apart: 27, of which 8 were waited for; matrix products, arithmetic and copies ran while one was open for 3% of the time, Pallas kernels for 22%

profile of v10, /device:TPU:1, one launch (start us, length us, event | category | flops | bytes accessed | tf_op | source)
XLA Modules:
  0.0 248.9 jit_solution(13107935479207350100)
XLA Ops:
  9.5 2.7 %collective-permute-start.1 = (bf16[768,2304]{1,0:T(8,128)(2,1)}, bf16[768,2304]{1,0:T(8,128)(2,1)}, u32[]{:S(2)}, u32[]{:S(2)}) collective-permute-start(bf16[768,2304]{1,0:T(8,128)(2,1)} %refs_0_.3), channel_id=1, source_target_pairs={{0,8},{4,12},{8,0},{12,4},{1,9},{5,13},{9,1},{13,5},{2,10},{6,14},... | collective-permute-start | bytes 10616840 | tf_op jit(solution)/shard_map/ppermute | solution.py:18
  12.7 4.4 %norm_in.1.refs_4_ = bf16[256,3072]{1,0:T(8,128)(2,1)} custom-call(s32[4]{0:T(128)} %pad_add_fusion.starts_ref, bf16[256,3072]{1,0:T(8,128)(2,1)} %bitcast.35, f32[5,3072]{1,0:T(8,128)} %refs_14_.1), custom_call_target="tpu_custom_call" | custom-call | tf_op jit(solution)/shard_map/norm_in/pallas_call | solution.py:78
  17.2 4.3 %collective-permute-start.3 = (bf16[256,3072]{1,0:T(8,128)(2,1)}, bf16[256,3072]{1,0:T(8,128)(2,1)}, u32[]{:S(2)}, u32[]{:S(2)}) collective-permute-start(bf16[256,3072]{1,0:T(8,128)(2,1)} %norm_in.1.refs_4_), channel_id=1, source_target_pairs={{0,1},{1,2},{2,3},{4,5},{5,6},{6,7},{8,9},{9,10},{10,11},{12,13},{... | collective-permute-start | bytes 4718600 | tf_op jit(solution)/shard_map/ppermute | solution.py:461
  22.8 4.7 %collective-permute-start.4 = (bf16[1,256]{1,0:T(2,128)(2,1)S(1)}, bf16[1,256]{1,0:T(2,128)(2,1)S(1)}, u32[]{:S(2)}, u32[]{:S(2)}) collective-permute-start(bf16[1,256]{1,0:T(2,128)(2,1)S(1)} %get-tuple-element.165), channel_id=1, source_target_pairs={{2,4},{3,5},{6,8},{7,9},{10,12},{11,13},{4,2},{5,3},{8,6},{9,7},{1... | collective-permute-start | bytes 1544 | tf_op jit(solution)/shard_map/ppermute | solution.py:446
  29.2 65.9 %collective-permute-done.4 = bf16[1,256]{1,0:T(2,128)(2,1)S(1)} collective-permute-done((bf16[1,256]{1,0:T(2,128)(2,1)S(1)}, bf16[1,256]{1,0:T(2,128)(2,1)S(1)}, u32[]{:S(2)}, u32[]{:S(2)}) %collective-permute-start.4) | collective-permute-done | bytes 544 | tf_op jit(solution)/shard_map/ppermute | solution.py:446
  95.2 1.3 collective-permute-start.6
  98.6 1.5 collective-permute-start.10
  100.0 1.6 collective-permute-done.5.refs_3_
  101.7 1.8 copy-done.7
  103.4 2.0 copy-done.1
  105.4 1.4 copy-done.3
  106.8 10.7 %project.2 = (bf16[6,512,128]{2,1,0:T(8,128)(2,1)S(1)}, bf16[6,512,128]{2,1,0:T(8,128)(2,1)S(1)}, bf16[6,512,128]{2,1,0:T(8,128)(2,1)S(1)}) custom-call(s32[1]{0:T(128)} %bitcast.18.place_ref, bf16[768,2304]{1,0:T(8,128)(2,1)S(1)} %copy-done.1, bf16[768,2304]{1,0:T(8,128)(2,1)} %collective-permute-done.refs_1_, ...), custom_call_target="tpu_custom_call" | custom-call | tf_op jit(solution)/shard_map/project/pallas_call | solution.py:152
  117.5 15.2 %collective-permute-done.6.refs_4_.refs_12_ = bf16[256,3072]{1,0:T(8,128)(2,1)S(1)} collective-permute-done((bf16[256,3072]{1,0:T(8,128)(2,1)S(1)}, bf16[256,3072]{1,0:T(8,128)(2,1)S(1)}, u32[]{:S(2)}, u32[]{:S(2)}) %collective-permute-start.6) | collective-permute-done | bytes 1572896 | tf_op jit(solution)/shard_map/ppermute | solution.py:461
  136.0 14.0 %collective-permute-done.11.refs_6_.refs_4_ = bf16[3072,384]{1,0:T(8,128)(2,1)} collective-permute-done((bf16[3072,384]{1,0:T(8,128)(2,1)}, bf16[3072,384]{1,0:T(8,128)(2,1)}, u32[]{:S(2)}, u32[]{:S(2)}) %collective-permute-start.11) | collective-permute-done | bytes 2359328 | tf_op jit(solution)/shard_map/ppermute | solution.py:33
  150.0 2.4 slice.17
  152.4 2.4 slice.16
  154.8 7.2 %project.3 = (bf16[6,256,128]{2,1,0:T(8,128)(2,1)S(1)}, bf16[6,256,128]{2,1,0:T(8,128)(2,1)S(1)}, bf16[6,256,128]{2,1,0:T(8,128)(2,1)S(1)}) custom-call(s32[1]{0:T(128)} %bitcast.18.place_ref, bf16[768,2304]{1,0:T(8,128)(2,1)S(1)} %copy-done.1, bf16[768,2304]{1,0:T(8,128)(2,1)} %collective-permute-done.refs_1_, ...), custom_call_target="tpu_custom_call" | custom-call | tf_op jit(solution)/shard_map/project/pallas_call | solution.py:152
  162.1 5.6 %early.1.refs_4_ = f32[6,768,256]{2,1,0:T(8,128)S(1)} custom-call(bf16[6,512,128]{2,1,0:T(8,128)(2,1)S(1)} %get-tuple-element.112.refs_0_.refs_5_, bf16[6,512,128]{2,1,0:T(8,128)(2,1)S(1)} %get-tuple-element.113.refs_1_.refs_6_, bf16[6,512,128]{2,1,0:T(8,128)(2,1)S(1)} %get-tuple-element.114.refs_2_.refs_7_, ...), custom_call_target="tpu_custom_call" | custom-call | tf_op jit(solution)/shard_map/early/pallas_call | solution.py:202
  167.7 2.1 copy-done.2
  169.8 2.6 %collective-permute-done.8.refs_11_ = bf16[256,3072]{1,0:T(8,128)(2,1)S(1)} collective-permute-done((bf16[256,3072]{1,0:T(8,128)(2,1)S(1)}, bf16[256,3072]{1,0:T(8,128)(2,1)S(1)}, u32[]{:S(2)}, u32[]{:S(2)}) %collective-permute-start.8) | collective-permute-done | bytes 1572896 | tf_op jit(solution)/shard_map/ppermute | solution.py:461
  175.5 8.2 %attend.2 = (bf16[256,384]{1,0:T(8,128)(2,1)S(1)}, bf16[256,384]{1,0:T(8,128)(2,1)S(1)}, bf16[256,384]{1,0:T(8,128)(2,1)S(1)}, bf16[256,384]{1,0:T(8,128)(2,1)S(1)}) custom-call(s32[1]{0:T(128)} %bitcast.18.place_ref, s32[4]{0:T(128)S(1)} %dynamic-slice_bitcast_fusion.slots_ref, bf16[768,2304]{1,0:T(8,128)(2,1)} %refs_0_.3, ...), custom_call_target="tpu_custom_call" | custom-call | tf_op jit(solution)/shard_map/attend/pallas_call | solution.py:254
  183.7 2.5 collective-permute-start.15
  186.2 2.2 collective-permute-start.16
  189.4 8.2 %attend.3 = (bf16[256,384]{1,0:T(8,128)(2,1)S(1)}, bf16[256,384]{1,0:T(8,128)(2,1)S(1)}, bf16[256,384]{1,0:T(8,128)(2,1)S(1)}, bf16[256,384]{1,0:T(8,128)(2,1)S(1)}) custom-call(s32[1]{0:T(128)} %bitcast.18.place_ref, s32[4]{0:T(128)S(1)} %dynamic-slice_bitcast_fusion.slots_ref, bf16[768,2304]{1,0:T(8,128)(2,1)} %refs_0_.3, ...), custom_call_target="tpu_custom_call" | custom-call | tf_op jit(solution)/shard_map/attend/pallas_call | solution.py:254
  197.7 2.8 %collective-permute-done.18.refs_10_.refs_8_ = bf16[1536,384]{1,0:T(8,128)(2,1)S(1)} collective-permute-done((bf16[1536,384]{1,0:T(8,128)(2,1)}, bf16[1536,384]{1,0:T(8,128)(2,1)S(1)}, u32[]{:S(2)}, u32[]{:S(2)}) %collective-permute-start.18) | collective-permute-done | bytes 1179680 | tf_op jit(solution)/shard_map/ppermute | solution.py:33
  201.3 1.7 collective-permute-start.23
  203.1 4.1 %collective-permute-start.20 = (bf16[256,384]{1,0:T(8,128)(2,1)S(1)}, bf16[256,384]{1,0:T(8,128)(2,1)S(1)}, u32[]{:S(2)}, u32[]{:S(2)}) collective-permute-start(bf16[256,384]{1,0:T(8,128)(2,1)S(1)} %get-tuple-element.143), channel_id=1, source_target_pairs={{0,2},{1,3},{2,0},{3,1},{4,6},{5,7},{6,4},{7,5},{8,10},{9,11},{10,... | collective-permute-start | bytes 589832 | tf_op jit(solution)/shard_map/ppermute | solution.py:33
  207.7 2.8 %collective-permute-start.22 = (bf16[256,384]{1,0:T(8,128)(2,1)S(1)}, bf16[256,384]{1,0:T(8,128)(2,1)S(1)}, u32[]{:S(2)}, u32[]{:S(2)}) collective-permute-start(bf16[256,384]{1,0:T(8,128)(2,1)S(1)} %get-tuple-element.145), channel_id=1, source_target_pairs={{0,3},{1,0},{2,1},{3,2},{4,7},{5,4},{6,5},{7,6},{8,11},{9,8},{10,9... | collective-permute-start | bytes 589832 | tf_op jit(solution)/shard_map/ppermute | solution.py:33
  212.6 10.5 %add_parts.1.refs_13_ = f32[256,3072]{1,0:T(8,128)} custom-call(s32[8]{0:T(128)S(1)} %stack.79.starts_ref, s32[4]{0:T(128)S(1)} %pad_add_fusion.1.rows_ref, bf16[256,384]{1,0:T(8,128)(2,1)S(1)} %get-tuple-element.154.refs_0_, bf16[256,384]{1,0:T(8,128)(2,1)S(1)} %get-tuple-element.155.refs_1_, bf16[256,384]{1,0:T(8,128)(2,1)S(1)} %collective-permute-done.15.refs_2_, ...), custom_call_target="tpu_custom_call" | custom-call | tf_op jit(solution)/shard_map/add_parts/pallas_call | solution.py:399
  223.1 8.9 %finish.1 = (f32[128,256]{1,0:T(8,128)S(1)}, bf16[128,256]{1,0:T(8,128)(2,1)S(1)}) custom-call(s32[8]{0:T(128)S(1)} %stack.79.starts_ref, s32[4]{0:T(128)S(1)} %pad_add_fusion.1.rows_ref, f32[2]{0:T(128)S(1)} %pad_maximum_fusion.coef_ref, bf16[256,384]{1,0:T(8,128)(2,1)S(1)} %collective-permute-done.20.refs_0_, ...), custom_call_target="tpu_custom_call" | custom-call | tf_op jit(solution)/shard_map/finish/pallas_call | solution.py:411
  232.0 6.1 %collective-permute-start.25 = (bf16[128,256]{1,0:T(8,128)(2,1)S(1)}, bf16[128,256]{1,0:T(8,128)(2,1)S(1)}, u32[]{:S(2)}, u32[]{:S(2)}) collective-permute-start(bf16[128,256]{1,0:T(8,128)(2,1)S(1)} %get-tuple-element.160), channel_id=1, source_target_pairs={{2,4},{3,5},{6,8},{7,9},{10,12},{11,13},{4,2},{5,3},{8,6},{9,7},{1... | collective-permute-start | bytes 196616 | tf_op jit(solution)/shard_map/ppermute | solution.py:602
  238.1 3.3 %collective-permute-done.25 = bf16[128,256]{1,0:T(8,128)(2,1)S(1)} collective-permute-done((bf16[128,256]{1,0:T(8,128)(2,1)S(1)}, bf16[128,256]{1,0:T(8,128)(2,1)S(1)}, u32[]{:S(2)}, u32[]{:S(2)}) %collective-permute-start.25) | collective-permute-done | bytes 65568 | tf_op jit(solution)/shard_map/ppermute | solution.py:602
  (75 shorter events, 18.8 us)
Async XLA Ops:
  7.2 87.9 %all-gather.2.cloned.1.call-start = ((), (), s32[]{:S(2)}) async-start(), calls=%async_computation | async-start | bytes 2949120 | tf_op jit(solution)/shard_map/all_gather | solution.py:473
  9.3 85.8 %collective-permute-start = (bf16[768,2304]{1,0:T(8,128)(2,1)}, bf16[768,2304]{1,0:T(8,128)(2,1)}, u32[]{:S(2)}, u32[]{:S(2)}) collective-permute-start(bf16[768,2304]{1,0:T(8,128)(2,1)} %refs_0_.3), channel_id=1, source_target_pairs={{0,4},{4,0},{8,12},{12,8},{1,5},{5,1},{9,13},{13,9},{2,6},{6,2},{1... | collective-permute-start | bytes 10616840 | tf_op jit(solution)/shard_map/ppermute | solution.py:18
  9.5 85.7 %collective-permute-start.1 = (bf16[768,2304]{1,0:T(8,128)(2,1)}, bf16[768,2304]{1,0:T(8,128)(2,1)}, u32[]{:S(2)}, u32[]{:S(2)}) collective-permute-start(bf16[768,2304]{1,0:T(8,128)(2,1)} %refs_0_.3), channel_id=1, source_target_pairs={{0,8},{4,12},{8,0},{12,4},{1,9},{5,13},{9,1},{13,5},{2,10},{6,14},... | collective-permute-start | bytes 10616840 | tf_op jit(solution)/shard_map/ppermute | solution.py:18
  17.2 77.9 %collective-permute-start.3 = (bf16[256,3072]{1,0:T(8,128)(2,1)}, bf16[256,3072]{1,0:T(8,128)(2,1)}, u32[]{:S(2)}, u32[]{:S(2)}) collective-permute-start(bf16[256,3072]{1,0:T(8,128)(2,1)} %norm_in.1.refs_4_), channel_id=1, source_target_pairs={{0,1},{1,2},{2,3},{4,5},{5,6},{6,7},{8,9},{9,10},{10,11},{12,13},{... | collective-permute-start | bytes 4718600 | tf_op jit(solution)/shard_map/ppermute | solution.py:461
  21.5 73.6 %collective-permute-start.2 = (bf16[256,3072]{1,0:T(8,128)(2,1)}, bf16[256,3072]{1,0:T(8,128)(2,1)S(1)}, u32[]{:S(2)}, u32[]{:S(2)}) collective-permute-start(bf16[256,3072]{1,0:T(8,128)(2,1)} %norm_in.1.refs_4_), channel_id=1, source_target_pairs={{1,0},{2,1},{3,2},{5,4},{6,5},{7,6},{9,8},{10,9},{11,10},{13,12},{... | collective-permute-start | bytes 4718600 | tf_op jit(solution)/shard_map/ppermute | solution.py:461
  22.8 72.3 %collective-permute-start.4 = (bf16[1,256]{1,0:T(2,128)(2,1)S(1)}, bf16[1,256]{1,0:T(2,128)(2,1)S(1)}, u32[]{:S(2)}, u32[]{:S(2)}) collective-permute-start(bf16[1,256]{1,0:T(2,128)(2,1)S(1)} %get-tuple-element.165), channel_id=1, source_target_pairs={{2,4},{3,5},{6,8},{7,9},{10,12},{11,13},{4,2},{5,3},{8,6},{9,7},{1... | collective-permute-start | bytes 1544 | tf_op jit(solution)/shard_map/ppermute | solution.py:446
  95.2 6.5 %collective-permute-start.5 = (bf16[768,2304]{1,0:T(8,128)(2,1)}, bf16[768,2304]{1,0:T(8,128)(2,1)S(1)}, u32[]{:S(2)}, u32[]{:S(2)}) collective-permute-start(bf16[768,2304]{1,0:T(8,128)(2,1)} %collective-permute-done.1.refs_2_), channel_id=1, source_target_pairs={{0,4},{4,0},{8,12},{12,8},{1,5},{5,1},{9,13},{13,9},{2,6},{6,2},{1... | collective-permute-start | bytes 10616840 | tf_op jit(solution)/shard_map/ppermute | solution.py:18
  95.2 37.5 %collective-permute-start.6 = (bf16[256,3072]{1,0:T(8,128)(2,1)S(1)}, bf16[256,3072]{1,0:T(8,128)(2,1)S(1)}, u32[]{:S(2)}, u32[]{:S(2)}) collective-permute-start(bf16[256,3072]{1,0:T(8,128)(2,1)S(1)} %collective-permute-done.2.refs_5_), channel_id=1, source_target_pairs={{1,0},{2,1},{5,4},{6,5},{9,8},{10,9},{13,12},{14,13},{17,16},{18,1... | collective-permute-start | bytes 4718600 | tf_op jit(solution)/shard_map/ppermute | solution.py:461
  96.5 36.2 %collective-permute-start.7 = (bf16[256,3072]{1,0:T(8,128)(2,1)}, bf16[256,3072]{1,0:T(8,128)(2,1)S(1)}, u32[]{:S(2)}, u32[]{:S(2)}) collective-permute-start(bf16[256,3072]{1,0:T(8,128)(2,1)} %collective-permute-done.3.refs_6_), channel_id=1, source_target_pairs={{1,2},{2,3},{5,6},{6,7},{9,10},{10,11},{13,14},{14,15},{17,18},{18... | collective-permute-start | bytes 4718600 | tf_op jit(solution)/shard_map/ppermute | solution.py:461
  97.3 52.7 %collective-permute-start.11 = (bf16[3072,384]{1,0:T(8,128)(2,1)}, bf16[3072,384]{1,0:T(8,128)(2,1)}, u32[]{:S(2)}, u32[]{:S(2)}) collective-permute-start(bf16[3072,384]{1,0:T(8,128)(2,1)} %all-gather.2.cloned.1.call-done.refs_5_.refs_3_), channel_id=1, source_target_pairs={{0,16},{16,0},{1,17},{17,1},{2,18},{18,2},{3,19},{19,3},{4,20},{20... | collective-permute-start | bytes 7077896 | tf_op jit(solution)/shard_map/ppermute | solution.py:33
  98.6 53.9 %collective-permute-start.10 = (bf16[3072,384]{1,0:T(8,128)(2,1)}, bf16[3072,384]{1,0:T(8,128)(2,1)}, u32[]{:S(2)}, u32[]{:S(2)}) collective-permute-start(bf16[3072,384]{1,0:T(8,128)(2,1)} %all-gather.2.cloned.1.call-done.refs_5_.refs_3_), channel_id=1, source_target_pairs={{0,8},{4,12},{8,0},{12,4},{1,9},{5,13},{9,1},{13,5},{2,10},{6,14},... | collective-permute-start | bytes 7077896 | tf_op jit(solution)/shard_map/ppermute | solution.py:18
  106.8 25.9 %copy-start.8 = (bf16[3072,384]{1,0:T(8,128)(2,1)S(1)}, bf16[3072,384]{1,0:T(8,128)(2,1)}, u32[]{:S(2)}) copy-start(bf16[3072,384]{1,0:T(8,128)(2,1)} %all-gather.2.cloned.1.call-done.refs_5_.refs_3_) | copy-start | bytes 7077892
  132.7 39.7 %collective-permute-start.12 = (bf16[3072,384]{1,0:T(8,128)(2,1)S(1)}, bf16[3072,384]{1,0:T(8,128)(2,1)}, u32[]{:S(2)}, u32[]{:S(2)}) collective-permute-start(bf16[3072,384]{1,0:T(8,128)(2,1)S(1)} %copy-done.8), channel_id=1, source_target_pairs={{0,4},{4,0},{8,12},{12,8},{1,5},{5,1},{9,13},{13,9},{2,6},{6,2},{1... | collective-permute-start | bytes 7077896 | tf_op jit(solution)/shard_map/ppermute | solution.py:18
  133.9 38.5 %collective-permute-start.8 = (bf16[256,3072]{1,0:T(8,128)(2,1)S(1)}, bf16[256,3072]{1,0:T(8,128)(2,1)S(1)}, u32[]{:S(2)}, u32[]{:S(2)}) collective-permute-start(bf16[256,3072]{1,0:T(8,128)(2,1)S(1)} %collective-permute-done.6.refs_4_.refs_12_), channel_id=1, source_target_pairs={{1,0},{5,4},{9,8},{13,12},{17,16},{21,20},{25,24},{29,28}} | collective-permute-start | bytes 4718600 | tf_op jit(solution)/shard_map/ppermute | solution.py:461
  135.2 37.2 %collective-permute-start.9 = (bf16[256,3072]{1,0:T(8,128)(2,1)S(1)}, bf16[256,3072]{1,0:T(8,128)(2,1)S(1)}, u32[]{:S(2)}, u32[]{:S(2)}) collective-permute-start(bf16[256,3072]{1,0:T(8,128)(2,1)S(1)} %collective-permute-done.7.refs_6_.refs_13_), channel_id=1, source_target_pairs={{2,3},{6,7},{10,11},{14,15},{18,19},{22,23},{26,27},{30,31}} | collective-permute-start | bytes 4718600 | tf_op jit(solution)/shard_map/ppermute | solution.py:461
  172.5 11.2 %collective-permute-start.13 = (bf16[3072,384]{1,0:T(8,128)(2,1)}, bf16[3072,384]{1,0:T(8,128)(2,1)S(1)}, u32[]{:S(2)}, u32[]{:S(2)}) collective-permute-start(bf16[3072,384]{1,0:T(8,128)(2,1)} %collective-permute-done.11.refs_6_.refs_4_), channel_id=1, source_target_pairs={{0,4},{4,0},{8,12},{12,8},{1,5},{5,1},{9,13},{13,9},{2,6},{6,2},{1... | collective-permute-start | bytes 7077896 | tf_op jit(solution)/shard_map/ppermute | solution.py:18
  173.0 10.6 %collective-permute-start.14 = (bf16[3072,384]{1,0:T(8,128)(2,1)}, bf16[3072,384]{1,0:T(8,128)(2,1)S(1)}, u32[]{:S(2)}, u32[]{:S(2)}) collective-permute-start(bf16[3072,384]{1,0:T(8,128)(2,1)} %collective-permute-done.10.refs_9_.refs_7_), channel_id=1, source_target_pairs={{0,4},{4,0},{8,12},{12,8},{1,5},{5,1},{9,13},{13,9},{2,6},{6,2},{1... | collective-permute-start | bytes 7077896 | tf_op jit(solution)/shard_map/ppermute | solution.py:18
  173.1 27.3 %collective-permute-start.18 = (bf16[1536,384]{1,0:T(8,128)(2,1)}, bf16[1536,384]{1,0:T(8,128)(2,1)S(1)}, u32[]{:S(2)}, u32[]{:S(2)}) collective-permute-start(bf16[1536,384]{1,0:T(8,128)(2,1)} %slice.16), channel_id=1, source_target_pairs={{0,16},{16,0},{1,17},{17,1},{2,18},{18,2},{3,19},{19,3},{4,20},{20... | collective-permute-start | bytes 3538952 | tf_op jit(solution)/shard_map/ppermute | solution.py:33
  174.3 27.0 %collective-permute-start.19 = (bf16[1536,384]{1,0:T(8,128)(2,1)}, bf16[1536,384]{1,0:T(8,128)(2,1)S(1)}, u32[]{:S(2)}, u32[]{:S(2)}) collective-permute-start(bf16[1536,384]{1,0:T(8,128)(2,1)} %slice.17), channel_id=1, source_target_pairs={{0,8},{4,12},{8,0},{12,4},{1,9},{5,13},{9,1},{13,5},{2,10},{6,14},... | collective-permute-start | bytes 3538952 | tf_op jit(solution)/shard_map/ppermute | solution.py:18
  183.7 14.0 %copy-start.9 = (bf16[3072,384]{1,0:T(8,128)(2,1)}, bf16[3072,384]{1,0:T(8,128)(2,1)S(1)}, u32[]{:S(2)}) copy-start(bf16[3072,384]{1,0:T(8,128)(2,1)S(1)} %collective-permute-done.13.refs_8_.refs_6_) | copy-start | bytes 7077892
  183.7 28.9 %copy-start.4 = (f32[5,3072]{1,0:T(8,128)S(1)}, f32[5,3072]{1,0:T(8,128)}, u32[]{:S(2)}) copy-start(f32[5,3072]{1,0:T(8,128)} %refs_14_.1) | copy-start | bytes 184324
  183.7 17.6 %collective-permute-start.15 = (bf16[256,384]{1,0:T(8,128)(2,1)S(1)}, bf16[256,384]{1,0:T(8,128)(2,1)S(1)}, u32[]{:S(2)}, u32[]{:S(2)}) collective-permute-start(bf16[256,384]{1,0:T(8,128)(2,1)S(1)} %get-tuple-element.138), channel_id=1, source_target_pairs={{0,2},{1,3},{2,0},{3,1},{4,6},{5,7},{6,4},{7,5},{8,10},{9,11},{10,... | collective-permute-start | bytes 589832 | tf_op jit(solution)/shard_map/ppermute | solution.py:33
  186.2 15.1 %collective-permute-start.16 = (bf16[256,384]{1,0:T(8,128)(2,1)S(1)}, bf16[256,384]{1,0:T(8,128)(2,1)S(1)}, u32[]{:S(2)}, u32[]{:S(2)}) collective-permute-start(bf16[256,384]{1,0:T(8,128)(2,1)S(1)} %get-tuple-element.139), channel_id=1, source_target_pairs={{0,1},{1,2},{2,3},{3,0},{4,5},{5,6},{6,7},{7,4},{8,9},{9,10},{10,1... | collective-permute-start | bytes 589832 | tf_op jit(solution)/shard_map/ppermute | solution.py:33
  188.4 12.9 %collective-permute-start.17 = (bf16[256,384]{1,0:T(8,128)(2,1)S(1)}, bf16[256,384]{1,0:T(8,128)(2,1)S(1)}, u32[]{:S(2)}, u32[]{:S(2)}) collective-permute-start(bf16[256,384]{1,0:T(8,128)(2,1)S(1)} %get-tuple-element.140), channel_id=1, source_target_pairs={{0,3},{1,0},{2,1},{3,2},{4,7},{5,4},{6,5},{7,6},{8,11},{9,8},{10,9... | collective-permute-start | bytes 589832 | tf_op jit(solution)/shard_map/ppermute | solution.py:33
  201.3 21.8 %copy-start.5 = (bf16[3072,64]{0,1:T(8,128)(2,1)S(1)}, bf16[3072,64]{0,1:T(8,128)(2,1)}, u32[]{:S(2)}) copy-start(bf16[3072,64]{0,1:T(8,128)(2,1)} %param.13) | copy-start | bytes 1179652
  201.3 21.8 %copy-start.6 = (f32[1,256,64]{1,2,0:T(8,128)S(1)}, f32[1,256,64]{1,2,0:T(8,128)}, u32[]{:S(2)}) copy-start(f32[1,256,64]{1,2,0:T(8,128)} %param.14) | copy-start | bytes 196612
  201.3 9.1 %collective-permute-start.23 = (bf16[1536,384]{1,0:T(8,128)(2,1)S(1)}, bf16[1536,384]{1,0:T(8,128)(2,1)S(1)}, u32[]{:S(2)}, u32[]{:S(2)}) collective-permute-start(bf16[1536,384]{1,0:T(8,128)(2,1)S(1)} %collective-permute-done.18.refs_10_.refs_8_), channel_id=1, source_target_pairs={{0,4},{4,0},{8,12},{12,8},{1,5},{5,1},{9,13},{13,9},{2,6},{6,2},{1... | collective-permute-start | bytes 3538952 | tf_op jit(solution)/shard_map/ppermute | solution.py:18
  203.0 7.5 %collective-permute-start.24 = (bf16[1536,384]{1,0:T(8,128)(2,1)S(1)}, bf16[1536,384]{1,0:T(8,128)(2,1)S(1)}, u32[]{:S(2)}, u32[]{:S(2)}) collective-permute-start(bf16[1536,384]{1,0:T(8,128)(2,1)S(1)} %collective-permute-done.19.refs_11_.refs_9_), channel_id=1, source_target_pairs={{0,4},{4,0},{8,12},{12,8},{1,5},{5,1},{9,13},{13,9},{2,6},{6,2},{1... | collective-permute-start | bytes 3538952 | tf_op jit(solution)/shard_map/ppermute | solution.py:18
  203.1 20.0 %collective-permute-start.20 = (bf16[256,384]{1,0:T(8,128)(2,1)S(1)}, bf16[256,384]{1,0:T(8,128)(2,1)S(1)}, u32[]{:S(2)}, u32[]{:S(2)}) collective-permute-start(bf16[256,384]{1,0:T(8,128)(2,1)S(1)} %get-tuple-element.143), channel_id=1, source_target_pairs={{0,2},{1,3},{2,0},{3,1},{4,6},{5,7},{6,4},{7,5},{8,10},{9,11},{10,... | collective-permute-start | bytes 589832 | tf_op jit(solution)/shard_map/ppermute | solution.py:33
  207.2 15.9 %collective-permute-start.21 = (bf16[256,384]{1,0:T(8,128)(2,1)S(1)}, bf16[256,384]{1,0:T(8,128)(2,1)S(1)}, u32[]{:S(2)}, u32[]{:S(2)}) collective-permute-start(bf16[256,384]{1,0:T(8,128)(2,1)S(1)} %get-tuple-element.144), channel_id=1, source_target_pairs={{0,1},{1,2},{2,3},{3,0},{4,5},{5,6},{6,7},{7,4},{8,9},{9,10},{10,1... | collective-permute-start | bytes 589832 | tf_op jit(solution)/shard_map/ppermute | solution.py:33
  207.7 15.4 %collective-permute-start.22 = (bf16[256,384]{1,0:T(8,128)(2,1)S(1)}, bf16[256,384]{1,0:T(8,128)(2,1)S(1)}, u32[]{:S(2)}, u32[]{:S(2)}) collective-permute-start(bf16[256,384]{1,0:T(8,128)(2,1)S(1)} %get-tuple-element.145), channel_id=1, source_target_pairs={{0,3},{1,0},{2,1},{3,2},{4,7},{5,4},{6,5},{7,6},{8,11},{9,8},{10,9... | collective-permute-start | bytes 589832 | tf_op jit(solution)/shard_map/ppermute | solution.py:33
  232.0 9.4 %collective-permute-start.25 = (bf16[128,256]{1,0:T(8,128)(2,1)S(1)}, bf16[128,256]{1,0:T(8,128)(2,1)S(1)}, u32[]{:S(2)}, u32[]{:S(2)}) collective-permute-start(bf16[128,256]{1,0:T(8,128)(2,1)S(1)} %get-tuple-element.160), channel_id=1, source_target_pairs={{2,4},{3,5},{6,8},{7,9},{10,12},{11,13},{4,2},{5,3},{8,6},{9,7},{1... | collective-permute-start | bytes 196616 | tf_op jit(solution)/shard_map/ppermute | solution.py:602
  (11 other events, 54.0 us)
Sparse Core Ops, SparseCore 0:
  9.6 82.3 all-gather.1

commit v11 on v10

--- a/solution.py
+++ b/solution.py
@@ -193,7 +193,7 @@
     gather_known(known, counts, queries, keys, values)
     for first in range(0, sum(counts), rows):
         part = slice(first, first + rows)
-        out_ref[0, part] = weigh(queries[part], keys[...], values[...])
+        out_ref[0, part] = weigh(queries[part], keys[...], values[...]).astype(jnp.bfloat16)
 
 
 def early(known, rows):
@@ -206,7 +206,7 @@
             pl.BlockSpec((1, count, HD), lambda h: (h, 0, 0)) for count in counts for _ in range(3)
         ],
         out_specs=pl.BlockSpec((1, length, 2 * HD), lambda h: (h, 0, 0)),
-        out_shape=jax.ShapeDtypeStruct((heads, length, 2 * HD), jnp.float32),
+        out_shape=jax.ShapeDtypeStruct((heads, length, 2 * HD), jnp.bfloat16),
         scratch_shapes=[
             pltpu.VMEM((length, HD), jnp.bfloat16),
             pltpu.VMEM((length, HD), jnp.bfloat16),
@@ -235,7 +235,8 @@
     queries[start:] = root_norm(proj[:, :HD])
     keys[start:] = root_norm(proj[:, HD : 2 * HD])
     values[start:, :HD] = proj[:, 2 * HD :].astype(jnp.bfloat16)
-    mixed = before_ref[0] + weigh(queries[:start], keys[start:], values[start:])
+    mixed = before_ref[0].astype(jnp.float32)
+    mixed += weigh(queries[:start], keys[start:], values[start:])
     done[:start] = (mixed[:, :HD] / mixed[:, HD:]).astype(jnp.bfloat16)
     mixed = weigh(queries[start:], keys[...], values[...])
     done[start:] = (mixed[:, :HD] / mixed[:, HD:]).astype(jnp.bfloat16)
@@ -332,8 +333,8 @@
 def finish_kernel(offsets, splits, starts_ref, rows_ref, coef_ref, *refs):
     parts = refs[: len(offsets)]
     sources, refs = split_refs(refs[len(offsets) :], splits)
-    before_ref, mod_ref, head_ref, latent_ref, weight_ref, out_ref, sent_ref = refs[:7]
-    weights, wide, sems, mixed = refs[7:]
+    before_ref, mod_ref, head_ref, latent_ref, weight_ref = refs[:5]
+    moved_ref, guess_ref, sent_ref, weights, wide, sems, mixed = refs[5:]
     count = len(splits)
     width = weights.shape[2]
     held = {}
@@ -371,8 +372,8 @@
     base, weight = latent_ref[...], weight_ref[...]
     moved = (base + coef_ref[1] * velocity) * weight
     guess = (base - coef_ref[0] * velocity) * weight
-    out_ref[:channels, :] = moved
-    out_ref[channels:, :] = guess
+    moved_ref[...] = moved
+    guess_ref[...] = guess
     sent_ref[:channels, :] = moved.astype(jnp.bfloat16)
     sent_ref[channels:, :] = guess.astype(jnp.bfloat16)
 
@@ -411,9 +412,10 @@
     return pl.pallas_call(
         functools.partial(finish_kernel, offsets, splits),
         in_specs=[smem] * 3 + [vmem] * len(parts) + [hbm] * len(pieces) + [vmem] * 5,
-        out_specs=[vmem, vmem],
+        out_specs=[vmem] * 3,
         out_shape=[
-            jax.ShapeDtypeStruct((2 * channels, rows), jnp.float32),
+            jax.ShapeDtypeStruct((channels, rows), jnp.float32),
+            jax.ShapeDtypeStruct((channels, rows), jnp.float32),
             jax.ShapeDtypeStruct((2 * channels, rows), jnp.bfloat16),
         ],
         scratch_shapes=scratch
@@ -589,7 +591,7 @@
         local,
         modulation,
     )
-    weighted, to_join = accumulate(
+    moved, guess, to_join = accumulate(
         received[1],
         offsets[1],
         starts,
@@ -600,9 +602,10 @@
         (coef, w_head.T, latent[0].T, weight),
     )
     other = lax.ppermute(to_join, ("tile", "seq"), joins).astype(jnp.float32)
-    joined = (weighted + other) / norms
     channels = w_head.shape[1]
-    return (joined[:channels].T[None], joined[channels:].T[None])
+    stepped = (moved + other[:channels]) / norms
+    clean = (guess + other[channels:]) / norms
+    return (stepped.T[None], clean.T[None])
 
 
 def solution(mesh):

time: 250 us -> 250 us (level)
  no operation moved by 1% of the time
where the time goes in v11:
time: 250 us; the launch traced here: 249 us
  waiting for transfers between devices  107 us (43%)
  Pallas kernels  63.3 us (25%)
  starting transfers between devices  45.4 us (18%)
  local copies, waits for them, and re-layouts  16.6 us (7%)
  between operations  15.1 us (6%)
    ppermute x1, waiting for transfers between devices, shards(): lax.ppermute(weight.astype(jnp.bfloat16), ('tile', 'seq'), joins)  65.9 us
    ppermute x6, waiting for transfers between devices, hop(): lax.ppermute(blocks_by[way * (step - 1)], 'seq', step_pairs(devices, step...  18.3 us
    pallas_call x2, Pallas kernels, project(): pl.pallas_call(functools.partial(project_kernel, plan, len(blocks)), grid...  17.9 us
    ppermute x8, waiting for transfers between devices, turned(): lax.ppermute(value, axis, [(i, (i + turn) % count) for i in range(count)])  17.2 us
    pallas_call x2, Pallas kernels, attend(): pl.pallas_call(functools.partial(attend_kernel, plan, len(blocks), counts...  16 us
    ppermute x8, starting transfers between devices, turned(): lax.ppermute(value, axis, [(i, (i + turn) % count) for i in range(count)])  15.4 us
    pallas_call x1, Pallas kernels, accumulate(): pl.pallas_call(functools.partial(add_kernel, offsets, splits), in_specs=[...  10.5 us
    unnamed x32, local copies, waits for them, and re-layouts  10.1 us
  transfers between devices with their start and end apart: 27, of which 8 were waited for; matrix products, arithmetic and copies ran while one was open for 3% of the time, Pallas kernels for 22%

profile of v11, /device:TPU:1, one launch (start us, length us, event | category | flops | bytes accessed | tf_op | source)
XLA Modules:
  0.0 249.1 jit_solution(8367008367884960676)
XLA Ops:
  9.5 2.7 %collective-permute-start.1 = (bf16[768,2304]{1,0:T(8,128)(2,1)}, bf16[768,2304]{1,0:T(8,128)(2,1)}, u32[]{:S(2)}, u32[]{:S(2)}) collective-permute-start(bf16[768,2304]{1,0:T(8,128)(2,1)} %refs_0_.3), channel_id=1, source_target_pairs={{0,8},{4,12},{8,0},{12,4},{1,9},{5,13},{9,1},{13,5},{2,10},{6,14},... | collective-permute-start | bytes 10616840 | tf_op jit(solution)/shard_map/ppermute | solution.py:18
  12.8 4.4 %norm_in.1.refs_4_ = bf16[256,3072]{1,0:T(8,128)(2,1)} custom-call(s32[4]{0:T(128)} %pad_add_fusion.starts_ref, bf16[256,3072]{1,0:T(8,128)(2,1)} %bitcast.35, f32[5,3072]{1,0:T(8,128)} %refs_14_.1), custom_call_target="tpu_custom_call" | custom-call | tf_op jit(solution)/shard_map/norm_in/pallas_call | solution.py:78
  17.2 4.3 %collective-permute-start.3 = (bf16[256,3072]{1,0:T(8,128)(2,1)}, bf16[256,3072]{1,0:T(8,128)(2,1)}, u32[]{:S(2)}, u32[]{:S(2)}) collective-permute-start(bf16[256,3072]{1,0:T(8,128)(2,1)} %norm_in.1.refs_4_), channel_id=1, source_target_pairs={{0,1},{1,2},{2,3},{4,5},{5,6},{6,7},{8,9},{9,10},{10,11},{12,13},{... | collective-permute-start | bytes 4718600 | tf_op jit(solution)/shard_map/ppermute | solution.py:463
  22.8 4.7 %collective-permute-start.4 = (bf16[1,256]{1,0:T(2,128)(2,1)S(1)}, bf16[1,256]{1,0:T(2,128)(2,1)S(1)}, u32[]{:S(2)}, u32[]{:S(2)}) collective-permute-start(bf16[1,256]{1,0:T(2,128)(2,1)S(1)} %get-tuple-element.167), channel_id=1, source_target_pairs={{2,4},{3,5},{6,8},{7,9},{10,12},{11,13},{4,2},{5,3},{8,6},{9,7},{1... | collective-permute-start | bytes 1544 | tf_op jit(solution)/shard_map/ppermute | solution.py:448
  29.2 65.9 %collective-permute-done.4 = bf16[1,256]{1,0:T(2,128)(2,1)S(1)} collective-permute-done((bf16[1,256]{1,0:T(2,128)(2,1)S(1)}, bf16[1,256]{1,0:T(2,128)(2,1)S(1)}, u32[]{:S(2)}, u32[]{:S(2)}) %collective-permute-start.4) | collective-permute-done | bytes 544 | tf_op jit(solution)/shard_map/ppermute | solution.py:448
  95.2 1.3 collective-permute-start.6
  98.6 1.5 collective-permute-start.10
  100.0 1.6 collective-permute-done.5.refs_3_
  101.7 1.9 copy-done.7
  103.5 2.0 copy-done.1
  105.5 1.4 copy-done.3
  107.0 10.7 %project.2 = (bf16[6,512,128]{2,1,0:T(8,128)(2,1)S(1)}, bf16[6,512,128]{2,1,0:T(8,128)(2,1)S(1)}, bf16[6,512,128]{2,1,0:T(8,128)(2,1)S(1)}) custom-call(s32[1]{0:T(128)} %bitcast.18.place_ref, bf16[768,2304]{1,0:T(8,128)(2,1)S(1)} %copy-done.1, bf16[768,2304]{1,0:T(8,128)(2,1)} %collective-permute-done.refs_1_, ...), custom_call_target="tpu_custom_call" | custom-call | tf_op jit(solution)/shard_map/project/pallas_call | solution.py:152
  117.7 15.1 %collective-permute-done.6.refs_4_.refs_12_ = bf16[256,3072]{1,0:T(8,128)(2,1)S(1)} collective-permute-done((bf16[256,3072]{1,0:T(8,128)(2,1)S(1)}, bf16[256,3072]{1,0:T(8,128)(2,1)S(1)}, u32[]{:S(2)}, u32[]{:S(2)}) %collective-permute-start.6) | collective-permute-done | bytes 1572896 | tf_op jit(solution)/shard_map/ppermute | solution.py:463
  136.0 14.0 %collective-permute-done.11.refs_6_.refs_4_ = bf16[3072,384]{1,0:T(8,128)(2,1)} collective-permute-done((bf16[3072,384]{1,0:T(8,128)(2,1)}, bf16[3072,384]{1,0:T(8,128)(2,1)}, u32[]{:S(2)}, u32[]{:S(2)}) %collective-permute-start.11) | collective-permute-done | bytes 2359328 | tf_op jit(solution)/shard_map/ppermute | solution.py:33
  150.0 2.5 slice.17
  152.5 2.4 slice.16
  154.9 7.2 %project.3 = (bf16[6,256,128]{2,1,0:T(8,128)(2,1)S(1)}, bf16[6,256,128]{2,1,0:T(8,128)(2,1)S(1)}, bf16[6,256,128]{2,1,0:T(8,128)(2,1)S(1)}) custom-call(s32[1]{0:T(128)} %bitcast.18.place_ref, bf16[768,2304]{1,0:T(8,128)(2,1)S(1)} %copy-done.1, bf16[768,2304]{1,0:T(8,128)(2,1)} %collective-permute-done.refs_1_, ...), custom_call_target="tpu_custom_call" | custom-call | tf_op jit(solution)/shard_map/project/pallas_call | solution.py:152
  162.1 5.6 %early.1.refs_4_ = bf16[6,768,256]{2,1,0:T(8,128)(2,1)S(1)} custom-call(bf16[6,512,128]{2,1,0:T(8,128)(2,1)S(1)} %get-tuple-element.113.refs_0_.refs_5_, bf16[6,512,128]{2,1,0:T(8,128)(2,1)S(1)} %get-tuple-element.114.refs_1_.refs_6_, bf16[6,512,128]{2,1,0:T(8,128)(2,1)S(1)} %get-tuple-element.115.refs_2_.refs_7_, ...), custom_call_target="tpu_custom_call" | custom-call | tf_op jit(solution)/shard_map/early/pallas_call | solution.py:202
  167.8 1.5 copy-done.2
  169.2 3.2 %collective-permute-done.8.refs_11_ = bf16[256,3072]{1,0:T(8,128)(2,1)S(1)} collective-permute-done((bf16[256,3072]{1,0:T(8,128)(2,1)S(1)}, bf16[256,3072]{1,0:T(8,128)(2,1)S(1)}, u32[]{:S(2)}, u32[]{:S(2)}) %collective-permute-start.8) | collective-permute-done | bytes 1572896 | tf_op jit(solution)/shard_map/ppermute | solution.py:463
  175.6 8.0 %attend.2 = (bf16[256,384]{1,0:T(8,128)(2,1)S(1)}, bf16[256,384]{1,0:T(8,128)(2,1)S(1)}, bf16[256,384]{1,0:T(8,128)(2,1)S(1)}, bf16[256,384]{1,0:T(8,128)(2,1)S(1)}) custom-call(s32[1]{0:T(128)} %bitcast.18.place_ref, s32[4]{0:T(128)S(1)} %dynamic-slice_bitcast_fusion.slots_ref, bf16[768,2304]{1,0:T(8,128)(2,1)} %refs_0_.3, ...), custom_call_target="tpu_custom_call" | custom-call | tf_op jit(solution)/shard_map/attend/pallas_call | solution.py:255
  183.6 2.5 collective-permute-start.15
  186.1 2.2 collective-permute-start.16
  189.4 8.0 %attend.3 = (bf16[256,384]{1,0:T(8,128)(2,1)S(1)}, bf16[256,384]{1,0:T(8,128)(2,1)S(1)}, bf16[256,384]{1,0:T(8,128)(2,1)S(1)}, bf16[256,384]{1,0:T(8,128)(2,1)S(1)}) custom-call(s32[1]{0:T(128)} %bitcast.18.place_ref, s32[4]{0:T(128)S(1)} %dynamic-slice_bitcast_fusion.slots_ref, bf16[768,2304]{1,0:T(8,128)(2,1)} %refs_0_.3, ...), custom_call_target="tpu_custom_call" | custom-call | tf_op jit(solution)/shard_map/attend/pallas_call | solution.py:255
  197.5 3.1 %collective-permute-done.18.refs_10_.refs_8_ = bf16[1536,384]{1,0:T(8,128)(2,1)S(1)} collective-permute-done((bf16[1536,384]{1,0:T(8,128)(2,1)}, bf16[1536,384]{1,0:T(8,128)(2,1)S(1)}, u32[]{:S(2)}, u32[]{:S(2)}) %collective-permute-start.18) | collective-permute-done | bytes 1179680 | tf_op jit(solution)/shard_map/ppermute | solution.py:33
  201.5 1.7 collective-permute-start.23
  203.3 3.9 %collective-permute-start.20 = (bf16[256,384]{1,0:T(8,128)(2,1)S(1)}, bf16[256,384]{1,0:T(8,128)(2,1)S(1)}, u32[]{:S(2)}, u32[]{:S(2)}) collective-permute-start(bf16[256,384]{1,0:T(8,128)(2,1)S(1)} %get-tuple-element.144), channel_id=1, source_target_pairs={{0,2},{1,3},{2,0},{3,1},{4,6},{5,7},{6,4},{7,5},{8,10},{9,11},{10,... | collective-permute-start | bytes 589832 | tf_op jit(solution)/shard_map/ppermute | solution.py:33
  207.9 2.6 %collective-permute-start.22 = (bf16[256,384]{1,0:T(8,128)(2,1)S(1)}, bf16[256,384]{1,0:T(8,128)(2,1)S(1)}, u32[]{:S(2)}, u32[]{:S(2)}) collective-permute-start(bf16[256,384]{1,0:T(8,128)(2,1)S(1)} %get-tuple-element.146), channel_id=1, source_target_pairs={{0,3},{1,0},{2,1},{3,2},{4,7},{5,4},{6,5},{7,6},{8,11},{9,8},{10,9... | collective-permute-start | bytes 589832 | tf_op jit(solution)/shard_map/ppermute | solution.py:33
  212.5 10.5 %add_parts.1.refs_13_ = f32[256,3072]{1,0:T(8,128)} custom-call(s32[8]{0:T(128)S(1)} %stack.79.starts_ref, s32[4]{0:T(128)S(1)} %pad_add_fusion.1.rows_ref, bf16[256,384]{1,0:T(8,128)(2,1)S(1)} %get-tuple-element.155.refs_0_, bf16[256,384]{1,0:T(8,128)(2,1)S(1)} %get-tuple-element.156.refs_1_, bf16[256,384]{1,0:T(8,128)(2,1)S(1)} %collective-permute-done.15.refs_2_, ...), custom_call_target="tpu_custom_call" | custom-call | tf_op jit(solution)/shard_map/add_parts/pallas_call | solution.py:400
  223.0 8.9 %finish.1 = (f32[64,256]{1,0:T(8,128)S(1)}, f32[64,256]{1,0:T(8,128)S(1)}, bf16[128,256]{1,0:T(8,128)(2,1)S(1)}) custom-call(s32[8]{0:T(128)S(1)} %stack.79.starts_ref, s32[4]{0:T(128)S(1)} %pad_add_fusion.1.rows_ref, f32[2]{0:T(128)S(1)} %pad_maximum_fusion.coef_ref, bf16[256,384]{1,0:T(8,128)(2,1)S(1)} %collective-permute-done.20.refs_0_, ...), custom_call_target="tpu_custom_call" | custom-call | tf_op jit(solution)/shard_map/finish/pallas_call | solution.py:412
  231.9 6.3 %collective-permute-start.25 = (bf16[128,256]{1,0:T(8,128)(2,1)S(1)}, bf16[128,256]{1,0:T(8,128)(2,1)S(1)}, u32[]{:S(2)}, u32[]{:S(2)}) collective-permute-start(bf16[128,256]{1,0:T(8,128)(2,1)S(1)} %get-tuple-element.161), channel_id=1, source_target_pairs={{2,4},{3,5},{6,8},{7,9},{10,12},{11,13},{4,2},{5,3},{8,6},{9,7},{1... | collective-permute-start | bytes 196616 | tf_op jit(solution)/shard_map/ppermute | solution.py:604
  238.2 3.3 %collective-permute-done.25 = bf16[128,256]{1,0:T(8,128)(2,1)S(1)} collective-permute-done((bf16[128,256]{1,0:T(8,128)(2,1)S(1)}, bf16[128,256]{1,0:T(8,128)(2,1)S(1)}, u32[]{:S(2)}, u32[]{:S(2)}) %collective-permute-start.25) | collective-permute-done | bytes 65568 | tf_op jit(solution)/shard_map/ppermute | solution.py:604
  (75 shorter events, 19.2 us)
Async XLA Ops:
  7.2 87.9 %all-gather.2.cloned.1.call-start = ((), (), s32[]{:S(2)}) async-start(), calls=%async_computation | async-start | bytes 2949120 | tf_op jit(solution)/shard_map/all_gather | solution.py:475
  9.4 85.7 %collective-permute-start = (bf16[768,2304]{1,0:T(8,128)(2,1)}, bf16[768,2304]{1,0:T(8,128)(2,1)}, u32[]{:S(2)}, u32[]{:S(2)}) collective-permute-start(bf16[768,2304]{1,0:T(8,128)(2,1)} %refs_0_.3), channel_id=1, source_target_pairs={{0,4},{4,0},{8,12},{12,8},{1,5},{5,1},{9,13},{13,9},{2,6},{6,2},{1... | collective-permute-start | bytes 10616840 | tf_op jit(solution)/shard_map/ppermute | solution.py:18
  9.5 85.6 %collective-permute-start.1 = (bf16[768,2304]{1,0:T(8,128)(2,1)}, bf16[768,2304]{1,0:T(8,128)(2,1)}, u32[]{:S(2)}, u32[]{:S(2)}) collective-permute-start(bf16[768,2304]{1,0:T(8,128)(2,1)} %refs_0_.3), channel_id=1, source_target_pairs={{0,8},{4,12},{8,0},{12,4},{1,9},{5,13},{9,1},{13,5},{2,10},{6,14},... | collective-permute-start | bytes 10616840 | tf_op jit(solution)/shard_map/ppermute | solution.py:18
  17.2 77.9 %collective-permute-start.3 = (bf16[256,3072]{1,0:T(8,128)(2,1)}, bf16[256,3072]{1,0:T(8,128)(2,1)}, u32[]{:S(2)}, u32[]{:S(2)}) collective-permute-start(bf16[256,3072]{1,0:T(8,128)(2,1)} %norm_in.1.refs_4_), channel_id=1, source_target_pairs={{0,1},{1,2},{2,3},{4,5},{5,6},{6,7},{8,9},{9,10},{10,11},{12,13},{... | collective-permute-start | bytes 4718600 | tf_op jit(solution)/shard_map/ppermute | solution.py:463
  21.5 73.6 %collective-permute-start.2 = (bf16[256,3072]{1,0:T(8,128)(2,1)}, bf16[256,3072]{1,0:T(8,128)(2,1)S(1)}, u32[]{:S(2)}, u32[]{:S(2)}) collective-permute-start(bf16[256,3072]{1,0:T(8,128)(2,1)} %norm_in.1.refs_4_), channel_id=1, source_target_pairs={{1,0},{2,1},{3,2},{5,4},{6,5},{7,6},{9,8},{10,9},{11,10},{13,12},{... | collective-permute-start | bytes 4718600 | tf_op jit(solution)/shard_map/ppermute | solution.py:463
  22.8 72.2 %collective-permute-start.4 = (bf16[1,256]{1,0:T(2,128)(2,1)S(1)}, bf16[1,256]{1,0:T(2,128)(2,1)S(1)}, u32[]{:S(2)}, u32[]{:S(2)}) collective-permute-start(bf16[1,256]{1,0:T(2,128)(2,1)S(1)} %get-tuple-element.167), channel_id=1, source_target_pairs={{2,4},{3,5},{6,8},{7,9},{10,12},{11,13},{4,2},{5,3},{8,6},{9,7},{1... | collective-permute-start | bytes 1544 | tf_op jit(solution)/shard_map/ppermute | solution.py:448
  95.2 6.5 %collective-permute-start.5 = (bf16[768,2304]{1,0:T(8,128)(2,1)}, bf16[768,2304]{1,0:T(8,128)(2,1)S(1)}, u32[]{:S(2)}, u32[]{:S(2)}) collective-permute-start(bf16[768,2304]{1,0:T(8,128)(2,1)} %collective-permute-done.1.refs_2_), channel_id=1, source_target_pairs={{0,4},{4,0},{8,12},{12,8},{1,5},{5,1},{9,13},{13,9},{2,6},{6,2},{1... | collective-permute-start | bytes 10616840 | tf_op jit(solution)/shard_map/ppermute | solution.py:18
  95.2 37.5 %collective-permute-start.6 = (bf16[256,3072]{1,0:T(8,128)(2,1)S(1)}, bf16[256,3072]{1,0:T(8,128)(2,1)S(1)}, u32[]{:S(2)}, u32[]{:S(2)}) collective-permute-start(bf16[256,3072]{1,0:T(8,128)(2,1)S(1)} %collective-permute-done.2.refs_5_), channel_id=1, source_target_pairs={{1,0},{2,1},{5,4},{6,5},{9,8},{10,9},{13,12},{14,13},{17,16},{18,1... | collective-permute-start | bytes 4718600 | tf_op jit(solution)/shard_map/ppermute | solution.py:463
  96.5 36.2 %collective-permute-start.7 = (bf16[256,3072]{1,0:T(8,128)(2,1)}, bf16[256,3072]{1,0:T(8,128)(2,1)S(1)}, u32[]{:S(2)}, u32[]{:S(2)}) collective-permute-start(bf16[256,3072]{1,0:T(8,128)(2,1)} %collective-permute-done.3.refs_6_), channel_id=1, source_target_pairs={{1,2},{2,3},{5,6},{6,7},{9,10},{10,11},{13,14},{14,15},{17,18},{18... | collective-permute-start | bytes 4718600 | tf_op jit(solution)/shard_map/ppermute | solution.py:463
  97.3 52.7 %collective-permute-start.11 = (bf16[3072,384]{1,0:T(8,128)(2,1)}, bf16[3072,384]{1,0:T(8,128)(2,1)}, u32[]{:S(2)}, u32[]{:S(2)}) collective-permute-start(bf16[3072,384]{1,0:T(8,128)(2,1)} %all-gather.2.cloned.1.call-done.refs_5_.refs_3_), channel_id=1, source_target_pairs={{0,16},{16,0},{1,17},{17,1},{2,18},{18,2},{3,19},{19,3},{4,20},{20... | collective-permute-start | bytes 7077896 | tf_op jit(solution)/shard_map/ppermute | solution.py:33
  98.6 53.9 %collective-permute-start.10 = (bf16[3072,384]{1,0:T(8,128)(2,1)}, bf16[3072,384]{1,0:T(8,128)(2,1)}, u32[]{:S(2)}, u32[]{:S(2)}) collective-permute-start(bf16[3072,384]{1,0:T(8,128)(2,1)} %all-gather.2.cloned.1.call-done.refs_5_.refs_3_), channel_id=1, source_target_pairs={{0,8},{4,12},{8,0},{12,4},{1,9},{5,13},{9,1},{13,5},{2,10},{6,14},... | collective-permute-start | bytes 7077896 | tf_op jit(solution)/shard_map/ppermute | solution.py:18
  107.0 25.8 %copy-start.8 = (bf16[3072,384]{1,0:T(8,128)(2,1)S(1)}, bf16[3072,384]{1,0:T(8,128)(2,1)}, u32[]{:S(2)}) copy-start(bf16[3072,384]{1,0:T(8,128)(2,1)} %all-gather.2.cloned.1.call-done.refs_5_.refs_3_) | copy-start | bytes 7077892
  132.7 39.7 %collective-permute-start.12 = (bf16[3072,384]{1,0:T(8,128)(2,1)S(1)}, bf16[3072,384]{1,0:T(8,128)(2,1)S(1)}, u32[]{:S(2)}, u32[]{:S(2)}) collective-permute-start(bf16[3072,384]{1,0:T(8,128)(2,1)S(1)} %copy-done.8), channel_id=1, source_target_pairs={{0,4},{4,0},{8,12},{12,8},{1,5},{5,1},{9,13},{13,9},{2,6},{6,2},{1... | collective-permute-start | bytes 7077896 | tf_op jit(solution)/shard_map/ppermute | solution.py:18
  133.9 38.5 %collective-permute-start.8 = (bf16[256,3072]{1,0:T(8,128)(2,1)S(1)}, bf16[256,3072]{1,0:T(8,128)(2,1)S(1)}, u32[]{:S(2)}, u32[]{:S(2)}) collective-permute-start(bf16[256,3072]{1,0:T(8,128)(2,1)S(1)} %collective-permute-done.6.refs_4_.refs_12_), channel_id=1, source_target_pairs={{1,0},{5,4},{9,8},{13,12},{17,16},{21,20},{25,24},{29,28}} | collective-permute-start | bytes 4718600 | tf_op jit(solution)/shard_map/ppermute | solution.py:463
  135.2 37.2 %collective-permute-start.9 = (bf16[256,3072]{1,0:T(8,128)(2,1)S(1)}, bf16[256,3072]{1,0:T(8,128)(2,1)S(1)}, u32[]{:S(2)}, u32[]{:S(2)}) collective-permute-start(bf16[256,3072]{1,0:T(8,128)(2,1)S(1)} %collective-permute-done.7.refs_6_.refs_13_), channel_id=1, source_target_pairs={{2,3},{6,7},{10,11},{14,15},{18,19},{22,23},{26,27},{30,31}} | collective-permute-start | bytes 4718600 | tf_op jit(solution)/shard_map/ppermute | solution.py:463
  172.5 11.1 %collective-permute-start.13 = (bf16[3072,384]{1,0:T(8,128)(2,1)}, bf16[3072,384]{1,0:T(8,128)(2,1)S(1)}, u32[]{:S(2)}, u32[]{:S(2)}) collective-permute-start(bf16[3072,384]{1,0:T(8,128)(2,1)} %collective-permute-done.11.refs_6_.refs_4_), channel_id=1, source_target_pairs={{0,4},{4,0},{8,12},{12,8},{1,5},{5,1},{9,13},{13,9},{2,6},{6,2},{1... | collective-permute-start | bytes 7077896 | tf_op jit(solution)/shard_map/ppermute | solution.py:18
  173.1 10.5 %collective-permute-start.14 = (bf16[3072,384]{1,0:T(8,128)(2,1)}, bf16[3072,384]{1,0:T(8,128)(2,1)S(1)}, u32[]{:S(2)}, u32[]{:S(2)}) collective-permute-start(bf16[3072,384]{1,0:T(8,128)(2,1)} %collective-permute-done.10.refs_9_.refs_7_), channel_id=1, source_target_pairs={{0,4},{4,0},{8,12},{12,8},{1,5},{5,1},{9,13},{13,9},{2,6},{6,2},{1... | collective-permute-start | bytes 7077896 | tf_op jit(solution)/shard_map/ppermute | solution.py:18
  173.2 27.4 %collective-permute-start.18 = (bf16[1536,384]{1,0:T(8,128)(2,1)}, bf16[1536,384]{1,0:T(8,128)(2,1)S(1)}, u32[]{:S(2)}, u32[]{:S(2)}) collective-permute-start(bf16[1536,384]{1,0:T(8,128)(2,1)} %slice.16), channel_id=1, source_target_pairs={{0,16},{16,0},{1,17},{17,1},{2,18},{18,2},{3,19},{19,3},{4,20},{20... | collective-permute-start | bytes 3538952 | tf_op jit(solution)/shard_map/ppermute | solution.py:33
  174.4 27.1 %collective-permute-start.19 = (bf16[1536,384]{1,0:T(8,128)(2,1)}, bf16[1536,384]{1,0:T(8,128)(2,1)}, u32[]{:S(2)}, u32[]{:S(2)}) collective-permute-start(bf16[1536,384]{1,0:T(8,128)(2,1)} %slice.17), channel_id=1, source_target_pairs={{0,8},{4,12},{8,0},{12,4},{1,9},{5,13},{9,1},{13,5},{2,10},{6,14},... | collective-permute-start | bytes 3538952 | tf_op jit(solution)/shard_map/ppermute | solution.py:18
  183.6 13.9 %copy-start.10 = (bf16[3072,384]{1,0:T(8,128)(2,1)}, bf16[3072,384]{1,0:T(8,128)(2,1)S(1)}, u32[]{:S(2)}) copy-start(bf16[3072,384]{1,0:T(8,128)(2,1)S(1)} %collective-permute-done.13.refs_8_.refs_6_) | copy-start | bytes 7077892
  183.6 28.8 %copy-start.4 = (f32[5,3072]{1,0:T(8,128)S(1)}, f32[5,3072]{1,0:T(8,128)}, u32[]{:S(2)}) copy-start(f32[5,3072]{1,0:T(8,128)} %refs_14_.1) | copy-start | bytes 184324
  183.6 17.8 %collective-permute-start.15 = (bf16[256,384]{1,0:T(8,128)(2,1)S(1)}, bf16[256,384]{1,0:T(8,128)(2,1)S(1)}, u32[]{:S(2)}, u32[]{:S(2)}) collective-permute-start(bf16[256,384]{1,0:T(8,128)(2,1)S(1)} %get-tuple-element.139), channel_id=1, source_target_pairs={{0,2},{1,3},{2,0},{3,1},{4,6},{5,7},{6,4},{7,5},{8,10},{9,11},{10,... | collective-permute-start | bytes 589832 | tf_op jit(solution)/shard_map/ppermute | solution.py:33
  186.1 15.4 %collective-permute-start.16 = (bf16[256,384]{1,0:T(8,128)(2,1)S(1)}, bf16[256,384]{1,0:T(8,128)(2,1)S(1)}, u32[]{:S(2)}, u32[]{:S(2)}) collective-permute-start(bf16[256,384]{1,0:T(8,128)(2,1)S(1)} %get-tuple-element.140), channel_id=1, source_target_pairs={{0,1},{1,2},{2,3},{3,0},{4,5},{5,6},{6,7},{7,4},{8,9},{9,10},{10,1... | collective-permute-start | bytes 589832 | tf_op jit(solution)/shard_map/ppermute | solution.py:33
  188.3 13.2 %collective-permute-start.17 = (bf16[256,384]{1,0:T(8,128)(2,1)S(1)}, bf16[256,384]{1,0:T(8,128)(2,1)S(1)}, u32[]{:S(2)}, u32[]{:S(2)}) collective-permute-start(bf16[256,384]{1,0:T(8,128)(2,1)S(1)} %get-tuple-element.141), channel_id=1, source_target_pairs={{0,3},{1,0},{2,1},{3,2},{4,7},{5,4},{6,5},{7,6},{8,11},{9,8},{10,9... | collective-permute-start | bytes 589832 | tf_op jit(solution)/shard_map/ppermute | solution.py:33
  201.5 21.5 %copy-start.5 = (bf16[3072,64]{0,1:T(8,128)(2,1)S(1)}, bf16[3072,64]{0,1:T(8,128)(2,1)}, u32[]{:S(2)}) copy-start(bf16[3072,64]{0,1:T(8,128)(2,1)} %param.13) | copy-start | bytes 1179652
  201.5 21.5 %copy-start.6 = (f32[1,256,64]{1,2,0:T(8,128)S(1)}, f32[1,256,64]{1,2,0:T(8,128)}, u32[]{:S(2)}) copy-start(f32[1,256,64]{1,2,0:T(8,128)} %param.14) | copy-start | bytes 196612
  201.5 8.9 %collective-permute-start.23 = (bf16[1536,384]{1,0:T(8,128)(2,1)S(1)}, bf16[1536,384]{1,0:T(8,128)(2,1)S(1)}, u32[]{:S(2)}, u32[]{:S(2)}) collective-permute-start(bf16[1536,384]{1,0:T(8,128)(2,1)S(1)} %collective-permute-done.18.refs_10_.refs_8_), channel_id=1, source_target_pairs={{0,4},{4,0},{8,12},{12,8},{1,5},{5,1},{9,13},{13,9},{2,6},{6,2},{1... | collective-permute-start | bytes 3538952 | tf_op jit(solution)/shard_map/ppermute | solution.py:18
  203.2 7.2 %collective-permute-start.24 = (bf16[1536,384]{1,0:T(8,128)(2,1)}, bf16[1536,384]{1,0:T(8,128)(2,1)S(1)}, u32[]{:S(2)}, u32[]{:S(2)}) collective-permute-start(bf16[1536,384]{1,0:T(8,128)(2,1)} %collective-permute-done.19.refs_11_.refs_9_), channel_id=1, source_target_pairs={{0,4},{4,0},{8,12},{12,8},{1,5},{5,1},{9,13},{13,9},{2,6},{6,2},{1... | collective-permute-start | bytes 3538952 | tf_op jit(solution)/shard_map/ppermute | solution.py:18
  203.3 19.7 %collective-permute-start.20 = (bf16[256,384]{1,0:T(8,128)(2,1)S(1)}, bf16[256,384]{1,0:T(8,128)(2,1)S(1)}, u32[]{:S(2)}, u32[]{:S(2)}) collective-permute-start(bf16[256,384]{1,0:T(8,128)(2,1)S(1)} %get-tuple-element.144), channel_id=1, source_target_pairs={{0,2},{1,3},{2,0},{3,1},{4,6},{5,7},{6,4},{7,5},{8,10},{9,11},{10,... | collective-permute-start | bytes 589832 | tf_op jit(solution)/shard_map/ppermute | solution.py:33
  207.1 15.8 %collective-permute-start.21 = (bf16[256,384]{1,0:T(8,128)(2,1)S(1)}, bf16[256,384]{1,0:T(8,128)(2,1)S(1)}, u32[]{:S(2)}, u32[]{:S(2)}) collective-permute-start(bf16[256,384]{1,0:T(8,128)(2,1)S(1)} %get-tuple-element.145), channel_id=1, source_target_pairs={{0,1},{1,2},{2,3},{3,0},{4,5},{5,6},{6,7},{7,4},{8,9},{9,10},{10,1... | collective-permute-start | bytes 589832 | tf_op jit(solution)/shard_map/ppermute | solution.py:33
  207.9 15.1 %collective-permute-start.22 = (bf16[256,384]{1,0:T(8,128)(2,1)S(1)}, bf16[256,384]{1,0:T(8,128)(2,1)S(1)}, u32[]{:S(2)}, u32[]{:S(2)}) collective-permute-start(bf16[256,384]{1,0:T(8,128)(2,1)S(1)} %get-tuple-element.146), channel_id=1, source_target_pairs={{0,3},{1,0},{2,1},{3,2},{4,7},{5,4},{6,5},{7,6},{8,11},{9,8},{10,9... | collective-permute-start | bytes 589832 | tf_op jit(solution)/shard_map/ppermute | solution.py:33
  231.9 9.7 %collective-permute-start.25 = (bf16[128,256]{1,0:T(8,128)(2,1)S(1)}, bf16[128,256]{1,0:T(8,128)(2,1)S(1)}, u32[]{:S(2)}, u32[]{:S(2)}) collective-permute-start(bf16[128,256]{1,0:T(8,128)(2,1)S(1)} %get-tuple-element.161), channel_id=1, source_target_pairs={{2,4},{3,5},{6,8},{7,9},{10,12},{11,13},{4,2},{5,3},{8,6},{9,7},{1... | collective-permute-start | bytes 196616 | tf_op jit(solution)/shard_map/ppermute | solution.py:604
  (11 other events, 45.8 us)
Sparse Core Ops, SparseCore 0:
  9.6 82.3 all-gather.1

commit v12 on v11

--- a/solution.py
+++ b/solution.py
@@ -114,7 +114,7 @@
     return pltpu.make_async_copy(refs[0], to, sem)
 
 
-def load_all(place, plan, refs, tokens, sems):
+def start_all(place, plan, refs, tokens, sems):
     rows = tokens.shape[0] // len(plan)
     copies, used = [], 0
     for n, choices in enumerate(plan):
@@ -122,7 +122,11 @@
         to = tokens.at[pl.ds(n * rows, rows)]
         copies.append(load(place, choices, refs[used : used + many], to, sems.at[n]))
         used += many
-    for copy in copies:
+    return copies
+
+
+def load_all(*args):
+    for copy in start_all(*args):
         copy.wait()
 
 
@@ -227,11 +231,17 @@
 
     @pl.when(pl.program_id(0) == 0)
     def _():
+        copies = start_all(place_ref[0], plan, sources, tokens, sems)
         values[:, HD:] = jnp.ones((start + rows, HD), jnp.bfloat16)
-        load_all(place_ref[0], plan, sources, tokens, sems)
+        gather_known(known, counts, queries, keys, values)
+        for copy in copies:
+            copy.wait()
+
+    @pl.when(pl.program_id(0) != 0)
+    def _():
+        gather_known(known, counts, queries, keys, values)
 
     proj = product(tokens, w_refs)
-    gather_known(known, counts, queries, keys, values)
     queries[start:] = root_norm(proj[:, :HD])
     keys[start:] = root_norm(proj[:, HD : 2 * HD])
     values[start:, :HD] = proj[:, 2 * HD :].astype(jnp.bfloat16)
@@ -393,7 +403,7 @@
         pltpu.SemaphoreType.DMA((count, len(parts))),
     ]
     params = dict(
-        compiler_params=pltpu.CompilerParams(vmem_limit_bytes=52 * MIB),
+        compiler_params=pltpu.CompilerParams(vmem_limit_bytes=48 * MIB),
     )
     if last is None:
         aliased = before.dtype == jnp.float32

time: 250 us -> 248 us (level)
    unnamed x32 -> x24, local copies, waits for them, and re-layouts: 10.1 us -> 8.01 us
where the time goes in v12:
time: 248 us; the launch traced here: 247 us
  waiting for transfers between devices  106 us (43%)
  Pallas kernels  63.4 us (26%)
  starting transfers between devices  47.3 us (19%)
  between operations  15.1 us (6%)
  local copies, waits for them, and re-layouts  14.5 us (6%)
    ppermute x1, waiting for transfers between devices, shards(): lax.ppermute(weight.astype(jnp.bfloat16), ('tile', 'seq'), joins)  65.9 us
    ppermute x6, waiting for transfers between devices, hop(): lax.ppermute(blocks_by[way * (step - 1)], 'seq', step_pairs(devices, step...  18.5 us
    pallas_call x2, Pallas kernels, project(): pl.pallas_call(functools.partial(project_kernel, plan, len(blocks)), grid...  17.8 us
    ppermute x8, waiting for transfers between devices, turned(): lax.ppermute(value, axis, [(i, (i + turn) % count) for i in range(count)])  17 us
    pallas_call x2, Pallas kernels, attend(): pl.pallas_call(functools.partial(attend_kernel, plan, len(blocks), counts...  16.2 us
    ppermute x8, starting transfers between devices, turned(): lax.ppermute(value, axis, [(i, (i + turn) % count) for i in range(count)])  15.7 us
    pallas_call x1, Pallas kernels, accumulate(): pl.pallas_call(functools.partial(add_kernel, offsets, splits), in_specs=[...  10.5 us
    ppermute x6, starting transfers between devices, hop(): lax.ppermute(blocks_by[way * (step - 1)], 'seq', step_pairs(devices, step...  9.72 us
  transfers between devices with their start and end apart: 27, of which 8 were waited for; matrix products, arithmetic and copies ran while one was open for 3% of the time, Pallas kernels for 22%

profile of v12, /device:TPU:1, one launch (start us, length us, event | category | flops | bytes accessed | tf_op | source)
XLA Modules:
  0.0 247.4 jit_solution(5471132636244444382)
XLA Ops:
  9.5 2.7 %collective-permute-start.1 = (bf16[768,2304]{1,0:T(8,128)(2,1)}, bf16[768,2304]{1,0:T(8,128)(2,1)}, u32[]{:S(2)}, u32[]{:S(2)}) collective-permute-start(bf16[768,2304]{1,0:T(8,128)(2,1)} %refs_0_.3), channel_id=1, source_target_pairs={{0,8},{4,12},{8,0},{12,4},{1,9},{5,13},{9,1},{13,5},{2,10},{6,14},... | collective-permute-start | bytes 10616840 | tf_op jit(solution)/shard_map/ppermute | solution.py:18
  12.8 4.4 %norm_in.1.refs_4_ = bf16[256,3072]{1,0:T(8,128)(2,1)} custom-call(s32[4]{0:T(128)} %pad_add_fusion.starts_ref, bf16[256,3072]{1,0:T(8,128)(2,1)} %bitcast.35, f32[5,3072]{1,0:T(8,128)} %refs_14_.1), custom_call_target="tpu_custom_call" | custom-call | tf_op jit(solution)/shard_map/norm_in/pallas_call | solution.py:78
  17.2 4.3 %collective-permute-start.3 = (bf16[256,3072]{1,0:T(8,128)(2,1)}, bf16[256,3072]{1,0:T(8,128)(2,1)}, u32[]{:S(2)}, u32[]{:S(2)}) collective-permute-start(bf16[256,3072]{1,0:T(8,128)(2,1)} %norm_in.1.refs_4_), channel_id=1, source_target_pairs={{0,1},{1,2},{2,3},{4,5},{5,6},{6,7},{8,9},{9,10},{10,11},{12,13},{... | collective-permute-start | bytes 4718600 | tf_op jit(solution)/shard_map/ppermute | solution.py:473
  22.9 4.7 %collective-permute-start.4 = (bf16[1,256]{1,0:T(2,128)(2,1)S(1)}, bf16[1,256]{1,0:T(2,128)(2,1)S(1)}, u32[]{:S(2)}, u32[]{:S(2)}) collective-permute-start(bf16[1,256]{1,0:T(2,128)(2,1)S(1)} %get-tuple-element.167), channel_id=1, source_target_pairs={{2,4},{3,5},{6,8},{7,9},{10,12},{11,13},{4,2},{5,3},{8,6},{9,7},{1... | collective-permute-start | bytes 1544 | tf_op jit(solution)/shard_map/ppermute | solution.py:458
  29.2 65.9 %collective-permute-done.4 = bf16[1,256]{1,0:T(2,128)(2,1)S(1)} collective-permute-done((bf16[1,256]{1,0:T(2,128)(2,1)S(1)}, bf16[1,256]{1,0:T(2,128)(2,1)S(1)}, u32[]{:S(2)}, u32[]{:S(2)}) %collective-permute-start.4) | collective-permute-done | bytes 544 | tf_op jit(solution)/shard_map/ppermute | solution.py:458
  95.2 1.3 collective-permute-start.6
  98.6 1.5 collective-permute-start.10
  100.0 1.6 collective-permute-done.5.refs_3_
  101.7 1.9 copy-done.7
  103.5 2.0 copy-done.1
  105.5 1.4 copy-done.3
  106.9 10.5 %project.2 = (bf16[6,512,128]{2,1,0:T(8,128)(2,1)S(1)}, bf16[6,512,128]{2,1,0:T(8,128)(2,1)S(1)}, bf16[6,512,128]{2,1,0:T(8,128)(2,1)S(1)}) custom-call(s32[1]{0:T(128)} %bitcast.18.place_ref, bf16[768,2304]{1,0:T(8,128)(2,1)S(1)} %copy-done.1, bf16[768,2304]{1,0:T(8,128)(2,1)} %collective-permute-done.refs_1_, ...), custom_call_target="tpu_custom_call" | custom-call | tf_op jit(solution)/shard_map/project/pallas_call | solution.py:156
  117.5 15.2 %collective-permute-done.6.refs_4_.refs_12_ = bf16[256,3072]{1,0:T(8,128)(2,1)S(1)} collective-permute-done((bf16[256,3072]{1,0:T(8,128)(2,1)S(1)}, bf16[256,3072]{1,0:T(8,128)(2,1)S(1)}, u32[]{:S(2)}, u32[]{:S(2)}) %collective-permute-start.6) | collective-permute-done | bytes 1572896 | tf_op jit(solution)/shard_map/ppermute | solution.py:473
  136.0 14.0 %collective-permute-done.11.refs_6_.refs_4_ = bf16[3072,384]{1,0:T(8,128)(2,1)} collective-permute-done((bf16[3072,384]{1,0:T(8,128)(2,1)}, bf16[3072,384]{1,0:T(8,128)(2,1)}, u32[]{:S(2)}, u32[]{:S(2)}) %collective-permute-start.11) | collective-permute-done | bytes 2359328 | tf_op jit(solution)/shard_map/ppermute | solution.py:33
  150.0 2.4 slice.17
  152.5 2.4 slice.16
  154.9 7.2 %project.3 = (bf16[6,256,128]{2,1,0:T(8,128)(2,1)S(1)}, bf16[6,256,128]{2,1,0:T(8,128)(2,1)S(1)}, bf16[6,256,128]{2,1,0:T(8,128)(2,1)S(1)}) custom-call(s32[1]{0:T(128)} %bitcast.18.place_ref, bf16[768,2304]{1,0:T(8,128)(2,1)S(1)} %copy-done.1, bf16[768,2304]{1,0:T(8,128)(2,1)} %collective-permute-done.refs_1_, ...), custom_call_target="tpu_custom_call" | custom-call | tf_op jit(solution)/shard_map/project/pallas_call | solution.py:156
  162.1 5.6 %early.1.refs_4_ = bf16[6,768,256]{2,1,0:T(8,128)(2,1)S(1)} custom-call(bf16[6,512,128]{2,1,0:T(8,128)(2,1)S(1)} %get-tuple-element.113.refs_0_.refs_5_, bf16[6,512,128]{2,1,0:T(8,128)(2,1)S(1)} %get-tuple-element.114.refs_1_.refs_6_, bf16[6,512,128]{2,1,0:T(8,128)(2,1)S(1)} %get-tuple-element.115.refs_2_.refs_7_, ...), custom_call_target="tpu_custom_call" | custom-call | tf_op jit(solution)/shard_map/early/pallas_call | solution.py:206
  167.7 1.5 copy-done.2
  169.2 3.2 %collective-permute-done.8.refs_11_ = bf16[256,3072]{1,0:T(8,128)(2,1)S(1)} collective-permute-done((bf16[256,3072]{1,0:T(8,128)(2,1)S(1)}, bf16[256,3072]{1,0:T(8,128)(2,1)S(1)}, u32[]{:S(2)}, u32[]{:S(2)}) %collective-permute-start.8) | collective-permute-done | bytes 1572896 | tf_op jit(solution)/shard_map/ppermute | solution.py:473
  175.6 8.1 %attend.2 = (bf16[256,384]{1,0:T(8,128)(2,1)S(1)}, bf16[256,384]{1,0:T(8,128)(2,1)S(1)}, bf16[256,384]{1,0:T(8,128)(2,1)S(1)}, bf16[256,384]{1,0:T(8,128)(2,1)S(1)}) custom-call(s32[1]{0:T(128)} %bitcast.18.place_ref, s32[4]{0:T(128)S(1)} %dynamic-slice_bitcast_fusion.slots_ref, bf16[768,2304]{1,0:T(8,128)(2,1)} %refs_0_.3, ...), custom_call_target="tpu_custom_call" | custom-call | tf_op jit(solution)/shard_map/attend/pallas_call | solution.py:265
  183.7 2.5 collective-permute-start.15
  186.2 2.2 collective-permute-start.16
  189.4 8.1 %attend.3 = (bf16[256,384]{1,0:T(8,128)(2,1)S(1)}, bf16[256,384]{1,0:T(8,128)(2,1)S(1)}, bf16[256,384]{1,0:T(8,128)(2,1)S(1)}, bf16[256,384]{1,0:T(8,128)(2,1)S(1)}) custom-call(s32[1]{0:T(128)} %bitcast.18.place_ref, s32[4]{0:T(128)S(1)} %dynamic-slice_bitcast_fusion.slots_ref, bf16[768,2304]{1,0:T(8,128)(2,1)} %refs_0_.3, ...), custom_call_target="tpu_custom_call" | custom-call | tf_op jit(solution)/shard_map/attend/pallas_call | solution.py:265
  197.6 2.9 %collective-permute-done.18.refs_10_.refs_8_ = bf16[1536,384]{1,0:T(8,128)(2,1)S(1)} collective-permute-done((bf16[1536,384]{1,0:T(8,128)(2,1)}, bf16[1536,384]{1,0:T(8,128)(2,1)S(1)}, u32[]{:S(2)}, u32[]{:S(2)}) %collective-permute-start.18) | collective-permute-done | bytes 1179680 | tf_op jit(solution)/shard_map/ppermute | solution.py:33
  201.2 1.7 collective-permute-start.23
  202.9 4.3 %collective-permute-start.20 = (bf16[256,384]{1,0:T(8,128)(2,1)S(1)}, bf16[256,384]{1,0:T(8,128)(2,1)S(1)}, u32[]{:S(2)}, u32[]{:S(2)}) collective-permute-start(bf16[256,384]{1,0:T(8,128)(2,1)S(1)} %get-tuple-element.144), channel_id=1, source_target_pairs={{0,2},{1,3},{2,0},{3,1},{4,6},{5,7},{6,4},{7,5},{8,10},{9,11},{10,... | collective-permute-start | bytes 589832 | tf_op jit(solution)/shard_map/ppermute | solution.py:33
  207.5 2.9 %collective-permute-start.22 = (bf16[256,384]{1,0:T(8,128)(2,1)S(1)}, bf16[256,384]{1,0:T(8,128)(2,1)S(1)}, u32[]{:S(2)}, u32[]{:S(2)}) collective-permute-start(bf16[256,384]{1,0:T(8,128)(2,1)S(1)} %get-tuple-element.146), channel_id=1, source_target_pairs={{0,3},{1,0},{2,1},{3,2},{4,7},{5,4},{6,5},{7,6},{8,11},{9,8},{10,9... | collective-permute-start | bytes 589832 | tf_op jit(solution)/shard_map/ppermute | solution.py:33
  210.5 10.5 %add_parts.1.refs_13_ = f32[256,3072]{1,0:T(8,128)} custom-call(s32[8]{0:T(128)S(1)} %stack.79.starts_ref, s32[4]{0:T(128)S(1)} %pad_add_fusion.1.rows_ref, bf16[256,384]{1,0:T(8,128)(2,1)S(1)} %get-tuple-element.155.refs_0_, bf16[256,384]{1,0:T(8,128)(2,1)S(1)} %get-tuple-element.156.refs_1_, bf16[256,384]{1,0:T(8,128)(2,1)S(1)} %collective-permute-done.15.refs_2_, ...), custom_call_target="tpu_custom_call" | custom-call | tf_op jit(solution)/shard_map/add_parts/pallas_call | solution.py:410
  221.0 8.9 %finish.1 = (f32[64,256]{1,0:T(8,128)S(1)}, f32[64,256]{1,0:T(8,128)S(1)}, bf16[128,256]{1,0:T(8,128)(2,1)S(1)}) custom-call(s32[8]{0:T(128)S(1)} %stack.79.starts_ref, s32[4]{0:T(128)S(1)} %pad_add_fusion.1.rows_ref, f32[2]{0:T(128)S(1)} %pad_maximum_fusion.coef_ref, bf16[256,384]{1,0:T(8,128)(2,1)S(1)} %collective-permute-done.20.refs_0_, ...), custom_call_target="tpu_custom_call" | custom-call | tf_op jit(solution)/shard_map/finish/pallas_call | solution.py:422
  229.9 8.0 %collective-permute-start.25 = (bf16[128,256]{1,0:T(8,128)(2,1)S(1)}, bf16[128,256]{1,0:T(8,128)(2,1)S(1)}, u32[]{:S(2)}, u32[]{:S(2)}) collective-permute-start(bf16[128,256]{1,0:T(8,128)(2,1)S(1)} %get-tuple-element.161), channel_id=1, source_target_pairs={{2,4},{3,5},{6,8},{7,9},{10,12},{11,13},{4,2},{5,3},{8,6},{9,7},{1... | collective-permute-start | bytes 196616 | tf_op jit(solution)/shard_map/ppermute | solution.py:614
  237.9 1.9 collective-permute-done.25
  (67 shorter events, 16.5 us)
Async XLA Ops:
  7.2 87.9 %all-gather.2.cloned.1.call-start = ((), (), s32[]{:S(2)}) async-start(), calls=%async_computation | async-start | bytes 2949120 | tf_op jit(solution)/shard_map/all_gather | solution.py:485
  9.4 85.8 %collective-permute-start = (bf16[768,2304]{1,0:T(8,128)(2,1)}, bf16[768,2304]{1,0:T(8,128)(2,1)}, u32[]{:S(2)}, u32[]{:S(2)}) collective-permute-start(bf16[768,2304]{1,0:T(8,128)(2,1)} %refs_0_.3), channel_id=1, source_target_pairs={{0,4},{4,0},{8,12},{12,8},{1,5},{5,1},{9,13},{13,9},{2,6},{6,2},{1... | collective-permute-start | bytes 10616840 | tf_op jit(solution)/shard_map/ppermute | solution.py:18
  9.5 85.6 %collective-permute-start.1 = (bf16[768,2304]{1,0:T(8,128)(2,1)}, bf16[768,2304]{1,0:T(8,128)(2,1)}, u32[]{:S(2)}, u32[]{:S(2)}) collective-permute-start(bf16[768,2304]{1,0:T(8,128)(2,1)} %refs_0_.3), channel_id=1, source_target_pairs={{0,8},{4,12},{8,0},{12,4},{1,9},{5,13},{9,1},{13,5},{2,10},{6,14},... | collective-permute-start | bytes 10616840 | tf_op jit(solution)/shard_map/ppermute | solution.py:18
  17.2 77.9 %collective-permute-start.3 = (bf16[256,3072]{1,0:T(8,128)(2,1)}, bf16[256,3072]{1,0:T(8,128)(2,1)}, u32[]{:S(2)}, u32[]{:S(2)}) collective-permute-start(bf16[256,3072]{1,0:T(8,128)(2,1)} %norm_in.1.refs_4_), channel_id=1, source_target_pairs={{0,1},{1,2},{2,3},{4,5},{5,6},{6,7},{8,9},{9,10},{10,11},{12,13},{... | collective-permute-start | bytes 4718600 | tf_op jit(solution)/shard_map/ppermute | solution.py:473
  21.5 73.6 %collective-permute-start.2 = (bf16[256,3072]{1,0:T(8,128)(2,1)}, bf16[256,3072]{1,0:T(8,128)(2,1)S(1)}, u32[]{:S(2)}, u32[]{:S(2)}) collective-permute-start(bf16[256,3072]{1,0:T(8,128)(2,1)} %norm_in.1.refs_4_), channel_id=1, source_target_pairs={{1,0},{2,1},{3,2},{5,4},{6,5},{7,6},{9,8},{10,9},{11,10},{13,12},{... | collective-permute-start | bytes 4718600 | tf_op jit(solution)/shard_map/ppermute | solution.py:473
  22.9 72.2 %collective-permute-start.4 = (bf16[1,256]{1,0:T(2,128)(2,1)S(1)}, bf16[1,256]{1,0:T(2,128)(2,1)S(1)}, u32[]{:S(2)}, u32[]{:S(2)}) collective-permute-start(bf16[1,256]{1,0:T(2,128)(2,1)S(1)} %get-tuple-element.167), channel_id=1, source_target_pairs={{2,4},{3,5},{6,8},{7,9},{10,12},{11,13},{4,2},{5,3},{8,6},{9,7},{1... | collective-permute-start | bytes 1544 | tf_op jit(solution)/shard_map/ppermute | solution.py:458
  95.2 6.5 %collective-permute-start.5 = (bf16[768,2304]{1,0:T(8,128)(2,1)}, bf16[768,2304]{1,0:T(8,128)(2,1)S(1)}, u32[]{:S(2)}, u32[]{:S(2)}) collective-permute-start(bf16[768,2304]{1,0:T(8,128)(2,1)} %collective-permute-done.1.refs_2_), channel_id=1, source_target_pairs={{0,4},{4,0},{8,12},{12,8},{1,5},{5,1},{9,13},{13,9},{2,6},{6,2},{1... | collective-permute-start | bytes 10616840 | tf_op jit(solution)/shard_map/ppermute | solution.py:18
  95.2 37.5 %collective-permute-start.6 = (bf16[256,3072]{1,0:T(8,128)(2,1)S(1)}, bf16[256,3072]{1,0:T(8,128)(2,1)S(1)}, u32[]{:S(2)}, u32[]{:S(2)}) collective-permute-start(bf16[256,3072]{1,0:T(8,128)(2,1)S(1)} %collective-permute-done.2.refs_5_), channel_id=1, source_target_pairs={{1,0},{2,1},{5,4},{6,5},{9,8},{10,9},{13,12},{14,13},{17,16},{18,1... | collective-permute-start | bytes 4718600 | tf_op jit(solution)/shard_map/ppermute | solution.py:473
  96.5 36.2 %collective-permute-start.7 = (bf16[256,3072]{1,0:T(8,128)(2,1)}, bf16[256,3072]{1,0:T(8,128)(2,1)S(1)}, u32[]{:S(2)}, u32[]{:S(2)}) collective-permute-start(bf16[256,3072]{1,0:T(8,128)(2,1)} %collective-permute-done.3.refs_6_), channel_id=1, source_target_pairs={{1,2},{2,3},{5,6},{6,7},{9,10},{10,11},{13,14},{14,15},{17,18},{18... | collective-permute-start | bytes 4718600 | tf_op jit(solution)/shard_map/ppermute | solution.py:473
  97.3 52.7 %collective-permute-start.11 = (bf16[3072,384]{1,0:T(8,128)(2,1)}, bf16[3072,384]{1,0:T(8,128)(2,1)}, u32[]{:S(2)}, u32[]{:S(2)}) collective-permute-start(bf16[3072,384]{1,0:T(8,128)(2,1)} %all-gather.2.cloned.1.call-done.refs_5_.refs_3_), channel_id=1, source_target_pairs={{0,16},{16,0},{1,17},{17,1},{2,18},{18,2},{3,19},{19,3},{4,20},{20... | collective-permute-start | bytes 7077896 | tf_op jit(solution)/shard_map/ppermute | solution.py:33
  98.6 53.9 %collective-permute-start.10 = (bf16[3072,384]{1,0:T(8,128)(2,1)}, bf16[3072,384]{1,0:T(8,128)(2,1)}, u32[]{:S(2)}, u32[]{:S(2)}) collective-permute-start(bf16[3072,384]{1,0:T(8,128)(2,1)} %all-gather.2.cloned.1.call-done.refs_5_.refs_3_), channel_id=1, source_target_pairs={{0,8},{4,12},{8,0},{12,4},{1,9},{5,13},{9,1},{13,5},{2,10},{6,14},... | collective-permute-start | bytes 7077896 | tf_op jit(solution)/shard_map/ppermute | solution.py:18
  132.7 39.7 %collective-permute-start.12 = (bf16[3072,384]{1,0:T(8,128)(2,1)}, bf16[3072,384]{1,0:T(8,128)(2,1)S(1)}, u32[]{:S(2)}, u32[]{:S(2)}) collective-permute-start(bf16[3072,384]{1,0:T(8,128)(2,1)} %all-gather.2.cloned.1.call-done.refs_5_.refs_3_), channel_id=1, source_target_pairs={{0,4},{4,0},{8,12},{12,8},{1,5},{5,1},{9,13},{13,9},{2,6},{6,2},{1... | collective-permute-start | bytes 7077896 | tf_op jit(solution)/shard_map/ppermute | solution.py:18
  133.9 38.5 %collective-permute-start.8 = (bf16[256,3072]{1,0:T(8,128)(2,1)S(1)}, bf16[256,3072]{1,0:T(8,128)(2,1)S(1)}, u32[]{:S(2)}, u32[]{:S(2)}) collective-permute-start(bf16[256,3072]{1,0:T(8,128)(2,1)S(1)} %collective-permute-done.6.refs_4_.refs_12_), channel_id=1, source_target_pairs={{1,0},{5,4},{9,8},{13,12},{17,16},{21,20},{25,24},{29,28}} | collective-permute-start | bytes 4718600 | tf_op jit(solution)/shard_map/ppermute | solution.py:473
  135.2 37.2 %collective-permute-start.9 = (bf16[256,3072]{1,0:T(8,128)(2,1)S(1)}, bf16[256,3072]{1,0:T(8,128)(2,1)S(1)}, u32[]{:S(2)}, u32[]{:S(2)}) collective-permute-start(bf16[256,3072]{1,0:T(8,128)(2,1)S(1)} %collective-permute-done.7.refs_6_.refs_13_), channel_id=1, source_target_pairs={{2,3},{6,7},{10,11},{14,15},{18,19},{22,23},{26,27},{30,31}} | collective-permute-start | bytes 4718600 | tf_op jit(solution)/shard_map/ppermute | solution.py:473
  162.1 12.3 %copy-start.10 = (bf16[1536,384]{1,0:T(8,128)(2,1)S(1)}, bf16[1536,384]{1,0:T(8,128)(2,1)}, u32[]{:S(2)}) copy-start(bf16[1536,384]{1,0:T(8,128)(2,1)} %slice.17) | copy-start | bytes 3538948
  172.5 11.2 %collective-permute-start.13 = (bf16[3072,384]{1,0:T(8,128)(2,1)}, bf16[3072,384]{1,0:T(8,128)(2,1)S(1)}, u32[]{:S(2)}, u32[]{:S(2)}) collective-permute-start(bf16[3072,384]{1,0:T(8,128)(2,1)} %collective-permute-done.11.refs_6_.refs_4_), channel_id=1, source_target_pairs={{0,4},{4,0},{8,12},{12,8},{1,5},{5,1},{9,13},{13,9},{2,6},{6,2},{1... | collective-permute-start | bytes 7077896 | tf_op jit(solution)/shard_map/ppermute | solution.py:18
  173.1 10.6 %collective-permute-start.14 = (bf16[3072,384]{1,0:T(8,128)(2,1)}, bf16[3072,384]{1,0:T(8,128)(2,1)}, u32[]{:S(2)}, u32[]{:S(2)}) collective-permute-start(bf16[3072,384]{1,0:T(8,128)(2,1)} %collective-permute-done.10.refs_9_.refs_7_), channel_id=1, source_target_pairs={{0,4},{4,0},{8,12},{12,8},{1,5},{5,1},{9,13},{13,9},{2,6},{6,2},{1... | collective-permute-start | bytes 7077896 | tf_op jit(solution)/shard_map/ppermute | solution.py:18
  173.2 27.3 %collective-permute-start.18 = (bf16[1536,384]{1,0:T(8,128)(2,1)}, bf16[1536,384]{1,0:T(8,128)(2,1)S(1)}, u32[]{:S(2)}, u32[]{:S(2)}) collective-permute-start(bf16[1536,384]{1,0:T(8,128)(2,1)} %slice.16), channel_id=1, source_target_pairs={{0,16},{16,0},{1,17},{17,1},{2,18},{18,2},{3,19},{19,3},{4,20},{20... | collective-permute-start | bytes 3538952 | tf_op jit(solution)/shard_map/ppermute | solution.py:33
  174.4 26.8 %collective-permute-start.19 = (bf16[1536,384]{1,0:T(8,128)(2,1)S(1)}, bf16[1536,384]{1,0:T(8,128)(2,1)S(1)}, u32[]{:S(2)}, u32[]{:S(2)}) collective-permute-start(bf16[1536,384]{1,0:T(8,128)(2,1)S(1)} %copy-done.10), channel_id=1, source_target_pairs={{0,8},{4,12},{8,0},{12,4},{1,9},{5,13},{9,1},{13,5},{2,10},{6,14},... | collective-permute-start | bytes 3538952 | tf_op jit(solution)/shard_map/ppermute | solution.py:18
  183.7 13.9 %copy-start.9 = (bf16[3072,384]{1,0:T(8,128)(2,1)}, bf16[3072,384]{1,0:T(8,128)(2,1)S(1)}, u32[]{:S(2)}) copy-start(bf16[3072,384]{1,0:T(8,128)(2,1)S(1)} %collective-permute-done.13.refs_8_.refs_6_) | copy-start | bytes 7077892
  183.7 26.8 %copy-start.4 = (f32[5,3072]{1,0:T(8,128)S(1)}, f32[5,3072]{1,0:T(8,128)}, u32[]{:S(2)}) copy-start(f32[5,3072]{1,0:T(8,128)} %refs_14_.1) | copy-start | bytes 184324
  183.7 17.5 %collective-permute-start.15 = (bf16[256,384]{1,0:T(8,128)(2,1)S(1)}, bf16[256,384]{1,0:T(8,128)(2,1)S(1)}, u32[]{:S(2)}, u32[]{:S(2)}) collective-permute-start(bf16[256,384]{1,0:T(8,128)(2,1)S(1)} %get-tuple-element.139), channel_id=1, source_target_pairs={{0,2},{1,3},{2,0},{3,1},{4,6},{5,7},{6,4},{7,5},{8,10},{9,11},{10,... | collective-permute-start | bytes 589832 | tf_op jit(solution)/shard_map/ppermute | solution.py:33
  186.2 15.0 %collective-permute-start.16 = (bf16[256,384]{1,0:T(8,128)(2,1)S(1)}, bf16[256,384]{1,0:T(8,128)(2,1)S(1)}, u32[]{:S(2)}, u32[]{:S(2)}) collective-permute-start(bf16[256,384]{1,0:T(8,128)(2,1)S(1)} %get-tuple-element.140), channel_id=1, source_target_pairs={{0,1},{1,2},{2,3},{3,0},{4,5},{5,6},{6,7},{7,4},{8,9},{9,10},{10,1... | collective-permute-start | bytes 589832 | tf_op jit(solution)/shard_map/ppermute | solution.py:33
  188.4 12.8 %collective-permute-start.17 = (bf16[256,384]{1,0:T(8,128)(2,1)S(1)}, bf16[256,384]{1,0:T(8,128)(2,1)S(1)}, u32[]{:S(2)}, u32[]{:S(2)}) collective-permute-start(bf16[256,384]{1,0:T(8,128)(2,1)S(1)} %get-tuple-element.141), channel_id=1, source_target_pairs={{0,3},{1,0},{2,1},{3,2},{4,7},{5,4},{6,5},{7,6},{8,11},{9,8},{10,9... | collective-permute-start | bytes 589832 | tf_op jit(solution)/shard_map/ppermute | solution.py:33
  201.2 19.8 %copy-start.5 = (bf16[3072,64]{0,1:T(8,128)(2,1)S(1)}, bf16[3072,64]{0,1:T(8,128)(2,1)}, u32[]{:S(2)}) copy-start(bf16[3072,64]{0,1:T(8,128)(2,1)} %param.13) | copy-start | bytes 1179652
  201.2 19.8 %copy-start.6 = (f32[1,256,64]{1,2,0:T(8,128)S(1)}, f32[1,256,64]{1,2,0:T(8,128)}, u32[]{:S(2)}) copy-start(f32[1,256,64]{1,2,0:T(8,128)} %param.14) | copy-start | bytes 196612
  201.2 9.3 %collective-permute-start.23 = (bf16[1536,384]{1,0:T(8,128)(2,1)S(1)}, bf16[1536,384]{1,0:T(8,128)(2,1)S(1)}, u32[]{:S(2)}, u32[]{:S(2)}) collective-permute-start(bf16[1536,384]{1,0:T(8,128)(2,1)S(1)} %collective-permute-done.18.refs_10_.refs_8_), channel_id=1, source_target_pairs={{0,4},{4,0},{8,12},{12,8},{1,5},{5,1},{9,13},{13,9},{2,6},{6,2},{1... | collective-permute-start | bytes 3538952 | tf_op jit(solution)/shard_map/ppermute | solution.py:18
  202.9 7.6 %collective-permute-start.24 = (bf16[1536,384]{1,0:T(8,128)(2,1)S(1)}, bf16[1536,384]{1,0:T(8,128)(2,1)S(1)}, u32[]{:S(2)}, u32[]{:S(2)}) collective-permute-start(bf16[1536,384]{1,0:T(8,128)(2,1)S(1)} %collective-permute-done.19.refs_11_.refs_9_), channel_id=1, source_target_pairs={{0,4},{4,0},{8,12},{12,8},{1,5},{5,1},{9,13},{13,9},{2,6},{6,2},{1... | collective-permute-start | bytes 3538952 | tf_op jit(solution)/shard_map/ppermute | solution.py:18
  202.9 18.1 %collective-permute-start.20 = (bf16[256,384]{1,0:T(8,128)(2,1)S(1)}, bf16[256,384]{1,0:T(8,128)(2,1)S(1)}, u32[]{:S(2)}, u32[]{:S(2)}) collective-permute-start(bf16[256,384]{1,0:T(8,128)(2,1)S(1)} %get-tuple-element.144), channel_id=1, source_target_pairs={{0,2},{1,3},{2,0},{3,1},{4,6},{5,7},{6,4},{7,5},{8,10},{9,11},{10,... | collective-permute-start | bytes 589832 | tf_op jit(solution)/shard_map/ppermute | solution.py:33
  207.2 13.8 %collective-permute-start.21 = (bf16[256,384]{1,0:T(8,128)(2,1)S(1)}, bf16[256,384]{1,0:T(8,128)(2,1)S(1)}, u32[]{:S(2)}, u32[]{:S(2)}) collective-permute-start(bf16[256,384]{1,0:T(8,128)(2,1)S(1)} %get-tuple-element.145), channel_id=1, source_target_pairs={{0,1},{1,2},{2,3},{3,0},{4,5},{5,6},{6,7},{7,4},{8,9},{9,10},{10,1... | collective-permute-start | bytes 589832 | tf_op jit(solution)/shard_map/ppermute | solution.py:33
  207.5 13.5 %collective-permute-start.22 = (bf16[256,384]{1,0:T(8,128)(2,1)S(1)}, bf16[256,384]{1,0:T(8,128)(2,1)S(1)}, u32[]{:S(2)}, u32[]{:S(2)}) collective-permute-start(bf16[256,384]{1,0:T(8,128)(2,1)S(1)} %get-tuple-element.146), channel_id=1, source_target_pairs={{0,3},{1,0},{2,1},{3,2},{4,7},{5,4},{6,5},{7,6},{8,11},{9,8},{10,9... | collective-permute-start | bytes 589832 | tf_op jit(solution)/shard_map/ppermute | solution.py:33
  229.9 9.9 %collective-permute-start.25 = (bf16[128,256]{1,0:T(8,128)(2,1)S(1)}, bf16[128,256]{1,0:T(8,128)(2,1)S(1)}, u32[]{:S(2)}, u32[]{:S(2)}) collective-permute-start(bf16[128,256]{1,0:T(8,128)(2,1)S(1)} %get-tuple-element.161), channel_id=1, source_target_pairs={{2,4},{3,5},{6,8},{7,9},{10,12},{11,13},{4,2},{5,3},{8,6},{9,7},{1... | collective-permute-start | bytes 196616 | tf_op jit(solution)/shard_map/ppermute | solution.py:614
  (7 other events, 29.3 us)
Sparse Core Ops, SparseCore 0:
  9.6 82.3 all-gather.1

commit v13 on v12

--- a/solution.py
+++ b/solution.py
@@ -74,7 +74,7 @@
 
 def norm_rows(hidden, modulation, starts, first, rows):
     width = hidden.shape[1]
-    block = math.gcd(math.gcd(first, rows), 64)
+    block = math.gcd(math.gcd(first, rows), 128)
     return pl.pallas_call(
         functools.partial(norm_kernel, starts.shape[0]),
         grid=(rows // block,),
@@ -174,7 +174,7 @@
     scores = lax.dot_general(
         query, key, (((1,), (1,)), ((), ())), preferred_element_type=jnp.float32
     )
-    expo = jnp.exp(scores * (1.0 / math.sqrt(HD))).astype(jnp.bfloat16)
+    expo = jnp.exp2(scores * (math.log2(math.e) / math.sqrt(HD))).astype(jnp.bfloat16)
     return jnp.dot(expo, values, preferred_element_type=jnp.float32)
 
 

time: 248 us -> 248 us (level)
  no operation moved by 1% of the time
where the time goes in v13:
time: 248 us; the launch traced here: 247 us
  waiting for transfers between devices  106 us (43%)
  Pallas kernels  62.7 us (25%)
  starting transfers between devices  47.4 us (19%)
  between operations  15.1 us (6%)
  local copies, waits for them, and re-layouts  14.5 us (6%)
    ppermute x1, waiting for transfers between devices, shards(): lax.ppermute(weight.astype(jnp.bfloat16), ('tile', 'seq'), joins)  66.5 us
    ppermute x6, waiting for transfers between devices, hop(): lax.ppermute(blocks_by[way * (step - 1)], 'seq', step_pairs(devices, step...  18.5 us
    pallas_call x2, Pallas kernels, project(): pl.pallas_call(functools.partial(project_kernel, plan, len(blocks)), grid...  17.8 us
    ppermute x8, waiting for transfers between devices, turned(): lax.ppermute(value, axis, [(i, (i + turn) % count) for i in range(count)])  17 us
    pallas_call x2, Pallas kernels, attend(): pl.pallas_call(functools.partial(attend_kernel, plan, len(blocks), counts...  16.2 us
    ppermute x8, starting transfers between devices, turned(): lax.ppermute(value, axis, [(i, (i + turn) % count) for i in range(count)])  15.7 us
    pallas_call x1, Pallas kernels, accumulate(): pl.pallas_call(functools.partial(add_kernel, offsets, splits), in_specs=[...  10.5 us
    ppermute x6, starting transfers between devices, hop(): lax.ppermute(blocks_by[way * (step - 1)], 'seq', step_pairs(devices, step...  9.72 us
  transfers between devices with their start and end apart: 27, of which 8 were waited for; matrix products, arithmetic and copies ran while one was open for 3% of the time, Pallas kernels for 22%

profile of v13, /device:TPU:1, one launch (start us, length us, event | category | flops | bytes accessed | tf_op | source)
XLA Modules:
  0.0 247.4 jit_solution(9890771004401335564)
XLA Ops:
  9.5 2.7 %collective-permute-start.1 = (bf16[768,2304]{1,0:T(8,128)(2,1)}, bf16[768,2304]{1,0:T(8,128)(2,1)}, u32[]{:S(2)}, u32[]{:S(2)}) collective-permute-start(bf16[768,2304]{1,0:T(8,128)(2,1)} %refs_0_.3), channel_id=1, source_target_pairs={{0,8},{4,12},{8,0},{12,4},{1,9},{5,13},{9,1},{13,5},{2,10},{6,14},... | collective-permute-start | bytes 10616840 | tf_op jit(solution)/shard_map/ppermute | solution.py:18
  12.8 3.8 %norm_in.1.refs_4_ = bf16[256,3072]{1,0:T(8,128)(2,1)} custom-call(s32[4]{0:T(128)} %pad_add_fusion.starts_ref, bf16[256,3072]{1,0:T(8,128)(2,1)} %bitcast.35, f32[5,3072]{1,0:T(8,128)} %refs_14_.1), custom_call_target="tpu_custom_call" | custom-call | tf_op jit(solution)/shard_map/norm_in/pallas_call | solution.py:78
  16.6 4.3 %collective-permute-start.3 = (bf16[256,3072]{1,0:T(8,128)(2,1)}, bf16[256,3072]{1,0:T(8,128)(2,1)}, u32[]{:S(2)}, u32[]{:S(2)}) collective-permute-start(bf16[256,3072]{1,0:T(8,128)(2,1)} %norm_in.1.refs_4_), channel_id=1, source_target_pairs={{0,1},{1,2},{2,3},{4,5},{5,6},{6,7},{8,9},{9,10},{10,11},{12,13},{... | collective-permute-start | bytes 4718600 | tf_op jit(solution)/shard_map/ppermute | solution.py:473
  22.2 4.7 %collective-permute-start.4 = (bf16[1,256]{1,0:T(2,128)(2,1)S(1)}, bf16[1,256]{1,0:T(2,128)(2,1)S(1)}, u32[]{:S(2)}, u32[]{:S(2)}) collective-permute-start(bf16[1,256]{1,0:T(2,128)(2,1)S(1)} %get-tuple-element.167), channel_id=1, source_target_pairs={{2,4},{3,5},{6,8},{7,9},{10,12},{11,13},{4,2},{5,3},{8,6},{9,7},{1... | collective-permute-start | bytes 1544 | tf_op jit(solution)/shard_map/ppermute | solution.py:458
  28.6 66.5 %collective-permute-done.4 = bf16[1,256]{1,0:T(2,128)(2,1)S(1)} collective-permute-done((bf16[1,256]{1,0:T(2,128)(2,1)S(1)}, bf16[1,256]{1,0:T(2,128)(2,1)S(1)}, u32[]{:S(2)}, u32[]{:S(2)}) %collective-permute-start.4) | collective-permute-done | bytes 544 | tf_op jit(solution)/shard_map/ppermute | solution.py:458
  95.2 1.3 collective-permute-start.6
  98.6 1.6 collective-permute-start.10
  100.1 1.5 collective-permute-done.5.refs_3_
  101.7 1.9 copy-done.7
  103.5 2.0 copy-done.1
  105.5 1.4 copy-done.3
  106.9 10.5 %project.2 = (bf16[6,512,128]{2,1,0:T(8,128)(2,1)S(1)}, bf16[6,512,128]{2,1,0:T(8,128)(2,1)S(1)}, bf16[6,512,128]{2,1,0:T(8,128)(2,1)S(1)}) custom-call(s32[1]{0:T(128)} %bitcast.18.place_ref, bf16[768,2304]{1,0:T(8,128)(2,1)S(1)} %copy-done.1, bf16[768,2304]{1,0:T(8,128)(2,1)} %collective-permute-done.refs_1_, ...), custom_call_target="tpu_custom_call" | custom-call | tf_op jit(solution)/shard_map/project/pallas_call | solution.py:156
  117.5 15.2 %collective-permute-done.6.refs_4_.refs_12_ = bf16[256,3072]{1,0:T(8,128)(2,1)S(1)} collective-permute-done((bf16[256,3072]{1,0:T(8,128)(2,1)S(1)}, bf16[256,3072]{1,0:T(8,128)(2,1)S(1)}, u32[]{:S(2)}, u32[]{:S(2)}) %collective-permute-start.6) | collective-permute-done | bytes 1572896 | tf_op jit(solution)/shard_map/ppermute | solution.py:473
  136.0 14.0 %collective-permute-done.11.refs_6_.refs_4_ = bf16[3072,384]{1,0:T(8,128)(2,1)} collective-permute-done((bf16[3072,384]{1,0:T(8,128)(2,1)}, bf16[3072,384]{1,0:T(8,128)(2,1)}, u32[]{:S(2)}, u32[]{:S(2)}) %collective-permute-start.11) | collective-permute-done | bytes 2359328 | tf_op jit(solution)/shard_map/ppermute | solution.py:33
  150.0 2.4 slice.17
  152.5 2.4 slice.16
  154.9 7.2 %project.3 = (bf16[6,256,128]{2,1,0:T(8,128)(2,1)S(1)}, bf16[6,256,128]{2,1,0:T(8,128)(2,1)S(1)}, bf16[6,256,128]{2,1,0:T(8,128)(2,1)S(1)}) custom-call(s32[1]{0:T(128)} %bitcast.18.place_ref, bf16[768,2304]{1,0:T(8,128)(2,1)S(1)} %copy-done.1, bf16[768,2304]{1,0:T(8,128)(2,1)} %collective-permute-done.refs_1_, ...), custom_call_target="tpu_custom_call" | custom-call | tf_op jit(solution)/shard_map/project/pallas_call | solution.py:156
  162.1 5.6 %early.1.refs_4_ = bf16[6,768,256]{2,1,0:T(8,128)(2,1)S(1)} custom-call(bf16[6,512,128]{2,1,0:T(8,128)(2,1)S(1)} %get-tuple-element.113.refs_0_.refs_5_, bf16[6,512,128]{2,1,0:T(8,128)(2,1)S(1)} %get-tuple-element.114.refs_1_.refs_6_, bf16[6,512,128]{2,1,0:T(8,128)(2,1)S(1)} %get-tuple-element.115.refs_2_.refs_7_, ...), custom_call_target="tpu_custom_call" | custom-call | tf_op jit(solution)/shard_map/early/pallas_call | solution.py:206
  167.7 1.5 copy-done.2
  169.2 3.3 %collective-permute-done.8.refs_11_ = bf16[256,3072]{1,0:T(8,128)(2,1)S(1)} collective-permute-done((bf16[256,3072]{1,0:T(8,128)(2,1)S(1)}, bf16[256,3072]{1,0:T(8,128)(2,1)S(1)}, u32[]{:S(2)}, u32[]{:S(2)}) %collective-permute-start.8) | collective-permute-done | bytes 1572896 | tf_op jit(solution)/shard_map/ppermute | solution.py:473
  175.6 8.1 %attend.2 = (bf16[256,384]{1,0:T(8,128)(2,1)S(1)}, bf16[256,384]{1,0:T(8,128)(2,1)S(1)}, bf16[256,384]{1,0:T(8,128)(2,1)S(1)}, bf16[256,384]{1,0:T(8,128)(2,1)S(1)}) custom-call(s32[1]{0:T(128)} %bitcast.18.place_ref, s32[4]{0:T(128)S(1)} %dynamic-slice_bitcast_fusion.slots_ref, bf16[768,2304]{1,0:T(8,128)(2,1)} %refs_0_.3, ...), custom_call_target="tpu_custom_call" | custom-call | tf_op jit(solution)/shard_map/attend/pallas_call | solution.py:265
  183.7 2.5 collective-permute-start.15
  186.2 2.2 collective-permute-start.16
  189.4 8.1 %attend.3 = (bf16[256,384]{1,0:T(8,128)(2,1)S(1)}, bf16[256,384]{1,0:T(8,128)(2,1)S(1)}, bf16[256,384]{1,0:T(8,128)(2,1)S(1)}, bf16[256,384]{1,0:T(8,128)(2,1)S(1)}) custom-call(s32[1]{0:T(128)} %bitcast.18.place_ref, s32[4]{0:T(128)S(1)} %dynamic-slice_bitcast_fusion.slots_ref, bf16[768,2304]{1,0:T(8,128)(2,1)} %refs_0_.3, ...), custom_call_target="tpu_custom_call" | custom-call | tf_op jit(solution)/shard_map/attend/pallas_call | solution.py:265
  197.6 3.0 %collective-permute-done.18.refs_10_.refs_8_ = bf16[1536,384]{1,0:T(8,128)(2,1)S(1)} collective-permute-done((bf16[1536,384]{1,0:T(8,128)(2,1)}, bf16[1536,384]{1,0:T(8,128)(2,1)S(1)}, u32[]{:S(2)}, u32[]{:S(2)}) %collective-permute-start.18) | collective-permute-done | bytes 1179680 | tf_op jit(solution)/shard_map/ppermute | solution.py:33
  201.2 1.7 collective-permute-start.23
  203.0 4.3 %collective-permute-start.20 = (bf16[256,384]{1,0:T(8,128)(2,1)S(1)}, bf16[256,384]{1,0:T(8,128)(2,1)S(1)}, u32[]{:S(2)}, u32[]{:S(2)}) collective-permute-start(bf16[256,384]{1,0:T(8,128)(2,1)S(1)} %get-tuple-element.144), channel_id=1, source_target_pairs={{0,2},{1,3},{2,0},{3,1},{4,6},{5,7},{6,4},{7,5},{8,10},{9,11},{10,... | collective-permute-start | bytes 589832 | tf_op jit(solution)/shard_map/ppermute | solution.py:33
  207.5 2.9 %collective-permute-start.22 = (bf16[256,384]{1,0:T(8,128)(2,1)S(1)}, bf16[256,384]{1,0:T(8,128)(2,1)S(1)}, u32[]{:S(2)}, u32[]{:S(2)}) collective-permute-start(bf16[256,384]{1,0:T(8,128)(2,1)S(1)} %get-tuple-element.146), channel_id=1, source_target_pairs={{0,3},{1,0},{2,1},{3,2},{4,7},{5,4},{6,5},{7,6},{8,11},{9,8},{10,9... | collective-permute-start | bytes 589832 | tf_op jit(solution)/shard_map/ppermute | solution.py:33
  210.5 10.5 %add_parts.1.refs_13_ = f32[256,3072]{1,0:T(8,128)} custom-call(s32[8]{0:T(128)S(1)} %stack.79.starts_ref, s32[4]{0:T(128)S(1)} %pad_add_fusion.1.rows_ref, bf16[256,384]{1,0:T(8,128)(2,1)S(1)} %get-tuple-element.155.refs_0_, bf16[256,384]{1,0:T(8,128)(2,1)S(1)} %get-tuple-element.156.refs_1_, bf16[256,384]{1,0:T(8,128)(2,1)S(1)} %collective-permute-done.15.refs_2_, ...), custom_call_target="tpu_custom_call" | custom-call | tf_op jit(solution)/shard_map/add_parts/pallas_call | solution.py:410
  221.0 8.9 %finish.1 = (f32[64,256]{1,0:T(8,128)S(1)}, f32[64,256]{1,0:T(8,128)S(1)}, bf16[128,256]{1,0:T(8,128)(2,1)S(1)}) custom-call(s32[8]{0:T(128)S(1)} %stack.79.starts_ref, s32[4]{0:T(128)S(1)} %pad_add_fusion.1.rows_ref, f32[2]{0:T(128)S(1)} %pad_maximum_fusion.coef_ref, bf16[256,384]{1,0:T(8,128)(2,1)S(1)} %collective-permute-done.20.refs_0_, ...), custom_call_target="tpu_custom_call" | custom-call | tf_op jit(solution)/shard_map/finish/pallas_call | solution.py:422
  229.9 8.0 %collective-permute-start.25 = (bf16[128,256]{1,0:T(8,128)(2,1)S(1)}, bf16[128,256]{1,0:T(8,128)(2,1)S(1)}, u32[]{:S(2)}, u32[]{:S(2)}) collective-permute-start(bf16[128,256]{1,0:T(8,128)(2,1)S(1)} %get-tuple-element.161), channel_id=1, source_target_pairs={{2,4},{3,5},{6,8},{7,9},{10,12},{11,13},{4,2},{5,3},{8,6},{9,7},{1... | collective-permute-start | bytes 196616 | tf_op jit(solution)/shard_map/ppermute | solution.py:614
  237.9 1.9 collective-permute-done.25
  (67 shorter events, 16.5 us)
Async XLA Ops:
  7.2 87.9 %all-gather.2.cloned.1.call-start = ((), (), s32[]{:S(2)}) async-start(), calls=%async_computation | async-start | bytes 2949120 | tf_op jit(solution)/shard_map/all_gather | solution.py:485
  9.4 85.8 %collective-permute-start = (bf16[768,2304]{1,0:T(8,128)(2,1)}, bf16[768,2304]{1,0:T(8,128)(2,1)}, u32[]{:S(2)}, u32[]{:S(2)}) collective-permute-start(bf16[768,2304]{1,0:T(8,128)(2,1)} %refs_0_.3), channel_id=1, source_target_pairs={{0,4},{4,0},{8,12},{12,8},{1,5},{5,1},{9,13},{13,9},{2,6},{6,2},{1... | collective-permute-start | bytes 10616840 | tf_op jit(solution)/shard_map/ppermute | solution.py:18
  9.5 85.6 %collective-permute-start.1 = (bf16[768,2304]{1,0:T(8,128)(2,1)}, bf16[768,2304]{1,0:T(8,128)(2,1)}, u32[]{:S(2)}, u32[]{:S(2)}) collective-permute-start(bf16[768,2304]{1,0:T(8,128)(2,1)} %refs_0_.3), channel_id=1, source_target_pairs={{0,8},{4,12},{8,0},{12,4},{1,9},{5,13},{9,1},{13,5},{2,10},{6,14},... | collective-permute-start | bytes 10616840 | tf_op jit(solution)/shard_map/ppermute | solution.py:18
  16.6 78.5 %collective-permute-start.3 = (bf16[256,3072]{1,0:T(8,128)(2,1)}, bf16[256,3072]{1,0:T(8,128)(2,1)}, u32[]{:S(2)}, u32[]{:S(2)}) collective-permute-start(bf16[256,3072]{1,0:T(8,128)(2,1)} %norm_in.1.refs_4_), channel_id=1, source_target_pairs={{0,1},{1,2},{2,3},{4,5},{5,6},{6,7},{8,9},{9,10},{10,11},{12,13},{... | collective-permute-start | bytes 4718600 | tf_op jit(solution)/shard_map/ppermute | solution.py:473
  20.9 74.2 %collective-permute-start.2 = (bf16[256,3072]{1,0:T(8,128)(2,1)}, bf16[256,3072]{1,0:T(8,128)(2,1)S(1)}, u32[]{:S(2)}, u32[]{:S(2)}) collective-permute-start(bf16[256,3072]{1,0:T(8,128)(2,1)} %norm_in.1.refs_4_), channel_id=1, source_target_pairs={{1,0},{2,1},{3,2},{5,4},{6,5},{7,6},{9,8},{10,9},{11,10},{13,12},{... | collective-permute-start | bytes 4718600 | tf_op jit(solution)/shard_map/ppermute | solution.py:473
  22.2 72.9 %collective-permute-start.4 = (bf16[1,256]{1,0:T(2,128)(2,1)S(1)}, bf16[1,256]{1,0:T(2,128)(2,1)S(1)}, u32[]{:S(2)}, u32[]{:S(2)}) collective-permute-start(bf16[1,256]{1,0:T(2,128)(2,1)S(1)} %get-tuple-element.167), channel_id=1, source_target_pairs={{2,4},{3,5},{6,8},{7,9},{10,12},{11,13},{4,2},{5,3},{8,6},{9,7},{1... | collective-permute-start | bytes 1544 | tf_op jit(solution)/shard_map/ppermute | solution.py:458
  95.2 6.5 %collective-permute-start.5 = (bf16[768,2304]{1,0:T(8,128)(2,1)}, bf16[768,2304]{1,0:T(8,128)(2,1)S(1)}, u32[]{:S(2)}, u32[]{:S(2)}) collective-permute-start(bf16[768,2304]{1,0:T(8,128)(2,1)} %collective-permute-done.1.refs_2_), channel_id=1, source_target_pairs={{0,4},{4,0},{8,12},{12,8},{1,5},{5,1},{9,13},{13,9},{2,6},{6,2},{1... | collective-permute-start | bytes 10616840 | tf_op jit(solution)/shard_map/ppermute | solution.py:18
  95.2 37.5 %collective-permute-start.6 = (bf16[256,3072]{1,0:T(8,128)(2,1)S(1)}, bf16[256,3072]{1,0:T(8,128)(2,1)S(1)}, u32[]{:S(2)}, u32[]{:S(2)}) collective-permute-start(bf16[256,3072]{1,0:T(8,128)(2,1)S(1)} %collective-permute-done.2.refs_5_), channel_id=1, source_target_pairs={{1,0},{2,1},{5,4},{6,5},{9,8},{10,9},{13,12},{14,13},{17,16},{18,1... | collective-permute-start | bytes 4718600 | tf_op jit(solution)/shard_map/ppermute | solution.py:473
  96.5 36.2 %collective-permute-start.7 = (bf16[256,3072]{1,0:T(8,128)(2,1)}, bf16[256,3072]{1,0:T(8,128)(2,1)S(1)}, u32[]{:S(2)}, u32[]{:S(2)}) collective-permute-start(bf16[256,3072]{1,0:T(8,128)(2,1)} %collective-permute-done.3.refs_6_), channel_id=1, source_target_pairs={{1,2},{2,3},{5,6},{6,7},{9,10},{10,11},{13,14},{14,15},{17,18},{18... | collective-permute-start | bytes 4718600 | tf_op jit(solution)/shard_map/ppermute | solution.py:473
  97.3 52.7 %collective-permute-start.11 = (bf16[3072,384]{1,0:T(8,128)(2,1)}, bf16[3072,384]{1,0:T(8,128)(2,1)}, u32[]{:S(2)}, u32[]{:S(2)}) collective-permute-start(bf16[3072,384]{1,0:T(8,128)(2,1)} %all-gather.2.cloned.1.call-done.refs_5_.refs_3_), channel_id=1, source_target_pairs={{0,16},{16,0},{1,17},{17,1},{2,18},{18,2},{3,19},{19,3},{4,20},{20... | collective-permute-start | bytes 7077896 | tf_op jit(solution)/shard_map/ppermute | solution.py:33
  98.6 53.9 %collective-permute-start.10 = (bf16[3072,384]{1,0:T(8,128)(2,1)}, bf16[3072,384]{1,0:T(8,128)(2,1)}, u32[]{:S(2)}, u32[]{:S(2)}) collective-permute-start(bf16[3072,384]{1,0:T(8,128)(2,1)} %all-gather.2.cloned.1.call-done.refs_5_.refs_3_), channel_id=1, source_target_pairs={{0,8},{4,12},{8,0},{12,4},{1,9},{5,13},{9,1},{13,5},{2,10},{6,14},... | collective-permute-start | bytes 7077896 | tf_op jit(solution)/shard_map/ppermute | solution.py:18
  132.7 39.7 %collective-permute-start.12 = (bf16[3072,384]{1,0:T(8,128)(2,1)}, bf16[3072,384]{1,0:T(8,128)(2,1)S(1)}, u32[]{:S(2)}, u32[]{:S(2)}) collective-permute-start(bf16[3072,384]{1,0:T(8,128)(2,1)} %all-gather.2.cloned.1.call-done.refs_5_.refs_3_), channel_id=1, source_target_pairs={{0,4},{4,0},{8,12},{12,8},{1,5},{5,1},{9,13},{13,9},{2,6},{6,2},{1... | collective-permute-start | bytes 7077896 | tf_op jit(solution)/shard_map/ppermute | solution.py:18
  133.9 38.5 %collective-permute-start.8 = (bf16[256,3072]{1,0:T(8,128)(2,1)S(1)}, bf16[256,3072]{1,0:T(8,128)(2,1)S(1)}, u32[]{:S(2)}, u32[]{:S(2)}) collective-permute-start(bf16[256,3072]{1,0:T(8,128)(2,1)S(1)} %collective-permute-done.6.refs_4_.refs_12_), channel_id=1, source_target_pairs={{1,0},{5,4},{9,8},{13,12},{17,16},{21,20},{25,24},{29,28}} | collective-permute-start | bytes 4718600 | tf_op jit(solution)/shard_map/ppermute | solution.py:473
  135.2 37.2 %collective-permute-start.9 = (bf16[256,3072]{1,0:T(8,128)(2,1)S(1)}, bf16[256,3072]{1,0:T(8,128)(2,1)S(1)}, u32[]{:S(2)}, u32[]{:S(2)}) collective-permute-start(bf16[256,3072]{1,0:T(8,128)(2,1)S(1)} %collective-permute-done.7.refs_6_.refs_13_), channel_id=1, source_target_pairs={{2,3},{6,7},{10,11},{14,15},{18,19},{22,23},{26,27},{30,31}} | collective-permute-start | bytes 4718600 | tf_op jit(solution)/shard_map/ppermute | solution.py:473
  162.1 12.3 %copy-start.10 = (bf16[1536,384]{1,0:T(8,128)(2,1)S(1)}, bf16[1536,384]{1,0:T(8,128)(2,1)}, u32[]{:S(2)}) copy-start(bf16[1536,384]{1,0:T(8,128)(2,1)} %slice.17) | copy-start | bytes 3538948
  172.5 11.2 %collective-permute-start.13 = (bf16[3072,384]{1,0:T(8,128)(2,1)}, bf16[3072,384]{1,0:T(8,128)(2,1)S(1)}, u32[]{:S(2)}, u32[]{:S(2)}) collective-permute-start(bf16[3072,384]{1,0:T(8,128)(2,1)} %collective-permute-done.11.refs_6_.refs_4_), channel_id=1, source_target_pairs={{0,4},{4,0},{8,12},{12,8},{1,5},{5,1},{9,13},{13,9},{2,6},{6,2},{1... | collective-permute-start | bytes 7077896 | tf_op jit(solution)/shard_map/ppermute | solution.py:18
  173.1 10.6 %collective-permute-start.14 = (bf16[3072,384]{1,0:T(8,128)(2,1)}, bf16[3072,384]{1,0:T(8,128)(2,1)}, u32[]{:S(2)}, u32[]{:S(2)}) collective-permute-start(bf16[3072,384]{1,0:T(8,128)(2,1)} %collective-permute-done.10.refs_9_.refs_7_), channel_id=1, source_target_pairs={{0,4},{4,0},{8,12},{12,8},{1,5},{5,1},{9,13},{13,9},{2,6},{6,2},{1... | collective-permute-start | bytes 7077896 | tf_op jit(solution)/shard_map/ppermute | solution.py:18
  173.2 27.3 %collective-permute-start.18 = (bf16[1536,384]{1,0:T(8,128)(2,1)}, bf16[1536,384]{1,0:T(8,128)(2,1)S(1)}, u32[]{:S(2)}, u32[]{:S(2)}) collective-permute-start(bf16[1536,384]{1,0:T(8,128)(2,1)} %slice.16), channel_id=1, source_target_pairs={{0,16},{16,0},{1,17},{17,1},{2,18},{18,2},{3,19},{19,3},{4,20},{20... | collective-permute-start | bytes 3538952 | tf_op jit(solution)/shard_map/ppermute | solution.py:33
  174.4 26.8 %collective-permute-start.19 = (bf16[1536,384]{1,0:T(8,128)(2,1)S(1)}, bf16[1536,384]{1,0:T(8,128)(2,1)S(1)}, u32[]{:S(2)}, u32[]{:S(2)}) collective-permute-start(bf16[1536,384]{1,0:T(8,128)(2,1)S(1)} %copy-done.10), channel_id=1, source_target_pairs={{0,8},{4,12},{8,0},{12,4},{1,9},{5,13},{9,1},{13,5},{2,10},{6,14},... | collective-permute-start | bytes 3538952 | tf_op jit(solution)/shard_map/ppermute | solution.py:18
  183.7 13.9 %copy-start.9 = (bf16[3072,384]{1,0:T(8,128)(2,1)}, bf16[3072,384]{1,0:T(8,128)(2,1)S(1)}, u32[]{:S(2)}) copy-start(bf16[3072,384]{1,0:T(8,128)(2,1)S(1)} %collective-permute-done.13.refs_8_.refs_6_) | copy-start | bytes 7077892
  183.7 26.8 %copy-start.4 = (f32[5,3072]{1,0:T(8,128)S(1)}, f32[5,3072]{1,0:T(8,128)}, u32[]{:S(2)}) copy-start(f32[5,3072]{1,0:T(8,128)} %refs_14_.1) | copy-start | bytes 184324
  183.7 17.5 %collective-permute-start.15 = (bf16[256,384]{1,0:T(8,128)(2,1)S(1)}, bf16[256,384]{1,0:T(8,128)(2,1)S(1)}, u32[]{:S(2)}, u32[]{:S(2)}) collective-permute-start(bf16[256,384]{1,0:T(8,128)(2,1)S(1)} %get-tuple-element.139), channel_id=1, source_target_pairs={{0,2},{1,3},{2,0},{3,1},{4,6},{5,7},{6,4},{7,5},{8,10},{9,11},{10,... | collective-permute-start | bytes 589832 | tf_op jit(solution)/shard_map/ppermute | solution.py:33
  186.2 15.0 %collective-permute-start.16 = (bf16[256,384]{1,0:T(8,128)(2,1)S(1)}, bf16[256,384]{1,0:T(8,128)(2,1)S(1)}, u32[]{:S(2)}, u32[]{:S(2)}) collective-permute-start(bf16[256,384]{1,0:T(8,128)(2,1)S(1)} %get-tuple-element.140), channel_id=1, source_target_pairs={{0,1},{1,2},{2,3},{3,0},{4,5},{5,6},{6,7},{7,4},{8,9},{9,10},{10,1... | collective-permute-start | bytes 589832 | tf_op jit(solution)/shard_map/ppermute | solution.py:33
  188.4 12.8 %collective-permute-start.17 = (bf16[256,384]{1,0:T(8,128)(2,1)S(1)}, bf16[256,384]{1,0:T(8,128)(2,1)S(1)}, u32[]{:S(2)}, u32[]{:S(2)}) collective-permute-start(bf16[256,384]{1,0:T(8,128)(2,1)S(1)} %get-tuple-element.141), channel_id=1, source_target_pairs={{0,3},{1,0},{2,1},{3,2},{4,7},{5,4},{6,5},{7,6},{8,11},{9,8},{10,9... | collective-permute-start | bytes 589832 | tf_op jit(solution)/shard_map/ppermute | solution.py:33
  201.2 19.8 %copy-start.5 = (bf16[3072,64]{0,1:T(8,128)(2,1)S(1)}, bf16[3072,64]{0,1:T(8,128)(2,1)}, u32[]{:S(2)}) copy-start(bf16[3072,64]{0,1:T(8,128)(2,1)} %param.13) | copy-start | bytes 1179652
  201.2 19.8 %copy-start.6 = (f32[1,256,64]{1,2,0:T(8,128)S(1)}, f32[1,256,64]{1,2,0:T(8,128)}, u32[]{:S(2)}) copy-start(f32[1,256,64]{1,2,0:T(8,128)} %param.14) | copy-start | bytes 196612
  201.2 9.3 %collective-permute-start.23 = (bf16[1536,384]{1,0:T(8,128)(2,1)S(1)}, bf16[1536,384]{1,0:T(8,128)(2,1)S(1)}, u32[]{:S(2)}, u32[]{:S(2)}) collective-permute-start(bf16[1536,384]{1,0:T(8,128)(2,1)S(1)} %collective-permute-done.18.refs_10_.refs_8_), channel_id=1, source_target_pairs={{0,4},{4,0},{8,12},{12,8},{1,5},{5,1},{9,13},{13,9},{2,6},{6,2},{1... | collective-permute-start | bytes 3538952 | tf_op jit(solution)/shard_map/ppermute | solution.py:18
  202.9 7.6 %collective-permute-start.24 = (bf16[1536,384]{1,0:T(8,128)(2,1)S(1)}, bf16[1536,384]{1,0:T(8,128)(2,1)S(1)}, u32[]{:S(2)}, u32[]{:S(2)}) collective-permute-start(bf16[1536,384]{1,0:T(8,128)(2,1)S(1)} %collective-permute-done.19.refs_11_.refs_9_), channel_id=1, source_target_pairs={{0,4},{4,0},{8,12},{12,8},{1,5},{5,1},{9,13},{13,9},{2,6},{6,2},{1... | collective-permute-start | bytes 3538952 | tf_op jit(solution)/shard_map/ppermute | solution.py:18
  203.0 18.0 %collective-permute-start.20 = (bf16[256,384]{1,0:T(8,128)(2,1)S(1)}, bf16[256,384]{1,0:T(8,128)(2,1)S(1)}, u32[]{:S(2)}, u32[]{:S(2)}) collective-permute-start(bf16[256,384]{1,0:T(8,128)(2,1)S(1)} %get-tuple-element.144), channel_id=1, source_target_pairs={{0,2},{1,3},{2,0},{3,1},{4,6},{5,7},{6,4},{7,5},{8,10},{9,11},{10,... | collective-permute-start | bytes 589832 | tf_op jit(solution)/shard_map/ppermute | solution.py:33
  207.2 13.8 %collective-permute-start.21 = (bf16[256,384]{1,0:T(8,128)(2,1)S(1)}, bf16[256,384]{1,0:T(8,128)(2,1)S(1)}, u32[]{:S(2)}, u32[]{:S(2)}) collective-permute-start(bf16[256,384]{1,0:T(8,128)(2,1)S(1)} %get-tuple-element.145), channel_id=1, source_target_pairs={{0,1},{1,2},{2,3},{3,0},{4,5},{5,6},{6,7},{7,4},{8,9},{9,10},{10,1... | collective-permute-start | bytes 589832 | tf_op jit(solution)/shard_map/ppermute | solution.py:33
  207.5 13.5 %collective-permute-start.22 = (bf16[256,384]{1,0:T(8,128)(2,1)S(1)}, bf16[256,384]{1,0:T(8,128)(2,1)S(1)}, u32[]{:S(2)}, u32[]{:S(2)}) collective-permute-start(bf16[256,384]{1,0:T(8,128)(2,1)S(1)} %get-tuple-element.146), channel_id=1, source_target_pairs={{0,3},{1,0},{2,1},{3,2},{4,7},{5,4},{6,5},{7,6},{8,11},{9,8},{10,9... | collective-permute-start | bytes 589832 | tf_op jit(solution)/shard_map/ppermute | solution.py:33
  229.9 9.9 %collective-permute-start.25 = (bf16[128,256]{1,0:T(8,128)(2,1)S(1)}, bf16[128,256]{1,0:T(8,128)(2,1)S(1)}, u32[]{:S(2)}, u32[]{:S(2)}) collective-permute-start(bf16[128,256]{1,0:T(8,128)(2,1)S(1)} %get-tuple-element.161), channel_id=1, source_target_pairs={{2,4},{3,5},{6,8},{7,9},{10,12},{11,13},{4,2},{5,3},{8,6},{9,7},{1... | collective-permute-start | bytes 196616 | tf_op jit(solution)/shard_map/ppermute | solution.py:614
  (7 other events, 28.7 us)
Sparse Core Ops, SparseCore 0:
  9.6 82.4 all-gather.1
